TPU v7x, 128 devices: a whole 4x4x4 slice. The times are simulated.
128 devices in a mesh: ctx: 32 (over x_lo, y, z), tp: 4 (over x_hi, core).
Axes of the slice: x: 4 (x_hi: 2, x_lo: 2; x = x_hi * 2 + x_lo), y: 4, z: 4, core: 2. Of those that a mesh axis runs over, the one named last changes fastest.
Arguments:
- queries: bfloat16 [32768, 2048], P('ctx', 'tp'), may hold values from -24 to 24
- keys: bfloat16 [32768, 2048], P('ctx', 'tp'), may hold values from -4 to 4
- values: bfloat16 [32768, 2048], P('ctx', 'tp'), may hold values from -6 to 6
- out_weight: bfloat16 [2048, 4096], P('tp'), may hold values from -0.125 to 0.125
- out_grad: bfloat16 [32768, 4096], P('ctx', 'tp'), may hold values from -6 to 6
- spans: int32 [64, 2], replicated, may hold values from 0 to 64, as said below
- pairs: int32 [192, 2], replicated, may hold values from 0 to 63, as said below
Outputs:
- mixed: bfloat16 [32768, 4096], P('ctx', 'tp')
- query_grad: bfloat16 [32768, 2048], P('ctx', 'tp')
- key_grad: bfloat16 [32768, 2048], P('ctx', 'tp')
- value_grad: bfloat16 [32768, 2048], P('ctx', 'tp')
- weight_grad: float32 [2048, 4096], P('tp', 'ctx')
Inputs may be any that keep to these rules, and one draw needn't show every extreme that they name: `spans`: recordings do not intersect and lie in order; an empty slot has 0 blocks; some recording has exactly 8 blocks, none more; unused slots start at 64. `pairs`: every listed pair (a, b) has 0 <= a - b < 4; each block a appears in exactly three rows as query block, one of them (a, a); rows may repeat and come in any order.
All inputs are finite; a program needn't handle non-finite values.
Results may differ from a plain program's by a relative error of at most 0.017.
Values may be sent and summed in bfloat16 or wider, within the bound.
No kernel may reach another device: no remote copies, remote signals or barrier semaphores. Data moves between devices by JAX's collectives and lax.ppermute only.
A program may use at most 256 MiB of HBM per device.

v0:
```python
import math

import jax
import jax.numpy as jnp
import numpy as np
from jax import lax
from jax.sharding import PartitionSpec as P

HDIM = 128
BLK = 512
WIN = 4


def from_behind(value, axis, steps):
    count = lax.axis_size(axis)
    leading, last = (max(0, -steps), min(count, count - steps))
    return lax.ppermute(value, axis, [(source, source + steps) for source in range(leading, last)])


def block_rule(spans, pairs, query_block, key_block):
    listed = jnp.any(
        (pairs[:, 0] == query_block[..., None]) & (pairs[:, 1] == key_block[..., None]), axis=-1
    )
    span_lower = spans[:, 0]
    span_upper = spans[:, 0] + spans[:, 1]
    query_inside = (span_lower <= query_block[..., None]) & (query_block[..., None] < span_upper)
    key_inside = (span_lower <= key_block[..., None]) & (key_block[..., None] < span_upper)
    same = jnp.any(query_inside & key_inside, axis=-1)
    reach = (query_block - key_block >= 0) & (query_block - key_block < WIN)
    return listed & same & reach


def tile_weights(query_rows, key_rows, block_fine):
    scale = 1.0 / math.sqrt(HDIM)
    scores = (
        jnp.einsum("thd,oshd->ohts", query_rows, key_rows, preferred_element_type=jnp.float32)
        * scale
    )
    position = jnp.arange(BLK, dtype=jnp.int32)
    causal = position[:, None] >= position[None, :]
    later = (jnp.arange(WIN, dtype=jnp.int32) > 0)[:, None, None]
    allowed = block_fine[:, None, None] & (later | causal[None])
    allowed_heads = allowed[:, None]
    masked = jnp.where(allowed_heads, scores, -jnp.inf)
    row_max = jnp.max(masked, axis=(0, 3))
    has_any = jnp.any(allowed, axis=(0, 2))
    row_max = jnp.where(has_any[None, :], row_max, 0.0)
    expo = jnp.where(allowed_heads, jnp.exp(scores - row_max[None, :, :, None]), 0.0)
    total = jnp.sum(expo, axis=(0, 3))
    return expo / jnp.where(total > 0, total, 1.0)[None, :, :, None]


def per_device(queries, keys, values, out_weight, out_grad, spans, pairs):
    scale = 1.0 / math.sqrt(HDIM)
    row_count, width = queries.shape
    q_blocks = row_count // BLK
    head_count = width // HDIM
    dev_back = (WIN + q_blocks - 2) // q_blocks
    first_block = lax.axis_index("ctx") * q_blocks
    packed = jnp.stack([keys, values])
    arrived = [packed]
    for distance in range(1, dev_back + 1):
        arrived.append(from_behind(packed, "ctx", distance))
    extended = jnp.concatenate(arrived[::-1], axis=1)
    total_blocks = (dev_back + 1) * q_blocks
    ext_blocks = extended.reshape(2, total_blocks, BLK, head_count, HDIM)
    tile_index = dev_back * q_blocks + np.arange(q_blocks)[:, None] - np.arange(WIN)[None, :]
    tiles = jnp.take(ext_blocks, tile_index.astype(np.int32), axis=1)
    key_tiles = tiles[0]
    value_tiles = tiles[1]
    query_four = queries.reshape(q_blocks, BLK, head_count, HDIM)
    query_block = (
        first_block
        + jnp.arange(q_blocks, dtype=jnp.int32)[:, None]
        + jnp.zeros((1, WIN), jnp.int32)
    )
    key_block = query_block - jnp.arange(WIN, dtype=jnp.int32)[None, :]
    block_fine = block_rule(spans, pairs, query_block, key_block)

    def forward_tile(inputs):
        query_rows, key_rows, value_rows, fine_row = inputs
        weights = tile_weights(query_rows, key_rows, fine_row)
        weights_low = weights.astype(jnp.bfloat16)
        out_rows = jnp.einsum(
            "ohts,oshd->thd", weights_low, value_rows, preferred_element_type=jnp.float32
        )
        return out_rows.astype(jnp.bfloat16)

    attention = lax.map(forward_tile, (query_four, key_tiles, value_tiles, block_fine)).reshape(
        row_count, width
    )
    partial_out = jnp.dot(attention, out_weight, preferred_element_type=jnp.float32)
    mixed = lax.psum_scatter(partial_out, "tp", scatter_dimension=1, tiled=True).astype(
        jnp.bfloat16
    )
    full_grad = lax.all_gather(out_grad, "tp", axis=1, tiled=True)
    attn_grad = lax.dot_general(
        full_grad, out_weight, (((1,), (1,)), ((), ())), preferred_element_type=jnp.float32
    ).astype(jnp.bfloat16)
    weight_term = lax.dot_general(
        attention, full_grad, (((0,), (0,)), ((), ())), preferred_element_type=jnp.float32
    )
    weight_grad = lax.psum_scatter(weight_term, "ctx", scatter_dimension=1, tiled=True)
    grad_four = attn_grad.reshape(q_blocks, BLK, head_count, HDIM)
    attn_four = attention.reshape(q_blocks, BLK, head_count, HDIM)

    def backward_tile(inputs):
        query_rows, key_rows, value_rows, fine_row, grad_rows, attn_rows = inputs
        weights = tile_weights(query_rows, key_rows, fine_row)
        weights_low = weights.astype(jnp.bfloat16)
        delta = jnp.einsum("thd,thd->ht", grad_rows, attn_rows, preferred_element_type=jnp.float32)
        weights_grad = jnp.einsum(
            "thd,oshd->ohts", grad_rows, value_rows, preferred_element_type=jnp.float32
        )
        score_grad = (weights * (weights_grad - delta[None, :, :, None])).astype(jnp.bfloat16)
        query_part = (
            jnp.einsum("ohts,oshd->thd", score_grad, key_rows, preferred_element_type=jnp.float32)
            * scale
        )
        key_part = (
            jnp.einsum("ohts,thd->oshd", score_grad, query_rows, preferred_element_type=jnp.float32)
            * scale
        )
        value_part = jnp.einsum(
            "ohts,thd->oshd", weights_low, grad_rows, preferred_element_type=jnp.float32
        )
        return (query_part.astype(jnp.bfloat16), key_part, value_part)

    query_grad, key_parts, value_parts = lax.map(
        backward_tile, (query_four, key_tiles, value_tiles, block_fine, grad_four, attn_four)
    )
    query_grad = query_grad.reshape(row_count, width)
    grad_tiles = jnp.stack([key_parts, value_parts])
    placement = (np.arange(total_blocks)[:, None, None] == tile_index[None]).astype(np.float32)
    ext_grad = jnp.einsum(
        "ebo,xboshd->xeshd", jnp.asarray(placement), grad_tiles, precision=lax.Precision.HIGHEST
    )
    ext_grad = ext_grad.reshape(2, dev_back + 1, row_count, width)
    summed = ext_grad[:, dev_back]
    for distance in range(1, dev_back + 1):
        summed = summed + from_behind(ext_grad[:, dev_back - distance], "ctx", -distance)
    key_grad = summed[0].astype(jnp.bfloat16)
    value_grad = summed[1].astype(jnp.bfloat16)
    return (mixed, query_grad, key_grad, value_grad, weight_grad)


def solution(mesh):
    placed = (
        P("ctx", "tp"),
        P("ctx", "tp"),
        P("ctx", "tp"),
        P("tp", None),
        P("ctx", "tp"),
        P(),
        P(),
    )
    return jax.shard_map(
        per_device,
        mesh=mesh,
        in_specs=placed,
        out_specs=(P("ctx", "tp"), P("ctx", "tp"), P("ctx", "tp"), P("ctx", "tp"), P("tp", "ctx")),
        check_vma=False,
    )
```

profile of v0, /device:TPU:30, one launch (start us, length us, event | category | flops | bytes accessed | tf_op | source)
XLA Modules:
  0.0 797.5 jit_solution(12926186837827423373)
XLA Ops:
  7.3 3.2 pad_maximum_fusion
  10.5 3.8 collective-permute-start.1
  14.3 5.5 collective-permute-start
  22.9 85.4 %collective-permute-done.1 = bf16[2,1024,512]{2,1,0:T(8,128)(2,1)} collective-permute-done((bf16[2,1024,512]{2,1,0:T(8,128)(2,1)}, bf16[2,1024,512]{2,1,0:T(8,128)(2,1)}, u32[]{:S(2)}, u32[]{:S(2)}) %collective-permute-start.1) | collective-permute-done | bytes 2097184 | tf_op jit(solution)/shard_map/ppermute | solution.py:17
  108.2 5.5 maximum_maximum_fusion
  113.8 9.7 %reshape.155 = bf16[2,6,512,4,128]{4,3,2,1,0:T(4,128)(2,1)} reshape(bf16[2,3072,512]{2,1,0:T(8,128)(2,1)} %maximum_maximum_fusion) | data formatting | bytes 12582912 | tf_op jit(solution)/shard_map/reshape | solution.py:66
  123.5 7.1 copy.101
  130.6 7.5 gather_fusion
  138.1 5.1 slice_bitcast_fusion.3
  146.7 43.8 %while.24 = (s32[]{:T(128)}, bf16[2,512,4,128]{3,2,1,0:T(4,128)(2,1)}, bf16[2,4,512,4,128]{4,2,3,1,0:T(8,128)(2,1)}, pred[2,4]{1,0:T(4,128)(4,1)S(1)}, bf16[2,4,...) while((s32[]{:T(128)}, bf16[2,512,4,128]{3,2,1,0:T(4,128)(2,1)}, ...), condition=%wide.region_6.7_spmd, body=%wide.region_2.6_spmd.sunk | while | flops 2201486848 | bytes 87632072 | solution.py:89
  151.8 4.5 fusion.115
  156.3 3.7 fusion.116
  160.0 7.0 fusion.117
  173.7 4.5 fusion.115
  178.2 3.7 fusion.116
  181.9 7.0 fusion.117
  190.6 12.8 %fusion.79 = f32[1024,4096]{1,0:T(8,128)} fusion(bf16[512,4096]{1,0:T(8,128)(2,1)} %param.16, bf16[128,8,4,128]{3,2,1,0:T(4,128)(2,1)} %bitcast.280), kind=kOutput, calls=%fused_computation.99 | convolution fusion | flops 4294967296 | bytes 22020096 | tf_op jit(solution)/shard_map/dot_general | solution.py:92
  203.4 10.1 %convolution_convert_fusion = bf16[1024,512]{1,0:T(8,128)(2,1)} fusion(bf16[1024,4096]{1,0:T(8,128)(2,1)} %all-gather.2.cloned.1.call-done, bf16[512,4096]{1,0:T(8,128)(2,1)} %param.16), kind=kOutput, calls=%fused_computation.95 | convolution fusion | flops 4295491584 | bytes 13631488 | tf_op jit(solution)/shard_map/dot_general | solution.py:97
  214.9 10.2 %fusion.77 = f32[512,4096]{1,0:T(8,128)} fusion(bf16[1024,4096]{1,0:T(8,128)(2,1)} %all-gather.2.cloned.1.call-done, bf16[128,8,4,128]{3,2,1,0:T(4,128)(2,1)S(1)} %bitcast.281), kind=kOutput, calls=%fused_computation.97 | convolution fusion | flops 4294967296 | bytes 17825792 | tf_op jit(solution)/shard_map/dot_general | solution.py:100
  226.5 133.8 %while.25 = (s32[]{:T(128)}, bf16[2,512,4,128]{3,2,1,0:T(4,128)(2,1)}, f32[2,4,512,4,128]{4,1,0,3,2:T(4,128)}, f32[2,4,512,4,128]{4,1,0,3,2:T(4,128)}, bf16[2,4,...) while((s32[]{:T(128)}, ...), condition=%wide.region_12.13_spmd, body=%wide.region_8.12_spmd.sunk | while | flops 5454429696 | bytes 268560672 | solution.py:129
  230.0 4.5 fusion.127
  234.5 3.7 fusion.128
  240.2 7.0 fusion.131
  247.2 11.6 %fusion.129 = bf16[4,4,512,512]{2,3,0,1:T(8,128)(2,1)} fusion(f32[4,512]{1,0:T(4,128)S(1)} %copy.197, f32[4,512]{1,0:T(4,128)S(1)} %compare_select_fusion.5, f32[4,512]{1,0:T(4,128)S(1)} %broadcast_select_fusion.5, f32[4,4,512,512]{3,2,1,0:T(8,128)} %copy-done.1, pred[4,512,512]{1,2,0:T(8,128)(4,1)S(1)} %get-tuple-element.337, ...), kind=kOutput, calls=%fused_computation.30.clone.1 | convolution fusion | flops 1103101952 | bytes 28860420 | tf_op jit(solution)/shard_map/while/body/eval_jaxpr/thd,oshd->ohts/dot_general | solution.py:112
  258.9 6.0 copy.199
  264.8 8.0 %fusion.130 = bf16[1,512,4,128]{1,3,2,0:T(8,128)(2,1)S(1)} fusion(bf16[4,4,512,512]{2,3,0,1:T(8,128)(2,1)} %fusion.129, bf16[2,4,512,4,128]{4,2,1,3,0:T(8,128)(2,1)} %get-tuple-element.390, s32[]{:T(128)S(6)} %copy.215), kind=kOutput, calls=%fused_computation.53.clone.1 | convolution fusion | flops 1074266112 | bytes 11010052 | tf_op jit(solution)/shard_map/while/body/eval_jaxpr/ohts,oshd->thd/dot_general | solution.py:117
  275.6 4.9 multiply_bitcast_fusion.2
  280.5 5.4 copy.200
  287.2 8.5 %constant_dynamic-update-slice_fusion.9 = (f32[2,4,512,4,128]{4,1,0,3,2:T(4,128)}, f32[2,4,512,4,128]{4,1,0,3,2:T(4,128)}) fusion(f32[2,4,512,4,128]{4,1,0,3,2:T(4,128)} %get-tuple-element.378, f32[1,4,512,4,128]{4,1,0,3,2:T(4,128)} %copy.199, s32[]{:T(128)S(6)} %copy.215, f32[2,4,512,4,128]{4,1,0,3,2:T(4,128)} %get-tuple-element.377, ...), kind=kLoop, calls=%fused_computation.68.clone.1 | loop fusion | bytes 16777220 | tf_op jit(solution)/shard_map/while/body/jit(dynamic_update_index_in_dim)/dynamic_update_slice | solution.py:129
  298.9 4.6 fusion.127
  303.6 3.7 fusion.128
  309.3 7.0 fusion.131
  316.3 11.7 %fusion.129 = bf16[4,4,512,512]{2,3,0,1:T(8,128)(2,1)} fusion(f32[4,512]{1,0:T(4,128)S(1)} %copy.197, f32[4,512]{1,0:T(4,128)S(1)} %compare_select_fusion.5, f32[4,512]{1,0:T(4,128)S(1)} %broadcast_select_fusion.5, f32[4,4,512,512]{3,2,1,0:T(8,128)} %copy-done.1, pred[4,512,512]{1,2,0:T(8,128)(4,1)S(1)} %get-tuple-element.337, ...), kind=kOutput, calls=%fused_computation.30.clone.1 | convolution fusion | flops 1103101952 | bytes 28860420 | tf_op jit(solution)/shard_map/while/body/eval_jaxpr/thd,oshd->ohts/dot_general | solution.py:112
  328.0 5.5 copy.199
  333.6 5.6 fusion.130
  340.2 4.9 multiply_bitcast_fusion.2
  345.1 5.4 copy.200
  351.8 8.3 %constant_dynamic-update-slice_fusion.9 = (f32[2,4,512,4,128]{4,1,0,3,2:T(4,128)}, f32[2,4,512,4,128]{4,1,0,3,2:T(4,128)}) fusion(f32[2,4,512,4,128]{4,1,0,3,2:T(4,128)} %get-tuple-element.378, f32[1,4,512,4,128]{4,1,0,3,2:T(4,128)} %copy.199, s32[]{:T(128)S(6)} %copy.215, f32[2,4,512,4,128]{4,1,0,3,2:T(4,128)} %get-tuple-element.377, ...), kind=kLoop, calls=%fused_computation.68.clone.1 | loop fusion | bytes 16777220 | tf_op jit(solution)/shard_map/while/body/jit(dynamic_update_index_in_dim)/dynamic_update_slice | solution.py:129
  360.3 26.9 %fusion.71 = f32[2,6,512,4,128]{4,1,3,2,0:T(8,128)} fusion(f32[6,2,4,1,1,1]{0,2,1,5,4,3:T(4,128)S(1)} %copy-done.15, f32[1,2,4,512,4,128]{5,2,1,4,3,0:T(4,128)} %bitcast.290, f32[1,2,4,512,4,128]{5,2,1,4,3,0:T(4,128)} %bitcast.291), kind=kOutput, calls=%fused_computation.84 | convolution fusion | flops 306184192 | bytes 29360320 | tf_op jit(solution)/shard_map/ebo,xboshd->xeshd/dot_general | solution.py:135
  387.1 15.0 %copy.114 = f32[2,6,512,4,128]{4,3,2,1,0:T(4,128)} copy(f32[2,6,512,4,128]{4,1,3,2,0:T(8,128)} %fusion.71) | data formatting | bytes 25165824 | tf_op jit(solution)/shard_map/ebo,xboshd->xeshd/transpose | solution.py:135
  402.1 15.3 %reshape.160 = f32[2,3,1024,512]{3,2,1,0:T(8,128)} reshape(f32[2,6,512,4,128]{4,3,2,1,0:T(4,128)} %copy.114) | data formatting | bytes 25165824 | tf_op jit(solution)/shard_map/reshape | solution.py:138
  417.5 4.6 slice_bitcast_fusion.1
  422.1 43.6 %collective-permute-start.2 = (f32[2,1024,512]{2,1,0:T(8,128)S(1)}, f32[2,1024,512]{2,1,0:T(8,128)S(1)}, u32[]{:S(2)}, u32[]{:S(2)}) collective-permute-start(f32[2,1024,512]{2,1,0:T(8,128)S(1)} %get-tuple-element.217), channel_id=1, source_target_pairs={{4,0},{8,4},{12,8},{16,12},{20,16},{24,20},{28,24},{32,28},{36,32}... | collective-permute-start | bytes 12582920 | tf_op jit(solution)/shard_map/ppermute | solution.py:17
  465.7 3.6 collective-permute-start.3
  470.5 221.7 %collective-permute-done.2 = f32[2,1024,512]{2,1,0:T(8,128)S(1)} collective-permute-done((f32[2,1024,512]{2,1,0:T(8,128)S(1)}, f32[2,1024,512]{2,1,0:T(8,128)S(1)}, u32[]{:S(2)}, u32[]{:S(2)}) %collective-permute-start.2) | collective-permute-done | bytes 4194336 | tf_op jit(solution)/shard_map/ppermute | solution.py:17
  692.1 89.7 %collective-permute-done.3 = f32[2,1024,512]{2,1,0:T(8,128)S(1)} collective-permute-done((f32[2,1024,512]{2,1,0:T(8,128)S(1)}, f32[2,1024,512]{2,1,0:T(8,128)S(1)}, u32[]{:S(2)}, u32[]{:S(2)}) %collective-permute-start.3) | collective-permute-done | bytes 4194336 | tf_op jit(solution)/shard_map/ppermute | solution.py:17
  781.9 3.5 fusion.76
  786.9 3.8 convert_element_type.35
  (122 shorter events, 42.0 us)
Async XLA Ops:
  7.2 15.2 %copy-start.13 = (s32[8]{0:T(128)S(1)}, s32[8]{0:T(128)}, u32[]{:S(2)}) copy-start(s32[8]{0:T(128)} %constant.105) | copy-start | bytes 100
  7.2 101.0 %copy-start.9 = (bf16[1024,512]{1,0:T(8,128)(2,1)S(1)}, bf16[1024,512]{1,0:T(8,128)(2,1)}, u32[]{:S(2)}) copy-start(bf16[1024,512]{1,0:T(8,128)(2,1)} %param.15) | copy-start | bytes 3145732
  7.2 101.0 %copy-start.10 = (bf16[1024,512]{1,0:T(8,128)(2,1)S(1)}, bf16[1024,512]{1,0:T(8,128)(2,1)}, u32[]{:S(2)}) copy-start(bf16[1024,512]{1,0:T(8,128)(2,1)} %param.14) | copy-start | bytes 3145732
  7.2 15.1 %copy-start.14 = (s32[64,2]{0,1:T(2,128)S(1)}, s32[64,2]{0,1:T(2,128)}, u32[]{:S(2)}) copy-start(s32[64,2]{0,1:T(2,128)} %param.18) | copy-start | bytes 1540
  7.2 15.4 %copy-start.12 = (s32[192,2]{0,1:T(2,128)S(1)}, s32[192,2]{0,1:T(2,128)}, u32[]{:S(2)}) copy-start(s32[192,2]{0,1:T(2,128)} %param.19) | copy-start | bytes 4612
  7.2 196.2 %all-gather.2.cloned.1.call-start = ((), (), s32[]{:S(2)}) async-start(), calls=%async_computation.3 | async-start | bytes 10485760 | tf_op jit(solution)/shard_map/all_gather | solution.py:96
  10.5 97.8 %collective-permute-start.1 = (bf16[2,1024,512]{2,1,0:T(8,128)(2,1)}, bf16[2,1024,512]{2,1,0:T(8,128)(2,1)}, u32[]{:S(2)}, u32[]{:S(2)}) collective-permute-start(bf16[2,1024,512]{2,1,0:T(8,128)(2,1)} %pad_maximum_fusion), channel_id=1, source_target_pairs={{0,4},{4,8},{8,12},{12,16},{16,20},{20,24},{24,28},{28,32},{32,36}... | collective-permute-start | bytes 6291464 | tf_op jit(solution)/shard_map/ppermute | solution.py:17
  14.3 93.9 %collective-permute-start = (bf16[2,1024,512]{2,1,0:T(8,128)(2,1)}, bf16[2,1024,512]{2,1,0:T(8,128)(2,1)}, u32[]{:S(2)}, u32[]{:S(2)}) collective-permute-start(bf16[2,1024,512]{2,1,0:T(8,128)(2,1)} %pad_maximum_fusion), channel_id=1, source_target_pairs={{0,8},{4,12},{8,16},{12,20},{16,24},{20,28},{24,32},{28,36},{32,40... | collective-permute-start | bytes 6291464 | tf_op jit(solution)/shard_map/ppermute | solution.py:17
  19.8 767.1 %reduce-scatter.3.cloned.1.call-start = ((), (), s32[]{:S(2)}) async-start(), calls=%async_computation.2 | async-start | bytes 20971520 | tf_op jit(solution)/shard_map/reduce_scatter | solution.py:93
  156.3 3.7 copy-start.2
  160.0 7.3 copy-start.3
  167.6 1.0 copy-start.4
  178.2 3.7 copy-start.2
  181.9 7.3 copy-start.3
  189.4 1.0 copy-start.4
  203.3 587.4 %reduce-scatter.5.cloned.1.call-start = ((), (), s32[]{:S(2)}) async-start(), calls=%async_computation.4 | async-start | bytes 8650752 | tf_op jit(solution)/shard_map/reduce_scatter | solution.py:103
  203.4 11.5 %copy-start.5 = (bf16[2,512,4,128]{3,2,1,0:T(4,128)(2,1)S(1)}, bf16[2,512,4,128]{3,2,1,0:T(4,128)(2,1)}, u32[]{:S(2)}) copy-start(bf16[2,512,4,128]{3,2,1,0:T(4,128)(2,1)} %get-tuple-element.373) | copy-start | bytes 3145732
  226.5 133.8 %copy-start.15 = (f32[6,2,4,1,1,1]{0,2,1,5,4,3:T(4,128)S(1)}, f32[6,2,4,1,1,1]{0,2,1,5,4,3:T(4,128)}, u32[]{:S(2)}) copy-start(f32[6,2,4,1,1,1]{0,2,1,5,4,3:T(4,128)} %constant.107) | copy-start | bytes 580
  226.9 1.0 copy-start.7
  234.5 5.7 copy-start.1
  258.9 14.0 %copy-start.6 = (bf16[2,512,4,128]{3,1,2,0:T(8,128)(2,1)S(1)}, bf16[2,512,4,128]{3,1,2,0:T(8,128)(2,1)}, u32[]{:S(2)}) copy-start(bf16[2,512,4,128]{3,1,2,0:T(8,128)(2,1)} %get-tuple-element.392) | copy-start | bytes 3145732 | tf_op jit(solution)/shard_map/while
  264.8 10.8 %copy-start = (bf16[4,4,512,512]{2,3,0,1:T(8,128)(2,1)S(1)}, bf16[4,4,512,512]{2,3,0,1:T(8,128)(2,1)}, u32[]{:S(2)}) copy-start(bf16[4,4,512,512]{2,3,0,1:T(8,128)(2,1)} %fusion.129) | copy-start | bytes 25165828 | tf_op jit(solution)/shard_map/while
  287.2 8.6 %copy-start.8 = (bf16[2,512,4,128]{3,2,1,0:T(4,128)(2,1)S(1)}, bf16[2,512,4,128]{3,2,1,0:T(4,128)(2,1)}, u32[]{:S(2)}) copy-start(bf16[2,512,4,128]{3,2,1,0:T(4,128)(2,1)} %copy-done.7) | copy-start | bytes 3145732 | tf_op jit(solution)/shard_map/while
  295.8 1.0 copy-start.7
  303.5 5.8 copy-start.1
  328.0 11.1 %copy-start.6 = (bf16[2,512,4,128]{3,1,2,0:T(8,128)(2,1)S(1)}, bf16[2,512,4,128]{3,1,2,0:T(8,128)(2,1)}, u32[]{:S(2)}) copy-start(bf16[2,512,4,128]{3,1,2,0:T(8,128)(2,1)} %get-tuple-element.392) | copy-start | bytes 3145732 | tf_op jit(solution)/shard_map/while
  333.6 6.7 copy-start
  351.8 8.3 %copy-start.8 = (bf16[2,512,4,128]{3,2,1,0:T(4,128)(2,1)S(1)}, bf16[2,512,4,128]{3,2,1,0:T(4,128)(2,1)}, u32[]{:S(2)}) copy-start(bf16[2,512,4,128]{3,2,1,0:T(4,128)(2,1)} %copy-done.7) | copy-start | bytes 3145732 | tf_op jit(solution)/shard_map/while
  417.4 51.9 %copy-start.11 = (bf16[2,512,4,128]{3,2,1,0:T(4,128)(2,1)S(1)}, bf16[2,512,4,128]{3,2,1,0:T(4,128)(2,1)}, u32[]{:S(2)}) copy-start(bf16[2,512,4,128]{3,2,1,0:T(4,128)(2,1)} %get-tuple-element.92) | copy-start | bytes 3145732
  422.1 270.1 %collective-permute-start.2 = (f32[2,1024,512]{2,1,0:T(8,128)S(1)}, f32[2,1024,512]{2,1,0:T(8,128)S(1)}, u32[]{:S(2)}, u32[]{:S(2)}) collective-permute-start(f32[2,1024,512]{2,1,0:T(8,128)S(1)} %get-tuple-element.217), channel_id=1, source_target_pairs={{4,0},{8,4},{12,8},{16,12},{20,16},{24,20},{28,24},{32,28},{36,32}... | collective-permute-start | bytes 12582920 | tf_op jit(solution)/shard_map/ppermute | solution.py:17
  465.7 316.2 %collective-permute-start.3 = (f32[2,1024,512]{2,1,0:T(8,128)S(1)}, f32[2,1024,512]{2,1,0:T(8,128)S(1)}, u32[]{:S(2)}, u32[]{:S(2)}) collective-permute-start(f32[2,1024,512]{2,1,0:T(8,128)S(1)} %get-tuple-element.218), channel_id=1, source_target_pairs={{8,0},{12,4},{16,8},{20,12},{24,16},{28,20},{32,24},{36,28},{40,32... | collective-permute-start | bytes 12582920 | tf_op jit(solution)/shard_map/ppermute | solution.py:17
Sparse Core Ops, SparseCore 0:
  19.9 60.4 all-gather.1
  203.5 179.9 reduce-scatter.2
  386.5 311.5 reduce-scatter.4
where the time goes:
time: 811 us; the launch traced here: 797 us
  waiting for transfers between devices  397 us (49%)
  matrix products  153 us (19%)
  local copies, waits for them, and re-layouts  139 us (17%)
  starting transfers between devices  56.6 us (7%)
  other arithmetic  37.2 us (5%)
  between operations  14.2 us (2%)
    ppermute x4, waiting for transfers between devices, from_behind(): lax.ppermute(value, axis, [(source, source + steps) for source in range(l...  397 us
    ppermute x4, starting transfers between devices, from_behind(): lax.ppermute(value, axis, [(source, source + steps) for source in range(l...  56.5 us
    dynamic_update_slice x6, local copies, waits for them, and re-layouts, per_device(): lax.map(backward_tile, (query_four, key_tiles, value_tiles, block_fine, g...  39.2 us
    dot_general x1, matrix products, per_device(): jnp.einsum('ebo,xboshd->xeshd', jnp.asarray(placement), grad_tiles, preci...  26.9 us
    dot_general x2, matrix products, backward_tile(): jnp.einsum('thd,oshd->ohts', grad_rows, value_rows, preferred_element_typ...  23.3 us
    dot_general x4, matrix products, tile_weights(): jnp.einsum('thd,oshd->ohts', query_rows, key_rows, preferred_element_type...  18 us
    reshape x2, local copies, waits for them, and re-layouts, per_device(): ext_blocks = extended.reshape(2, total_blocks, BLK, head_count, HDIM)  16.8 us
  transfers between devices with their start and end apart: 7, of which 3 were waited for; matrix products, arithmetic and copies ran while one was open for 39% of the time, Pallas kernels for 0%

commit v1 on v0

v1 whole, which is shorter than its diff:
```python
import functools
import math

import jax
import jax.numpy as jnp
from jax import lax
from jax.experimental import pallas as pl
from jax.experimental.pallas import tpu as pltpu
from jax.sharding import PartitionSpec as P

HDIM = 128
BLK = 512
WIN = 4
SCALE = 1.0 / math.sqrt(HDIM)
SCALE2 = SCALE * math.log2(math.e)
AXES = ("ctx", "tp")
NT = (((1,), (1,)), ((), ()))
NN = (((1,), (0,)), ((), ()))
f32 = jnp.float32
bf16 = jnp.bfloat16


def places():
    for x_lo in range(2):
        for y in range(4):
            for z in range(4):
                for x_hi in range(2):
                    for core in range(2):
                        yield x_lo, y, z, x_hi, core


def number(x_lo, y, z, x_hi, core):
    return ((x_lo * 4 + y) * 4 + z) * 4 + x_hi * 2 + core


def move(value, target):
    pairs = [(number(*place), number(*target(*place))) for place in places()]
    return lax.ppermute(value, AXES, pairs)


def to_core(value):
    return move(value, lambda x_lo, y, z, x_hi, core: (x_lo, y, z, x_hi, 1 - core))


def to_x_hi(value):
    return move(value, lambda x_lo, y, z, x_hi, core: (x_lo, y, z, 1 - x_hi, core))


def to_x_lo(value):
    return move(value, lambda x_lo, y, z, x_hi, core: (1 - x_lo, y, z, x_hi, core))


def to_y(value, steps):
    return move(value, lambda x_lo, y, z, x_hi, core: (x_lo, (y + steps) % 4, z, x_hi, core))


def to_z(value, steps):
    return move(value, lambda x_lo, y, z, x_hi, core: (x_lo, y, (z + steps) % 4, x_hi, core))


def along_ctx(value, steps):
    pairs = [(s, s + steps) for s in range(32) if 0 <= s + steps < 32]
    return lax.ppermute(value, "ctx", pairs)


def two_along_ctx(value, sign):
    value = to_z(value, -sign)
    pairs = []
    for source in range(32):
        if 0 <= source + 2 * sign < 32:
            middle = source // 4 * 4 + (source % 4 - sign) % 4
            pairs.append((middle, source + 2 * sign))
    return lax.ppermute(value, "ctx", pairs)


def block_rule(spans, pairs, query_block, key_block):
    listed = jnp.any(
        (pairs[:, 0] == query_block[..., None]) & (pairs[:, 1] == key_block[..., None]), axis=-1
    )
    span_lower = spans[:, 0]
    span_upper = spans[:, 0] + spans[:, 1]
    query_inside = (span_lower <= query_block[..., None]) & (query_block[..., None] < span_upper)
    key_inside = (span_lower <= key_block[..., None]) & (key_block[..., None] < span_upper)
    same = jnp.any(query_inside & key_inside, axis=-1)
    reach = (query_block - key_block >= 0) & (query_block - key_block < WIN)
    return listed & same & reach


def dot(a, b, dims):
    return lax.dot_general(a, b, dims, preferred_element_type=f32)


def key_tile(index, far, near, own):
    if index == 0:
        return far[...]
    if index < 3:
        return near[pl.ds((index - 1) * BLK, BLK), :]
    return own[pl.ds((index - 3) * BLK, BLK), :]


def causal():
    key_row = lax.broadcasted_iota(jnp.int32, (BLK, BLK), 0)
    query_column = lax.broadcasted_iota(jnp.int32, (BLK, BLK), 1)
    return key_row <= query_column


def forward_kernel(
    flags, q_ref, k_ref, v_ref, k1_ref, v1_ref, k2_ref, v2_ref,
    out_ref, turned_ref, log_ref, top, total, acc,
):
    for qb in range(2):
        rows = pl.ds(qb * BLK, BLK)
        diagonal = flags[qb * WIN] == 1

        @pl.when(jnp.logical_not(diagonal))
        def _():
            out_ref[rows, :] = jnp.zeros((BLK, HDIM), bf16)
            turned_ref[:, rows] = jnp.zeros((HDIM, BLK), bf16)
            log_ref[0, qb : qb + 1, :] = jnp.zeros((1, BLK), f32)

        @pl.when(diagonal)
        def _():
            for o in range(WIN):

                def tile(o=o):
                    keys = key_tile(3 + qb - o, k2_ref, k1_ref, k_ref)
                    vals = key_tile(3 + qb - o, v2_ref, v1_ref, v_ref)
                    s = dot(keys, q_ref[rows, :], NT)
                    if o == 0:
                        s = jnp.where(causal(), s, -jnp.inf)
                        m = jnp.max(s, axis=0, keepdims=True)
                    else:
                        m = jnp.maximum(top[...], jnp.max(s, axis=0, keepdims=True))
                    p = jnp.exp2(s * SCALE2 - m * SCALE2)
                    row_sum = jnp.sum(p, axis=0, keepdims=True)
                    part = dot(vals.T, p.astype(bf16), NN)
                    if o == 0:
                        total[...] = row_sum
                        acc[...] = part
                    else:
                        fix = jnp.exp2((top[...] - m) * SCALE2)
                        total[...] = total[...] * fix + row_sum
                        acc[...] = acc[...] * fix + part
                    top[...] = m

                if o == 0:
                    tile()
                else:
                    pl.when(flags[qb * WIN + o] == 1)(tile)
            result = acc[...] * (1.0 / total[...])
            turned_ref[:, rows] = result.astype(bf16)
            out_ref[rows, :] = result.T.astype(bf16)
            log_ref[0, qb : qb + 1, :] = top[...] * SCALE2 + jnp.log2(total[...])


def backward_kernel(
    flags, q_ref, k_ref, v_ref, k1_ref, v1_ref, k2_ref, v2_ref, out_ref, grad_ref, log_ref,
    dq_ref, own_ref, near_ref, far_ref, dk, dv, dq,
):
    dk[...] = jnp.zeros_like(dk)
    dv[...] = jnp.zeros_like(dv)
    for qb in range(2):
        rows = pl.ds(qb * BLK, BLK)
        diagonal = flags[qb * WIN] == 1

        @pl.when(jnp.logical_not(diagonal))
        def _():
            dq_ref[rows, :] = jnp.zeros((BLK, HDIM), bf16)

        @pl.when(diagonal)
        def _():
            grad = grad_ref[rows, :]
            product = grad.astype(f32) * out_ref[rows, :].astype(f32)
            delta = jnp.sum(product.T, axis=0, keepdims=True)
            log_sum = log_ref[0, qb : qb + 1, :]
            for o in range(WIN):

                def tile(o=o):
                    index = 3 + qb - o
                    keys = key_tile(index, k2_ref, k1_ref, k_ref)
                    vals = key_tile(index, v2_ref, v1_ref, v_ref)
                    s = dot(keys, q_ref[rows, :], NT)
                    p = jnp.exp2(s * SCALE2 - log_sum)
                    if o == 0:
                        p = jnp.where(causal(), p, 0.0)
                    key_rows = pl.ds(index * BLK, BLK)
                    dv[key_rows, :] += dot(p.astype(bf16), grad, NN)
                    dp = dot(vals, grad, NT)
                    ds = (p * (dp - delta)).astype(bf16)
                    dk[key_rows, :] += dot(ds, q_ref[rows, :], NN)
                    part = dot(keys.T, ds, NN)
                    if o == 0:
                        dq[...] = part
                    else:
                        dq[...] += part

                if o == 0:
                    tile()
                else:
                    pl.when(flags[qb * WIN + o] == 1)(tile)
            dq_ref[rows, :] = (dq[...] * SCALE).T.astype(bf16)
    far_ref[0] = (dk[pl.ds(0, BLK), :] * SCALE).astype(bf16)
    far_ref[1] = dv[pl.ds(0, BLK), :].astype(bf16)
    near_ref[0] = (dk[pl.ds(BLK, 2 * BLK), :] * SCALE).astype(bf16)
    near_ref[1] = dv[pl.ds(BLK, 2 * BLK), :].astype(bf16)
    own_ref[0] = dk[pl.ds(3 * BLK, 2 * BLK), :] * SCALE
    own_ref[1] = dv[pl.ds(3 * BLK, 2 * BLK), :]


def head(rows):
    return pl.BlockSpec((rows, HDIM), lambda h, *_: (0, h))


def head_pair(rows):
    return pl.BlockSpec((2, rows, HDIM), lambda h, *_: (0, 0, h))


HEAD_LOG = pl.BlockSpec((1, 2, BLK), lambda h, *_: (h, 0, 0))


def shape(dims, dtype):
    return jax.ShapeDtypeStruct(dims, dtype)


def call(kernel, name, grid, ins, outs, out_shape, scratch, flops, args):
    return pl.pallas_call(
        kernel,
        grid_spec=pltpu.PrefetchScalarGridSpec(
            num_scalar_prefetch=1,
            grid=grid,
            in_specs=ins,
            out_specs=outs,
            scratch_shapes=scratch,
        ),
        out_shape=out_shape,
        compiler_params=pltpu.CompilerParams(vmem_limit_bytes=40 << 20),
        cost_estimate=pl.CostEstimate(flops=flops, bytes_accessed=16 << 20, transcendentals=0),
        name=name,
    )(*args)


def forward(flags, q, k, v, k1, v1, k2, v2):
    width = q.shape[1]
    heads = width // HDIM
    return call(
        forward_kernel, "attention_forward", (heads,),
        [head(1024)] * 5 + [head(512)] * 2,
        [head(1024), pl.BlockSpec((HDIM, 1024), lambda h, *_: (h, 0)), HEAD_LOG],
        [shape((1024, width), bf16), shape((width, 1024), bf16), shape((heads, 2, BLK), f32)],
        [pltpu.VMEM((1, BLK), f32), pltpu.VMEM((1, BLK), f32), pltpu.VMEM((HDIM, BLK), f32)],
        10**10, (flags, q, k, v, k1, v1, k2, v2),
    )


def backward(flags, q, k, v, k1, v1, k2, v2, out, grad, log_sum):
    width = q.shape[1]
    held = pltpu.VMEM((5 * BLK, HDIM), f32)
    return call(
        backward_kernel, "attention_backward", (width // HDIM,),
        [head(1024)] * 5 + [head(512)] * 2 + [head(1024)] * 2 + [HEAD_LOG],
        [head(1024), head_pair(1024), head_pair(1024), head_pair(512)],
        [
            shape((1024, width), bf16),
            shape((2, 1024, width), f32),
            shape((2, 1024, width), bf16),
            shape((2, 512, width), bf16),
        ],
        [held, held, pltpu.VMEM((HDIM, BLK), f32)],
        15 * 10**9, (flags, q, k, v, k1, v1, k2, v2, out, grad, log_sum),
    )


def grad_kernel(place, a_ref, b_ref, wa_ref, wb_ref, *rest):
    total = dot(a_ref[...], wa_ref[...], NT) + dot(b_ref[...], wb_ref[...], NT)
    if len(rest) == 2:
        total += rest[0][...]
    rest[-1][...] = total.astype(rest[-1].dtype)


def grad_terms(place, first, a, b, weight, before=None):
    tile = 256
    row = pl.BlockSpec((tile, 1024), lambda i, place: (i, 0))
    result = pl.BlockSpec((tile, 512), lambda i, place: (i, 0))

    def columns(flip):
        return pl.BlockSpec((512, 1024), lambda i, place: (0, place[0] ^ flip))

    ins = [row, row, columns(first), columns(first + 1)] + ([result] if before is not None else [])
    args = (place, a, b, weight, weight) + ((before,) if before is not None else ())
    dtype = bf16 if before is not None else f32
    return call(
        grad_kernel, "projection_backward", (1024 // tile,), ins, result,
        shape((1024, 512), dtype), [], 2 * 10**9, args,
    )


def weight_kernel(place, turned_ref, *refs):
    out_ref = refs[-1]
    for part in range(4):

        @pl.when(pl.program_id(0) == part)
        def _():
            out_ref[0, 0] = dot(turned_ref[...], refs[part][...], NN).astype(bf16)


def weight_terms(place, turned, cotangents):
    def piece(part):
        return pl.BlockSpec(
            (1024, 512),
            lambda i, half, place: (
                0, jnp.where(i == part, half, jnp.where(i < part, 0, 1)),
            ),
        )

    def target(i, half, place):
        owner = place[0] ^ i
        y = (owner % 2) * 2 + half
        return ((y - place[1] + 4) % 4, owner // 2, 0, 0)

    return call(
        weight_kernel, "weight_gradient", (4, 2),
        [pl.BlockSpec((512, 1024), lambda i, half, place: (0, 0))] + [piece(p) for p in range(4)],
        pl.BlockSpec((1, 1, 512, 512), target),
        shape((4, 2, 512, 512), bf16), [], 4 * 10**9, (place, turned, *cotangents),
    )


def mix_kernel(place, a_ref, w_ref, out_ref):
    out_ref[0] = dot(a_ref[...], w_ref[...], NN).astype(bf16)


def mix_terms(place, attention, weight, flip):
    return call(
        mix_kernel, "projection", (2, 2),
        [
            pl.BlockSpec((512, 512), lambda s, i, place: (i, 0)),
            pl.BlockSpec((512, 1024), lambda s, i, place: (0, place[0] ^ (2 - 2 * s + flip))),
        ],
        pl.BlockSpec((1, 512, 1024), lambda s, i, place: (s, i, 0)),
        shape((2, 1024, 1024), bf16), [], 2 * 10**9, (place, attention, weight),
    )


def per_device(queries, keys, values, out_weight, out_grad, spans, pairs):
    ctx = lax.axis_index("ctx")
    tp = lax.axis_index("tp")
    x_lo, y, z = ctx // 16, ctx // 4 % 4, ctx % 4
    place = jnp.stack([tp, y]).astype(jnp.int32)

    far_grad = to_x_hi(out_grad)
    near_keys = along_ctx(keys, 1)
    near_values = along_ctx(values, 1)
    far_keys = two_along_ctx(keys[BLK:], 1)
    far_values = two_along_ctx(values[BLK:], 1)
    core_grad = to_core(out_grad)

    query_block = ctx * 2 + jnp.arange(2, dtype=jnp.int32)[:, None] + jnp.zeros((1, WIN), jnp.int32)
    key_block = query_block - jnp.arange(WIN, dtype=jnp.int32)[None, :]
    flags = block_rule(spans, pairs, query_block, key_block).astype(jnp.int32).reshape(-1)

    terms = grad_terms(place, 0, out_grad, core_grad, out_weight)
    tiles = (flags, queries, keys, values, near_keys, near_values, far_keys, far_values)
    attention, turned, log_sum = forward(*tiles)
    far_core_grad = to_core(far_grad)
    attn_grad = grad_terms(place, 2, far_grad, far_core_grad, out_weight, terms)

    weight_parts = weight_terms(place, turned, (out_grad, core_grad, far_grad, far_core_grad))
    weight_one = to_y(weight_parts[1], 1)
    weight_three = to_y(weight_parts[3], 3)
    weight_two = to_y(weight_parts[2], 2)

    mix_core = to_core(mix_terms(place, attention, out_weight, 1))
    mix_own = mix_terms(place, attention, out_weight, 0)
    mix_far = to_x_hi((mix_own[0].astype(f32) + mix_core[0].astype(f32)).astype(bf16))

    query_grad, own, near, far = backward(*tiles, attention, attn_grad, log_sum)
    far_back = two_along_ctx(far, -1)
    near_back = along_ctx(near, -1)

    mixed = (
        mix_own[1].astype(f32) + mix_core[1].astype(f32) + mix_far.astype(f32)
    ).astype(bf16)

    weight_sum = (
        weight_parts[0].astype(f32)
        + weight_one.astype(f32)
        + weight_two.astype(f32)
        + weight_three.astype(f32)
    ).astype(bf16)

    def z_piece(steps):
        return lax.dynamic_slice_in_dim(weight_sum, (z + steps) % 4 * 128, 128, 2)

    z_sum = z_piece(0).astype(f32)
    for steps in (1, 3, 2):
        z_sum = z_sum + to_z(z_piece(steps), steps).astype(f32)
    z_sum = z_sum.astype(bf16)
    kept = lax.dynamic_index_in_dim(z_sum, x_lo, 0, keepdims=False)
    sent = lax.dynamic_index_in_dim(z_sum, 1 - x_lo, 0, keepdims=False)
    weight_grad = kept.astype(f32) + to_x_lo(sent).astype(f32)

    summed = own + near_back.astype(f32)
    summed = summed.at[:, BLK:].add(far_back.astype(f32))
    key_grad = summed[0].astype(bf16)
    value_grad = summed[1].astype(bf16)
    return (mixed, query_grad, key_grad, value_grad, weight_grad)


def solution(mesh):
    placed = (
        P("ctx", "tp"),
        P("ctx", "tp"),
        P("ctx", "tp"),
        P("tp", None),
        P("ctx", "tp"),
        P(),
        P(),
    )
    return jax.shard_map(
        per_device,
        mesh=mesh,
        in_specs=placed,
        out_specs=(P("ctx", "tp"), P("ctx", "tp"), P("ctx", "tp"), P("ctx", "tp"), P("tp", "ctx")),
        check_vma=False,
    )
```

time: 811 us -> 302 us (0.37)
  the two profiles are of different devices: /device:TPU:30 before, /device:TPU:36 now
where the time goes in v1:
time: 302 us; the launch traced here: 299 us
  waiting for transfers between devices  115 us (38%)
  starting transfers between devices  77.3 us (26%)
  Pallas kernels  63.9 us (21%)
  local copies, waits for them, and re-layouts  22.7 us (8%)
  other arithmetic  19.7 us (7%)
    ppermute x15, waiting for transfers between devices, move(): return lax.ppermute(value, AXES, pairs)  108 us
    pallas_call x7, Pallas kernels, call(): pl.pallas_call(kernel, grid_spec=pltpu.PrefetchScalarGridSpec(num_scalar_...  63.9 us
    ppermute x15, starting transfers between devices, move(): return lax.ppermute(value, AXES, pairs)  47.5 us
    ppermute x3, starting transfers between devices, two_along_ctx(): return lax.ppermute(value, 'ctx', pairs)  20.3 us
    unnamed x40, local copies, waits for them, and re-layouts  14.7 us
    ppermute x3, starting transfers between devices, along_ctx(): return lax.ppermute(value, 'ctx', pairs)  9.49 us
    ppermute x3, waiting for transfers between devices, two_along_ctx(): return lax.ppermute(value, 'ctx', pairs)  6.38 us
  transfers between devices with their start and end apart: 21, of which 8 were waited for; matrix products, arithmetic and copies ran while one was open for 8% of the time, Pallas kernels for 21%

profile of v1, /device:TPU:36, one launch (start us, length us, event | category | flops | bytes accessed | tf_op | source)
XLA Modules:
  0.0 299.5 jit_solution(11483097380393519952)
XLA Ops:
  1.2 3.8 %collective-permute-start.1 = (bf16[1024,512]{1,0:T(8,128)(2,1)}, bf16[1024,512]{1,0:T(8,128)(2,1)S(1)}, u32[]{:S(2)}, u32[]{:S(2)}) collective-permute-start(bf16[1024,512]{1,0:T(8,128)(2,1)} %v_ref.3), channel_id=1, source_target_pairs={{0,4},{4,8},{8,12},{12,16},{16,20},{20,24},{24,28},{28,32},{32,36}... | collective-permute-start | bytes 3145736 | tf_op jit(solution)/shard_map/ppermute | solution.py:63
  5.1 1.9 slice.80
  7.1 3.8 %collective-permute-start = (bf16[1024,512]{1,0:T(8,128)(2,1)}, bf16[1024,512]{1,0:T(8,128)(2,1)}, u32[]{:S(2)}, u32[]{:S(2)}) collective-permute-start(bf16[1024,512]{1,0:T(8,128)(2,1)} %k_ref.3), channel_id=1, source_target_pairs={{0,4},{4,8},{8,12},{12,16},{16,20},{20,24},{24,28},{28,32},{32,36}... | collective-permute-start | bytes 3145736 | tf_op jit(solution)/shard_map/ppermute | solution.py:63
  10.9 1.9 slice.79
  12.8 1.1 collective-permute-start.2
  13.9 8.2 %collective-permute-done.4 = bf16[512,512]{1,0:T(8,128)(2,1)} collective-permute-done((bf16[512,512]{1,0:T(8,128)(2,1)}, bf16[512,512]{1,0:T(8,128)(2,1)}, u32[]{:S(2)}, u32[]{:S(2)}) %collective-permute-start.4) | collective-permute-done | bytes 524320 | tf_op jit(solution)/shard_map/ppermute | solution.py:38
  22.1 3.8 %collective-permute-start.5 = (bf16[512,512]{1,0:T(8,128)(2,1)}, bf16[512,512]{1,0:T(8,128)(2,1)}, u32[]{:S(2)}, u32[]{:S(2)}) collective-permute-start(bf16[512,512]{1,0:T(8,128)(2,1)} %collective-permute-done.4), channel_id=1, source_target_pairs={{12,8},{0,12},{4,16},{8,20},{28,24},{16,28},{20,32},{24,36},{44,40... | collective-permute-start | bytes 1572872 | tf_op jit(solution)/shard_map/ppermute | solution.py:73
  26.0 5.6 %collective-permute-done.2 = bf16[512,512]{1,0:T(8,128)(2,1)} collective-permute-done((bf16[512,512]{1,0:T(8,128)(2,1)}, bf16[512,512]{1,0:T(8,128)(2,1)}, u32[]{:S(2)}, u32[]{:S(2)}) %collective-permute-start.2) | collective-permute-done | bytes 524320 | tf_op jit(solution)/shard_map/ppermute | solution.py:38
  31.6 15.2 %collective-permute-start.3 = (bf16[512,512]{1,0:T(8,128)(2,1)}, bf16[512,512]{1,0:T(8,128)(2,1)}, u32[]{:S(2)}, u32[]{:S(2)}) collective-permute-start(bf16[512,512]{1,0:T(8,128)(2,1)} %collective-permute-done.2), channel_id=1, source_target_pairs={{12,8},{0,12},{4,16},{8,20},{28,24},{16,28},{20,32},{24,36},{44,40... | collective-permute-start | bytes 1572872 | tf_op jit(solution)/shard_map/ppermute | solution.py:73
  47.5 2.3 collective-permute-done.8.a_ref.refs_2_
  49.8 6.4 %collective-permute-done.3.k2_ref = bf16[512,512]{1,0:T(8,128)(2,1)} collective-permute-done((bf16[512,512]{1,0:T(8,128)(2,1)}, bf16[512,512]{1,0:T(8,128)(2,1)}, u32[]{:S(2)}, u32[]{:S(2)}) %collective-permute-start.3) | collective-permute-done | bytes 524320 | tf_op jit(solution)/shard_map/ppermute | solution.py:73
  57.2 1.2 copy-done.8
  58.4 1.2 copy-done.10
  59.6 1.2 copy-done.12
  60.9 1.2 copy-done.15
  62.1 16.0 %attention_forward.1 = (bf16[1024,512]{1,0:T(8,128)(2,1)S(1)}, bf16[512,1024]{1,0:T(8,128)(2,1)S(1)}, f32[4,2,512]{2,1,0:T(2,128)S(1)}) custom-call(s32[8]{0:T(128)S(1)} %reshape.104.flags, bf16[1024,512]{1,0:T(8,128)(2,1)S(1)} %copy-done.12, bf16[1024,512]{1,0:T(8,128)(2,1)S(1)} %copy-done.8, bf16[1024,512]{1,0:T(8,128)(2,1)S(1)} %copy-done.10, ...), custom_call_target="tpu_custom_call" | custom-call | flops 10000000000 | bytes 16777216 | tf_op jit(solution)/shard_map/attention_forward/pallas_call | solution.py:226
  78.1 5.0 %projection.3 = bf16[2,1024,1024]{2,1,0:T(8,128)(2,1)} custom-call(s32[2]{0:T(128)S(1)} %pad_add_fusion.place, bf16[1024,512]{1,0:T(8,128)(2,1)S(1)} %get-tuple-element.24.a_ref.out_ref, bf16[512,4096]{1,0:T(8,128)(2,1)S(1)} %copy-done), custom_call_target="tpu_custom_call" | custom-call | flops 2000000000 | bytes 16777216 | tf_op jit(solution)/shard_map/projection/pallas_call | solution.py:226
  83.2 5.0 %projection_backward.2.rest_0_ = f32[1024,512]{1,0:T(8,128)S(1)} custom-call(s32[2]{0:T(128)S(1)} %pad_add_fusion.place, bf16[1024,1024]{1,0:T(8,128)(2,1)S(1)} %copy-done.7, bf16[1024,1024]{1,0:T(8,128)(2,1)} %collective-permute-done.10.b_ref.refs_1_, bf16[512,4096]{1,0:T(8,128)(2,1)S(1)} %copy-done, bf16[512,4096]{1,0:T(8,128)(2,1)S(1)} %copy-done), custom_call_target="tpu_custom_call" | custom-call | flops 2000000000 | bytes 16777216 | tf_op jit(solution)/shard_map/projection_backward/pallas_call | solution.py:226
  88.1 1.3 copy-done.5
  89.5 1.6 copy-done.6
  91.0 8.7 %weight_gradient.1 = bf16[4,2,512,512]{3,2,1,0:T(8,128)(2,1)S(1)} custom-call(s32[2]{0:T(128)S(1)} %pad_add_fusion.place, bf16[512,1024]{1,0:T(8,128)(2,1)S(1)} %get-tuple-element.30.turned_ref, bf16[1024,1024]{1,0:T(8,128)(2,1)S(1)} %copy-done.7, bf16[1024,1024]{1,0:T(8,128)(2,1)} %collective-permute-done.10.b_ref.refs_1_, ...), custom_call_target="tpu_custom_call" | custom-call | flops 4000000000 | bytes 16777216 | tf_op jit(solution)/shard_map/weight_gradient/pallas_call | solution.py:226
  99.8 1.8 slice_bitcast_fusion.2
  101.6 1.2 copy-done.4
  102.8 15.8 %collective-permute-start.16 = (bf16[2,512,512]{2,1,0:T(8,128)(2,1)}, bf16[2,512,512]{2,1,0:T(8,128)(2,1)}, u32[]{:S(2)}, u32[]{:S(2)}) collective-permute-start(bf16[2,512,512]{2,1,0:T(8,128)(2,1)} %get-tuple-element.32), channel_id=1, source_target_pairs={{0,48},{1,49},{2,50},{3,51},{4,52},{5,53},{6,54},{7,55},{8,56},{9,... | collective-permute-start | bytes 3145736 | tf_op jit(solution)/shard_map/ppermute | solution.py:38
  118.6 1.7 collective-permute-start.15
  120.3 3.7 %projection_backward.3.grad_ref = bf16[1024,512]{1,0:T(8,128)(2,1)S(1)} custom-call(s32[2]{0:T(128)S(1)} %pad_add_fusion.place, bf16[1024,1024]{1,0:T(8,128)(2,1)S(1)} %collective-permute-done.8.a_ref.refs_2_, bf16[1024,1024]{1,0:T(8,128)(2,1)S(1)} %copy-done.6, bf16[512,4096]{1,0:T(8,128)(2,1)S(1)} %copy-done, bf16[512,4096]{1,0:T(8,128)(2,1)S(1)} %copy-done, ...), custom_call_target="tpu_custom_call" | custom-call | flops 2000000000 | bytes 16777216 | tf_op jit(solution)/shard_map/projection_backward/pallas_call | solution.py:226
  124.1 21.9 %attention_backward.1 = (bf16[1024,512]{1,0:T(8,128)(2,1)}, f32[2,1024,512]{2,1,0:T(8,128)}, bf16[2,1024,512]{2,1,0:T(8,128)(2,1)S(1)}, bf16[2,512,512]{2,1,0:T(8,128)(2,1)S(1)}) custom-call(s32[8]{0:T(128)S(1)} %reshape.104.flags, bf16[1024,512]{1,0:T(8,128)(2,1)S(1)} %copy-done.13, bf16[1024,512]{1,0:T(8,128)(2,1)S(1)} %copy-done.9, ...), custom_call_target="tpu_custom_call" | custom-call | flops 15000000512 | bytes 16777216 | tf_op jit(solution)/shard_map/attention_backward/pallas_call | solution.py:226
  146.9 1.9 collective-permute-start.11
  148.9 2.1 collective-permute-start.12
  151.0 2.2 copy-done.1
  153.2 3.6 %projection.2 = bf16[2,1024,1024]{2,1,0:T(8,128)(2,1)S(1)} custom-call(s32[2]{0:T(128)S(1)} %pad_add_fusion.place, bf16[1024,512]{1,0:T(8,128)(2,1)S(1)} %get-tuple-element.24.a_ref.out_ref, bf16[512,4096]{1,0:T(8,128)(2,1)S(1)} %copy-done.1), custom_call_target="tpu_custom_call" | custom-call | flops 2000000000 | bytes 16777216 | tf_op jit(solution)/shard_map/projection/pallas_call | solution.py:226
  156.8 7.6 %collective-permute-done.16 = bf16[2,512,512]{2,1,0:T(8,128)(2,1)} collective-permute-done((bf16[2,512,512]{2,1,0:T(8,128)(2,1)}, bf16[2,512,512]{2,1,0:T(8,128)(2,1)}, u32[]{:S(2)}, u32[]{:S(2)}) %collective-permute-start.16) | collective-permute-done | bytes 1048608 | tf_op jit(solution)/shard_map/ppermute | solution.py:38
  164.4 1.9 collective-permute-done.15
  166.4 2.7 fusion.5
  170.0 10.6 %collective-permute-start.17 = (bf16[2,512,128]{2,1,0:T(8,128)(2,1)}, bf16[2,512,128]{2,1,0:T(8,128)(2,1)}, u32[]{:S(2)}, u32[]{:S(2)}) collective-permute-start(bf16[2,512,128]{2,1,0:T(8,128)(2,1)} %get-tuple-element.36), channel_id=1, source_target_pairs={{0,4},{1,5},{2,6},{3,7},{4,8},{5,9},{6,10},{7,11},{8,12},{9,13},{1... | collective-permute-start | bytes 786440 | tf_op jit(solution)/shard_map/ppermute | solution.py:38
  180.6 9.4 %collective-permute-start.19 = (bf16[2,512,128]{2,1,0:T(8,128)(2,1)}, bf16[2,512,128]{2,1,0:T(8,128)(2,1)}, u32[]{:S(2)}, u32[]{:S(2)}) collective-permute-start(bf16[2,512,128]{2,1,0:T(8,128)(2,1)} %get-tuple-element.37), channel_id=1, source_target_pairs={{0,8},{1,9},{2,10},{3,11},{4,12},{5,13},{6,14},{7,15},{8,0},{9,1},... | collective-permute-start | bytes 786440 | tf_op jit(solution)/shard_map/ppermute | solution.py:38
  190.0 2.6 collective-permute-start.18
  192.7 3.9 %fusion.1 = bf16[1024,1024]{1,0:T(8,128)(2,1)} fusion(bf16[2,1024,1024]{2,1,0:T(8,128)(2,1)} %collective-permute-done.6, bf16[2,1024,1024]{2,1,0:T(8,128)(2,1)S(1)} %projection.2), kind=kLoop, calls=%fused_computation.4 | loop fusion | flops 4194304 | bytes 6291456 | tf_op jit(solution)/shard_map/convert_element_type | solution.py:374
  196.5 3.0 %collective-permute-start.7 = (bf16[1024,1024]{1,0:T(8,128)(2,1)}, bf16[1024,1024]{1,0:T(8,128)(2,1)}, u32[]{:S(2)}, u32[]{:S(2)}) collective-permute-start(bf16[1024,1024]{1,0:T(8,128)(2,1)} %fusion.1), channel_id=1, source_target_pairs={{0,2},{1,3},{2,0},{3,1},{4,6},{5,7},{6,4},{7,5},{8,10},{9,11},{10,... | collective-permute-start | bytes 6291464 | tf_op jit(solution)/shard_map/ppermute | solution.py:38
  199.6 1.3 collective-permute-start.13
  200.9 20.1 %collective-permute-done.19 = bf16[2,512,128]{2,1,0:T(8,128)(2,1)} collective-permute-done((bf16[2,512,128]{2,1,0:T(8,128)(2,1)}, bf16[2,512,128]{2,1,0:T(8,128)(2,1)}, u32[]{:S(2)}, u32[]{:S(2)}) %collective-permute-start.19) | collective-permute-done | bytes 262176 | tf_op jit(solution)/shard_map/ppermute | solution.py:38
  221.0 1.2 add_convert_fusion.1
  222.6 62.6 %collective-permute-done.20 = bf16[512,128]{1,0:T(8,128)(2,1)S(1)} collective-permute-done((bf16[512,128]{1,0:T(8,128)(2,1)S(1)}, bf16[512,128]{1,0:T(8,128)(2,1)S(1)}, u32[]{:S(2)}, u32[]{:S(2)}) %collective-permute-start.20) | collective-permute-done | bytes 131104 | tf_op jit(solution)/shard_map/ppermute | solution.py:38
  285.9 3.6 %convert_add_fusion = f32[2,1024,512]{2,1,0:T(8,128)S(1)} fusion(f32[2,1024,512]{2,1,0:T(8,128)} %get-tuple-element.27, bf16[2,1024,512]{2,1,0:T(8,128)(2,1)} %collective-permute-done.11), kind=kLoop, calls=%fused_computation.2 | loop fusion | flops 2097152 | bytes 10485760 | tf_op jit(solution)/shard_map/add | solution.py:402
  289.6 1.7 fusion.2
  291.5 1.5 slice_bitcast_fusion.4
  293.0 1.5 copy-done.3
  294.5 5.0 %fusion = bf16[1024,1024]{1,0:T(8,128)(2,1)} fusion(bf16[1024,1024]{1,0:T(8,128)(2,1)} %collective-permute-done.7, bf16[2,1024,1024]{2,1,0:T(8,128)(2,1)} %collective-permute-done.6, bf16[2,1024,1024]{2,1,0:T(8,128)(2,1)S(1)} %copy-done.3), kind=kLoop, calls=%fused_computation.1 | loop fusion | flops 6291456 | bytes 8388608 | tf_op jit(solution)/shard_map/convert_element_type | solution.py:382
  (65 shorter events, 5.8 us)
Async XLA Ops:
  0.6 13.2 %copy-start.19 = (s32[64,2]{0,1:T(2,128)S(1)}, s32[64,2]{0,1:T(2,128)}, u32[]{:S(2)}) copy-start(s32[64,2]{0,1:T(2,128)} %param.14) | copy-start | bytes 1540
  0.6 13.3 %copy-start.18 = (s32[192,2]{0,1:T(2,128)S(1)}, s32[192,2]{0,1:T(2,128)}, u32[]{:S(2)}) copy-start(s32[192,2]{0,1:T(2,128)} %param.15) | copy-start | bytes 4612
  0.7 49.2 %collective-permute-start.8 = (bf16[1024,1024]{1,0:T(8,128)(2,1)}, bf16[1024,1024]{1,0:T(8,128)(2,1)S(1)}, u32[]{:S(2)}, u32[]{:S(2)}) collective-permute-start(bf16[1024,1024]{1,0:T(8,128)(2,1)} %refs_0_.1), channel_id=1, source_target_pairs={{0,2},{1,3},{2,0},{3,1},{4,6},{5,7},{6,4},{7,5},{8,10},{9,11},{10,... | collective-permute-start | bytes 6291464 | tf_op jit(solution)/shard_map/ppermute | solution.py:38
  1.2 55.0 %collective-permute-start.1 = (bf16[1024,512]{1,0:T(8,128)(2,1)}, bf16[1024,512]{1,0:T(8,128)(2,1)S(1)}, u32[]{:S(2)}, u32[]{:S(2)}) collective-permute-start(bf16[1024,512]{1,0:T(8,128)(2,1)} %v_ref.3), channel_id=1, source_target_pairs={{0,4},{4,8},{8,12},{12,16},{16,20},{20,24},{24,28},{28,32},{32,36}... | collective-permute-start | bytes 3145736 | tf_op jit(solution)/shard_map/ppermute | solution.py:63
  6.9 15.2 %collective-permute-start.4 = (bf16[512,512]{1,0:T(8,128)(2,1)}, bf16[512,512]{1,0:T(8,128)(2,1)}, u32[]{:S(2)}, u32[]{:S(2)}) collective-permute-start(bf16[512,512]{1,0:T(8,128)(2,1)} %slice.80), channel_id=1, source_target_pairs={{0,12},{1,13},{2,14},{3,15},{4,0},{5,1},{6,2},{7,3},{8,4},{9,5},{1... | collective-permute-start | bytes 1572872 | tf_op jit(solution)/shard_map/ppermute | solution.py:38
  7.1 49.1 %collective-permute-start = (bf16[1024,512]{1,0:T(8,128)(2,1)}, bf16[1024,512]{1,0:T(8,128)(2,1)}, u32[]{:S(2)}, u32[]{:S(2)}) collective-permute-start(bf16[1024,512]{1,0:T(8,128)(2,1)} %k_ref.3), channel_id=1, source_target_pairs={{0,4},{4,8},{8,12},{12,16},{16,20},{20,24},{24,28},{28,32},{32,36}... | collective-permute-start | bytes 3145736 | tf_op jit(solution)/shard_map/ppermute | solution.py:63
  12.8 18.8 %collective-permute-start.2 = (bf16[512,512]{1,0:T(8,128)(2,1)}, bf16[512,512]{1,0:T(8,128)(2,1)}, u32[]{:S(2)}, u32[]{:S(2)}) collective-permute-start(bf16[512,512]{1,0:T(8,128)(2,1)} %slice.79), channel_id=1, source_target_pairs={{0,12},{1,13},{2,14},{3,15},{4,0},{5,1},{6,2},{7,3},{8,4},{9,5},{1... | collective-permute-start | bytes 1572872 | tf_op jit(solution)/shard_map/ppermute | solution.py:38
  22.1 25.1 %collective-permute-start.5 = (bf16[512,512]{1,0:T(8,128)(2,1)}, bf16[512,512]{1,0:T(8,128)(2,1)}, u32[]{:S(2)}, u32[]{:S(2)}) collective-permute-start(bf16[512,512]{1,0:T(8,128)(2,1)} %collective-permute-done.4), channel_id=1, source_target_pairs={{12,8},{0,12},{4,16},{8,20},{28,24},{16,28},{20,32},{24,36},{44,40... | collective-permute-start | bytes 1572872 | tf_op jit(solution)/shard_map/ppermute | solution.py:73
  31.6 24.6 %collective-permute-start.3 = (bf16[512,512]{1,0:T(8,128)(2,1)}, bf16[512,512]{1,0:T(8,128)(2,1)}, u32[]{:S(2)}, u32[]{:S(2)}) collective-permute-start(bf16[512,512]{1,0:T(8,128)(2,1)} %collective-permute-done.2), channel_id=1, source_target_pairs={{12,8},{0,12},{4,16},{8,20},{28,24},{16,28},{20,32},{24,36},{44,40... | collective-permute-start | bytes 1572872 | tf_op jit(solution)/shard_map/ppermute | solution.py:73
  47.2 35.9 %collective-permute-start.10 = (bf16[1024,1024]{1,0:T(8,128)(2,1)}, bf16[1024,1024]{1,0:T(8,128)(2,1)}, u32[]{:S(2)}, u32[]{:S(2)}) collective-permute-start(bf16[1024,1024]{1,0:T(8,128)(2,1)} %refs_0_.1), channel_id=1, source_target_pairs={{0,1},{1,0},{2,3},{3,2},{4,5},{5,4},{6,7},{7,6},{8,9},{9,8},{10,11... | collective-permute-start | bytes 6291464 | tf_op jit(solution)/shard_map/ppermute | solution.py:38
  47.5 30.7 %copy-start = (bf16[512,4096]{1,0:T(8,128)(2,1)S(1)}, bf16[512,4096]{1,0:T(8,128)(2,1)}, u32[]{:S(2)}) copy-start(bf16[512,4096]{1,0:T(8,128)(2,1)} %wb_ref.3) | copy-start | bytes 12582916
  49.8 38.3 %collective-permute-start.9 = (bf16[1024,1024]{1,0:T(8,128)(2,1)S(1)}, bf16[1024,1024]{1,0:T(8,128)(2,1)S(1)}, u32[]{:S(2)}, u32[]{:S(2)}) collective-permute-start(bf16[1024,1024]{1,0:T(8,128)(2,1)S(1)} %collective-permute-done.8.a_ref.refs_2_), channel_id=1, source_target_pairs={{0,1},{1,0},{2,3},{3,2},{4,5},{5,4},{6,7},{7,6},{8,9},{9,8},{10,11... | collective-permute-start | bytes 6291464 | tf_op jit(solution)/shard_map/ppermute | solution.py:38
  56.2 1.0 copy-start.14
  57.2 1.2 copy-start.8
  58.4 1.2 copy-start.10
  59.6 1.2 copy-start.12
  60.9 1.2 copy-start.15
  78.1 5.0 %copy-start.7 = (bf16[1024,1024]{1,0:T(8,128)(2,1)S(1)}, bf16[1024,1024]{1,0:T(8,128)(2,1)}, u32[]{:S(2)}) copy-start(bf16[1024,1024]{1,0:T(8,128)(2,1)} %refs_0_.1) | copy-start | bytes 6291460
  83.1 106.9 %collective-permute-start.6 = (bf16[2,1024,1024]{2,1,0:T(8,128)(2,1)}, bf16[2,1024,1024]{2,1,0:T(8,128)(2,1)}, u32[]{:S(2)}, u32[]{:S(2)}) collective-permute-start(bf16[2,1024,1024]{2,1,0:T(8,128)(2,1)} %projection.3), channel_id=1, source_target_pairs={{0,1},{1,0},{2,3},{3,2},{4,5},{5,4},{6,7},{7,6},{8,9},{9,8},{10,11... | collective-permute-start | bytes 12582920 | tf_op jit(solution)/shard_map/ppermute | solution.py:38
  88.1 1.3 copy-start.5
  89.4 1.6 copy-start.6
  99.8 3.0 %copy-start.4 = (bf16[4,2,512,512]{3,2,1,0:T(8,128)(2,1)}, bf16[4,2,512,512]{3,2,1,0:T(8,128)(2,1)S(1)}, u32[]{:S(2)}) copy-start(bf16[4,2,512,512]{3,2,1,0:T(8,128)(2,1)S(1)} %weight_gradient.1) | copy-start | bytes 12582916
  102.8 46.1 %collective-permute-start.14 = (bf16[2,512,512]{2,1,0:T(8,128)(2,1)}, bf16[2,512,512]{2,1,0:T(8,128)(2,1)}, u32[]{:S(2)}, u32[]{:S(2)}) collective-permute-start(bf16[2,512,512]{2,1,0:T(8,128)(2,1)} %get-tuple-element.31), channel_id=1, source_target_pairs={{0,16},{1,17},{2,18},{3,19},{4,20},{5,21},{6,22},{7,23},{8,24},{9,... | collective-permute-start | bytes 3145736 | tf_op jit(solution)/shard_map/ppermute | solution.py:38
  102.8 61.6 %collective-permute-start.16 = (bf16[2,512,512]{2,1,0:T(8,128)(2,1)}, bf16[2,512,512]{2,1,0:T(8,128)(2,1)}, u32[]{:S(2)}, u32[]{:S(2)}) collective-permute-start(bf16[2,512,512]{2,1,0:T(8,128)(2,1)} %get-tuple-element.32), channel_id=1, source_target_pairs={{0,48},{1,49},{2,50},{3,51},{4,52},{5,53},{6,54},{7,55},{8,56},{9,... | collective-permute-start | bytes 3145736 | tf_op jit(solution)/shard_map/ppermute | solution.py:38
  118.6 5.5 %copy-start.9 = (bf16[1024,512]{1,0:T(8,128)(2,1)S(1)}, bf16[1024,512]{1,0:T(8,128)(2,1)}, u32[]{:S(2)}) copy-start(bf16[1024,512]{1,0:T(8,128)(2,1)} %k_ref.3) | copy-start | bytes 3145732
  118.6 5.5 %copy-start.11 = (bf16[1024,512]{1,0:T(8,128)(2,1)S(1)}, bf16[1024,512]{1,0:T(8,128)(2,1)}, u32[]{:S(2)}) copy-start(bf16[1024,512]{1,0:T(8,128)(2,1)} %v_ref.3) | copy-start | bytes 3145732
  118.6 5.5 %copy-start.13 = (bf16[1024,512]{1,0:T(8,128)(2,1)S(1)}, bf16[1024,512]{1,0:T(8,128)(2,1)}, u32[]{:S(2)}) copy-start(bf16[1024,512]{1,0:T(8,128)(2,1)} %q_ref.3) | copy-start | bytes 3145732
  118.6 5.5 %copy-start.16 = (bf16[1024,512]{1,0:T(8,128)(2,1)S(1)}, bf16[1024,512]{1,0:T(8,128)(2,1)}, u32[]{:S(2)}) copy-start(bf16[1024,512]{1,0:T(8,128)(2,1)} %copy-done.14) | copy-start | bytes 3145732
  118.6 47.8 %collective-permute-start.15 = (bf16[2,512,512]{2,1,0:T(8,128)(2,1)}, bf16[2,512,512]{2,1,0:T(8,128)(2,1)}, u32[]{:S(2)}, u32[]{:S(2)}) collective-permute-start(bf16[2,512,512]{2,1,0:T(8,128)(2,1)} %get-tuple-element.33), channel_id=1, source_target_pairs={{0,32},{1,33},{2,34},{3,35},{4,36},{5,37},{6,38},{7,39},{8,40},{9,... | collective-permute-start | bytes 3145736 | tf_op jit(solution)/shard_map/ppermute | solution.py:38
  145.9 1.0 copy-start.17
  146.9 139.0 %collective-permute-start.11 = (bf16[2,1024,512]{2,1,0:T(8,128)(2,1)S(1)}, bf16[2,1024,512]{2,1,0:T(8,128)(2,1)}, u32[]{:S(2)}, u32[]{:S(2)}) collective-permute-start(bf16[2,1024,512]{2,1,0:T(8,128)(2,1)S(1)} %get-tuple-element.28), channel_id=1, source_target_pairs={{4,0},{8,4},{12,8},{16,12},{20,16},{24,20},{28,24},{32,28},{36,32}... | collective-permute-start | bytes 6291464 | tf_op jit(solution)/shard_map/ppermute | solution.py:63
  148.9 47.6 %collective-permute-start.12 = (bf16[2,512,512]{2,1,0:T(8,128)(2,1)}, bf16[2,512,512]{2,1,0:T(8,128)(2,1)}, u32[]{:S(2)}, u32[]{:S(2)}) collective-permute-start(bf16[2,512,512]{2,1,0:T(8,128)(2,1)} %copy-done.17), channel_id=1, source_target_pairs={{0,4},{1,5},{2,6},{3,7},{4,8},{5,9},{6,10},{7,11},{8,12},{9,13},{1... | collective-permute-start | bytes 3145736 | tf_op jit(solution)/shard_map/ppermute | solution.py:38
  151.0 2.2 copy-start.1
  156.8 35.8 %copy-start.2 = (bf16[2,1024,1024]{2,1,0:T(8,128)(2,1)}, bf16[2,1024,1024]{2,1,0:T(8,128)(2,1)S(1)}, u32[]{:S(2)}) copy-start(bf16[2,1024,1024]{2,1,0:T(8,128)(2,1)S(1)} %projection.2) | copy-start | bytes 12582916
  170.0 29.5 %collective-permute-start.17 = (bf16[2,512,128]{2,1,0:T(8,128)(2,1)}, bf16[2,512,128]{2,1,0:T(8,128)(2,1)}, u32[]{:S(2)}, u32[]{:S(2)}) collective-permute-start(bf16[2,512,128]{2,1,0:T(8,128)(2,1)} %get-tuple-element.36), channel_id=1, source_target_pairs={{0,4},{1,5},{2,6},{3,7},{4,8},{5,9},{6,10},{7,11},{8,12},{9,13},{1... | collective-permute-start | bytes 786440 | tf_op jit(solution)/shard_map/ppermute | solution.py:38
  180.6 40.4 %collective-permute-start.19 = (bf16[2,512,128]{2,1,0:T(8,128)(2,1)}, bf16[2,512,128]{2,1,0:T(8,128)(2,1)}, u32[]{:S(2)}, u32[]{:S(2)}) collective-permute-start(bf16[2,512,128]{2,1,0:T(8,128)(2,1)} %get-tuple-element.37), channel_id=1, source_target_pairs={{0,8},{1,9},{2,10},{3,11},{4,12},{5,13},{6,14},{7,15},{8,0},{9,1},... | collective-permute-start | bytes 786440 | tf_op jit(solution)/shard_map/ppermute | solution.py:38
  190.0 31.0 %collective-permute-start.18 = (bf16[2,512,128]{2,1,0:T(8,128)(2,1)S(1)}, bf16[2,512,128]{2,1,0:T(8,128)(2,1)}, u32[]{:S(2)}, u32[]{:S(2)}) collective-permute-start(bf16[2,512,128]{2,1,0:T(8,128)(2,1)S(1)} %get-tuple-element.38), channel_id=1, source_target_pairs={{0,12},{1,13},{2,14},{3,15},{4,0},{5,1},{6,2},{7,3},{8,4},{9,5},{1... | collective-permute-start | bytes 786440 | tf_op jit(solution)/shard_map/ppermute | solution.py:38
  196.5 96.5 %collective-permute-start.7 = (bf16[1024,1024]{1,0:T(8,128)(2,1)}, bf16[1024,1024]{1,0:T(8,128)(2,1)}, u32[]{:S(2)}, u32[]{:S(2)}) collective-permute-start(bf16[1024,1024]{1,0:T(8,128)(2,1)} %fusion.1), channel_id=1, source_target_pairs={{0,2},{1,3},{2,0},{3,1},{4,6},{5,7},{6,4},{7,5},{8,10},{9,11},{10,... | collective-permute-start | bytes 6291464 | tf_op jit(solution)/shard_map/ppermute | solution.py:38
  199.6 90.0 %collective-permute-start.13 = (bf16[2,512,512]{2,1,0:T(8,128)(2,1)}, bf16[2,512,512]{2,1,0:T(8,128)(2,1)}, u32[]{:S(2)}, u32[]{:S(2)}) collective-permute-start(bf16[2,512,512]{2,1,0:T(8,128)(2,1)} %collective-permute-done.12), channel_id=1, source_target_pairs={{12,0},{0,4},{20,8},{24,12},{28,16},{16,20},{36,24},{40,28},{44,32... | collective-permute-start | bytes 3145736 | tf_op jit(solution)/shard_map/ppermute | solution.py:73
  222.3 62.9 %collective-permute-start.20 = (bf16[512,128]{1,0:T(8,128)(2,1)S(1)}, bf16[512,128]{1,0:T(8,128)(2,1)S(1)}, u32[]{:S(2)}, u32[]{:S(2)}) collective-permute-start(bf16[512,128]{1,0:T(8,128)(2,1)S(1)} %dynamic-slice_bitcast_fusion), channel_id=1, source_target_pairs={{0,64},{1,65},{2,66},{3,67},{4,68},{5,69},{6,70},{7,71},{8,72},{9,... | collective-permute-start | bytes 393224 | tf_op jit(solution)/shard_map/ppermute | solution.py:38
  291.5 2.9 copy-start.3

commit v2 on v1

v2 whole, which is shorter than its diff:
```python
import functools
import math

import jax
import jax.numpy as jnp
from jax import lax
from jax.experimental import pallas as pl
from jax.experimental.pallas import tpu as pltpu
from jax.sharding import PartitionSpec as P

HDIM = 128
BLK = 512
WIN = 4
SCALE = 1.0 / math.sqrt(HDIM)
SCALE2 = SCALE * math.log2(math.e)
AXES = ("ctx", "tp")
NT = (((1,), (1,)), ((), ()))
NN = (((1,), (0,)), ((), ()))
f32 = jnp.float32
bf16 = jnp.bfloat16


def places():
    for x_lo in range(2):
        for y in range(4):
            for z in range(4):
                for x_hi in range(2):
                    for core in range(2):
                        yield x_lo, y, z, x_hi, core


def number(x_lo, y, z, x_hi, core):
    return ((x_lo * 4 + y) * 4 + z) * 4 + x_hi * 2 + core


def move(value, target):
    pairs = [(number(*place), number(*target(*place))) for place in places()]
    return lax.ppermute(value, AXES, pairs)


def to_core(value):
    return move(value, lambda x_lo, y, z, x_hi, core: (x_lo, y, z, x_hi, 1 - core))


def to_x_hi(value):
    return move(value, lambda x_lo, y, z, x_hi, core: (x_lo, y, z, 1 - x_hi, core))


def to_x_lo(value):
    return move(value, lambda x_lo, y, z, x_hi, core: (1 - x_lo, y, z, x_hi, core))


def to_z(value, steps):
    return move(value, lambda x_lo, y, z, x_hi, core: (x_lo, y, (z + steps) % 4, x_hi, core))


EDGE = 15


def along_ctx(value, steps, without=()):
    pairs = [(s, s + steps) for s in range(32) if 0 <= s + steps < 32 and s not in without]
    return lax.ppermute(value, "ctx", pairs)


def from_next_z(value, sign, without):
    pairs = []
    for source in range(32):
        if 0 <= source + 2 * sign < 32 and source != without:
            middle = source // 4 * 4 + (source % 4 - sign) % 4
            pairs.append((middle, source + 2 * sign))
    return lax.ppermute(value, "ctx", pairs)


def across(value, sources):
    return lax.ppermute(value, "ctx", [(s, (s + 16) % 32) for s in sources])


def gathered(value, sources, target):
    return [lax.ppermute(value, "ctx", [((s + 16) % 32, target)]) for s in sources]


def block_rule(spans, pairs, query_block, key_block):
    listed = jnp.any(
        (pairs[:, 0] == query_block[..., None]) & (pairs[:, 1] == key_block[..., None]), axis=-1
    )
    span_lower = spans[:, 0]
    span_upper = spans[:, 0] + spans[:, 1]
    query_inside = (span_lower <= query_block[..., None]) & (query_block[..., None] < span_upper)
    key_inside = (span_lower <= key_block[..., None]) & (key_block[..., None] < span_upper)
    same = jnp.any(query_inside & key_inside, axis=-1)
    reach = (query_block - key_block >= 0) & (query_block - key_block < WIN)
    return listed & same & reach


def dot(a, b, dims):
    return lax.dot_general(a, b, dims, preferred_element_type=f32)


def causal():
    key_row = lax.broadcasted_iota(jnp.int32, (BLK, BLK), 0)
    query_column = lax.broadcasted_iota(jnp.int32, (BLK, BLK), 1)
    return key_row <= query_column


def block_rows(index):
    return pl.ds(index * BLK, BLK)


OWN_TILES = ((0, 0, 0), (1, 0, 1), (1, 1, 0))
BEHIND_TILES = ((0, 3, 0), (0, 2, 1), (0, 1, 2), (1, 3, 1), (1, 2, 2))


def key_value(index, near_k, near_v, far, edge_v, edge_far):
    if index == 0:
        return far[0] + edge_far[0], far[1] + edge_far[1]
    rows = block_rows(index - 1)
    return near_k[rows, :], near_v[rows, :] + edge_v[index - 1]


def absorb(keys, vals, query, top, total, acc, rows):
    s = dot(keys, query, NT)
    old = top
    m = jnp.maximum(old, jnp.max(s, axis=0, keepdims=True))
    p = jnp.exp2(s * SCALE2 - m * SCALE2)
    fix = jnp.exp2((old - m) * SCALE2)
    part = dot(vals.T, p.astype(bf16), NN)
    acc[:, rows] = acc[:, rows] * fix + part
    return m, total * fix + jnp.sum(p, axis=0, keepdims=True)


def forward_own_kernel(flags, q_ref, k_ref, v_ref, after, acc, top, total):
    for qb, o, index in OWN_TILES:
        rows = block_rows(qb)
        line = slice(qb, qb + 1)

        def diagonal(rows=rows, line=line):
            s = jnp.where(causal(), dot(k_ref[rows, :], q_ref[rows, :], NT), -jnp.inf)
            m = jnp.max(s, axis=0, keepdims=True)
            p = jnp.exp2(s * SCALE2 - m * SCALE2)
            acc[:, rows] = dot(v_ref[rows, :].T, p.astype(bf16), NN)
            top[0, line, :] = m
            total[0, line, :] = jnp.sum(p, axis=0, keepdims=True)

        def nothing(rows=rows, line=line):
            acc[:, rows] = jnp.zeros((HDIM, BLK), f32)
            top[0, line, :] = jnp.zeros((1, BLK), f32)
            total[0, line, :] = jnp.ones((1, BLK), f32)

        def tile(rows=rows, line=line, index=index):
            held = block_rows(index)
            top[0, line, :], total[0, line, :] = absorb(
                k_ref[held, :], v_ref[held, :], q_ref[rows, :],
                top[0, line, :], total[0, line, :], acc, rows,
            )

        listed = flags[qb * WIN + o] == 1
        if o == 0:
            pl.when(listed)(diagonal)
            pl.when(jnp.logical_not(listed))(nothing)
        else:
            pl.when(listed)(tile)


def forward_behind_kernel(
    flags, q_ref, k1_ref, v1_ref, far_ref, e0, e1, acc_in, top_in, total_in,
    after, out_ref, turned_ref, log_ref, acc, top, total,
):
    acc[...] = acc_in[...]
    top[...] = top_in[0]
    total[...] = total_in[0]
    for qb, o, index in BEHIND_TILES:
        rows = block_rows(qb)
        line = slice(qb, qb + 1)

        @pl.when(flags[qb * WIN + o] == 1)
        def _(rows=rows, line=line, index=index):
            keys, vals = key_value(index, k1_ref, v1_ref, far_ref, e0, e1)
            top[line, :], total[line, :] = absorb(
                keys, vals, q_ref[rows, :], top[line, :], total[line, :], acc, rows
            )

    for qb in range(2):
        rows = block_rows(qb)
        result = acc[:, rows] * (1.0 / total[qb : qb + 1, :])
        turned_ref[:, rows] = result.astype(bf16)
        out_ref[rows, :] = result.T.astype(bf16)
    log_ref[0] = top[...] * SCALE2 + jnp.log2(total[...])


def tile_grads(keys, vals, query, grad, log_sum, delta, diagonal):
    p = jnp.exp2(dot(keys, query, NT) * SCALE2 - log_sum)
    if diagonal:
        p = jnp.where(causal(), p, 0.0)
    value_part = dot(p.astype(bf16), grad, NN)
    dp = dot(vals, grad, NT)
    ds = (p * (dp - delta)).astype(bf16)
    return dot(ds, query, NN), value_part, dot(keys.T, ds, NN)


def backward_behind_kernel(
    flags, q_ref, k1_ref, v1_ref, far_ref, e0, e1, out_ref, grad_ref, log_ref,
    after, near_back, far_back, dq, delta_ref, dk, dv,
):
    dk[...] = jnp.zeros_like(dk)
    dv[...] = jnp.zeros_like(dv)
    dq[...] = jnp.zeros_like(dq)
    product = grad_ref[...].astype(f32) * out_ref[...].astype(f32)
    delta = jnp.sum(product.T, axis=0, keepdims=True)
    for qb in range(2):
        delta_ref[0, qb : qb + 1, :] = delta[:, qb * BLK : (qb + 1) * BLK]
    for qb, o, index in BEHIND_TILES:
        rows = block_rows(qb)
        line = slice(qb, qb + 1)

        @pl.when(flags[qb * WIN + o] == 1)
        def _(rows=rows, line=line, index=index):
            keys, vals = key_value(index, k1_ref, v1_ref, far_ref, e0, e1)
            key_part, value_part, query_part = tile_grads(
                keys, vals, q_ref[rows, :], grad_ref[rows, :],
                log_ref[0, line, :], delta_ref[0, line, :], False,
            )
            dk[block_rows(index), :] += key_part
            dv[block_rows(index), :] += value_part
            dq[:, rows] += query_part

    far_back[0] = (dk[block_rows(0), :] * SCALE).astype(bf16)
    far_back[1] = dv[block_rows(0), :].astype(bf16)
    near_back[0] = (dk[pl.ds(BLK, 2 * BLK), :] * SCALE).astype(bf16)
    near_back[1] = dv[pl.ds(BLK, 2 * BLK), :].astype(bf16)


def backward_own_kernel(
    flags, q_ref, k_ref, v_ref, grad_ref, log_ref, dq_in, delta_ref, after,
    dq_ref, own_ref, dk, dv, dq,
):
    dk[...] = jnp.zeros_like(dk)
    dv[...] = jnp.zeros_like(dv)
    dq[...] = dq_in[...]
    for qb, o, index in OWN_TILES:
        rows = block_rows(qb)
        line = slice(qb, qb + 1)

        @pl.when(flags[qb * WIN + o] == 1)
        def _(rows=rows, line=line, index=index, o=o):
            held = block_rows(index)
            key_part, value_part, query_part = tile_grads(
                k_ref[held, :], v_ref[held, :], q_ref[rows, :], grad_ref[rows, :],
                log_ref[0, line, :], delta_ref[0, line, :], o == 0,
            )
            dk[held, :] += key_part
            dv[held, :] += value_part
            dq[:, rows] += query_part

    own_ref[0] = dk[...] * SCALE
    own_ref[1] = dv[...]
    dq_ref[...] = (dq[...] * SCALE).T.astype(bf16)


def finish_kernel(place, own_ref, near_ref, far_ref, after, key_ref, value_ref):
    for part, result in enumerate((key_ref, value_ref)):
        for block in range(2):
            rows = block_rows(block)
            total = own_ref[part, rows, :] + near_ref[part, rows, :].astype(f32)
            if block == 1:
                total += far_ref[part].astype(f32)
            result[rows, :] = total.astype(bf16)


def head(rows):
    return pl.BlockSpec((rows, HDIM), lambda h, *_: (0, h))


def head_pair(rows):
    return pl.BlockSpec((2, rows, HDIM), lambda h, *_: (0, 0, h))


HEAD_LINES = pl.BlockSpec((1, 2, BLK), lambda h, *_: (h, 0, 0))
ANY = pl.BlockSpec(memory_space=pl.ANY)
HEAD_TURNED = pl.BlockSpec((HDIM, 1024), lambda h, *_: (h, 0))


def shape(dims, dtype):
    return jax.ShapeDtypeStruct(dims, dtype)


WIDTH = 512
HEADS = WIDTH // HDIM
LINES = shape((HEADS, 2, BLK), f32)
TURNED = shape((WIDTH, 1024), f32)


def call(kernel, name, grid, ins, outs, out_shape, scratch, args):
    return pl.pallas_call(
        kernel,
        grid_spec=pltpu.PrefetchScalarGridSpec(
            num_scalar_prefetch=1,
            grid=grid,
            in_specs=ins,
            out_specs=outs,
            scratch_shapes=scratch,
        ),
        out_shape=out_shape,
        compiler_params=pltpu.CompilerParams(vmem_limit_bytes=64 << 20),
        cost_estimate=pl.CostEstimate(flops=1, bytes_accessed=1, transcendentals=0),
        name=name,
    )(*args)


def forward_own(flags, q, k, v, after):
    return call(
        forward_own_kernel, "forward_own", (HEADS,),
        [head(1024)] * 3 + [ANY],
        [HEAD_TURNED, HEAD_LINES, HEAD_LINES],
        [TURNED, LINES, LINES],
        [], (flags, q, k, v, after),
    )


def forward_behind(flags, q, near_k, near_v, far, edge, state, after):
    lines = pltpu.VMEM((2, BLK), f32)
    return call(
        forward_behind_kernel, "forward_behind", (HEADS,),
        [head(1024)] * 3 + [head_pair(512)] * 3
        + [HEAD_TURNED, HEAD_LINES, HEAD_LINES, ANY],
        [head(1024), HEAD_TURNED, HEAD_LINES],
        [shape((1024, WIDTH), bf16), shape((WIDTH, 1024), bf16), LINES],
        [pltpu.VMEM((HDIM, 1024), f32), lines, lines],
        (flags, q, near_k, near_v, far, *edge, *state, after),
    )


def backward_behind(flags, q, near_k, near_v, far, edge, out, grad, log_sum, after):
    held = pltpu.VMEM((3 * BLK, HDIM), f32)
    return call(
        backward_behind_kernel, "backward_behind", (HEADS,),
        [head(1024)] * 3 + [head_pair(512)] * 3
        + [head(1024), head(1024), HEAD_LINES, ANY],
        [head_pair(1024), head_pair(512), HEAD_TURNED, HEAD_LINES],
        [shape((2, 1024, WIDTH), bf16), shape((2, 512, WIDTH), bf16), TURNED, LINES],
        [held, held], (flags, q, near_k, near_v, far, *edge, out, grad, log_sum, after),
    )


def backward_own(flags, q, k, v, grad, log_sum, dq, delta, after):
    held = pltpu.VMEM((2 * BLK, HDIM), f32)
    return call(
        backward_own_kernel, "backward_own", (HEADS,),
        [head(1024)] * 4 + [HEAD_LINES, HEAD_TURNED, HEAD_LINES, ANY],
        [head(1024), head_pair(1024)],
        [shape((1024, WIDTH), bf16), shape((2, 1024, WIDTH), f32)],
        [held, held, pltpu.VMEM((HDIM, 1024), f32)],
        (flags, q, k, v, grad, log_sum, dq, delta, after),
    )


def finish(place, own, near, far, after):
    return call(
        finish_kernel, "key_value_sum", (HEADS,),
        [head_pair(1024)] * 2 + [head_pair(512), ANY],
        [head(1024), head(1024)],
        [shape((1024, WIDTH), bf16)] * 2,
        [], (place, own, near, far, after),
    )


def pack_kernel(flags, k_ref, v_ref, second_ref, crossing_ref):
    second_ref[0] = k_ref[block_rows(1), :]
    second_ref[1] = v_ref[block_rows(1), :]
    first = flags[0] == EDGE - 1
    for part in range(2):
        crossing_ref[part] = jnp.where(first, second_ref[part], v_ref[block_rows(part), :])


def pack(ctx, k, v):
    return call(
        pack_kernel, "halo_pack", (HEADS,), [head(1024)] * 2, [head_pair(512)] * 2,
        [shape((2, 512, WIDTH), bf16)] * 2, [], (ctx, k, v),
    )


def nothing_kernel(*refs):
    pass


def behind(value, *after):
    return pl.pallas_call(
        nothing_kernel,
        in_specs=[ANY] * (1 + len(after)),
        out_specs=ANY,
        out_shape=shape(value.shape, value.dtype),
        input_output_aliases={0: 0},
        compiler_params=pltpu.CompilerParams(vmem_limit_bytes=64 << 20),
        name="order",
    )(value, *after)


def grad_kernel(place, a_ref, b_ref, wa_ref, wb_ref, *rest):
    total = dot(a_ref[...], wa_ref[...], NT) + dot(b_ref[...], wb_ref[...], NT)
    if len(rest) == 3:
        total += rest[0][...]
    rest[-1][...] = total.astype(rest[-1].dtype)


def grad_terms(place, first, a, b, weight, before, after):
    tile = 256
    row = pl.BlockSpec((tile, 1024), lambda i, place: (i, 0))
    result = pl.BlockSpec((tile, 512), lambda i, place: (i, 0))

    def columns(flip):
        return pl.BlockSpec((512, 1024), lambda i, place: (0, place[0] ^ flip))

    more = [] if before is None else [before]
    return call(
        grad_kernel, "projection_backward", (1024 // tile,),
        [row, row, columns(first), columns(first + 1)] + [result] * len(more) + [ANY], result,
        shape((1024, 512), bf16 if more else f32), [], (place, a, b, weight, weight, *more, after),
    )


def weight_kernel(place, turned_ref, *refs):
    out_ref = refs[-1]
    for part in range(4):

        @pl.when(pl.program_id(0) == part)
        def _(part=part):
            out_ref[0, 0] = dot(turned_ref[...], refs[part][...], NN).astype(bf16)


def weight_terms(place, turned, cotangents):
    def piece(part):
        return pl.BlockSpec(
            (1024, 512),
            lambda i, half, place: (
                0, jnp.where(i == part, half, jnp.where(i < part, 0, 1)),
            ),
        )

    def target(i, half, place):
        owner = place[0] ^ i
        return (owner % 2 * 2 + half, owner // 2, 0, 0)

    return call(
        weight_kernel, "weight_gradient", (4, 2),
        [pl.BlockSpec((512, 1024), lambda i, half, place: (0, 0))] + [piece(p) for p in range(4)],
        pl.BlockSpec((1, 1, 512, 512), target),
        shape((4, 2, 512, 512), bf16), [], (place, turned, *cotangents),
    )


def groups_along(axis):
    groups = {}
    for ctx in range(32):
        spot = [ctx // 16, ctx // 4 % 4, ctx % 4]
        spot[axis] = None
        groups.setdefault(tuple(spot), []).append(ctx)
    return list(groups.values())


def pieces_kernel(place, in_ref, after, *outs):
    for slot, out_ref in enumerate(outs):

        @pl.when(pl.program_id(0) == slot)
        def _(out_ref=out_ref):
            out_ref[...] = in_ref[...]


def pieces_by_z(place, total, after):
    return call(
        pieces_kernel, "weight_by_z", (4,),
        [pl.BlockSpec((2, 512, 128), lambda i, place: (0, 0, (place[2] + i + 1) % 4)), ANY],
        [pl.BlockSpec((2, 512, 128), lambda i, place: (0, 0, 0))] * 4,
        [shape((2, 512, 128), bf16)] * 4, [], (place, total, after),
    )


def weight_z_kernel(place, a_ref, b_ref, c_ref, d_ref, kept_ref, sent_ref):
    def total(index):
        return sum(ref[index].astype(f32) for ref in (a_ref, b_ref, c_ref, d_ref))

    kept_ref[...] = total(place[3])
    sent_ref[...] = total(1 - place[3]).astype(bf16)


def weight_z_sum(place, terms):
    whole = pl.BlockSpec((2, 512, 128), lambda i, place: (0, 0, 0))
    result = pl.BlockSpec((512, 128), lambda i, place: (0, 0))
    return call(
        weight_z_kernel, "weight_z_sum", (1,), [whole] * 4, [result] * 2,
        [shape((512, 128), f32), shape((512, 128), bf16)], [], (place, *terms),
    )


def copy_kernel(place, in_ref, *refs):
    refs[-1][...] = in_ref[...]


def far_columns(place, weight):
    return call(
        copy_kernel, "projection_quarter", (1,),
        [pl.BlockSpec((128, 2048), lambda i, place: (place[1], 1 - place[0] // 2))],
        pl.BlockSpec((128, 2048), lambda i, place: (0, 0)),
        shape((128, 2048), bf16), [], (place, weight),
    )


def two_kernel(place, a_ref, b_ref, after, a_out, b_out):
    a_out[...] = a_ref[...]
    b_out[...] = b_ref[...]


def late_copies(a, b, after):
    def rows(value):
        return pl.BlockSpec((256, value.shape[1]), lambda i, place: (i, 0))

    return call(
        two_kernel, "late_copies", (4,), [rows(a), rows(b), ANY], [rows(a), rows(b)],
        [shape(a.shape, a.dtype), shape(b.shape, b.dtype)],
        [], (jnp.zeros(1, jnp.int32), a, b, after),
    )


def core_kernel(place, own_ref, far_ref, after, out_ref):
    out_ref[0] = own_ref[...]
    out_ref[1] = far_ref[...]


def core_columns(place, weight, far_weight, after):
    return call(
        core_kernel, "projection_core", (1,),
        [
            pl.BlockSpec((512, 1024), lambda i, place: (0, place[0] ^ 1)),
            pl.BlockSpec((512, 1024), lambda i, place: (0, 1 - place[0] % 2)),
            ANY,
        ],
        pl.BlockSpec((2, 512, 1024), lambda i, place: (0, 0, 0)),
        shape((2, 512, 1024), bf16), [], (place, weight, far_weight, after),
    )


def mix_kernel(place, own, core, far, far_core, w_own, w_far, w_core, after, out_ref):
    total = dot(own[...], w_own[...], NN) + dot(core[...], w_core[0], NN)
    total += dot(far[...], w_far[...], NN) + dot(far_core[...], w_core[1], NN)
    out_ref[...] = total.astype(bf16)


def mix(place, attentions, weight, far_weight, core_weight, after):
    rows = pl.BlockSpec((256, 512), lambda i, place: (i, 0))
    return call(
        mix_kernel, "projection", (4,),
        [rows] * 4 + [
            pl.BlockSpec((512, 1024), lambda i, place: (0, place[0])),
            pl.BlockSpec((512, 1024), lambda i, place: (0, place[0] % 2)),
            pl.BlockSpec((2, 512, 1024), lambda i, place: (0, 0, 0)),
            ANY,
        ],
        pl.BlockSpec((256, 1024), lambda i, place: (i, 0)),
        shape((1024, 1024), bf16), [],
        (place, *attentions, weight, far_weight, core_weight, after),
    )


def per_device(queries, keys, values, out_weight, out_grad, spans, pairs):
    ctx = lax.axis_index("ctx")
    tp = lax.axis_index("tp")
    place = jnp.stack([tp, ctx // 4 % 4, ctx % 4, ctx // 16]).astype(jnp.int32)

    core_grad = to_core(out_grad)
    near_keys = along_ctx(keys, 1)
    second_half, crossing = pack(ctx.astype(jnp.int32).reshape(1), keys, values)
    far_moved = to_z(second_half, -1)
    crossed = across(crossing, (EDGE - 1, EDGE))
    far_weight = to_x_hi(far_columns(place, out_weight))

    query_block = ctx * 2 + jnp.arange(2, dtype=jnp.int32)[:, None] + jnp.zeros((1, WIN), jnp.int32)
    key_block = query_block - jnp.arange(WIN, dtype=jnp.int32)[None, :]
    listed = block_rule(spans, pairs, query_block, key_block).astype(jnp.int32).reshape(-1)
    flags = jnp.concatenate([listed, ctx.astype(jnp.int32).reshape(1)])
    own_state = forward_own(flags, queries, keys, values, crossing)
    held_values, held_grad = late_copies(values, out_grad, own_state[1])

    near_keys = behind(near_keys, held_grad)
    near_values = along_ctx(behind(held_values, near_keys), 1, (EDGE,))
    far = from_next_z(behind(far_moved, near_keys), 1, EDGE - 1)
    edge_far, edge_values = gathered(behind(crossed, near_keys), (EDGE - 1, EDGE), EDGE + 1)
    far_grad = to_x_hi(behind(held_grad, near_keys))
    far_weight = behind(far_weight, near_keys)
    terms = grad_terms(place, 0, out_grad, core_grad, out_weight, None, far_weight)
    far_weight = lax.all_gather(
        far_weight, "ctx", axis=0, tiled=True, axis_index_groups=groups_along(1)
    )
    keys_values = (flags, queries, near_keys, near_values, far, (edge_values, edge_far))
    attention, turned, log_sum = forward_behind(*keys_values, own_state, terms)
    far_grad = behind(far_grad, log_sum, far_weight)
    far_core_grad = to_core(far_grad)

    core_attention = to_core(attention)
    far_attention = to_x_hi(attention)
    weight_parts = weight_terms(place, turned, (out_grad, core_grad, far_grad, far_core_grad))
    weight_y = lax.psum_scatter(
        weight_parts, "ctx", scatter_dimension=0, axis_index_groups=groups_along(1)
    )
    attn_grad = grad_terms(place, 2, far_grad, far_core_grad, out_weight, terms, weight_parts)
    near_back, far_back, dq, delta = backward_behind(
        *keys_values, attention, attn_grad, log_sum, attn_grad
    )
    near_back = along_ctx(near_back, -1)
    far_moved = to_z(far_back, 1)
    far_attention = behind(far_attention, delta)
    far_core_attention = to_core(far_attention)
    query_grad, own = backward_own(
        flags, queries, keys, values, attn_grad, log_sum, dq, delta, delta
    )
    core_weight = to_core(core_columns(place, out_weight, far_weight, delta))
    attentions = (attention, core_attention, far_attention, far_core_attention)
    mixed = mix(place, attentions, out_weight, far_weight, core_weight, own)

    far_back = from_next_z(behind(far_moved, mixed), -1, None)
    weight_pieces = pieces_by_z(place, weight_y, mixed)
    kept, sent = weight_z_sum(
        place, [weight_pieces[3]] + [to_z(weight_pieces[s], s + 1) for s in (0, 2, 1)]
    )
    weight_grad = kept + to_x_lo(sent).astype(f32)
    key_grad, value_grad = finish(place, own, near_back, far_back, kept)
    return (mixed, query_grad, key_grad, value_grad, weight_grad)


def solution(mesh):
    placed = (
        P("ctx", "tp"),
        P("ctx", "tp"),
        P("ctx", "tp"),
        P("tp", None),
        P("ctx", "tp"),
        P(),
        P(),
    )
    return jax.shard_map(
        per_device,
        mesh=mesh,
        in_specs=placed,
        out_specs=(P("ctx", "tp"), P("ctx", "tp"), P("ctx", "tp"), P("ctx", "tp"), P("tp", "ctx")),
        check_vma=False,
    )
```

time: 302 us -> 301 us (level)
  the two profiles are of different devices: /device:TPU:36 before, /device:TPU:30 now
where the time goes in v2:
time: 301 us; the launch traced here: 295 us
  Pallas kernels  97.1 us (32%)
  waiting for transfers between devices  97 us (32%)
  starting transfers between devices  77.6 us (26%)
  between operations  14.2 us (5%)
  other arithmetic  7.24 us (2%)
    pallas_call x15, Pallas kernels, call(): pl.pallas_call(kernel, grid_spec=pltpu.PrefetchScalarGridSpec(num_scalar_...  97.1 us
    ppermute x14, waiting for transfers between devices, move(): return lax.ppermute(value, AXES, pairs)  67.5 us
    ppermute x2, starting transfers between devices, from_next_z(): return lax.ppermute(value, 'ctx', pairs)  30.6 us
    ppermute x14, starting transfers between devices, move(): return lax.ppermute(value, AXES, pairs)  29.5 us
    ppermute x3, waiting for transfers between devices, along_ctx(): return lax.ppermute(value, 'ctx', pairs)  15.6 us
    reduce_scatter x1, waiting for transfers between devices, per_device(): lax.psum_scatter(weight_parts, 'ctx', scatter_dimension=0, axis_index_gro...  13.9 us
    ppermute x3, starting transfers between devices, along_ctx(): return lax.ppermute(value, 'ctx', pairs)  12.6 us
  transfers between devices with their start and end apart: 24, of which 8 were waited for; matrix products, arithmetic and copies ran while one was open for 2% of the time, Pallas kernels for 28%

profile of v2, /device:TPU:30, one launch (start us, length us, event | category | flops | bytes accessed | tf_op | source)
XLA Modules:
  0.0 295.3 jit_solution(7583763112451028746)
XLA Ops:
  7.3 0.7 pad_add_fusion.place
  7.9 2.6 projection_quarter.1
  10.5 1.4 collective-permute-start.8
  11.9 3.8 %collective-permute-start = (bf16[1024,512]{1,0:T(8,128)(2,1)}, bf16[1024,512]{1,0:T(8,128)(2,1)}, u32[]{:S(2)}, u32[]{:S(2)}) collective-permute-start(bf16[1024,512]{1,0:T(8,128)(2,1)} %k_ref.5), channel_id=1, source_target_pairs={{0,4},{4,8},{8,12},{12,16},{16,20},{20,24},{24,28},{28,32},{32,36}... | collective-permute-start | bytes 3145736 | tf_op jit(solution)/shard_map/ppermute | solution.py:62
  15.8 1.3 bitcast_add_fusion
  17.1 1.3 slice_bitcast_fusion
  18.3 0.5 iota_add_fusion
  18.9 3.9 %halo_pack.1 = (bf16[2,512,512]{2,1,0:T(8,128)(2,1)}, bf16[2,512,512]{2,1,0:T(8,128)(2,1)}) custom-call(s32[1]{0:T(128)} %bitcast.8.flags, bf16[1024,512]{1,0:T(8,128)(2,1)} %k_ref.5, bf16[1024,512]{1,0:T(8,128)(2,1)} %v_ref.5), custom_call_target="tpu_custom_call" | custom-call | flops 1 | bytes 1 | tf_op jit(solution)/shard_map/halo_pack/pallas_call | solution.py:293
  22.7 0.7 iota_subtract_fusion
  23.5 0.8 fusion
  24.2 0.9 and_reduce_fusion.1
  25.1 0.8 and_reduce_fusion
  26.0 0.6 pad_add_fusion.1.flags
  26.7 7.4 %forward_own.1 = (f32[512,1024]{1,0:T(8,128)}, f32[4,2,512]{2,1,0:T(2,128)}, f32[4,2,512]{2,1,0:T(2,128)}) custom-call(s32[9]{0:T(128)} %pad_add_fusion.1.flags, bf16[1024,512]{1,0:T(8,128)(2,1)} %q_ref.7, bf16[1024,512]{1,0:T(8,128)(2,1)} %k_ref.5, bf16[1024,512]{1,0:T(8,128)(2,1)} %v_ref.5, bf16[2,512,512]{2,1,0:T(8,128)(2,1)} %get-tuple-element.29.after), custom_call_target="tpu_custom_call" | custom-call | flops 1 | bytes 1 | tf_op jit(solution)/shard_map/forward_own/pallas_call | solution.py:293
  34.1 4.2 %late_copies.1 = (bf16[1024,512]{1,0:T(8,128)(2,1)}, bf16[1024,1024]{1,0:T(8,128)(2,1)}) custom-call(s32[1]{0:T(128)} %constant.56.clone.1.place, bf16[1024,512]{1,0:T(8,128)(2,1)} %v_ref.5, bf16[1024,1024]{1,0:T(8,128)(2,1)} %refs_0_.1, f32[4,2,512]{2,1,0:T(2,128)} %get-tuple-element.30.after.top_in), custom_call_target="tpu_custom_call" | custom-call | flops 1 | bytes 1 | tf_op jit(solution)/shard_map/late_copies/pallas_call | solution.py:293
  38.3 2.9 collective-permute-done.refs_0_
  41.3 1.6 collective-permute-start.4
  42.9 1.3 collective-permute-start.2
  44.2 2.1 collective-permute-start.11
  46.3 1.6 collective-permute-start.5
  48.0 1.7 collective-permute-start.6
  49.6 19.0 %collective-permute-done.2.refs_0_ = bf16[2,512,512]{2,1,0:T(8,128)(2,1)} collective-permute-done((bf16[2,512,512]{2,1,0:T(8,128)(2,1)}, bf16[2,512,512]{2,1,0:T(8,128)(2,1)}, u32[]{:S(2)}, u32[]{:S(2)}) %collective-permute-start.2) | collective-permute-done | bytes 1048608 | tf_op jit(solution)/shard_map/ppermute | solution.py:38
  68.6 3.6 %collective-permute-start.1 = (bf16[1024,512]{1,0:T(8,128)(2,1)}, bf16[1024,512]{1,0:T(8,128)(2,1)}, u32[]{:S(2)}, u32[]{:S(2)}) collective-permute-start(bf16[1024,512]{1,0:T(8,128)(2,1)} %order.10), channel_id=1, source_target_pairs={{0,4},{4,8},{8,12},{12,16},{16,20},{20,24},{24,28},{28,32},{32,36}... | collective-permute-start | bytes 3145736 | tf_op jit(solution)/shard_map/ppermute | solution.py:62
  72.2 10.5 %collective-permute-start.3 = (bf16[2,512,512]{2,1,0:T(8,128)(2,1)}, bf16[2,512,512]{2,1,0:T(8,128)(2,1)}, u32[]{:S(2)}, u32[]{:S(2)}) collective-permute-start(bf16[2,512,512]{2,1,0:T(8,128)(2,1)} %order.11), channel_id=1, source_target_pairs={{12,8},{0,12},{4,16},{8,20},{28,24},{16,28},{20,32},{24,36},{44,40... | collective-permute-start | bytes 3145736 | tf_op jit(solution)/shard_map/ppermute | solution.py:71
  82.7 7.1 %projection_backward.2.after.rest_0_ = f32[1024,512]{1,0:T(8,128)} custom-call(s32[4]{0:T(128)} %pad_add_fusion.place, bf16[1024,1024]{1,0:T(8,128)(2,1)} %refs_0_.1, bf16[1024,1024]{1,0:T(8,128)(2,1)} %collective-permute-done.7.b_ref.refs_1_, bf16[512,4096]{1,0:T(8,128)(2,1)} %w_own.1, bf16[512,4096]{1,0:T(8,128)(2,1)} %w_own.1, ...), custom_call_target="tpu_custom_call" | custom-call | flops 1 | bytes 1 | tf_op jit(solution)/shard_map/projection_backward/pallas_call | solution.py:293
  89.8 12.6 %collective-permute-done.1.v1_ref = bf16[1024,512]{1,0:T(8,128)(2,1)} collective-permute-done((bf16[1024,512]{1,0:T(8,128)(2,1)}, bf16[1024,512]{1,0:T(8,128)(2,1)}, u32[]{:S(2)}, u32[]{:S(2)}) %collective-permute-start.1) | collective-permute-done | bytes 1048608 | tf_op jit(solution)/shard_map/ppermute | solution.py:62
  102.5 7.6 %forward_behind.1 = (bf16[1024,512]{1,0:T(8,128)(2,1)}, bf16[512,1024]{1,0:T(8,128)(2,1)}, f32[4,2,512]{2,1,0:T(2,128)}) custom-call(s32[9]{0:T(128)} %pad_add_fusion.1.flags, bf16[1024,512]{1,0:T(8,128)(2,1)} %q_ref.7, bf16[1024,512]{1,0:T(8,128)(2,1)} %order.9.refs_1_.k1_ref, bf16[1024,512]{1,0:T(8,128)(2,1)} %collective-permute-done.1.v1_ref, ...), custom_call_target="tpu_custom_call" | custom-call | flops 1 | bytes 1 | tf_op jit(solution)/shard_map/forward_behind/pallas_call | solution.py:293
  110.3 4.5 %collective-permute-done.12.refs_3_.b_ref = bf16[1024,1024]{1,0:T(8,128)(2,1)} collective-permute-done((bf16[1024,1024]{1,0:T(8,128)(2,1)}, bf16[1024,1024]{1,0:T(8,128)(2,1)}, u32[]{:S(2)}, u32[]{:S(2)}) %collective-permute-start.12) | collective-permute-done | bytes 2097184 | tf_op jit(solution)/shard_map/ppermute | solution.py:38
  114.8 12.1 %weight_gradient.1.rest_1_ = bf16[4,2,512,512]{3,2,1,0:T(8,128)(2,1)} custom-call(s32[4]{0:T(128)} %pad_add_fusion.place, bf16[512,1024]{1,0:T(8,128)(2,1)} %get-tuple-element.38.turned_ref, bf16[1024,1024]{1,0:T(8,128)(2,1)} %refs_0_.1, bf16[1024,1024]{1,0:T(8,128)(2,1)} %collective-permute-done.7.b_ref.refs_1_, bf16[1024,1024]{1,0:T(8,128)(2,1)} %order.15.refs_2_.a_ref, ...), custom_call_target="tpu_custom_call" | custom-call | flops 1 | bytes 1 | tf_op jit(solution)/shard_map/weight_gradient/pallas_call | solution.py:293
  126.8 7.4 %projection_backward.3.grad_ref.after = bf16[1024,512]{1,0:T(8,128)(2,1)} custom-call(s32[4]{0:T(128)} %pad_add_fusion.place, bf16[1024,1024]{1,0:T(8,128)(2,1)} %order.15.refs_2_.a_ref, bf16[1024,1024]{1,0:T(8,128)(2,1)} %collective-permute-done.12.refs_3_.b_ref, bf16[512,4096]{1,0:T(8,128)(2,1)} %w_own.1, bf16[512,4096]{1,0:T(8,128)(2,1)} %w_own.1, ...), custom_call_target="tpu_custom_call" | custom-call | flops 1 | bytes 1 | tf_op jit(solution)/shard_map/projection_backward/pallas_call | solution.py:293
  134.3 3.2 %collective-permute-start.10 = (bf16[1024,512]{1,0:T(8,128)(2,1)}, bf16[1024,512]{1,0:T(8,128)(2,1)}, u32[]{:S(2)}, u32[]{:S(2)}) collective-permute-start(bf16[1024,512]{1,0:T(8,128)(2,1)} %get-tuple-element.36.out_ref.own), channel_id=1, source_target_pairs={{0,2},{1,3},{2,0},{3,1},{4,6},{5,7},{6,4},{7,5},{8,10},{9,11},{10,... | collective-permute-start | bytes 3145736 | tf_op jit(solution)/shard_map/ppermute | solution.py:38
  137.5 9.2 %backward_behind.1 = (bf16[2,1024,512]{2,1,0:T(8,128)(2,1)}, bf16[2,512,512]{2,1,0:T(8,128)(2,1)}, f32[512,1024]{1,0:T(8,128)}, f32[4,2,512]{2,1,0:T(2,128)}) custom-call(s32[9]{0:T(128)} %pad_add_fusion.1.flags, bf16[1024,512]{1,0:T(8,128)(2,1)} %q_ref.7, bf16[1024,512]{1,0:T(8,128)(2,1)} %order.9.refs_1_.k1_ref, ...), custom_call_target="tpu_custom_call" | custom-call | flops 1 | bytes 1 | tf_op jit(solution)/shard_map/backward_behind/pallas_call | solution.py:293
  146.7 3.7 %projection_core.1 = bf16[2,512,1024]{2,1,0:T(8,128)(2,1)} custom-call(s32[4]{0:T(128)} %pad_add_fusion.place, bf16[512,4096]{1,0:T(8,128)(2,1)} %w_own.1, bf16[512,2048]{1,0:T(8,128)(2,1)} %all-gather.2.cloned.1.call-done.refs_2_.far_ref.w_far, f32[4,2,512]{2,1,0:T(2,128)} %get-tuple-element.39.refs_1_.after.delta_ref), custom_call_target="tpu_custom_call" | custom-call | flops 1 | bytes 1 | tf_op jit(solution)/shard_map/projection_core/pallas_call | solution.py:293
  150.4 0.5 collective-permute-start.9
  150.9 10.4 %collective-permute-done.10.refs_0_ = bf16[1024,512]{1,0:T(8,128)(2,1)} collective-permute-done((bf16[1024,512]{1,0:T(8,128)(2,1)}, bf16[1024,512]{1,0:T(8,128)(2,1)}, u32[]{:S(2)}, u32[]{:S(2)}) %collective-permute-start.10) | collective-permute-done | bytes 1048608 | tf_op jit(solution)/shard_map/ppermute | solution.py:38
  161.3 5.1 %collective-permute-start.15 = (bf16[2,1024,512]{2,1,0:T(8,128)(2,1)}, bf16[2,1024,512]{2,1,0:T(8,128)(2,1)}, u32[]{:S(2)}, u32[]{:S(2)}) collective-permute-start(bf16[2,1024,512]{2,1,0:T(8,128)(2,1)} %get-tuple-element.43), channel_id=1, source_target_pairs={{4,0},{8,4},{12,8},{16,12},{20,16},{24,20},{28,24},{32,28},{36,32}... | collective-permute-start | bytes 6291464 | tf_op jit(solution)/shard_map/ppermute | solution.py:62
  166.4 10.6 %backward_own.1 = (bf16[1024,512]{1,0:T(8,128)(2,1)}, f32[2,1024,512]{2,1,0:T(8,128)}) custom-call(s32[9]{0:T(128)} %pad_add_fusion.1.flags, bf16[1024,512]{1,0:T(8,128)(2,1)} %q_ref.7, bf16[1024,512]{1,0:T(8,128)(2,1)} %k_ref.5, bf16[1024,512]{1,0:T(8,128)(2,1)} %v_ref.5, bf16[1024,512]{1,0:T(8,128)(2,1)} %projection_backward.3.grad_ref.after, ...), custom_call_target="tpu_custom_call" | custom-call | flops 1 | bytes 1 | tf_op jit(solution)/shard_map/backward_own/pallas_call | solution.py:293
  177.1 9.4 %projection.1.refs_1_.after = bf16[1024,1024]{1,0:T(8,128)(2,1)} custom-call(s32[4]{0:T(128)} %pad_add_fusion.place, bf16[1024,512]{1,0:T(8,128)(2,1)} %get-tuple-element.36.out_ref.own, bf16[1024,512]{1,0:T(8,128)(2,1)} %collective-permute-done.9.core, bf16[1024,512]{1,0:T(8,128)(2,1)} %order.16.far, bf16[1024,512]{1,0:T(8,128)(2,1)} %collective-permute-done.13.far_core, ...), custom_call_target="tpu_custom_call" | custom-call | flops 1 | bytes 1 | tf_op jit(solution)/shard_map/projection/pallas_call | solution.py:293
  186.4 18.1 %collective-permute-done.16.refs_0_ = bf16[2,512,512]{2,1,0:T(8,128)(2,1)} collective-permute-done((bf16[2,512,512]{2,1,0:T(8,128)(2,1)}, bf16[2,512,512]{2,1,0:T(8,128)(2,1)}, u32[]{:S(2)}, u32[]{:S(2)}) %collective-permute-start.16) | collective-permute-done | bytes 1048608 | tf_op jit(solution)/shard_map/ppermute | solution.py:38
  204.5 20.1 %collective-permute-start.17 = (bf16[2,512,512]{2,1,0:T(8,128)(2,1)}, bf16[2,512,512]{2,1,0:T(8,128)(2,1)}, u32[]{:S(2)}, u32[]{:S(2)}) collective-permute-start(bf16[2,512,512]{2,1,0:T(8,128)(2,1)} %order.17), channel_id=1, source_target_pairs={{12,0},{0,4},{20,8},{24,12},{28,16},{16,20},{36,24},{40,28},{44,32... | collective-permute-start | bytes 3145736 | tf_op jit(solution)/shard_map/ppermute | solution.py:71
  224.7 13.9 %reduce-scatter.2.cloned.1.call-done = bf16[1,2,512,512]{3,2,1,0:T(8,128)(2,1)} async-done(((bf16[4,2,512,512]{3,2,1,0:T(8,128)(2,1)}), bf16[1,2,512,512]{3,2,1,0:T(8,128)(2,1)}) %reduce-scatter.2.cloned.1.call-update) | async-done | bytes 1048592 | tf_op jit(solution)/shard_map/reduce_scatter | solution.py:599
  238.5 3.7 %weight_by_z.1 = (bf16[2,512,128]{2,1,0:T(8,128)(2,1)}, bf16[2,512,128]{2,1,0:T(8,128)(2,1)}, bf16[2,512,128]{2,1,0:T(8,128)(2,1)}, bf16[2,512,128]{2,1,0:T(8,128)(2,1)}) custom-call(s32[4]{0:T(128)} %pad_add_fusion.place, bf16[2,512,512]{2,1,0:T(8,128)(2,1)} %bitcast.14, bf16[1024,1024]{1,0:T(8,128)(2,1)} %projection.1.refs_1_.after), custom_call_target="tpu_custom_call" | custom-call | flops 1 | bytes 1 | tf_op jit(solution)/shard_map/weight_by_z/pallas_call | solution.py:293
  242.2 3.2 %collective-permute-start.19 = (bf16[2,512,128]{2,1,0:T(8,128)(2,1)}, bf16[2,512,128]{2,1,0:T(8,128)(2,1)}, u32[]{:S(2)}, u32[]{:S(2)}) collective-permute-start(bf16[2,512,128]{2,1,0:T(8,128)(2,1)} %get-tuple-element.47), channel_id=1, source_target_pairs={{0,12},{1,13},{2,14},{3,15},{4,0},{5,1},{6,2},{7,3},{8,4},{9,5},{1... | collective-permute-start | bytes 786440 | tf_op jit(solution)/shard_map/ppermute | solution.py:38
  245.5 15.6 %collective-permute-done.18.b_ref = bf16[2,512,128]{2,1,0:T(8,128)(2,1)} collective-permute-done((bf16[2,512,128]{2,1,0:T(8,128)(2,1)}, bf16[2,512,128]{2,1,0:T(8,128)(2,1)}, u32[]{:S(2)}, u32[]{:S(2)}) %collective-permute-start.18) | collective-permute-done | bytes 262176 | tf_op jit(solution)/shard_map/ppermute | solution.py:38
  261.1 2.7 weight_z_sum.1
  263.7 17.5 %collective-permute-start.21 = (bf16[512,128]{1,0:T(8,128)(2,1)}, bf16[512,128]{1,0:T(8,128)(2,1)}, u32[]{:S(2)}, u32[]{:S(2)}) collective-permute-start(bf16[512,128]{1,0:T(8,128)(2,1)} %get-tuple-element.52), channel_id=1, source_target_pairs={{0,64},{1,65},{2,66},{3,67},{4,68},{5,69},{6,70},{7,71},{8,72},{9,... | collective-permute-start | bytes 393224 | tf_op jit(solution)/shard_map/ppermute | solution.py:38
  281.2 5.6 %key_value_sum.1 = (bf16[1024,512]{1,0:T(8,128)(2,1)}, bf16[1024,512]{1,0:T(8,128)(2,1)}) custom-call(s32[4]{0:T(128)} %pad_add_fusion.place, f32[2,1024,512]{2,1,0:T(8,128)} %get-tuple-element.41.after.own_ref, bf16[2,1024,512]{2,1,0:T(8,128)(2,1)} %collective-permute-done.15.near_ref, bf16[2,512,512]{2,1,0:T(8,128)(2,1)} %collective-permute-done.17.far_ref, ...), custom_call_target="tpu_custom_call" | custom-call | flops 1 | bytes 1 | tf_op jit(solution)/shard_map/key_value_sum/pallas_call | solution.py:293
  286.8 1.7 convert_add_fusion
  (38 shorter events, 0.5 us)
Async XLA Ops:
  7.2 103.0 %all-gather.2.cloned.1.call-start = ((), (), s32[]{:S(2)}) async-start(), calls=%async_computation.1 | async-start | bytes 2621440 | tf_op jit(solution)/shard_map/all_gather | solution.py:588
  10.5 30.7 %collective-permute-start.8 = (bf16[128,2048]{1,0:T(8,128)(2,1)}, bf16[128,2048]{1,0:T(8,128)(2,1)}, u32[]{:S(2)}, u32[]{:S(2)}) collective-permute-start(bf16[128,2048]{1,0:T(8,128)(2,1)} %projection_quarter.1), channel_id=1, source_target_pairs={{0,2},{1,3},{2,0},{3,1},{4,6},{5,7},{6,4},{7,5},{8,10},{9,11},{10,... | collective-permute-start | bytes 1572872 | tf_op jit(solution)/shard_map/ppermute | solution.py:38
  11.9 29.3 %collective-permute-start = (bf16[1024,512]{1,0:T(8,128)(2,1)}, bf16[1024,512]{1,0:T(8,128)(2,1)}, u32[]{:S(2)}, u32[]{:S(2)}) collective-permute-start(bf16[1024,512]{1,0:T(8,128)(2,1)} %k_ref.5), channel_id=1, source_target_pairs={{0,4},{4,8},{8,12},{12,16},{16,20},{20,24},{24,28},{28,32},{32,36}... | collective-permute-start | bytes 3145736 | tf_op jit(solution)/shard_map/ppermute | solution.py:62
  15.7 56.5 %collective-permute-start.7 = (bf16[1024,1024]{1,0:T(8,128)(2,1)}, bf16[1024,1024]{1,0:T(8,128)(2,1)}, u32[]{:S(2)}, u32[]{:S(2)}) collective-permute-start(bf16[1024,1024]{1,0:T(8,128)(2,1)} %refs_0_.1), channel_id=1, source_target_pairs={{0,1},{1,0},{2,3},{3,2},{4,5},{5,4},{6,7},{7,6},{8,9},{9,8},{10,11... | collective-permute-start | bytes 6291464 | tf_op jit(solution)/shard_map/ppermute | solution.py:38
  41.2 197.3 %reduce-scatter.2.cloned.1.call-start = ((), (), s32[]{:S(2)}) async-start(), calls=%async_computation.2 | async-start | bytes 5242880 | tf_op jit(solution)/shard_map/reduce_scatter | solution.py:599
  41.3 5.1 %collective-permute-start.4 = (bf16[2,512,512]{2,1,0:T(8,128)(2,1)}, bf16[2,512,512]{2,1,0:T(8,128)(2,1)}, u32[]{:S(2)}, u32[]{:S(2)}) collective-permute-start(bf16[2,512,512]{2,1,0:T(8,128)(2,1)} %get-tuple-element.29.after), channel_id=1, source_target_pairs={{56,120},{60,124},{57,121},{61,125},{58,122},{62,126},{59,123},{63... | collective-permute-start | bytes 3145736 | tf_op jit(solution)/shard_map/ppermute | solution.py:75
  42.9 25.7 %collective-permute-start.2 = (bf16[2,512,512]{2,1,0:T(8,128)(2,1)}, bf16[2,512,512]{2,1,0:T(8,128)(2,1)}, u32[]{:S(2)}, u32[]{:S(2)}) collective-permute-start(bf16[2,512,512]{2,1,0:T(8,128)(2,1)} %get-tuple-element.33), channel_id=1, source_target_pairs={{0,12},{1,13},{2,14},{3,15},{4,0},{5,1},{6,2},{7,3},{8,4},{9,5},{1... | collective-permute-start | bytes 3145736 | tf_op jit(solution)/shard_map/ppermute | solution.py:38
  44.2 65.9 %collective-permute-start.11 = (bf16[1024,1024]{1,0:T(8,128)(2,1)}, bf16[1024,1024]{1,0:T(8,128)(2,1)}, u32[]{:S(2)}, u32[]{:S(2)}) collective-permute-start(bf16[1024,1024]{1,0:T(8,128)(2,1)} %order.14), channel_id=1, source_target_pairs={{0,2},{1,3},{2,0},{3,1},{4,6},{5,7},{6,4},{7,5},{8,10},{9,11},{10,... | collective-permute-start | bytes 6291464 | tf_op jit(solution)/shard_map/ppermute | solution.py:38
  46.3 56.2 %collective-permute-start.5 = (bf16[2,512,512]{2,1,0:T(8,128)(2,1)}, bf16[2,512,512]{2,1,0:T(8,128)(2,1)}, u32[]{:S(2)}, u32[]{:S(2)}) collective-permute-start(bf16[2,512,512]{2,1,0:T(8,128)(2,1)} %order.12), channel_id=1, source_target_pairs={{124,64},{125,65},{126,66},{127,67}} | collective-permute-start | bytes 3145736 | tf_op jit(solution)/shard_map/ppermute | solution.py:79
  48.0 54.5 %collective-permute-start.6 = (bf16[2,512,512]{2,1,0:T(8,128)(2,1)}, bf16[2,512,512]{2,1,0:T(8,128)(2,1)}, u32[]{:S(2)}, u32[]{:S(2)}) collective-permute-start(bf16[2,512,512]{2,1,0:T(8,128)(2,1)} %order.12), channel_id=1, source_target_pairs={{120,64},{121,65},{122,66},{123,67}} | collective-permute-start | bytes 3145736 | tf_op jit(solution)/shard_map/ppermute | solution.py:79
  68.6 33.9 %collective-permute-start.1 = (bf16[1024,512]{1,0:T(8,128)(2,1)}, bf16[1024,512]{1,0:T(8,128)(2,1)}, u32[]{:S(2)}, u32[]{:S(2)}) collective-permute-start(bf16[1024,512]{1,0:T(8,128)(2,1)} %order.10), channel_id=1, source_target_pairs={{0,4},{4,8},{8,12},{12,16},{16,20},{20,24},{24,28},{28,32},{32,36}... | collective-permute-start | bytes 3145736 | tf_op jit(solution)/shard_map/ppermute | solution.py:62
  72.2 30.3 %collective-permute-start.3 = (bf16[2,512,512]{2,1,0:T(8,128)(2,1)}, bf16[2,512,512]{2,1,0:T(8,128)(2,1)}, u32[]{:S(2)}, u32[]{:S(2)}) collective-permute-start(bf16[2,512,512]{2,1,0:T(8,128)(2,1)} %order.11), channel_id=1, source_target_pairs={{12,8},{0,12},{4,16},{8,20},{28,24},{16,28},{20,32},{24,36},{44,40... | collective-permute-start | bytes 3145736 | tf_op jit(solution)/shard_map/ppermute | solution.py:71
  110.2 4.6 %collective-permute-start.12 = (bf16[1024,1024]{1,0:T(8,128)(2,1)}, bf16[1024,1024]{1,0:T(8,128)(2,1)}, u32[]{:S(2)}, u32[]{:S(2)}) collective-permute-start(bf16[1024,1024]{1,0:T(8,128)(2,1)} %order.15.refs_2_.a_ref), channel_id=1, source_target_pairs={{0,1},{1,0},{2,3},{3,2},{4,5},{5,4},{6,7},{7,6},{8,9},{9,8},{10,11... | collective-permute-start | bytes 6291464 | tf_op jit(solution)/shard_map/ppermute | solution.py:38
  134.3 27.0 %collective-permute-start.10 = (bf16[1024,512]{1,0:T(8,128)(2,1)}, bf16[1024,512]{1,0:T(8,128)(2,1)}, u32[]{:S(2)}, u32[]{:S(2)}) collective-permute-start(bf16[1024,512]{1,0:T(8,128)(2,1)} %get-tuple-element.36.out_ref.own), channel_id=1, source_target_pairs={{0,2},{1,3},{2,0},{3,1},{4,6},{5,7},{6,4},{7,5},{8,10},{9,11},{10,... | collective-permute-start | bytes 3145736 | tf_op jit(solution)/shard_map/ppermute | solution.py:38
  150.4 26.7 %collective-permute-start.14 = (bf16[2,512,1024]{2,1,0:T(8,128)(2,1)}, bf16[2,512,1024]{2,1,0:T(8,128)(2,1)}, u32[]{:S(2)}, u32[]{:S(2)}) collective-permute-start(bf16[2,512,1024]{2,1,0:T(8,128)(2,1)} %projection_core.1), channel_id=1, source_target_pairs={{0,1},{1,0},{2,3},{3,2},{4,5},{5,4},{6,7},{7,6},{8,9},{9,8},{10,11... | collective-permute-start | bytes 6291464 | tf_op jit(solution)/shard_map/ppermute | solution.py:38
  150.4 26.6 %collective-permute-start.9 = (bf16[1024,512]{1,0:T(8,128)(2,1)}, bf16[1024,512]{1,0:T(8,128)(2,1)}, u32[]{:S(2)}, u32[]{:S(2)}) collective-permute-start(bf16[1024,512]{1,0:T(8,128)(2,1)} %get-tuple-element.36.out_ref.own), channel_id=1, source_target_pairs={{0,1},{1,0},{2,3},{3,2},{4,5},{5,4},{6,7},{7,6},{8,9},{9,8},{10,11... | collective-permute-start | bytes 3145736 | tf_op jit(solution)/shard_map/ppermute | solution.py:38
  161.3 15.8 %collective-permute-start.13 = (bf16[1024,512]{1,0:T(8,128)(2,1)}, bf16[1024,512]{1,0:T(8,128)(2,1)}, u32[]{:S(2)}, u32[]{:S(2)}) collective-permute-start(bf16[1024,512]{1,0:T(8,128)(2,1)} %order.16.far), channel_id=1, source_target_pairs={{0,1},{1,0},{2,3},{3,2},{4,5},{5,4},{6,7},{7,6},{8,9},{9,8},{10,11... | collective-permute-start | bytes 3145736 | tf_op jit(solution)/shard_map/ppermute | solution.py:38
  161.3 43.2 %collective-permute-start.16 = (bf16[2,512,512]{2,1,0:T(8,128)(2,1)}, bf16[2,512,512]{2,1,0:T(8,128)(2,1)}, u32[]{:S(2)}, u32[]{:S(2)}) collective-permute-start(bf16[2,512,512]{2,1,0:T(8,128)(2,1)} %get-tuple-element.44), channel_id=1, source_target_pairs={{0,4},{1,5},{2,6},{3,7},{4,8},{5,9},{6,10},{7,11},{8,12},{9,13},{1... | collective-permute-start | bytes 3145736 | tf_op jit(solution)/shard_map/ppermute | solution.py:38
  161.3 119.9 %collective-permute-start.15 = (bf16[2,1024,512]{2,1,0:T(8,128)(2,1)}, bf16[2,1024,512]{2,1,0:T(8,128)(2,1)}, u32[]{:S(2)}, u32[]{:S(2)}) collective-permute-start(bf16[2,1024,512]{2,1,0:T(8,128)(2,1)} %get-tuple-element.43), channel_id=1, source_target_pairs={{4,0},{8,4},{12,8},{16,12},{20,16},{24,20},{28,24},{32,28},{36,32}... | collective-permute-start | bytes 6291464 | tf_op jit(solution)/shard_map/ppermute | solution.py:62
  204.5 76.7 %collective-permute-start.17 = (bf16[2,512,512]{2,1,0:T(8,128)(2,1)}, bf16[2,512,512]{2,1,0:T(8,128)(2,1)}, u32[]{:S(2)}, u32[]{:S(2)}) collective-permute-start(bf16[2,512,512]{2,1,0:T(8,128)(2,1)} %order.17), channel_id=1, source_target_pairs={{12,0},{0,4},{20,8},{24,12},{28,16},{16,20},{36,24},{40,28},{44,32... | collective-permute-start | bytes 3145736 | tf_op jit(solution)/shard_map/ppermute | solution.py:71
  242.2 18.8 %collective-permute-start.18 = (bf16[2,512,128]{2,1,0:T(8,128)(2,1)}, bf16[2,512,128]{2,1,0:T(8,128)(2,1)}, u32[]{:S(2)}, u32[]{:S(2)}) collective-permute-start(bf16[2,512,128]{2,1,0:T(8,128)(2,1)} %get-tuple-element.46), channel_id=1, source_target_pairs={{0,4},{1,5},{2,6},{3,7},{4,8},{5,9},{6,10},{7,11},{8,12},{9,13},{1... | collective-permute-start | bytes 786440 | tf_op jit(solution)/shard_map/ppermute | solution.py:38
  242.2 18.8 %collective-permute-start.19 = (bf16[2,512,128]{2,1,0:T(8,128)(2,1)}, bf16[2,512,128]{2,1,0:T(8,128)(2,1)}, u32[]{:S(2)}, u32[]{:S(2)}) collective-permute-start(bf16[2,512,128]{2,1,0:T(8,128)(2,1)} %get-tuple-element.47), channel_id=1, source_target_pairs={{0,12},{1,13},{2,14},{3,15},{4,0},{5,1},{6,2},{7,3},{8,4},{9,5},{1... | collective-permute-start | bytes 786440 | tf_op jit(solution)/shard_map/ppermute | solution.py:38
  245.5 15.6 %collective-permute-start.20 = (bf16[2,512,128]{2,1,0:T(8,128)(2,1)}, bf16[2,512,128]{2,1,0:T(8,128)(2,1)}, u32[]{:S(2)}, u32[]{:S(2)}) collective-permute-start(bf16[2,512,128]{2,1,0:T(8,128)(2,1)} %get-tuple-element.48), channel_id=1, source_target_pairs={{0,8},{1,9},{2,10},{3,11},{4,12},{5,13},{6,14},{7,15},{8,0},{9,1},... | collective-permute-start | bytes 786440 | tf_op jit(solution)/shard_map/ppermute | solution.py:38
  263.7 23.1 %collective-permute-start.21 = (bf16[512,128]{1,0:T(8,128)(2,1)}, bf16[512,128]{1,0:T(8,128)(2,1)}, u32[]{:S(2)}, u32[]{:S(2)}) collective-permute-start(bf16[512,128]{1,0:T(8,128)(2,1)} %get-tuple-element.52), channel_id=1, source_target_pairs={{0,64},{1,65},{2,66},{3,67},{4,68},{5,69},{6,70},{7,71},{8,72},{9,... | collective-permute-start | bytes 393224 | tf_op jit(solution)/shard_map/ppermute | solution.py:38
Sparse Core Ops, SparseCore 0:
  41.3 36.5 all-gather.1
  127.0 111.5 reduce-scatter.1

commit v3 on v2

--- a/solution.py
+++ b/solution.py
@@ -62,21 +62,22 @@
     return lax.ppermute(value, "ctx", pairs)
 
 
-def from_next_z(value, sign, without):
-    pairs = []
-    for source in range(32):
-        if 0 <= source + 2 * sign < 32 and source != without:
-            middle = source // 4 * 4 + (source % 4 - sign) % 4
-            pairs.append((middle, source + 2 * sign))
-    return lax.ppermute(value, "ctx", pairs)
-
-
-def across(value, sources):
-    return lax.ppermute(value, "ctx", [(s, (s + 16) % 32) for s in sources])
-
-
-def gathered(value, sources, target):
-    return [lax.ppermute(value, "ctx", [((s + 16) % 32, target)]) for s in sources]
+def middle(source, sign):
+    place = source // 4 * 4 + (source % 4 - sign) % 4
+    return place if source // 16 == (source + 2 * sign) // 16 else (place + 16) % 32
+
+
+def two_pairs(sign):
+    sources = [s for s in range(32) if 0 <= s + 2 * sign < 32]
+    return [(s, middle(s, sign), s + 2 * sign) for s in sources]
+
+
+def first_hop(value, sign):
+    return lax.ppermute(value, "ctx", [(s, m) for s, m, _ in two_pairs(sign)])
+
+
+def second_hop(value, sign):
+    return lax.ppermute(value, "ctx", [(m, t) for _, m, t in two_pairs(sign)])
 
 
 def block_rule(spans, pairs, query_block, key_block):
@@ -110,11 +111,11 @@
 BEHIND_TILES = ((0, 3, 0), (0, 2, 1), (0, 1, 2), (1, 3, 1), (1, 2, 2))
 
 
-def key_value(index, near_k, near_v, far, edge_v, edge_far):
+def key_value(index, near_k, near_v, edge_v, far):
     if index == 0:
-        return far[0] + edge_far[0], far[1] + edge_far[1]
+        return far[0], far[1]
     rows = block_rows(index - 1)
-    return near_k[rows, :], near_v[rows, :] + edge_v[index - 1]
+    return near_k[rows, :], near_v[rows, :] + edge_v[rows, :]
 
 
 def absorb(keys, vals, query, top, total, acc, rows):
@@ -162,7 +163,7 @@
 
 
 def forward_behind_kernel(
-    flags, q_ref, k1_ref, v1_ref, far_ref, e0, e1, acc_in, top_in, total_in,
+    flags, q_ref, k1_ref, v1_ref, edge_ref, far_ref, acc_in, top_in, total_in,
     after, out_ref, turned_ref, log_ref, acc, top, total,
 ):
     acc[...] = acc_in[...]
@@ -174,7 +175,7 @@
 
         @pl.when(flags[qb * WIN + o] == 1)
         def _(rows=rows, line=line, index=index):
-            keys, vals = key_value(index, k1_ref, v1_ref, far_ref, e0, e1)
+            keys, vals = key_value(index, k1_ref, v1_ref, edge_ref, far_ref)
             top[line, :], total[line, :] = absorb(
                 keys, vals, q_ref[rows, :], top[line, :], total[line, :], acc, rows
             )
@@ -198,7 +199,7 @@
 
 
 def backward_behind_kernel(
-    flags, q_ref, k1_ref, v1_ref, far_ref, e0, e1, out_ref, grad_ref, log_ref,
+    flags, q_ref, k1_ref, v1_ref, edge_ref, far_ref, out_ref, grad_ref, log_ref,
     after, near_back, far_back, dq, delta_ref, dk, dv,
 ):
     dk[...] = jnp.zeros_like(dk)
@@ -214,7 +215,7 @@
 
         @pl.when(flags[qb * WIN + o] == 1)
         def _(rows=rows, line=line, index=index):
-            keys, vals = key_value(index, k1_ref, v1_ref, far_ref, e0, e1)
+            keys, vals = key_value(index, k1_ref, v1_ref, edge_ref, far_ref)
             key_part, value_part, query_part = tile_grads(
                 keys, vals, q_ref[rows, :], grad_ref[rows, :],
                 log_ref[0, line, :], delta_ref[0, line, :], False,
@@ -316,28 +317,28 @@
     )
 
 
-def forward_behind(flags, q, near_k, near_v, far, edge, state, after):
+def forward_behind(flags, q, near_k, near_v, edge_v, far, state, after):
     lines = pltpu.VMEM((2, BLK), f32)
     return call(
         forward_behind_kernel, "forward_behind", (HEADS,),
-        [head(1024)] * 3 + [head_pair(512)] * 3
+        [head(1024)] * 4 + [head_pair(512)]
         + [HEAD_TURNED, HEAD_LINES, HEAD_LINES, ANY],
         [head(1024), HEAD_TURNED, HEAD_LINES],
         [shape((1024, WIDTH), bf16), shape((WIDTH, 1024), bf16), LINES],
         [pltpu.VMEM((HDIM, 1024), f32), lines, lines],
-        (flags, q, near_k, near_v, far, *edge, *state, after),
-    )
-
-
-def backward_behind(flags, q, near_k, near_v, far, edge, out, grad, log_sum, after):
+        (flags, q, near_k, near_v, edge_v, far, *state, after),
+    )
+
+
+def backward_behind(flags, q, near_k, near_v, edge_v, far, out, grad, log_sum, after):
     held = pltpu.VMEM((3 * BLK, HDIM), f32)
     return call(
         backward_behind_kernel, "backward_behind", (HEADS,),
-        [head(1024)] * 3 + [head_pair(512)] * 3
+        [head(1024)] * 4 + [head_pair(512)]
         + [head(1024), head(1024), HEAD_LINES, ANY],
         [head_pair(1024), head_pair(512), HEAD_TURNED, HEAD_LINES],
         [shape((2, 1024, WIDTH), bf16), shape((2, 512, WIDTH), bf16), TURNED, LINES],
-        [held, held], (flags, q, near_k, near_v, far, *edge, out, grad, log_sum, after),
+        [held, held], (flags, q, near_k, near_v, edge_v, far, out, grad, log_sum, after),
     )
 
 
@@ -363,18 +364,17 @@
     )
 
 
-def pack_kernel(flags, k_ref, v_ref, second_ref, crossing_ref):
-    second_ref[0] = k_ref[block_rows(1), :]
-    second_ref[1] = v_ref[block_rows(1), :]
-    first = flags[0] == EDGE - 1
-    for part in range(2):
-        crossing_ref[part] = jnp.where(first, second_ref[part], v_ref[block_rows(part), :])
-
-
-def pack(ctx, k, v):
-    return call(
-        pack_kernel, "halo_pack", (HEADS,), [head(1024)] * 2, [head_pair(512)] * 2,
-        [shape((2, 512, WIDTH), bf16)] * 2, [], (ctx, k, v),
+def pack_kernel(place, k_ref, v_ref, second_ref):
+    second_ref[0] = k_ref[...]
+    second_ref[1] = v_ref[...]
+
+
+def pack(place, k, v):
+    second = pl.BlockSpec((BLK, WIDTH), lambda i, place: (1, 0))
+    return call(
+        pack_kernel, "second_blocks", (1,), [second, second],
+        pl.BlockSpec((2, BLK, WIDTH), lambda i, place: (0, 0, 0)),
+        shape((2, BLK, WIDTH), bf16), [], (place, k, v),
     )
 
 
@@ -382,16 +382,16 @@
     pass
 
 
-def behind(value, *after):
+def together(values, after=()):
     return pl.pallas_call(
         nothing_kernel,
-        in_specs=[ANY] * (1 + len(after)),
-        out_specs=ANY,
-        out_shape=shape(value.shape, value.dtype),
-        input_output_aliases={0: 0},
+        in_specs=[ANY] * (len(values) + len(after)),
+        out_specs=[ANY] * len(values),
+        out_shape=[shape(value.shape, value.dtype) for value in values],
+        input_output_aliases={index: index for index in range(len(values))},
         compiler_params=pltpu.CompilerParams(vmem_limit_bytes=64 << 20),
         name="order",
-    )(value, *after)
+    )(*values, *after)
 
 
 def grad_kernel(place, a_ref, b_ref, wa_ref, wb_ref, *rest):
@@ -402,7 +402,7 @@
 
 
 def grad_terms(place, first, a, b, weight, before, after):
-    tile = 256
+    tile = 512
     row = pl.BlockSpec((tile, 1024), lambda i, place: (i, 0))
     result = pl.BlockSpec((tile, 512), lambda i, place: (i, 0))
 
@@ -417,33 +417,31 @@
     )
 
 
-def weight_kernel(place, turned_ref, *refs):
-    out_ref = refs[-1]
-    for part in range(4):
+def weight_kernel(place, turned_ref, a_ref, b_ref, after, out_ref):
+    for part, ref in enumerate((a_ref, b_ref)):
 
         @pl.when(pl.program_id(0) == part)
-        def _(part=part):
-            out_ref[0, 0] = dot(turned_ref[...], refs[part][...], NN).astype(bf16)
-
-
-def weight_terms(place, turned, cotangents):
-    def piece(part):
-        return pl.BlockSpec(
-            (1024, 512),
-            lambda i, half, place: (
-                0, jnp.where(i == part, half, jnp.where(i < part, 0, 1)),
-            ),
-        )
-
-    def target(i, half, place):
-        owner = place[0] ^ i
-        return (owner % 2 * 2 + half, owner // 2, 0, 0)
-
-    return call(
-        weight_kernel, "weight_gradient", (4, 2),
-        [pl.BlockSpec((512, 1024), lambda i, half, place: (0, 0))] + [piece(p) for p in range(4)],
-        pl.BlockSpec((1, 1, 512, 512), target),
-        shape((4, 2, 512, 512), bf16), [], (place, turned, *cotangents),
+        def _(ref=ref):
+            out_ref[0] = dot(turned_ref[...], ref[...], NN).astype(bf16)
+
+
+def weight_terms(place, turned, a, b, after):
+    return call(
+        weight_kernel, "weight_gradient", (2, 2),
+        [
+            pl.BlockSpec((512, 1024), lambda i, half, place: (0, 0)),
+            pl.BlockSpec((1024, 512), lambda i, half, place: (0, jnp.where(i == 0, half, 1))),
+            pl.BlockSpec((1024, 512), lambda i, half, place: (0, jnp.where(i == 0, 0, half))),
+            ANY,
+        ],
+        pl.BlockSpec((1, 512, 512), lambda i, half, place: ((place[0] ^ i) % 2 * 2 + half, 0, 0)),
+        shape((4, 512, 512), bf16), [], (place, turned, a, b, after),
+    )
+
+
+def sum_over_y(parts):
+    return lax.psum_scatter(
+        parts, "ctx", scatter_dimension=0, axis_index_groups=groups_along(1)
     )
 
 
@@ -456,37 +454,39 @@
     return list(groups.values())
 
 
-def pieces_kernel(place, in_ref, after, *outs):
+def pieces_kernel(place, a_ref, b_ref, after, *outs):
     for slot, out_ref in enumerate(outs):
 
         @pl.when(pl.program_id(0) == slot)
         def _(out_ref=out_ref):
-            out_ref[...] = in_ref[...]
-
-
-def pieces_by_z(place, total, after):
-    return call(
-        pieces_kernel, "weight_by_z", (4,),
-        [pl.BlockSpec((2, 512, 128), lambda i, place: (0, 0, (place[2] + i + 1) % 4)), ANY],
+            out_ref[0] = a_ref[...]
+            out_ref[1] = b_ref[...]
+
+
+def pieces_by_z(place, a, b, after):
+    piece = pl.BlockSpec((512, 128), lambda i, place: (0, (place[2] + i + 1) % 4))
+    return call(
+        pieces_kernel, "weight_by_z", (4,), [piece, piece, ANY],
         [pl.BlockSpec((2, 512, 128), lambda i, place: (0, 0, 0))] * 4,
-        [shape((2, 512, 128), bf16)] * 4, [], (place, total, after),
-    )
-
-
-def weight_z_kernel(place, a_ref, b_ref, c_ref, d_ref, kept_ref, sent_ref):
+        [shape((2, 512, 128), bf16)] * 4, [], (place, a, b, after),
+    )
+
+
+def weight_z_kernel(place, a_ref, b_ref, c_ref, d_ref, after, kept_ref, sent_ref):
     def total(index):
         return sum(ref[index].astype(f32) for ref in (a_ref, b_ref, c_ref, d_ref))
 
-    kept_ref[...] = total(place[3])
-    sent_ref[...] = total(1 - place[3]).astype(bf16)
-
-
-def weight_z_sum(place, terms):
+    kept = place[3] ^ (place[0] // 2)
+    kept_ref[...] = total(kept)
+    sent_ref[...] = total(1 - kept).astype(bf16)
+
+
+def weight_z_sum(place, terms, after):
     whole = pl.BlockSpec((2, 512, 128), lambda i, place: (0, 0, 0))
     result = pl.BlockSpec((512, 128), lambda i, place: (0, 0))
     return call(
-        weight_z_kernel, "weight_z_sum", (1,), [whole] * 4, [result] * 2,
-        [shape((512, 128), f32), shape((512, 128), bf16)], [], (place, *terms),
+        weight_z_kernel, "weight_z_sum", (1,), [whole] * 4 + [ANY], [result] * 2,
+        [shape((512, 128), f32), shape((512, 128), bf16)], [], (place, *terms, after),
     )
 
 
@@ -510,10 +510,10 @@
 
 def late_copies(a, b, after):
     def rows(value):
-        return pl.BlockSpec((256, value.shape[1]), lambda i, place: (i, 0))
-
-    return call(
-        two_kernel, "late_copies", (4,), [rows(a), rows(b), ANY], [rows(a), rows(b)],
+        return pl.BlockSpec((512, value.shape[1]), lambda i, place: (i, 0))
+
+    return call(
+        two_kernel, "late_copies", (2,), [rows(a), rows(b), ANY], [rows(a), rows(b)],
         [shape(a.shape, a.dtype), shape(b.shape, b.dtype)],
         [], (jnp.zeros(1, jnp.int32), a, b, after),
     )
@@ -544,16 +544,16 @@
 
 
 def mix(place, attentions, weight, far_weight, core_weight, after):
-    rows = pl.BlockSpec((256, 512), lambda i, place: (i, 0))
-    return call(
-        mix_kernel, "projection", (4,),
+    rows = pl.BlockSpec((512, 512), lambda i, place: (i, 0))
+    return call(
+        mix_kernel, "projection", (2,),
         [rows] * 4 + [
             pl.BlockSpec((512, 1024), lambda i, place: (0, place[0])),
             pl.BlockSpec((512, 1024), lambda i, place: (0, place[0] % 2)),
             pl.BlockSpec((2, 512, 1024), lambda i, place: (0, 0, 0)),
             ANY,
         ],
-        pl.BlockSpec((256, 1024), lambda i, place: (i, 0)),
+        pl.BlockSpec((512, 1024), lambda i, place: (i, 0)),
         shape((1024, 1024), bf16), [],
         (place, *attentions, weight, far_weight, core_weight, after),
     )
@@ -564,61 +564,62 @@
     tp = lax.axis_index("tp")
     place = jnp.stack([tp, ctx // 4 % 4, ctx % 4, ctx // 16]).astype(jnp.int32)
 
+    near_keys = along_ctx(keys, 1)
+    crossed = lax.ppermute(values, "ctx", [(EDGE, EDGE + 16)])
     core_grad = to_core(out_grad)
-    near_keys = along_ctx(keys, 1)
-    second_half, crossing = pack(ctx.astype(jnp.int32).reshape(1), keys, values)
-    far_moved = to_z(second_half, -1)
-    crossed = across(crossing, (EDGE - 1, EDGE))
+    far_moved = first_hop(pack(place, keys, values), 1)
     far_weight = to_x_hi(far_columns(place, out_weight))
 
     query_block = ctx * 2 + jnp.arange(2, dtype=jnp.int32)[:, None] + jnp.zeros((1, WIN), jnp.int32)
     key_block = query_block - jnp.arange(WIN, dtype=jnp.int32)[None, :]
-    listed = block_rule(spans, pairs, query_block, key_block).astype(jnp.int32).reshape(-1)
-    flags = jnp.concatenate([listed, ctx.astype(jnp.int32).reshape(1)])
-    own_state = forward_own(flags, queries, keys, values, crossing)
+    flags = block_rule(spans, pairs, query_block, key_block).astype(jnp.int32).reshape(-1)
+    own_state = forward_own(flags, queries, keys, values, keys)
     held_values, held_grad = late_copies(values, out_grad, own_state[1])
 
-    near_keys = behind(near_keys, held_grad)
-    near_values = along_ctx(behind(held_values, near_keys), 1, (EDGE,))
-    far = from_next_z(behind(far_moved, near_keys), 1, EDGE - 1)
-    edge_far, edge_values = gathered(behind(crossed, near_keys), (EDGE - 1, EDGE), EDGE + 1)
-    far_grad = to_x_hi(behind(held_grad, near_keys))
-    far_weight = behind(far_weight, near_keys)
-    terms = grad_terms(place, 0, out_grad, core_grad, out_weight, None, far_weight)
+    near_keys, crossed, core_grad, far_moved, far_weight, held_values, held_grad = together(
+        [near_keys, crossed, core_grad, far_moved, far_weight, held_values, held_grad]
+    )
+    near_values = along_ctx(held_values, 1, (EDGE,))
+    edge_values = lax.ppermute(crossed, "ctx", [(EDGE + 16, EDGE + 1)])
+    far = second_hop(far_moved, 1)
+    far_grad = to_x_hi(held_grad)
     far_weight = lax.all_gather(
         far_weight, "ctx", axis=0, tiled=True, axis_index_groups=groups_along(1)
     )
-    keys_values = (flags, queries, near_keys, near_values, far, (edge_values, edge_far))
-    attention, turned, log_sum = forward_behind(*keys_values, own_state, terms)
-    far_grad = behind(far_grad, log_sum, far_weight)
-    far_core_grad = to_core(far_grad)
+    terms = grad_terms(place, 0, out_grad, core_grad, out_weight, None, near_keys)
+    behind = (flags, queries, near_keys, near_values, edge_values, far)
+    attention, turned, log_sum = forward_behind(*behind, own_state, terms)
 
     core_attention = to_core(attention)
     far_attention = to_x_hi(attention)
-    weight_parts = weight_terms(place, turned, (out_grad, core_grad, far_grad, far_core_grad))
-    weight_y = lax.psum_scatter(
-        weight_parts, "ctx", scatter_dimension=0, axis_index_groups=groups_along(1)
-    )
-    attn_grad = grad_terms(place, 2, far_grad, far_core_grad, out_weight, terms, weight_parts)
+    own_parts = weight_terms(place, turned, out_grad, core_grad, log_sum)
+    own_sum = sum_over_y(own_parts)
+    far_grad, far_weight = together([far_grad, far_weight], [own_parts])
+    far_core_grad = to_core(far_grad)
+    core_weight = core_columns(place, out_weight, far_weight, own_parts)
+    far_parts = weight_terms(place, turned, far_grad, far_core_grad, core_weight)
+    far_sum = sum_over_y(far_parts)
+    attn_grad = grad_terms(place, 2, far_grad, far_core_grad, out_weight, terms, far_parts)
     near_back, far_back, dq, delta = backward_behind(
-        *keys_values, attention, attn_grad, log_sum, attn_grad
+        *behind, attention, attn_grad, log_sum, attn_grad
     )
     near_back = along_ctx(near_back, -1)
-    far_moved = to_z(far_back, 1)
-    far_attention = behind(far_attention, delta)
-    far_core_attention = to_core(far_attention)
+    far_moved = first_hop(far_back, -1)
+    core_weight = to_core(core_weight)
     query_grad, own = backward_own(
         flags, queries, keys, values, attn_grad, log_sum, dq, delta, delta
     )
-    core_weight = to_core(core_columns(place, out_weight, far_weight, delta))
+    core_attention, far_attention, core_weight, far_moved = together(
+        [core_attention, far_attention, core_weight, far_moved], [own]
+    )
+    far_back = second_hop(far_moved, -1)
+    far_core_attention = to_core(far_attention)
     attentions = (attention, core_attention, far_attention, far_core_attention)
-    mixed = mix(place, attentions, out_weight, far_weight, core_weight, own)
-
-    far_back = from_next_z(behind(far_moved, mixed), -1, None)
-    weight_pieces = pieces_by_z(place, weight_y, mixed)
-    kept, sent = weight_z_sum(
-        place, [weight_pieces[3]] + [to_z(weight_pieces[s], s + 1) for s in (0, 2, 1)]
-    )
+
+    weight_pieces = pieces_by_z(place, own_sum, far_sum, far_attention)
+    weight_terms_z = [weight_pieces[3]] + [to_z(weight_pieces[s], s + 1) for s in (0, 2, 1)]
+    mixed = mix(place, attentions, out_weight, far_weight, core_weight, weight_pieces[3])
+    kept, sent = weight_z_sum(place, weight_terms_z, mixed)
     weight_grad = kept + to_x_lo(sent).astype(f32)
     key_grad, value_grad = finish(place, own, near_back, far_back, kept)
     return (mixed, query_grad, key_grad, value_grad, weight_grad)

time: 301 us -> 315 us (1.047); the launches traced: 295 us -> 313 us
  starting transfers between devices: 77.6 us -> 123 us
  waiting for transfers between devices: 97 us -> 81.9 us
  Pallas kernels: 97.1 us -> 88.4 us
  other arithmetic: 7.24 us -> 3.56 us
    ppermute x14 -> x12, waiting for transfers between devices: 67.5 us -> 17.4 us  [move(): return lax.ppermute(value, AXES, pairs)]
    ppermute x5 -> x6, waiting for transfers between devices: 0.01 us -> 36.8 us  [the longest x2 25 us: first_hop(): return lax.ppermute(value, 'ctx', [(s, m) for s, m, _ in two_pairs(sign)])]
    ppermute x5 -> x6, starting transfers between devices: 35.5 us -> 71.6 us  [the longest x2 38.5 us: first_hop(): return lax.ppermute(value, 'ctx', [(s, m) for s, m, _ in two_pairs(sign)])]
    ppermute x3, waiting for transfers between devices: 15.6 us -> 0.01 us  [along_ctx(): return lax.ppermute(value, 'ctx', pairs)]
    reduce_scatter x1 -> x2, waiting for transfers between devices: 13.9 us -> 27.6 us  [sum_over_y(): lax.psum_scatter(parts, 'ctx', scatter_dimension=0, axis_index_groups=gro...]
    ppermute x14 -> x12, starting transfers between devices: 29.5 us -> 41.5 us  [move(): return lax.ppermute(value, AXES, pairs)]
    pallas_call x15 -> x16, Pallas kernels: 97.1 us -> 88.4 us  [call(): pl.pallas_call(kernel, grid_spec=pltpu.PrefetchScalarGridSpec(num_scalar_...]
  transfers between devices with their start and end apart: 24 -> 24, of which waited for: 8 -> 7; matrix products, arithmetic and copies ran while one was open for 2% -> 1% of each run, Pallas kernels for 28% -> 28%
where the time goes in v3:
time: 315 us; the launch traced here: 313 us
  starting transfers between devices  123 us (39%)
  Pallas kernels  88.4 us (28%)
  waiting for transfers between devices  81.9 us (26%)
  between operations  13.9 us (4%)
  other arithmetic  3.56 us (1%)
    pallas_call x16, Pallas kernels, call(): pl.pallas_call(kernel, grid_spec=pltpu.PrefetchScalarGridSpec(num_scalar_...  88.4 us
    ppermute x12, starting transfers between devices, move(): return lax.ppermute(value, AXES, pairs)  41.5 us
    ppermute x2, starting transfers between devices, first_hop(): return lax.ppermute(value, 'ctx', [(s, m) for s, m, _ in two_pairs(sign)])  38.5 us
    ppermute x2, starting transfers between devices, second_hop(): return lax.ppermute(value, 'ctx', [(m, t) for _, m, t in two_pairs(sign)])  29.9 us
    reduce_scatter x2, waiting for transfers between devices, sum_over_y(): lax.psum_scatter(parts, 'ctx', scatter_dimension=0, axis_index_groups=gro...  27.6 us
    ppermute x2, waiting for transfers between devices, first_hop(): return lax.ppermute(value, 'ctx', [(s, m) for s, m, _ in two_pairs(sign)])  25 us
    ppermute x12, waiting for transfers between devices, move(): return lax.ppermute(value, AXES, pairs)  17.4 us
    ppermute x2, waiting for transfers between devices, second_hop(): return lax.ppermute(value, 'ctx', [(m, t) for _, m, t in two_pairs(sign)])  11.8 us
  transfers between devices with their start and end apart: 24, of which 7 were waited for; matrix products, arithmetic and copies ran while one was open for 1% of the time, Pallas kernels for 28%

profile of v3, /device:TPU:30, one launch (start us, length us, event | category | flops | bytes accessed | tf_op | source)
XLA Modules:
  0.0 313.4 jit_solution(18066439579169589337)
XLA Ops:
  7.2 0.1 collective-permute-start.2
  7.3 0.6 pad_add_fusion.place
  8.0 2.5 projection_quarter.1
  10.5 1.4 collective-permute-start.4
  11.9 3.8 %collective-permute-start = (bf16[1024,512]{1,0:T(8,128)(2,1)}, bf16[1024,512]{1,0:T(8,128)(2,1)}, u32[]{:S(2)}, u32[]{:S(2)}) collective-permute-start(bf16[1024,512]{1,0:T(8,128)(2,1)} %k_ref.5), channel_id=1, source_target_pairs={{0,4},{4,8},{8,12},{12,16},{16,20},{20,24},{24,28},{28,32},{32,36}... | collective-permute-start | bytes 3145736 | tf_op jit(solution)/shard_map/ppermute | solution.py:62
  15.7 1.6 collective-permute-start.1
  17.4 2.9 second_blocks.1
  20.3 3.1 collective-permute-start.3
  23.4 0.8 bitcast_add_fusion
  24.1 0.7 slice_bitcast_fusion
  24.9 0.2 and_reduce_fusion.1
  25.1 0.8 fusion
  25.8 0.2 and_reduce_fusion
  26.0 0.6 reshape.60.flags
  26.6 5.8 %forward_own.1 = (f32[512,1024]{1,0:T(8,128)}, f32[4,2,512]{2,1,0:T(2,128)}, f32[4,2,512]{2,1,0:T(2,128)}) custom-call(s32[8]{0:T(128)} %reshape.60.flags, bf16[1024,512]{1,0:T(8,128)(2,1)} %q_ref.7, bf16[1024,512]{1,0:T(8,128)(2,1)} %k_ref.5, bf16[1024,512]{1,0:T(8,128)(2,1)} %v_ref.5, bf16[1024,512]{1,0:T(8,128)(2,1)} %k_ref.5), custom_call_target="tpu_custom_call" | custom-call | flops 1 | bytes 1 | tf_op jit(solution)/shard_map/forward_own/pallas_call | solution.py:294
  32.4 3.2 %late_copies.1 = (bf16[1024,512]{1,0:T(8,128)(2,1)}, bf16[1024,1024]{1,0:T(8,128)(2,1)}) custom-call(s32[1]{0:T(128)} %constant.56.clone.1.place, bf16[1024,512]{1,0:T(8,128)(2,1)} %v_ref.5, bf16[1024,1024]{1,0:T(8,128)(2,1)} %a_ref.5, f32[4,2,512]{2,1,0:T(2,128)} %get-tuple-element.40.after.top_in), custom_call_target="tpu_custom_call" | custom-call | flops 1 | bytes 1 | tf_op jit(solution)/shard_map/late_copies/pallas_call | solution.py:294
  35.6 12.0 %collective-permute-done.3.refs_3_ = bf16[2,512,512]{2,1,0:T(8,128)(2,1)} collective-permute-done((bf16[2,512,512]{2,1,0:T(8,128)(2,1)}, bf16[2,512,512]{2,1,0:T(8,128)(2,1)}, u32[]{:S(2)}, u32[]{:S(2)}) %collective-permute-start.3) | collective-permute-done | bytes 1048608 | tf_op jit(solution)/shard_map/ppermute | solution.py:76
  47.7 4.5 %collective-permute-start.5 = (bf16[1024,512]{1,0:T(8,128)(2,1)}, bf16[1024,512]{1,0:T(8,128)(2,1)}, u32[]{:S(2)}, u32[]{:S(2)}) collective-permute-start(bf16[1024,512]{1,0:T(8,128)(2,1)} %get-tuple-element.44), channel_id=1, source_target_pairs={{0,4},{4,8},{8,12},{12,16},{16,20},{20,24},{24,28},{28,32},{32,36}... | collective-permute-start | bytes 3145736 | tf_op jit(solution)/shard_map/ppermute | solution.py:62
  52.3 1.6 collective-permute-start.6
  53.9 25.5 %collective-permute-start.7 = (bf16[2,512,512]{2,1,0:T(8,128)(2,1)}, bf16[2,512,512]{2,1,0:T(8,128)(2,1)}, u32[]{:S(2)}, u32[]{:S(2)}) collective-permute-start(bf16[2,512,512]{2,1,0:T(8,128)(2,1)} %get-tuple-element.46), channel_id=1, source_target_pairs={{12,8},{0,12},{4,16},{8,20},{28,24},{16,28},{20,32},{24,36},{44,40... | collective-permute-start | bytes 3145736 | tf_op jit(solution)/shard_map/ppermute | solution.py:80
  79.4 3.7 %collective-permute-start.10 = (bf16[1024,1024]{1,0:T(8,128)(2,1)}, bf16[1024,1024]{1,0:T(8,128)(2,1)}, u32[]{:S(2)}, u32[]{:S(2)}) collective-permute-start(bf16[1024,1024]{1,0:T(8,128)(2,1)} %get-tuple-element.51), channel_id=1, source_target_pairs={{0,2},{1,3},{2,0},{3,1},{4,6},{5,7},{6,4},{7,5},{8,10},{9,11},{10,... | collective-permute-start | bytes 6291464 | tf_op jit(solution)/shard_map/ppermute | solution.py:38
  83.1 6.5 %projection_backward.2.after.rest_0_ = f32[1024,512]{1,0:T(8,128)} custom-call(s32[4]{0:T(128)} %pad_add_fusion.place, bf16[1024,1024]{1,0:T(8,128)(2,1)} %a_ref.5, bf16[1024,1024]{1,0:T(8,128)(2,1)} %get-tuple-element.49.b_ref, bf16[512,4096]{1,0:T(8,128)(2,1)} %w_own.1, bf16[512,4096]{1,0:T(8,128)(2,1)} %w_own.1, ...), custom_call_target="tpu_custom_call" | custom-call | flops 1 | bytes 1 | tf_op jit(solution)/shard_map/projection_backward/pallas_call | solution.py:294
  89.7 11.8 %collective-permute-done.7.far_ref = bf16[2,512,512]{2,1,0:T(8,128)(2,1)} collective-permute-done((bf16[2,512,512]{2,1,0:T(8,128)(2,1)}, bf16[2,512,512]{2,1,0:T(8,128)(2,1)}, u32[]{:S(2)}, u32[]{:S(2)}) %collective-permute-start.7) | collective-permute-done | bytes 1048608 | tf_op jit(solution)/shard_map/ppermute | solution.py:80
  101.5 5.9 %forward_behind.1 = (bf16[1024,512]{1,0:T(8,128)(2,1)}, bf16[512,1024]{1,0:T(8,128)(2,1)}, f32[4,2,512]{2,1,0:T(2,128)}) custom-call(s32[8]{0:T(128)} %reshape.60.flags, bf16[1024,512]{1,0:T(8,128)(2,1)} %q_ref.7, bf16[1024,512]{1,0:T(8,128)(2,1)} %get-tuple-element.43.rest_0_.k1_ref, bf16[1024,512]{1,0:T(8,128)(2,1)} %collective-permute-done.5.v1_ref, ...), custom_call_target="tpu_custom_call" | custom-call | flops 1 | bytes 1 | tf_op jit(solution)/shard_map/forward_behind/pallas_call | solution.py:294
  107.4 7.0 %weight_gradient.2.refs_2_.after = bf16[4,512,512]{2,1,0:T(8,128)(2,1)} custom-call(s32[4]{0:T(128)} %pad_add_fusion.place, bf16[512,1024]{1,0:T(8,128)(2,1)} %get-tuple-element.53.turned_ref, bf16[1024,1024]{1,0:T(8,128)(2,1)} %a_ref.5, bf16[1024,1024]{1,0:T(8,128)(2,1)} %get-tuple-element.49.b_ref, f32[4,2,512]{2,1,0:T(2,128)} %get-tuple-element.54.after.log_ref), custom_call_target="tpu_custom_call" | custom-call | flops 1 | bytes 1 | tf_op jit(solution)/shard_map/weight_gradient/pallas_call | solution.py:294
  114.5 13.7 %collective-permute-done.10.refs_0_ = bf16[1024,1024]{1,0:T(8,128)(2,1)} collective-permute-done((bf16[1024,1024]{1,0:T(8,128)(2,1)}, bf16[1024,1024]{1,0:T(8,128)(2,1)}, u32[]{:S(2)}, u32[]{:S(2)}) %collective-permute-start.10) | collective-permute-done | bytes 2097184 | tf_op jit(solution)/shard_map/ppermute | solution.py:38
  128.2 3.7 %projection_core.1.after = bf16[2,512,1024]{2,1,0:T(8,128)(2,1)} custom-call(s32[4]{0:T(128)} %pad_add_fusion.place, bf16[512,4096]{1,0:T(8,128)(2,1)} %w_own.1, bf16[512,2048]{1,0:T(8,128)(2,1)} %get-tuple-element.55.far_ref.w_far, bf16[4,512,512]{2,1,0:T(8,128)(2,1)} %weight_gradient.2.refs_2_.after), custom_call_target="tpu_custom_call" | custom-call | flops 1 | bytes 1 | tf_op jit(solution)/shard_map/projection_core/pallas_call | solution.py:294
  131.8 0.8 collective-permute-done.12.b_ref
  132.7 7.0 %weight_gradient.3.rest_1_ = bf16[4,512,512]{2,1,0:T(8,128)(2,1)} custom-call(s32[4]{0:T(128)} %pad_add_fusion.place, bf16[512,1024]{1,0:T(8,128)(2,1)} %get-tuple-element.53.turned_ref, bf16[1024,1024]{1,0:T(8,128)(2,1)} %get-tuple-element.56.a_ref, bf16[1024,1024]{1,0:T(8,128)(2,1)} %collective-permute-done.12.b_ref, ...), custom_call_target="tpu_custom_call" | custom-call | flops 1 | bytes 1 | tf_op jit(solution)/shard_map/weight_gradient/pallas_call | solution.py:294
  139.7 0.2 collective-permute-start.11
  139.9 3.2 %collective-permute-start.9 = (bf16[1024,512]{1,0:T(8,128)(2,1)}, bf16[1024,512]{1,0:T(8,128)(2,1)}, u32[]{:S(2)}, u32[]{:S(2)}) collective-permute-start(bf16[1024,512]{1,0:T(8,128)(2,1)} %get-tuple-element.50.out_ref.own), channel_id=1, source_target_pairs={{0,2},{1,3},{2,0},{3,1},{4,6},{5,7},{6,4},{7,5},{8,10},{9,11},{10,... | collective-permute-start | bytes 3145736 | tf_op jit(solution)/shard_map/ppermute | solution.py:38
  143.2 6.9 %projection_backward.3.grad_ref.after = bf16[1024,512]{1,0:T(8,128)(2,1)} custom-call(s32[4]{0:T(128)} %pad_add_fusion.place, bf16[1024,1024]{1,0:T(8,128)(2,1)} %get-tuple-element.56.a_ref, bf16[1024,1024]{1,0:T(8,128)(2,1)} %collective-permute-done.12.b_ref, bf16[512,4096]{1,0:T(8,128)(2,1)} %w_own.1, bf16[512,4096]{1,0:T(8,128)(2,1)} %w_own.1, ...), custom_call_target="tpu_custom_call" | custom-call | flops 1 | bytes 1 | tf_op jit(solution)/shard_map/projection_backward/pallas_call | solution.py:294
  150.0 0.1 collective-permute-start.8
  150.1 7.2 %backward_behind.1 = (bf16[2,1024,512]{2,1,0:T(8,128)(2,1)}, bf16[2,512,512]{2,1,0:T(8,128)(2,1)}, f32[512,1024]{1,0:T(8,128)}, f32[4,2,512]{2,1,0:T(2,128)}) custom-call(s32[8]{0:T(128)} %reshape.60.flags, bf16[1024,512]{1,0:T(8,128)(2,1)} %q_ref.7, bf16[1024,512]{1,0:T(8,128)(2,1)} %get-tuple-element.43.rest_0_.k1_ref, ...), custom_call_target="tpu_custom_call" | custom-call | flops 1 | bytes 1 | tf_op jit(solution)/shard_map/backward_behind/pallas_call | solution.py:294
  157.3 35.4 %collective-permute-start.13 = (bf16[2,512,512]{2,1,0:T(8,128)(2,1)}, bf16[2,512,512]{2,1,0:T(8,128)(2,1)}, u32[]{:S(2)}, u32[]{:S(2)}) collective-permute-start(bf16[2,512,512]{2,1,0:T(8,128)(2,1)} %get-tuple-element.57), channel_id=1, source_target_pairs={{8,12},{12,0},{16,20},{20,24},{24,28},{28,16},{32,36},{36,40},{40,... | collective-permute-start | bytes 3145736 | tf_op jit(solution)/shard_map/ppermute | solution.py:76
  192.7 1.9 collective-permute-start.15
  194.7 8.3 %backward_own.1 = (bf16[1024,512]{1,0:T(8,128)(2,1)}, f32[2,1024,512]{2,1,0:T(8,128)}) custom-call(s32[8]{0:T(128)} %reshape.60.flags, bf16[1024,512]{1,0:T(8,128)(2,1)} %q_ref.7, bf16[1024,512]{1,0:T(8,128)(2,1)} %k_ref.5, bf16[1024,512]{1,0:T(8,128)(2,1)} %v_ref.5, bf16[1024,512]{1,0:T(8,128)(2,1)} %projection_backward.3.grad_ref.after, ...), custom_call_target="tpu_custom_call" | custom-call | flops 1 | bytes 1 | tf_op jit(solution)/shard_map/backward_own/pallas_call | solution.py:294
  203.0 13.0 %collective-permute-done.13.refs_3_ = bf16[2,512,512]{2,1,0:T(8,128)(2,1)} collective-permute-done((bf16[2,512,512]{2,1,0:T(8,128)(2,1)}, bf16[2,512,512]{2,1,0:T(8,128)(2,1)}, u32[]{:S(2)}, u32[]{:S(2)}) %collective-permute-start.13) | collective-permute-done | bytes 1048608 | tf_op jit(solution)/shard_map/ppermute | solution.py:76
  216.0 4.4 %collective-permute-start.16 = (bf16[2,512,512]{2,1,0:T(8,128)(2,1)}, bf16[2,512,512]{2,1,0:T(8,128)(2,1)}, u32[]{:S(2)}, u32[]{:S(2)}) collective-permute-start(bf16[2,512,512]{2,1,0:T(8,128)(2,1)} %get-tuple-element.67), channel_id=1, source_target_pairs={{12,0},{0,4},{20,8},{24,12},{28,16},{16,20},{36,24},{40,28},{44,32... | collective-permute-start | bytes 3145736 | tf_op jit(solution)/shard_map/ppermute | solution.py:80
  220.5 27.6 %reduce-scatter.5.cloned.1.call-done = bf16[1,512,512]{2,1,0:T(8,128)(2,1)} async-done(((bf16[4,512,512]{2,1,0:T(8,128)(2,1)}), bf16[1,512,512]{2,1,0:T(8,128)(2,1)}) %reduce-scatter.5.cloned.1.call-update) | async-done | bytes 524304 | tf_op jit(solution)/shard_map/reduce_scatter | solution.py:443
  248.1 3.8 %weight_by_z.1 = (bf16[2,512,128]{2,1,0:T(8,128)(2,1)}, bf16[2,512,128]{2,1,0:T(8,128)(2,1)}, bf16[2,512,128]{2,1,0:T(8,128)(2,1)}, bf16[2,512,128]{2,1,0:T(8,128)(2,1)}) custom-call(s32[4]{0:T(128)} %pad_add_fusion.place, bf16[512,512]{1,0:T(8,128)(2,1)} %bitcast.14, bf16[512,512]{1,0:T(8,128)(2,1)} %bitcast.15, bf16[1024,512]{1,0:T(8,128)(2,1)} %get-tuple-element.62.after.far), custom_call_target="tpu_custom_call" | custom-call | flops 1 | bytes 1 | tf_op jit(solution)/shard_map/weight_by_z/pallas_call | solution.py:294
  251.9 3.2 %collective-permute-start.18 = (bf16[2,512,128]{2,1,0:T(8,128)(2,1)}, bf16[2,512,128]{2,1,0:T(8,128)(2,1)}, u32[]{:S(2)}, u32[]{:S(2)}) collective-permute-start(bf16[2,512,128]{2,1,0:T(8,128)(2,1)} %get-tuple-element.69), channel_id=1, source_target_pairs={{0,12},{1,13},{2,14},{3,15},{4,0},{5,1},{6,2},{7,3},{8,4},{9,5},{1... | collective-permute-start | bytes 786440 | tf_op jit(solution)/shard_map/ppermute | solution.py:38
  255.1 9.4 %projection.1.after = bf16[1024,1024]{1,0:T(8,128)(2,1)} custom-call(s32[4]{0:T(128)} %pad_add_fusion.place, bf16[1024,512]{1,0:T(8,128)(2,1)} %get-tuple-element.50.out_ref.own, bf16[1024,512]{1,0:T(8,128)(2,1)} %get-tuple-element.61.core, bf16[1024,512]{1,0:T(8,128)(2,1)} %get-tuple-element.62.after.far, ...), custom_call_target="tpu_custom_call" | custom-call | flops 1 | bytes 1 | tf_op jit(solution)/shard_map/projection/pallas_call | solution.py:294
  264.5 2.9 collective-permute-done.17.b_ref
  267.4 2.7 weight_z_sum.1
  270.1 29.5 %collective-permute-start.20 = (bf16[512,128]{1,0:T(8,128)(2,1)}, bf16[512,128]{1,0:T(8,128)(2,1)}, u32[]{:S(2)}, u32[]{:S(2)}) collective-permute-start(bf16[512,128]{1,0:T(8,128)(2,1)} %get-tuple-element.74), channel_id=1, source_target_pairs={{0,64},{1,65},{2,66},{3,67},{4,68},{5,69},{6,70},{7,71},{8,72},{9,... | collective-permute-start | bytes 393224 | tf_op jit(solution)/shard_map/ppermute | solution.py:38
  299.5 5.6 %key_value_sum.1 = (bf16[1024,512]{1,0:T(8,128)(2,1)}, bf16[1024,512]{1,0:T(8,128)(2,1)}) custom-call(s32[4]{0:T(128)} %pad_add_fusion.place, f32[2,1024,512]{2,1,0:T(8,128)} %get-tuple-element.60.refs_4_.own_ref, bf16[2,1024,512]{2,1,0:T(8,128)(2,1)} %collective-permute-done.15.near_ref, bf16[2,512,512]{2,1,0:T(8,128)(2,1)} %collective-permute-done.16.far_ref, ...), custom_call_target="tpu_custom_call" | custom-call | flops 1 | bytes 1 | tf_op jit(solution)/shard_map/key_value_sum/pallas_call | solution.py:294
  305.1 1.7 convert_add_fusion
  (33 shorter events, 0.3 us)
Async XLA Ops:
  7.2 121.0 %all-gather.2.cloned.1.call-start = ((), (), s32[]{:S(2)}) async-start(), calls=%async_computation.2 | async-start | bytes 2621440 | tf_op jit(solution)/shard_map/all_gather | solution.py:586
  7.2 40.4 %collective-permute-start.2 = (bf16[1024,1024]{1,0:T(8,128)(2,1)}, bf16[1024,1024]{1,0:T(8,128)(2,1)}, u32[]{:S(2)}, u32[]{:S(2)}) collective-permute-start(bf16[1024,1024]{1,0:T(8,128)(2,1)} %a_ref.5), channel_id=1, source_target_pairs={{0,1},{1,0},{2,3},{3,2},{4,5},{5,4},{6,7},{7,6},{8,9},{9,8},{10,11... | collective-permute-start | bytes 6291464 | tf_op jit(solution)/shard_map/ppermute | solution.py:38
  10.5 25.1 %collective-permute-start.4 = (bf16[128,2048]{1,0:T(8,128)(2,1)}, bf16[128,2048]{1,0:T(8,128)(2,1)}, u32[]{:S(2)}, u32[]{:S(2)}) collective-permute-start(bf16[128,2048]{1,0:T(8,128)(2,1)} %projection_quarter.1), channel_id=1, source_target_pairs={{0,2},{1,3},{2,0},{3,1},{4,6},{5,7},{6,4},{7,5},{8,10},{9,11},{10,... | collective-permute-start | bytes 1572872 | tf_op jit(solution)/shard_map/ppermute | solution.py:38
  11.9 35.7 %collective-permute-start = (bf16[1024,512]{1,0:T(8,128)(2,1)}, bf16[1024,512]{1,0:T(8,128)(2,1)}, u32[]{:S(2)}, u32[]{:S(2)}) collective-permute-start(bf16[1024,512]{1,0:T(8,128)(2,1)} %k_ref.5), channel_id=1, source_target_pairs={{0,4},{4,8},{8,12},{12,16},{16,20},{20,24},{24,28},{28,32},{32,36}... | collective-permute-start | bytes 3145736 | tf_op jit(solution)/shard_map/ppermute | solution.py:62
  15.7 31.9 %collective-permute-start.1 = (bf16[1024,512]{1,0:T(8,128)(2,1)}, bf16[1024,512]{1,0:T(8,128)(2,1)}, u32[]{:S(2)}, u32[]{:S(2)}) collective-permute-start(bf16[1024,512]{1,0:T(8,128)(2,1)} %v_ref.5), channel_id=1, source_target_pairs={{60,124},{61,125},{62,126},{63,127}} | collective-permute-start | bytes 3145736 | tf_op jit(solution)/shard_map/ppermute | solution.py:568
  20.3 27.3 %collective-permute-start.3 = (bf16[2,512,512]{2,1,0:T(8,128)(2,1)}, bf16[2,512,512]{2,1,0:T(8,128)(2,1)}, u32[]{:S(2)}, u32[]{:S(2)}) collective-permute-start(bf16[2,512,512]{2,1,0:T(8,128)(2,1)} %second_blocks.1), channel_id=1, source_target_pairs={{0,12},{4,0},{8,4},{12,8},{16,28},{20,16},{24,20},{28,24},{32,44},... | collective-permute-start | bytes 3145736 | tf_op jit(solution)/shard_map/ppermute | solution.py:76
  47.7 172.8 %reduce-scatter.3.cloned.1.call-start = ((), (), s32[]{:S(2)}) async-start(), calls=%async_computation.3 | async-start | bytes 2621440 | tf_op jit(solution)/shard_map/reduce_scatter | solution.py:443
  47.7 41.9 %collective-permute-start.5 = (bf16[1024,512]{1,0:T(8,128)(2,1)}, bf16[1024,512]{1,0:T(8,128)(2,1)}, u32[]{:S(2)}, u32[]{:S(2)}) collective-permute-start(bf16[1024,512]{1,0:T(8,128)(2,1)} %get-tuple-element.44), channel_id=1, source_target_pairs={{0,4},{4,8},{8,12},{12,16},{16,20},{20,24},{24,28},{28,32},{32,36}... | collective-permute-start | bytes 3145736 | tf_op jit(solution)/shard_map/ppermute | solution.py:62
  52.3 37.4 %collective-permute-start.6 = (bf16[1024,512]{1,0:T(8,128)(2,1)}, bf16[1024,512]{1,0:T(8,128)(2,1)}, u32[]{:S(2)}, u32[]{:S(2)}) collective-permute-start(bf16[1024,512]{1,0:T(8,128)(2,1)} %get-tuple-element.45), channel_id=1, source_target_pairs={{124,64},{125,65},{126,66},{127,67}} | collective-permute-start | bytes 3145736 | tf_op jit(solution)/shard_map/ppermute | solution.py:583
  53.9 47.6 %collective-permute-start.7 = (bf16[2,512,512]{2,1,0:T(8,128)(2,1)}, bf16[2,512,512]{2,1,0:T(8,128)(2,1)}, u32[]{:S(2)}, u32[]{:S(2)}) collective-permute-start(bf16[2,512,512]{2,1,0:T(8,128)(2,1)} %get-tuple-element.46), channel_id=1, source_target_pairs={{12,8},{0,12},{4,16},{8,20},{28,24},{16,28},{20,32},{24,36},{44,40... | collective-permute-start | bytes 3145736 | tf_op jit(solution)/shard_map/ppermute | solution.py:80
  79.4 48.8 %collective-permute-start.10 = (bf16[1024,1024]{1,0:T(8,128)(2,1)}, bf16[1024,1024]{1,0:T(8,128)(2,1)}, u32[]{:S(2)}, u32[]{:S(2)}) collective-permute-start(bf16[1024,1024]{1,0:T(8,128)(2,1)} %get-tuple-element.51), channel_id=1, source_target_pairs={{0,2},{1,3},{2,0},{3,1},{4,6},{5,7},{6,4},{7,5},{8,10},{9,11},{10,... | collective-permute-start | bytes 6291464 | tf_op jit(solution)/shard_map/ppermute | solution.py:38
  114.4 133.6 %reduce-scatter.5.cloned.1.call-start = ((), (), s32[]{:S(2)}) async-start(), calls=%async_computation.4 | async-start | bytes 2621440 | tf_op jit(solution)/shard_map/reduce_scatter | solution.py:443
  128.2 4.5 %collective-permute-start.12 = (bf16[1024,1024]{1,0:T(8,128)(2,1)}, bf16[1024,1024]{1,0:T(8,128)(2,1)}, u32[]{:S(2)}, u32[]{:S(2)}) collective-permute-start(bf16[1024,1024]{1,0:T(8,128)(2,1)} %get-tuple-element.56.a_ref), channel_id=1, source_target_pairs={{0,1},{1,0},{2,3},{3,2},{4,5},{5,4},{6,7},{7,6},{8,9},{9,8},{10,11... | collective-permute-start | bytes 6291464 | tf_op jit(solution)/shard_map/ppermute | solution.py:38
  139.7 63.3 %collective-permute-start.11 = (bf16[2,512,1024]{2,1,0:T(8,128)(2,1)}, bf16[2,512,1024]{2,1,0:T(8,128)(2,1)}, u32[]{:S(2)}, u32[]{:S(2)}) collective-permute-start(bf16[2,512,1024]{2,1,0:T(8,128)(2,1)} %projection_core.1.after), channel_id=1, source_target_pairs={{0,1},{1,0},{2,3},{3,2},{4,5},{5,4},{6,7},{7,6},{8,9},{9,8},{10,11... | collective-permute-start | bytes 6291464 | tf_op jit(solution)/shard_map/ppermute | solution.py:38
  139.9 63.1 %collective-permute-start.9 = (bf16[1024,512]{1,0:T(8,128)(2,1)}, bf16[1024,512]{1,0:T(8,128)(2,1)}, u32[]{:S(2)}, u32[]{:S(2)}) collective-permute-start(bf16[1024,512]{1,0:T(8,128)(2,1)} %get-tuple-element.50.out_ref.own), channel_id=1, source_target_pairs={{0,2},{1,3},{2,0},{3,1},{4,6},{5,7},{6,4},{7,5},{8,10},{9,11},{10,... | collective-permute-start | bytes 3145736 | tf_op jit(solution)/shard_map/ppermute | solution.py:38
  150.0 52.9 %collective-permute-start.8 = (bf16[1024,512]{1,0:T(8,128)(2,1)}, bf16[1024,512]{1,0:T(8,128)(2,1)}, u32[]{:S(2)}, u32[]{:S(2)}) collective-permute-start(bf16[1024,512]{1,0:T(8,128)(2,1)} %get-tuple-element.50.out_ref.own), channel_id=1, source_target_pairs={{0,1},{1,0},{2,3},{3,2},{4,5},{5,4},{6,7},{7,6},{8,9},{9,8},{10,11... | collective-permute-start | bytes 3145736 | tf_op jit(solution)/shard_map/ppermute | solution.py:38
  157.3 58.7 %collective-permute-start.13 = (bf16[2,512,512]{2,1,0:T(8,128)(2,1)}, bf16[2,512,512]{2,1,0:T(8,128)(2,1)}, u32[]{:S(2)}, u32[]{:S(2)}) collective-permute-start(bf16[2,512,512]{2,1,0:T(8,128)(2,1)} %get-tuple-element.57), channel_id=1, source_target_pairs={{8,12},{12,0},{16,20},{20,24},{24,28},{28,16},{32,36},{36,40},{40,... | collective-permute-start | bytes 3145736 | tf_op jit(solution)/shard_map/ppermute | solution.py:76
  192.7 106.8 %collective-permute-start.15 = (bf16[2,1024,512]{2,1,0:T(8,128)(2,1)}, bf16[2,1024,512]{2,1,0:T(8,128)(2,1)}, u32[]{:S(2)}, u32[]{:S(2)}) collective-permute-start(bf16[2,1024,512]{2,1,0:T(8,128)(2,1)} %get-tuple-element.66), channel_id=1, source_target_pairs={{4,0},{8,4},{12,8},{16,12},{20,16},{24,20},{28,24},{32,28},{36,32}... | collective-permute-start | bytes 6291464 | tf_op jit(solution)/shard_map/ppermute | solution.py:62
  216.0 39.1 %collective-permute-start.14 = (bf16[1024,512]{1,0:T(8,128)(2,1)}, bf16[1024,512]{1,0:T(8,128)(2,1)}, u32[]{:S(2)}, u32[]{:S(2)}) collective-permute-start(bf16[1024,512]{1,0:T(8,128)(2,1)} %get-tuple-element.62.after.far), channel_id=1, source_target_pairs={{0,1},{1,0},{2,3},{3,2},{4,5},{5,4},{6,7},{7,6},{8,9},{9,8},{10,11... | collective-permute-start | bytes 3145736 | tf_op jit(solution)/shard_map/ppermute | solution.py:38
  216.0 83.5 %collective-permute-start.16 = (bf16[2,512,512]{2,1,0:T(8,128)(2,1)}, bf16[2,512,512]{2,1,0:T(8,128)(2,1)}, u32[]{:S(2)}, u32[]{:S(2)}) collective-permute-start(bf16[2,512,512]{2,1,0:T(8,128)(2,1)} %get-tuple-element.67), channel_id=1, source_target_pairs={{12,0},{0,4},{20,8},{24,12},{28,16},{16,20},{36,24},{40,28},{44,32... | collective-permute-start | bytes 3145736 | tf_op jit(solution)/shard_map/ppermute | solution.py:80
  251.9 15.5 %collective-permute-start.17 = (bf16[2,512,128]{2,1,0:T(8,128)(2,1)}, bf16[2,512,128]{2,1,0:T(8,128)(2,1)}, u32[]{:S(2)}, u32[]{:S(2)}) collective-permute-start(bf16[2,512,128]{2,1,0:T(8,128)(2,1)} %get-tuple-element.68), channel_id=1, source_target_pairs={{0,4},{1,5},{2,6},{3,7},{4,8},{5,9},{6,10},{7,11},{8,12},{9,13},{1... | collective-permute-start | bytes 786440 | tf_op jit(solution)/shard_map/ppermute | solution.py:38
  251.9 15.5 %collective-permute-start.18 = (bf16[2,512,128]{2,1,0:T(8,128)(2,1)}, bf16[2,512,128]{2,1,0:T(8,128)(2,1)}, u32[]{:S(2)}, u32[]{:S(2)}) collective-permute-start(bf16[2,512,128]{2,1,0:T(8,128)(2,1)} %get-tuple-element.69), channel_id=1, source_target_pairs={{0,12},{1,13},{2,14},{3,15},{4,0},{5,1},{6,2},{7,3},{8,4},{9,5},{1... | collective-permute-start | bytes 786440 | tf_op jit(solution)/shard_map/ppermute | solution.py:38
  255.1 12.3 %collective-permute-start.19 = (bf16[2,512,128]{2,1,0:T(8,128)(2,1)}, bf16[2,512,128]{2,1,0:T(8,128)(2,1)}, u32[]{:S(2)}, u32[]{:S(2)}) collective-permute-start(bf16[2,512,128]{2,1,0:T(8,128)(2,1)} %get-tuple-element.70), channel_id=1, source_target_pairs={{0,8},{1,9},{2,10},{3,11},{4,12},{5,13},{6,14},{7,15},{8,0},{9,1},... | collective-permute-start | bytes 786440 | tf_op jit(solution)/shard_map/ppermute | solution.py:38
  270.1 35.1 %collective-permute-start.20 = (bf16[512,128]{1,0:T(8,128)(2,1)}, bf16[512,128]{1,0:T(8,128)(2,1)}, u32[]{:S(2)}, u32[]{:S(2)}) collective-permute-start(bf16[512,128]{1,0:T(8,128)(2,1)} %get-tuple-element.74), channel_id=1, source_target_pairs={{0,64},{1,65},{2,66},{3,67},{4,68},{5,69},{6,70},{7,71},{8,72},{9,... | collective-permute-start | bytes 393224 | tf_op jit(solution)/shard_map/ppermute | solution.py:38
Sparse Core Ops, SparseCore 0:
  47.8 76.6 all-gather.1
  127.4 67.3 reduce-scatter.2
  197.4 50.6 reduce-scatter.4

commit v4 on v3

--- a/solution.py
+++ b/solution.py
@@ -50,6 +50,10 @@
     return move(value, lambda x_lo, y, z, x_hi, core: (1 - x_lo, y, z, x_hi, core))
 
 
+def to_y(value, steps):
+    return move(value, lambda x_lo, y, z, x_hi, core: (x_lo, (y + steps) % 4, z, x_hi, core))
+
+
 def to_z(value, steps):
     return move(value, lambda x_lo, y, z, x_hi, core: (x_lo, y, (z + steps) % 4, x_hi, core))
 
@@ -57,14 +61,15 @@
 EDGE = 15
 
 
-def along_ctx(value, steps, without=()):
-    pairs = [(s, s + steps) for s in range(32) if 0 <= s + steps < 32 and s not in without]
+def along_ctx(value, steps):
+    pairs = [(s, s + steps) for s in range(32) if 0 <= s + steps < 32]
     return lax.ppermute(value, "ctx", pairs)
 
 
 def middle(source, sign):
-    place = source // 4 * 4 + (source % 4 - sign) % 4
-    return place if source // 16 == (source + 2 * sign) // 16 else (place + 16) % 32
+    if source // 16 == (source + 2 * sign) // 16:
+        return source // 4 * 4 + (source % 4 - sign) % 4
+    return {14: 29, 15: 13, 17: 2, 16: 18}[source]
 
 
 def two_pairs(sign):
@@ -111,11 +116,11 @@
 BEHIND_TILES = ((0, 3, 0), (0, 2, 1), (0, 1, 2), (1, 3, 1), (1, 2, 2))
 
 
-def key_value(index, near_k, near_v, edge_v, far):
+def key_value(index, near_k, near_v, edge_k, edge_v, far):
     if index == 0:
         return far[0], far[1]
     rows = block_rows(index - 1)
-    return near_k[rows, :], near_v[rows, :] + edge_v[rows, :]
+    return near_k[rows, :] + edge_k[rows, :], near_v[rows, :] + edge_v[rows, :]
 
 
 def absorb(keys, vals, query, top, total, acc, rows):
@@ -163,7 +168,7 @@
 
 
 def forward_behind_kernel(
-    flags, q_ref, k1_ref, v1_ref, edge_ref, far_ref, acc_in, top_in, total_in,
+    flags, q_ref, k1_ref, v1_ref, k0_ref, v0_ref, far_ref, acc_in, top_in, total_in,
     after, out_ref, turned_ref, log_ref, acc, top, total,
 ):
     acc[...] = acc_in[...]
@@ -175,7 +180,7 @@
 
         @pl.when(flags[qb * WIN + o] == 1)
         def _(rows=rows, line=line, index=index):
-            keys, vals = key_value(index, k1_ref, v1_ref, edge_ref, far_ref)
+            keys, vals = key_value(index, k1_ref, v1_ref, k0_ref, v0_ref, far_ref)
             top[line, :], total[line, :] = absorb(
                 keys, vals, q_ref[rows, :], top[line, :], total[line, :], acc, rows
             )
@@ -199,7 +204,7 @@
 
 
 def backward_behind_kernel(
-    flags, q_ref, k1_ref, v1_ref, edge_ref, far_ref, out_ref, grad_ref, log_ref,
+    flags, q_ref, k1_ref, v1_ref, k0_ref, v0_ref, far_ref, out_ref, grad_ref, log_ref,
     after, near_back, far_back, dq, delta_ref, dk, dv,
 ):
     dk[...] = jnp.zeros_like(dk)
@@ -215,7 +220,7 @@
 
         @pl.when(flags[qb * WIN + o] == 1)
         def _(rows=rows, line=line, index=index):
-            keys, vals = key_value(index, k1_ref, v1_ref, edge_ref, far_ref)
+            keys, vals = key_value(index, k1_ref, v1_ref, k0_ref, v0_ref, far_ref)
             key_part, value_part, query_part = tile_grads(
                 keys, vals, q_ref[rows, :], grad_ref[rows, :],
                 log_ref[0, line, :], delta_ref[0, line, :], False,
@@ -317,28 +322,30 @@
     )
 
 
-def forward_behind(flags, q, near_k, near_v, edge_v, far, state, after):
+def forward_behind(flags, q, near_k, near_v, edge_k, edge_v, far, state, after):
     lines = pltpu.VMEM((2, BLK), f32)
     return call(
         forward_behind_kernel, "forward_behind", (HEADS,),
-        [head(1024)] * 4 + [head_pair(512)]
+        [head(1024)] * 5 + [head_pair(512)]
         + [HEAD_TURNED, HEAD_LINES, HEAD_LINES, ANY],
         [head(1024), HEAD_TURNED, HEAD_LINES],
         [shape((1024, WIDTH), bf16), shape((WIDTH, 1024), bf16), LINES],
         [pltpu.VMEM((HDIM, 1024), f32), lines, lines],
-        (flags, q, near_k, near_v, edge_v, far, *state, after),
-    )
-
-
-def backward_behind(flags, q, near_k, near_v, edge_v, far, out, grad, log_sum, after):
+        (flags, q, near_k, near_v, edge_k, edge_v, far, *state, after),
+    )
+
+
+def backward_behind(
+    flags, q, near_k, near_v, edge_k, edge_v, far, out, grad, log_sum, after
+):
     held = pltpu.VMEM((3 * BLK, HDIM), f32)
     return call(
         backward_behind_kernel, "backward_behind", (HEADS,),
-        [head(1024)] * 4 + [head_pair(512)]
+        [head(1024)] * 5 + [head_pair(512)]
         + [head(1024), head(1024), HEAD_LINES, ANY],
         [head_pair(1024), head_pair(512), HEAD_TURNED, HEAD_LINES],
         [shape((2, 1024, WIDTH), bf16), shape((2, 512, WIDTH), bf16), TURNED, LINES],
-        [held, held], (flags, q, near_k, near_v, edge_v, far, out, grad, log_sum, after),
+        [held, held], (flags, q, near_k, near_v, edge_k, edge_v, far, out, grad, log_sum, after),
     )
 
 
@@ -417,12 +424,14 @@
     )
 
 
-def weight_kernel(place, turned_ref, a_ref, b_ref, after, out_ref):
+def weight_kernel(place, turned_ref, a_ref, b_ref, after, *outs):
+    y = (place[0] ^ pl.program_id(0)) % 2 * 2 + pl.program_id(1)
     for part, ref in enumerate((a_ref, b_ref)):
-
-        @pl.when(pl.program_id(0) == part)
-        def _(ref=ref):
-            out_ref[0] = dot(turned_ref[...], ref[...], NN).astype(bf16)
+        for slot, out_ref in enumerate(outs):
+
+            @pl.when((pl.program_id(0) == part) & ((y - place[1] + 3) % 4 == slot))
+            def _(ref=ref, out_ref=out_ref):
+                out_ref[...] = dot(turned_ref[...], ref[...], NN).astype(bf16)
 
 
 def weight_terms(place, turned, a, b, after):
@@ -434,15 +443,13 @@
             pl.BlockSpec((1024, 512), lambda i, half, place: (0, jnp.where(i == 0, 0, half))),
             ANY,
         ],
-        pl.BlockSpec((1, 512, 512), lambda i, half, place: ((place[0] ^ i) % 2 * 2 + half, 0, 0)),
-        shape((4, 512, 512), bf16), [], (place, turned, a, b, after),
-    )
-
-
-def sum_over_y(parts):
-    return lax.psum_scatter(
-        parts, "ctx", scatter_dimension=0, axis_index_groups=groups_along(1)
-    )
+        [pl.BlockSpec((512, 512), lambda i, half, place: (0, 0))] * 4,
+        [shape((512, 512), bf16)] * 4, [], (place, turned, a, b, after),
+    )
+
+
+def over_y(parts):
+    return [to_y(parts[s], s + 1) for s in (0, 2, 1)]
 
 
 def groups_along(axis):
@@ -454,21 +461,24 @@
     return list(groups.values())
 
 
-def pieces_kernel(place, a_ref, b_ref, after, *outs):
+def pieces_kernel(place, a0, a1, a2, a3, b0, b1, b2, b3, after, *outs):
+    def total(refs):
+        return sum(ref[...].astype(f32) for ref in refs).astype(bf16)
+
     for slot, out_ref in enumerate(outs):
 
         @pl.when(pl.program_id(0) == slot)
         def _(out_ref=out_ref):
-            out_ref[0] = a_ref[...]
-            out_ref[1] = b_ref[...]
+            out_ref[0] = total((a0, a1, a2, a3))
+            out_ref[1] = total((b0, b1, b2, b3))
 
 
 def pieces_by_z(place, a, b, after):
     piece = pl.BlockSpec((512, 128), lambda i, place: (0, (place[2] + i + 1) % 4))
     return call(
-        pieces_kernel, "weight_by_z", (4,), [piece, piece, ANY],
+        pieces_kernel, "weight_by_z", (4,), [piece] * 8 + [ANY],
         [pl.BlockSpec((2, 512, 128), lambda i, place: (0, 0, 0))] * 4,
-        [shape((2, 512, 128), bf16)] * 4, [], (place, a, b, after),
+        [shape((2, 512, 128), bf16)] * 4, [], (place, *a, *b, after),
     )
 
 
@@ -519,35 +529,44 @@
     )
 
 
-def core_kernel(place, own_ref, far_ref, after, out_ref):
+def core_kernel(place, own_ref, far_ref, far_rows, own_rows, after, out_ref):
     out_ref[0] = own_ref[...]
     out_ref[1] = far_ref[...]
-
-
-def core_columns(place, weight, far_weight, after):
-    return call(
-        core_kernel, "projection_core", (1,),
+    for part, rows in ((2, far_rows), (3, own_rows)):
+        for half in range(2):
+            out_ref[part, :, block_rows(half)] = rows[block_rows(half), :]
+
+
+def for_core(place, weight, far_weight, far_attention, attention, after):
+    rows = pl.BlockSpec((1024, 512), lambda i, place: (0, 0))
+    return call(
+        core_kernel, "for_core", (1,),
         [
             pl.BlockSpec((512, 1024), lambda i, place: (0, place[0] ^ 1)),
             pl.BlockSpec((512, 1024), lambda i, place: (0, 1 - place[0] % 2)),
-            ANY,
+            rows, rows, ANY,
         ],
-        pl.BlockSpec((2, 512, 1024), lambda i, place: (0, 0, 0)),
-        shape((2, 512, 1024), bf16), [], (place, weight, far_weight, after),
+        pl.BlockSpec((4, 512, 1024), lambda i, place: (0, 0, 0)),
+        shape((4, 512, 1024), bf16), [],
+        (place, weight, far_weight, far_attention, attention, after),
     )
 
 
 def mix_kernel(place, own, core, far, far_core, w_own, w_far, w_core, after, out_ref):
-    total = dot(own[...], w_own[...], NN) + dot(core[...], w_core[0], NN)
-    total += dot(far[...], w_far[...], NN) + dot(far_core[...], w_core[1], NN)
+    total = dot(own[...], w_own[...], NN) + dot(core[0], w_core[0], NN)
+    total += dot(far[...], w_far[...], NN) + dot(far_core[0], w_core[1], NN)
     out_ref[...] = total.astype(bf16)
 
 
-def mix(place, attentions, weight, far_weight, core_weight, after):
+def mix(place, attention, far_attention, weight, far_weight, from_core, after):
     rows = pl.BlockSpec((512, 512), lambda i, place: (i, 0))
     return call(
         mix_kernel, "projection", (2,),
-        [rows] * 4 + [
+        [
+            rows,
+            pl.BlockSpec((1, 512, 512), lambda i, place: (3, 0, i)),
+            rows,
+            pl.BlockSpec((1, 512, 512), lambda i, place: (2, 0, i)),
             pl.BlockSpec((512, 1024), lambda i, place: (0, place[0])),
             pl.BlockSpec((512, 1024), lambda i, place: (0, place[0] % 2)),
             pl.BlockSpec((2, 512, 1024), lambda i, place: (0, 0, 0)),
@@ -555,7 +574,7 @@
         ],
         pl.BlockSpec((512, 1024), lambda i, place: (i, 0)),
         shape((1024, 1024), bf16), [],
-        (place, *attentions, weight, far_weight, core_weight, after),
+        (place, attention, from_core, far_attention, from_core, weight, far_weight, from_core, after),
     )
 
 
@@ -564,7 +583,8 @@
     tp = lax.axis_index("tp")
     place = jnp.stack([tp, ctx // 4 % 4, ctx % 4, ctx // 16]).astype(jnp.int32)
 
-    near_keys = along_ctx(keys, 1)
+    near_pairs = [(s, s + 1) for s in range(31) if s != EDGE]
+    near_keys = lax.ppermute(keys, "ctx", near_pairs + [(EDGE, 0)])
     crossed = lax.ppermute(values, "ctx", [(EDGE, EDGE + 16)])
     core_grad = to_core(out_grad)
     far_moved = first_hop(pack(place, keys, values), 1)
@@ -579,7 +599,8 @@
     near_keys, crossed, core_grad, far_moved, far_weight, held_values, held_grad = together(
         [near_keys, crossed, core_grad, far_moved, far_weight, held_values, held_grad]
     )
-    near_values = along_ctx(held_values, 1, (EDGE,))
+    near_values = lax.ppermute(held_values, "ctx", near_pairs)
+    edge_keys = lax.ppermute(near_keys, "ctx", [(0, EDGE + 1)])
     edge_values = lax.ppermute(crossed, "ctx", [(EDGE + 16, EDGE + 1)])
     far = second_hop(far_moved, 1)
     far_grad = to_x_hi(held_grad)
@@ -587,38 +608,43 @@
         far_weight, "ctx", axis=0, tiled=True, axis_index_groups=groups_along(1)
     )
     terms = grad_terms(place, 0, out_grad, core_grad, out_weight, None, near_keys)
-    behind = (flags, queries, near_keys, near_values, edge_values, far)
+    behind = (flags, queries, near_keys, near_values, edge_keys, edge_values, far)
     attention, turned, log_sum = forward_behind(*behind, own_state, terms)
 
-    core_attention = to_core(attention)
     far_attention = to_x_hi(attention)
     own_parts = weight_terms(place, turned, out_grad, core_grad, log_sum)
-    own_sum = sum_over_y(own_parts)
-    far_grad, far_weight = together([far_grad, far_weight], [own_parts])
+    far_grad, far_weight, far_attention = together(
+        [far_grad, far_weight, far_attention], [own_parts[3]]
+    )
+    own_moved = over_y(own_parts)
     far_core_grad = to_core(far_grad)
-    core_weight = core_columns(place, out_weight, far_weight, own_parts)
-    far_parts = weight_terms(place, turned, far_grad, far_core_grad, core_weight)
-    far_sum = sum_over_y(far_parts)
-    attn_grad = grad_terms(place, 2, far_grad, far_core_grad, out_weight, terms, far_parts)
+    from_core = to_core(
+        for_core(place, out_weight, far_weight, far_attention, attention, own_parts[3])
+    )
+    far_parts = weight_terms(place, turned, far_grad, far_core_grad, far_weight)
+    attn_grad = grad_terms(place, 2, far_grad, far_core_grad, out_weight, terms, far_parts[3])
+
+    *held, from_core, attn_grad = together([*own_moved, *far_parts, from_core, attn_grad])
+    own_moved, far_parts = held[:3], held[3:]
+    far_moved = over_y(far_parts)
     near_back, far_back, dq, delta = backward_behind(
         *behind, attention, attn_grad, log_sum, attn_grad
     )
     near_back = along_ctx(near_back, -1)
-    far_moved = first_hop(far_back, -1)
-    core_weight = to_core(core_weight)
+    back_moved = first_hop(far_back, -1)
     query_grad, own = backward_own(
         flags, queries, keys, values, attn_grad, log_sum, dq, delta, delta
     )
-    core_attention, far_attention, core_weight, far_moved = together(
-        [core_attention, far_attention, core_weight, far_moved], [own]
-    )
-    far_back = second_hop(far_moved, -1)
-    far_core_attention = to_core(far_attention)
-    attentions = (attention, core_attention, far_attention, far_core_attention)
-
-    weight_pieces = pieces_by_z(place, own_sum, far_sum, far_attention)
+    [back_moved] = together([back_moved], [own])
+    far_back = second_hop(back_moved, -1)
+
+    weight_pieces = pieces_by_z(
+        place, [own_parts[3], *own_moved], [far_parts[3], *far_moved], own
+    )
     weight_terms_z = [weight_pieces[3]] + [to_z(weight_pieces[s], s + 1) for s in (0, 2, 1)]
-    mixed = mix(place, attentions, out_weight, far_weight, core_weight, weight_pieces[3])
+    mixed = mix(
+        place, attention, far_attention, out_weight, far_weight, from_core, weight_pieces[3]
+    )
     kept, sent = weight_z_sum(place, weight_terms_z, mixed)
     weight_grad = kept + to_x_lo(sent).astype(f32)
     key_grad, value_grad = finish(place, own, near_back, far_back, kept)

time: 315 us -> 322 us (1.022)
  the two profiles are of different devices: /device:TPU:30 before, /device:TPU:24 now
where the time goes in v4:
time: 322 us; the launch traced here: 316 us
  waiting for transfers between devices  129 us (40%)
  Pallas kernels  104 us (32%)
  starting transfers between devices  63.7 us (20%)
  between operations  14.2 us (4%)
  other arithmetic  3.5 us (1%)
    pallas_call x16, Pallas kernels, call(): pl.pallas_call(kernel, grid_spec=pltpu.PrefetchScalarGridSpec(num_scalar_...  104 us
    ppermute x16, waiting for transfers between devices, move(): return lax.ppermute(value, AXES, pairs)  82.2 us
    ppermute x16, starting transfers between devices, move(): return lax.ppermute(value, AXES, pairs)  32.9 us
    ppermute x1, waiting for transfers between devices, per_device(): near_values = lax.ppermute(held_values, 'ctx', near_pairs)  25.1 us
    ppermute x2, waiting for transfers between devices, first_hop(): return lax.ppermute(value, 'ctx', [(s, m) for s, m, _ in two_pairs(sign)])  15.8 us
    ppermute x2, starting transfers between devices, first_hop(): return lax.ppermute(value, 'ctx', [(s, m) for s, m, _ in two_pairs(sign)])  7.16 us
  transfers between devices with their start and end apart: 27, of which 10 were waited for; matrix products, arithmetic and copies ran while one was open for 2% of the time, Pallas kernels for 26%

profile of v4, /device:TPU:24, one launch (start us, length us, event | category | flops | bytes accessed | tf_op | source)
XLA Modules:
  0.0 316.5 jit_solution(13783659450208080805)
XLA Ops:
  7.9 2.5 projection_quarter.1
  10.5 3.0 collective-permute-start.4
  13.5 3.8 %collective-permute-start = (bf16[1024,512]{1,0:T(8,128)(2,1)}, bf16[1024,512]{1,0:T(8,128)(2,1)}, u32[]{:S(2)}, u32[]{:S(2)}) collective-permute-start(bf16[1024,512]{1,0:T(8,128)(2,1)} %k_ref.5), channel_id=1, source_target_pairs={{0,4},{4,8},{8,12},{12,16},{16,20},{20,24},{24,28},{28,32},{32,36}... | collective-permute-start | bytes 3145736 | tf_op jit(solution)/shard_map/ppermute | solution.py:587
  17.3 1.6 collective-permute-start.1
  19.0 2.9 second_blocks.1
  21.9 5.2 %collective-permute-start.3 = (bf16[2,512,512]{2,1,0:T(8,128)(2,1)}, bf16[2,512,512]{2,1,0:T(8,128)(2,1)}, u32[]{:S(2)}, u32[]{:S(2)}) collective-permute-start(bf16[2,512,512]{2,1,0:T(8,128)(2,1)} %second_blocks.1), channel_id=1, source_target_pairs={{0,12},{4,0},{8,4},{12,8},{16,28},{20,16},{24,20},{28,24},{32,44},... | collective-permute-start | bytes 3145736 | tf_op jit(solution)/shard_map/ppermute | solution.py:81
  27.1 0.8 bitcast_add_fusion
  27.9 0.7 slice_bitcast_fusion
  28.8 0.8 fusion
  29.8 0.7 reshape.60.flags
  30.5 7.4 %forward_own.1 = (f32[512,1024]{1,0:T(8,128)}, f32[4,2,512]{2,1,0:T(2,128)}, f32[4,2,512]{2,1,0:T(2,128)}) custom-call(s32[8]{0:T(128)} %reshape.60.flags, bf16[1024,512]{1,0:T(8,128)(2,1)} %q_ref.7, bf16[1024,512]{1,0:T(8,128)(2,1)} %k_ref.5, bf16[1024,512]{1,0:T(8,128)(2,1)} %v_ref.5, bf16[1024,512]{1,0:T(8,128)(2,1)} %k_ref.5), custom_call_target="tpu_custom_call" | custom-call | flops 1 | bytes 1 | tf_op jit(solution)/shard_map/forward_own/pallas_call | solution.py:299
  37.9 3.2 %late_copies.1 = (bf16[1024,512]{1,0:T(8,128)(2,1)}, bf16[1024,1024]{1,0:T(8,128)(2,1)}) custom-call(s32[1]{0:T(128)} %constant.56.clone.1.place, bf16[1024,512]{1,0:T(8,128)(2,1)} %v_ref.5, bf16[1024,1024]{1,0:T(8,128)(2,1)} %a_ref.5, f32[4,2,512]{2,1,0:T(2,128)} %get-tuple-element.54.after.top_in), custom_call_target="tpu_custom_call" | custom-call | flops 1 | bytes 1 | tf_op jit(solution)/shard_map/late_copies/pallas_call | solution.py:299
  41.0 8.8 %collective-permute-done.3.refs_3_ = bf16[2,512,512]{2,1,0:T(8,128)(2,1)} collective-permute-done((bf16[2,512,512]{2,1,0:T(8,128)(2,1)}, bf16[2,512,512]{2,1,0:T(8,128)(2,1)}, u32[]{:S(2)}, u32[]{:S(2)}) %collective-permute-start.3) | collective-permute-done | bytes 1048608 | tf_op jit(solution)/shard_map/ppermute | solution.py:81
  49.9 4.5 %collective-permute-start.5 = (bf16[1024,512]{1,0:T(8,128)(2,1)}, bf16[1024,512]{1,0:T(8,128)(2,1)}, u32[]{:S(2)}, u32[]{:S(2)}) collective-permute-start(bf16[1024,512]{1,0:T(8,128)(2,1)} %get-tuple-element.58), channel_id=1, source_target_pairs={{0,4},{4,8},{8,12},{12,16},{16,20},{20,24},{24,28},{28,32},{32,36}... | collective-permute-start | bytes 3145736 | tf_op jit(solution)/shard_map/ppermute | solution.py:602
  54.4 1.7 collective-permute-start.7
  56.1 2.4 collective-permute-start.8
  58.5 1.6 collective-permute-start.6
  60.1 2.0 collective-permute-start.12
  62.2 6.4 %projection_backward.2.after.rest_0_ = f32[1024,512]{1,0:T(8,128)} custom-call(s32[4]{0:T(128)} %pad_add_fusion.place, bf16[1024,1024]{1,0:T(8,128)(2,1)} %a_ref.5, bf16[1024,1024]{1,0:T(8,128)(2,1)} %get-tuple-element.63.b_ref, bf16[512,4096]{1,0:T(8,128)(2,1)} %w_own.1, bf16[512,4096]{1,0:T(8,128)(2,1)} %w_own.1, ...), custom_call_target="tpu_custom_call" | custom-call | flops 1 | bytes 1 | tf_op jit(solution)/shard_map/projection_backward/pallas_call | solution.py:299
  68.6 25.1 %collective-permute-done.5.v1_ref = bf16[1024,512]{1,0:T(8,128)(2,1)} collective-permute-done((bf16[1024,512]{1,0:T(8,128)(2,1)}, bf16[1024,512]{1,0:T(8,128)(2,1)}, u32[]{:S(2)}, u32[]{:S(2)}) %collective-permute-start.5) | collective-permute-done | bytes 1048608 | tf_op jit(solution)/shard_map/ppermute | solution.py:602
  93.7 6.1 %collective-permute-done.8.far_ref = bf16[2,512,512]{2,1,0:T(8,128)(2,1)} collective-permute-done((bf16[2,512,512]{2,1,0:T(8,128)(2,1)}, bf16[2,512,512]{2,1,0:T(8,128)(2,1)}, u32[]{:S(2)}, u32[]{:S(2)}) %collective-permute-start.8) | collective-permute-done | bytes 1048608 | tf_op jit(solution)/shard_map/ppermute | solution.py:85
  99.9 9.5 %forward_behind.1 = (bf16[1024,512]{1,0:T(8,128)(2,1)}, bf16[512,1024]{1,0:T(8,128)(2,1)}, f32[4,2,512]{2,1,0:T(2,128)}) custom-call(s32[8]{0:T(128)} %reshape.60.flags, bf16[1024,512]{1,0:T(8,128)(2,1)} %q_ref.7, bf16[1024,512]{1,0:T(8,128)(2,1)} %get-tuple-element.57.rest_0_.k1_ref, bf16[1024,512]{1,0:T(8,128)(2,1)} %collective-permute-done.5.v1_ref, ...), custom_call_target="tpu_custom_call" | custom-call | flops 1 | bytes 1 | tf_op jit(solution)/shard_map/forward_behind/pallas_call | solution.py:299
  109.4 1.4 collective-permute-start.13
  110.8 7.5 %weight_gradient.2 = (bf16[512,512]{1,0:T(8,128)(2,1)}, bf16[512,512]{1,0:T(8,128)(2,1)}, bf16[512,512]{1,0:T(8,128)(2,1)}, bf16[512,512]{1,0:T(8,128)(2,1)}) custom-call(s32[4]{0:T(128)} %pad_add_fusion.place, bf16[512,1024]{1,0:T(8,128)(2,1)} %get-tuple-element.65.turned_ref, bf16[1024,1024]{1,0:T(8,128)(2,1)} %a_ref.5, ...), custom_call_target="tpu_custom_call" | custom-call | flops 1 | bytes 1 | tf_op jit(solution)/shard_map/weight_gradient/pallas_call | solution.py:299
  118.3 15.8 %collective-permute-done.13.refs_2_ = bf16[1024,512]{1,0:T(8,128)(2,1)} collective-permute-done((bf16[1024,512]{1,0:T(8,128)(2,1)}, bf16[1024,512]{1,0:T(8,128)(2,1)}, u32[]{:S(2)}, u32[]{:S(2)}) %collective-permute-start.13) | collective-permute-done | bytes 1048608 | tf_op jit(solution)/shard_map/ppermute | solution.py:38
  134.2 5.1 %for_core.1 = bf16[4,512,1024]{2,1,0:T(8,128)(2,1)} custom-call(s32[4]{0:T(128)} %pad_add_fusion.place, bf16[512,4096]{1,0:T(8,128)(2,1)} %w_own.1, bf16[512,2048]{1,0:T(8,128)(2,1)} %get-tuple-element.74.after.far_ref.w_far, bf16[1024,512]{1,0:T(8,128)(2,1)} %get-tuple-element.79.far_rows.far, bf16[1024,512]{1,0:T(8,128)(2,1)} %get-tuple-element.64.own_rows.out_ref.own, ...), custom_call_target="tpu_custom_call" | custom-call | flops 1 | bytes 1 | tf_op jit(solution)/shard_map/for_core/pallas_call | solution.py:299
  139.8 19.0 %collective-permute-start.9 = (bf16[512,512]{1,0:T(8,128)(2,1)}, bf16[512,512]{1,0:T(8,128)(2,1)}, u32[]{:S(2)}, u32[]{:S(2)}) collective-permute-start(bf16[512,512]{1,0:T(8,128)(2,1)} %get-tuple-element.67), channel_id=1, source_target_pairs={{0,16},{1,17},{2,18},{3,19},{4,20},{5,21},{6,22},{7,23},{8,24},{9,... | collective-permute-start | bytes 1572872 | tf_op jit(solution)/shard_map/ppermute | solution.py:38
  158.8 1.5 collective-permute-start.11
  160.3 7.5 %weight_gradient.3 = (bf16[512,512]{1,0:T(8,128)(2,1)}, bf16[512,512]{1,0:T(8,128)(2,1)}, bf16[512,512]{1,0:T(8,128)(2,1)}, bf16[512,512]{1,0:T(8,128)(2,1)}) custom-call(s32[4]{0:T(128)} %pad_add_fusion.place, bf16[512,1024]{1,0:T(8,128)(2,1)} %get-tuple-element.65.turned_ref, bf16[1024,1024]{1,0:T(8,128)(2,1)} %get-tuple-element.73.a_ref, ...), custom_call_target="tpu_custom_call" | custom-call | flops 1 | bytes 1 | tf_op jit(solution)/shard_map/weight_gradient/pallas_call | solution.py:299
  167.8 6.9 %projection_backward.3.refs_8_ = bf16[1024,512]{1,0:T(8,128)(2,1)} custom-call(s32[4]{0:T(128)} %pad_add_fusion.place, bf16[1024,1024]{1,0:T(8,128)(2,1)} %get-tuple-element.73.a_ref, bf16[1024,1024]{1,0:T(8,128)(2,1)} %collective-permute-done.14.b_ref, bf16[512,4096]{1,0:T(8,128)(2,1)} %w_own.1, bf16[512,4096]{1,0:T(8,128)(2,1)} %w_own.1, ...), custom_call_target="tpu_custom_call" | custom-call | flops 1 | bytes 1 | tf_op jit(solution)/shard_map/projection_backward/pallas_call | solution.py:299
  174.7 7.0 %collective-permute-done.9.refs_0_ = bf16[512,512]{1,0:T(8,128)(2,1)} collective-permute-done((bf16[512,512]{1,0:T(8,128)(2,1)}, bf16[512,512]{1,0:T(8,128)(2,1)}, u32[]{:S(2)}, u32[]{:S(2)}) %collective-permute-start.9) | collective-permute-done | bytes 524320 | tf_op jit(solution)/shard_map/ppermute | solution.py:38
  181.7 3.4 %collective-permute-done.10.refs_1_ = bf16[512,512]{1,0:T(8,128)(2,1)} collective-permute-done((bf16[512,512]{1,0:T(8,128)(2,1)}, bf16[512,512]{1,0:T(8,128)(2,1)}, u32[]{:S(2)}, u32[]{:S(2)}) %collective-permute-start.10) | collective-permute-done | bytes 524320 | tf_op jit(solution)/shard_map/ppermute | solution.py:38
  185.1 11.6 %backward_behind.1 = (bf16[2,1024,512]{2,1,0:T(8,128)(2,1)}, bf16[2,512,512]{2,1,0:T(8,128)(2,1)}, f32[512,1024]{1,0:T(8,128)}, f32[4,2,512]{2,1,0:T(2,128)}) custom-call(s32[8]{0:T(128)} %reshape.60.flags, bf16[1024,512]{1,0:T(8,128)(2,1)} %q_ref.7, bf16[1024,512]{1,0:T(8,128)(2,1)} %get-tuple-element.57.rest_0_.k1_ref, ...), custom_call_target="tpu_custom_call" | custom-call | flops 1 | bytes 1 | tf_op jit(solution)/shard_map/backward_behind/pallas_call | solution.py:299
  196.7 1.9 collective-permute-start.20
  198.6 5.8 %collective-permute-start.19 = (bf16[2,1024,512]{2,1,0:T(8,128)(2,1)}, bf16[2,1024,512]{2,1,0:T(8,128)(2,1)}, u32[]{:S(2)}, u32[]{:S(2)}) collective-permute-start(bf16[2,1024,512]{2,1,0:T(8,128)(2,1)} %get-tuple-element.94), channel_id=1, source_target_pairs={{4,0},{8,4},{12,8},{16,12},{20,16},{24,20},{28,24},{32,28},{36,32}... | collective-permute-start | bytes 6291464 | tf_op jit(solution)/shard_map/ppermute | solution.py:66
  204.5 2.0 collective-permute-start.17
  206.5 10.6 %backward_own.1 = (bf16[1024,512]{1,0:T(8,128)(2,1)}, f32[2,1024,512]{2,1,0:T(8,128)}) custom-call(s32[8]{0:T(128)} %reshape.60.flags, bf16[1024,512]{1,0:T(8,128)(2,1)} %q_ref.7, bf16[1024,512]{1,0:T(8,128)(2,1)} %k_ref.5, bf16[1024,512]{1,0:T(8,128)(2,1)} %v_ref.5, bf16[1024,512]{1,0:T(8,128)(2,1)} %get-tuple-element.88.grad_ref.after, ...), custom_call_target="tpu_custom_call" | custom-call | flops 1 | bytes 1 | tf_op jit(solution)/shard_map/backward_own/pallas_call | solution.py:299
  217.1 6.9 %collective-permute-done.20.refs_0_ = bf16[2,512,512]{2,1,0:T(8,128)(2,1)} collective-permute-done((bf16[2,512,512]{2,1,0:T(8,128)(2,1)}, bf16[2,512,512]{2,1,0:T(8,128)(2,1)}, u32[]{:S(2)}, u32[]{:S(2)}) %collective-permute-start.20) | collective-permute-done | bytes 1048608 | tf_op jit(solution)/shard_map/ppermute | solution.py:81
  224.0 2.1 collective-permute-start.21
  226.2 48.0 %collective-permute-done.17.b2 = bf16[512,512]{1,0:T(8,128)(2,1)} collective-permute-done((bf16[512,512]{1,0:T(8,128)(2,1)}, bf16[512,512]{1,0:T(8,128)(2,1)}, u32[]{:S(2)}, u32[]{:S(2)}) %collective-permute-start.17) | collective-permute-done | bytes 524320 | tf_op jit(solution)/shard_map/ppermute | solution.py:38
  274.2 5.0 %weight_by_z.1 = (bf16[2,512,128]{2,1,0:T(8,128)(2,1)}, bf16[2,512,128]{2,1,0:T(8,128)(2,1)}, bf16[2,512,128]{2,1,0:T(8,128)(2,1)}, bf16[2,512,128]{2,1,0:T(8,128)(2,1)}) custom-call(s32[4]{0:T(128)} %pad_add_fusion.place, bf16[512,512]{1,0:T(8,128)(2,1)} %get-tuple-element.72.refs_3_.after.a0, bf16[512,512]{1,0:T(8,128)(2,1)} %get-tuple-element.81.a1, ...), custom_call_target="tpu_custom_call" | custom-call | flops 1 | bytes 1 | tf_op jit(solution)/shard_map/weight_by_z/pallas_call | solution.py:299
  279.2 3.2 %collective-permute-start.23 = (bf16[2,512,128]{2,1,0:T(8,128)(2,1)}, bf16[2,512,128]{2,1,0:T(8,128)(2,1)}, u32[]{:S(2)}, u32[]{:S(2)}) collective-permute-start(bf16[2,512,128]{2,1,0:T(8,128)(2,1)} %get-tuple-element.97), channel_id=1, source_target_pairs={{0,12},{1,13},{2,14},{3,15},{4,0},{5,1},{6,2},{7,3},{8,4},{9,5},{1... | collective-permute-start | bytes 786440 | tf_op jit(solution)/shard_map/ppermute | solution.py:38
  282.4 9.4 %projection.1.after = bf16[1024,1024]{1,0:T(8,128)(2,1)} custom-call(s32[4]{0:T(128)} %pad_add_fusion.place, bf16[1024,512]{1,0:T(8,128)(2,1)} %get-tuple-element.64.own_rows.out_ref.own, bf16[4,512,1024]{2,1,0:T(8,128)(2,1)} %get-tuple-element.80.core.far_core.w_core, bf16[1024,512]{1,0:T(8,128)(2,1)} %get-tuple-element.79.far_rows.far, ...), custom_call_target="tpu_custom_call" | custom-call | flops 1 | bytes 1 | tf_op jit(solution)/shard_map/projection/pallas_call | solution.py:299
  291.8 2.7 collective-permute-done.22.b_ref
  294.5 2.7 weight_z_sum.1
  297.2 5.2 %collective-permute-done.25 = bf16[512,128]{1,0:T(8,128)(2,1)S(1)} collective-permute-done((bf16[512,128]{1,0:T(8,128)(2,1)}, bf16[512,128]{1,0:T(8,128)(2,1)S(1)}, u32[]{:S(2)}, u32[]{:S(2)}) %collective-permute-start.25) | collective-permute-done | bytes 131104 | tf_op jit(solution)/shard_map/ppermute | solution.py:38
  302.4 1.7 convert_add_fusion
  304.0 5.6 %key_value_sum.1 = (bf16[1024,512]{1,0:T(8,128)(2,1)}, bf16[1024,512]{1,0:T(8,128)(2,1)}) custom-call(s32[4]{0:T(128)} %pad_add_fusion.place, f32[2,1024,512]{2,1,0:T(8,128)} %get-tuple-element.91.after.refs_1_.own_ref, bf16[2,1024,512]{2,1,0:T(8,128)(2,1)} %collective-permute-done.19.near_ref, bf16[2,512,512]{2,1,0:T(8,128)(2,1)} %collective-permute-done.21.far_ref, ...), custom_call_target="tpu_custom_call" | custom-call | flops 1 | bytes 1 | tf_op jit(solution)/shard_map/key_value_sum/pallas_call | solution.py:299
  (38 shorter events, 1.9 us)
Async XLA Ops:
  7.2 127.0 %all-gather.2.cloned.1.call-start = ((), (), s32[]{:S(2)}) async-start(), calls=%async_computation | async-start | bytes 2621440 | tf_op jit(solution)/shard_map/all_gather | solution.py:607
  7.2 42.7 %collective-permute-start.2 = (bf16[1024,1024]{1,0:T(8,128)(2,1)}, bf16[1024,1024]{1,0:T(8,128)(2,1)}, u32[]{:S(2)}, u32[]{:S(2)}) collective-permute-start(bf16[1024,1024]{1,0:T(8,128)(2,1)} %a_ref.5), channel_id=1, source_target_pairs={{0,1},{1,0},{2,3},{3,2},{4,5},{5,4},{6,7},{7,6},{8,9},{9,8},{10,11... | collective-permute-start | bytes 6291464 | tf_op jit(solution)/shard_map/ppermute | solution.py:38
  10.5 30.6 %collective-permute-start.4 = (bf16[128,2048]{1,0:T(8,128)(2,1)}, bf16[128,2048]{1,0:T(8,128)(2,1)}, u32[]{:S(2)}, u32[]{:S(2)}) collective-permute-start(bf16[128,2048]{1,0:T(8,128)(2,1)} %projection_quarter.1), channel_id=1, source_target_pairs={{0,2},{1,3},{2,0},{3,1},{4,6},{5,7},{6,4},{7,5},{8,10},{9,11},{10,... | collective-permute-start | bytes 1572872 | tf_op jit(solution)/shard_map/ppermute | solution.py:38
  13.5 36.4 %collective-permute-start = (bf16[1024,512]{1,0:T(8,128)(2,1)}, bf16[1024,512]{1,0:T(8,128)(2,1)}, u32[]{:S(2)}, u32[]{:S(2)}) collective-permute-start(bf16[1024,512]{1,0:T(8,128)(2,1)} %k_ref.5), channel_id=1, source_target_pairs={{0,4},{4,8},{8,12},{12,16},{16,20},{20,24},{24,28},{28,32},{32,36}... | collective-permute-start | bytes 3145736 | tf_op jit(solution)/shard_map/ppermute | solution.py:587
  17.3 32.6 %collective-permute-start.1 = (bf16[1024,512]{1,0:T(8,128)(2,1)}, bf16[1024,512]{1,0:T(8,128)(2,1)}, u32[]{:S(2)}, u32[]{:S(2)}) collective-permute-start(bf16[1024,512]{1,0:T(8,128)(2,1)} %v_ref.5), channel_id=1, source_target_pairs={{60,124},{61,125},{62,126},{63,127}} | collective-permute-start | bytes 3145736 | tf_op jit(solution)/shard_map/ppermute | solution.py:588
  21.9 28.0 %collective-permute-start.3 = (bf16[2,512,512]{2,1,0:T(8,128)(2,1)}, bf16[2,512,512]{2,1,0:T(8,128)(2,1)}, u32[]{:S(2)}, u32[]{:S(2)}) collective-permute-start(bf16[2,512,512]{2,1,0:T(8,128)(2,1)} %second_blocks.1), channel_id=1, source_target_pairs={{0,12},{4,0},{8,4},{12,8},{16,28},{20,16},{24,20},{28,24},{32,44},... | collective-permute-start | bytes 3145736 | tf_op jit(solution)/shard_map/ppermute | solution.py:81
  49.9 43.8 %collective-permute-start.5 = (bf16[1024,512]{1,0:T(8,128)(2,1)}, bf16[1024,512]{1,0:T(8,128)(2,1)}, u32[]{:S(2)}, u32[]{:S(2)}) collective-permute-start(bf16[1024,512]{1,0:T(8,128)(2,1)} %get-tuple-element.58), channel_id=1, source_target_pairs={{0,4},{4,8},{8,12},{12,16},{16,20},{20,24},{24,28},{28,32},{32,36}... | collective-permute-start | bytes 3145736 | tf_op jit(solution)/shard_map/ppermute | solution.py:602
  54.4 39.3 %collective-permute-start.7 = (bf16[1024,512]{1,0:T(8,128)(2,1)}, bf16[1024,512]{1,0:T(8,128)(2,1)}, u32[]{:S(2)}, u32[]{:S(2)}) collective-permute-start(bf16[1024,512]{1,0:T(8,128)(2,1)} %get-tuple-element.59), channel_id=1, source_target_pairs={{124,64},{125,65},{126,66},{127,67}} | collective-permute-start | bytes 3145736 | tf_op jit(solution)/shard_map/ppermute | solution.py:604
  56.1 43.8 %collective-permute-start.8 = (bf16[2,512,512]{2,1,0:T(8,128)(2,1)}, bf16[2,512,512]{2,1,0:T(8,128)(2,1)}, u32[]{:S(2)}, u32[]{:S(2)}) collective-permute-start(bf16[2,512,512]{2,1,0:T(8,128)(2,1)} %get-tuple-element.60), channel_id=1, source_target_pairs={{12,8},{0,12},{4,16},{8,20},{28,24},{16,28},{20,32},{24,36},{44,40... | collective-permute-start | bytes 3145736 | tf_op jit(solution)/shard_map/ppermute | solution.py:85
  58.5 41.3 %collective-permute-start.6 = (bf16[1024,512]{1,0:T(8,128)(2,1)}, bf16[1024,512]{1,0:T(8,128)(2,1)}, u32[]{:S(2)}, u32[]{:S(2)}) collective-permute-start(bf16[1024,512]{1,0:T(8,128)(2,1)} %get-tuple-element.57.rest_0_.k1_ref), channel_id=1, source_target_pairs={{0,64},{1,65},{2,66},{3,67}} | collective-permute-start | bytes 3145736 | tf_op jit(solution)/shard_map/ppermute | solution.py:603
  60.1 74.0 %collective-permute-start.12 = (bf16[1024,1024]{1,0:T(8,128)(2,1)}, bf16[1024,1024]{1,0:T(8,128)(2,1)}, u32[]{:S(2)}, u32[]{:S(2)}) collective-permute-start(bf16[1024,1024]{1,0:T(8,128)(2,1)} %get-tuple-element.70), channel_id=1, source_target_pairs={{0,2},{1,3},{2,0},{3,1},{4,6},{5,7},{6,4},{7,5},{8,10},{9,11},{10,... | collective-permute-start | bytes 6291464 | tf_op jit(solution)/shard_map/ppermute | solution.py:38
  109.4 24.8 %collective-permute-start.13 = (bf16[1024,512]{1,0:T(8,128)(2,1)}, bf16[1024,512]{1,0:T(8,128)(2,1)}, u32[]{:S(2)}, u32[]{:S(2)}) collective-permute-start(bf16[1024,512]{1,0:T(8,128)(2,1)} %get-tuple-element.64.own_rows.out_ref.own), channel_id=1, source_target_pairs={{0,2},{1,3},{2,0},{3,1},{4,6},{5,7},{6,4},{7,5},{8,10},{9,11},{10,... | collective-permute-start | bytes 3145736 | tf_op jit(solution)/shard_map/ppermute | solution.py:38
  139.3 45.9 %collective-permute-start.15 = (bf16[4,512,1024]{2,1,0:T(8,128)(2,1)}, bf16[4,512,1024]{2,1,0:T(8,128)(2,1)}, u32[]{:S(2)}, u32[]{:S(2)}) collective-permute-start(bf16[4,512,1024]{2,1,0:T(8,128)(2,1)} %for_core.1), channel_id=1, source_target_pairs={{0,1},{1,0},{2,3},{3,2},{4,5},{5,4},{6,7},{7,6},{8,9},{9,8},{10,11... | collective-permute-start | bytes 12582920 | tf_op jit(solution)/shard_map/ppermute | solution.py:38
  139.3 21.0 %collective-permute-start.14 = (bf16[1024,1024]{1,0:T(8,128)(2,1)}, bf16[1024,1024]{1,0:T(8,128)(2,1)}, u32[]{:S(2)}, u32[]{:S(2)}) collective-permute-start(bf16[1024,1024]{1,0:T(8,128)(2,1)} %get-tuple-element.73.a_ref), channel_id=1, source_target_pairs={{0,1},{1,0},{2,3},{3,2},{4,5},{5,4},{6,7},{7,6},{8,9},{9,8},{10,11... | collective-permute-start | bytes 6291464 | tf_op jit(solution)/shard_map/ppermute | solution.py:38
  139.8 41.9 %collective-permute-start.9 = (bf16[512,512]{1,0:T(8,128)(2,1)}, bf16[512,512]{1,0:T(8,128)(2,1)}, u32[]{:S(2)}, u32[]{:S(2)}) collective-permute-start(bf16[512,512]{1,0:T(8,128)(2,1)} %get-tuple-element.67), channel_id=1, source_target_pairs={{0,16},{1,17},{2,18},{3,19},{4,20},{5,21},{6,22},{7,23},{8,24},{9,... | collective-permute-start | bytes 1572872 | tf_op jit(solution)/shard_map/ppermute | solution.py:38
  158.8 26.3 %collective-permute-start.10 = (bf16[512,512]{1,0:T(8,128)(2,1)}, bf16[512,512]{1,0:T(8,128)(2,1)}, u32[]{:S(2)}, u32[]{:S(2)}) collective-permute-start(bf16[512,512]{1,0:T(8,128)(2,1)} %get-tuple-element.68), channel_id=1, source_target_pairs={{0,48},{1,49},{2,50},{3,51},{4,52},{5,53},{6,54},{7,55},{8,56},{9,... | collective-permute-start | bytes 1572872 | tf_op jit(solution)/shard_map/ppermute | solution.py:38
  158.8 26.3 %collective-permute-start.11 = (bf16[512,512]{1,0:T(8,128)(2,1)}, bf16[512,512]{1,0:T(8,128)(2,1)}, u32[]{:S(2)}, u32[]{:S(2)}) collective-permute-start(bf16[512,512]{1,0:T(8,128)(2,1)} %get-tuple-element.69), channel_id=1, source_target_pairs={{0,32},{1,33},{2,34},{3,35},{4,36},{5,37},{6,38},{7,39},{8,40},{9,... | collective-permute-start | bytes 1572872 | tf_op jit(solution)/shard_map/ppermute | solution.py:38
  196.7 27.3 %collective-permute-start.20 = (bf16[2,512,512]{2,1,0:T(8,128)(2,1)}, bf16[2,512,512]{2,1,0:T(8,128)(2,1)}, u32[]{:S(2)}, u32[]{:S(2)}) collective-permute-start(bf16[2,512,512]{2,1,0:T(8,128)(2,1)} %get-tuple-element.95), channel_id=1, source_target_pairs={{8,12},{12,0},{16,20},{20,24},{24,28},{28,16},{32,36},{36,40},{40,... | collective-permute-start | bytes 3145736 | tf_op jit(solution)/shard_map/ppermute | solution.py:81
  198.6 105.4 %collective-permute-start.19 = (bf16[2,1024,512]{2,1,0:T(8,128)(2,1)}, bf16[2,1024,512]{2,1,0:T(8,128)(2,1)}, u32[]{:S(2)}, u32[]{:S(2)}) collective-permute-start(bf16[2,1024,512]{2,1,0:T(8,128)(2,1)} %get-tuple-element.94), channel_id=1, source_target_pairs={{4,0},{8,4},{12,8},{16,12},{20,16},{24,20},{28,24},{32,28},{36,32}... | collective-permute-start | bytes 6291464 | tf_op jit(solution)/shard_map/ppermute | solution.py:66
  204.4 21.7 %collective-permute-start.16 = (bf16[512,512]{1,0:T(8,128)(2,1)}, bf16[512,512]{1,0:T(8,128)(2,1)}, u32[]{:S(2)}, u32[]{:S(2)}) collective-permute-start(bf16[512,512]{1,0:T(8,128)(2,1)} %get-tuple-element.85), channel_id=1, source_target_pairs={{0,16},{1,17},{2,18},{3,19},{4,20},{5,21},{6,22},{7,23},{8,24},{9,... | collective-permute-start | bytes 1572872 | tf_op jit(solution)/shard_map/ppermute | solution.py:38
  204.5 69.7 %collective-permute-start.17 = (bf16[512,512]{1,0:T(8,128)(2,1)}, bf16[512,512]{1,0:T(8,128)(2,1)}, u32[]{:S(2)}, u32[]{:S(2)}) collective-permute-start(bf16[512,512]{1,0:T(8,128)(2,1)} %get-tuple-element.86), channel_id=1, source_target_pairs={{0,48},{1,49},{2,50},{3,51},{4,52},{5,53},{6,54},{7,55},{8,56},{9,... | collective-permute-start | bytes 1572872 | tf_op jit(solution)/shard_map/ppermute | solution.py:38
  206.5 67.6 %collective-permute-start.18 = (bf16[512,512]{1,0:T(8,128)(2,1)}, bf16[512,512]{1,0:T(8,128)(2,1)}, u32[]{:S(2)}, u32[]{:S(2)}) collective-permute-start(bf16[512,512]{1,0:T(8,128)(2,1)} %get-tuple-element.87), channel_id=1, source_target_pairs={{0,32},{1,33},{2,34},{3,35},{4,36},{5,37},{6,38},{7,39},{8,40},{9,... | collective-permute-start | bytes 1572872 | tf_op jit(solution)/shard_map/ppermute | solution.py:38
  224.0 80.0 %collective-permute-start.21 = (bf16[2,512,512]{2,1,0:T(8,128)(2,1)}, bf16[2,512,512]{2,1,0:T(8,128)(2,1)}, u32[]{:S(2)}, u32[]{:S(2)}) collective-permute-start(bf16[2,512,512]{2,1,0:T(8,128)(2,1)} %order.7), channel_id=1, source_target_pairs={{12,0},{0,4},{20,8},{24,12},{28,16},{16,20},{36,24},{40,28},{44,32... | collective-permute-start | bytes 3145736 | tf_op jit(solution)/shard_map/ppermute | solution.py:85
  279.1 15.4 %collective-permute-start.22 = (bf16[2,512,128]{2,1,0:T(8,128)(2,1)}, bf16[2,512,128]{2,1,0:T(8,128)(2,1)}, u32[]{:S(2)}, u32[]{:S(2)}) collective-permute-start(bf16[2,512,128]{2,1,0:T(8,128)(2,1)} %get-tuple-element.96), channel_id=1, source_target_pairs={{0,4},{1,5},{2,6},{3,7},{4,8},{5,9},{6,10},{7,11},{8,12},{9,13},{1... | collective-permute-start | bytes 786440 | tf_op jit(solution)/shard_map/ppermute | solution.py:38
  279.2 15.4 %collective-permute-start.23 = (bf16[2,512,128]{2,1,0:T(8,128)(2,1)}, bf16[2,512,128]{2,1,0:T(8,128)(2,1)}, u32[]{:S(2)}, u32[]{:S(2)}) collective-permute-start(bf16[2,512,128]{2,1,0:T(8,128)(2,1)} %get-tuple-element.97), channel_id=1, source_target_pairs={{0,12},{1,13},{2,14},{3,15},{4,0},{5,1},{6,2},{7,3},{8,4},{9,5},{1... | collective-permute-start | bytes 786440 | tf_op jit(solution)/shard_map/ppermute | solution.py:38
  282.4 12.1 %collective-permute-start.24 = (bf16[2,512,128]{2,1,0:T(8,128)(2,1)}, bf16[2,512,128]{2,1,0:T(8,128)(2,1)}, u32[]{:S(2)}, u32[]{:S(2)}) collective-permute-start(bf16[2,512,128]{2,1,0:T(8,128)(2,1)} %get-tuple-element.98), channel_id=1, source_target_pairs={{0,8},{1,9},{2,10},{3,11},{4,12},{5,13},{6,14},{7,15},{8,0},{9,1},... | collective-permute-start | bytes 786440 | tf_op jit(solution)/shard_map/ppermute | solution.py:38
  297.2 5.2 %collective-permute-start.25 = (bf16[512,128]{1,0:T(8,128)(2,1)}, bf16[512,128]{1,0:T(8,128)(2,1)S(1)}, u32[]{:S(2)}, u32[]{:S(2)}) collective-permute-start(bf16[512,128]{1,0:T(8,128)(2,1)} %get-tuple-element.102), channel_id=1, source_target_pairs={{0,64},{1,65},{2,66},{3,67},{4,68},{5,69},{6,70},{7,71},{8,72},{9,... | collective-permute-start | bytes 393224 | tf_op jit(solution)/shard_map/ppermute | solution.py:38
Sparse Core Ops, SparseCore 0:
  50.1 29.5 all-gather.1

commit v5 on v4

--- a/solution.py
+++ b/solution.py
@@ -67,9 +67,7 @@
 
 
 def middle(source, sign):
-    if source // 16 == (source + 2 * sign) // 16:
-        return source // 4 * 4 + (source % 4 - sign) % 4
-    return {14: 29, 15: 13, 17: 2, 16: 18}[source]
+    return source // 4 * 4 + (source % 4 - sign) % 4
 
 
 def two_pairs(sign):
@@ -116,11 +114,11 @@
 BEHIND_TILES = ((0, 3, 0), (0, 2, 1), (0, 1, 2), (1, 3, 1), (1, 2, 2))
 
 
-def key_value(index, near_k, near_v, edge_k, edge_v, far):
+def key_value(index, near_k, near_v, edge_v, far):
     if index == 0:
         return far[0], far[1]
     rows = block_rows(index - 1)
-    return near_k[rows, :] + edge_k[rows, :], near_v[rows, :] + edge_v[rows, :]
+    return near_k[rows, :], near_v[rows, :] + edge_v[rows, :]
 
 
 def absorb(keys, vals, query, top, total, acc, rows):
@@ -168,7 +166,7 @@
 
 
 def forward_behind_kernel(
-    flags, q_ref, k1_ref, v1_ref, k0_ref, v0_ref, far_ref, acc_in, top_in, total_in,
+    flags, q_ref, k1_ref, v1_ref, v0_ref, far_ref, acc_in, top_in, total_in,
     after, out_ref, turned_ref, log_ref, acc, top, total,
 ):
     acc[...] = acc_in[...]
@@ -180,7 +178,7 @@
 
         @pl.when(flags[qb * WIN + o] == 1)
         def _(rows=rows, line=line, index=index):
-            keys, vals = key_value(index, k1_ref, v1_ref, k0_ref, v0_ref, far_ref)
+            keys, vals = key_value(index, k1_ref, v1_ref, v0_ref, far_ref)
             top[line, :], total[line, :] = absorb(
                 keys, vals, q_ref[rows, :], top[line, :], total[line, :], acc, rows
             )
@@ -204,7 +202,7 @@
 
 
 def backward_behind_kernel(
-    flags, q_ref, k1_ref, v1_ref, k0_ref, v0_ref, far_ref, out_ref, grad_ref, log_ref,
+    flags, q_ref, k1_ref, v1_ref, v0_ref, far_ref, out_ref, grad_ref, log_ref,
     after, near_back, far_back, dq, delta_ref, dk, dv,
 ):
     dk[...] = jnp.zeros_like(dk)
@@ -220,7 +218,7 @@
 
         @pl.when(flags[qb * WIN + o] == 1)
         def _(rows=rows, line=line, index=index):
-            keys, vals = key_value(index, k1_ref, v1_ref, k0_ref, v0_ref, far_ref)
+            keys, vals = key_value(index, k1_ref, v1_ref, v0_ref, far_ref)
             key_part, value_part, query_part = tile_grads(
                 keys, vals, q_ref[rows, :], grad_ref[rows, :],
                 log_ref[0, line, :], delta_ref[0, line, :], False,
@@ -322,30 +320,30 @@
     )
 
 
-def forward_behind(flags, q, near_k, near_v, edge_k, edge_v, far, state, after):
+def forward_behind(flags, q, near_k, near_v, edge_v, far, state, after):
     lines = pltpu.VMEM((2, BLK), f32)
     return call(
         forward_behind_kernel, "forward_behind", (HEADS,),
-        [head(1024)] * 5 + [head_pair(512)]
+        [head(1024)] * 4 + [head_pair(512)]
         + [HEAD_TURNED, HEAD_LINES, HEAD_LINES, ANY],
         [head(1024), HEAD_TURNED, HEAD_LINES],
         [shape((1024, WIDTH), bf16), shape((WIDTH, 1024), bf16), LINES],
         [pltpu.VMEM((HDIM, 1024), f32), lines, lines],
-        (flags, q, near_k, near_v, edge_k, edge_v, far, *state, after),
+        (flags, q, near_k, near_v, edge_v, far, *state, after),
     )
 
 
 def backward_behind(
-    flags, q, near_k, near_v, edge_k, edge_v, far, out, grad, log_sum, after
+    flags, q, near_k, near_v, edge_v, far, out, grad, log_sum, after
 ):
     held = pltpu.VMEM((3 * BLK, HDIM), f32)
     return call(
         backward_behind_kernel, "backward_behind", (HEADS,),
-        [head(1024)] * 5 + [head_pair(512)]
+        [head(1024)] * 4 + [head_pair(512)]
         + [head(1024), head(1024), HEAD_LINES, ANY],
         [head_pair(1024), head_pair(512), HEAD_TURNED, HEAD_LINES],
         [shape((2, 1024, WIDTH), bf16), shape((2, 512, WIDTH), bf16), TURNED, LINES],
-        [held, held], (flags, q, near_k, near_v, edge_k, edge_v, far, out, grad, log_sum, after),
+        [held, held], (flags, q, near_k, near_v, edge_v, far, out, grad, log_sum, after),
     )
 
 
@@ -424,27 +422,31 @@
     )
 
 
-def weight_kernel(place, turned_ref, a_ref, b_ref, after, *outs):
-    y = (place[0] ^ pl.program_id(0)) % 2 * 2 + pl.program_id(1)
-    for part, ref in enumerate((a_ref, b_ref)):
+def weight_kernel(place, turned_ref, g0, g1, g2, g3, *outs):
+    owner = place[0] ^ pl.program_id(0)
+    y = owner % 2 * 2 + pl.program_id(1)
+    for part, ref in enumerate((g0, g1, g2, g3)):
         for slot, out_ref in enumerate(outs):
 
             @pl.when((pl.program_id(0) == part) & ((y - place[1] + 3) % 4 == slot))
-            def _(ref=ref, out_ref=out_ref):
-                out_ref[...] = dot(turned_ref[...], ref[...], NN).astype(bf16)
-
-
-def weight_terms(place, turned, a, b, after):
-    return call(
-        weight_kernel, "weight_gradient", (2, 2),
-        [
-            pl.BlockSpec((512, 1024), lambda i, half, place: (0, 0)),
-            pl.BlockSpec((1024, 512), lambda i, half, place: (0, jnp.where(i == 0, half, 1))),
-            pl.BlockSpec((1024, 512), lambda i, half, place: (0, jnp.where(i == 0, 0, half))),
-            ANY,
-        ],
-        [pl.BlockSpec((512, 512), lambda i, half, place: (0, 0))] * 4,
-        [shape((512, 512), bf16)] * 4, [], (place, turned, a, b, after),
+            def _(ref=ref, out_ref=out_ref, part=part):
+                out_ref[part // 2] = dot(turned_ref[...], ref[...], NN).astype(bf16)
+
+
+def weight_terms(place, turned, cotangents):
+    def piece(part):
+        return pl.BlockSpec(
+            (1024, 512),
+            lambda i, half, place: (
+                0, jnp.where(i == part, half, jnp.where(i < part, 0, 1)),
+            ),
+        )
+
+    return call(
+        weight_kernel, "weight_gradient", (4, 2),
+        [pl.BlockSpec((512, 1024), lambda i, half, place: (0, 0))] + [piece(p) for p in range(4)],
+        [pl.BlockSpec((2, 512, 512), lambda i, half, place: (0, 0, 0))] * 4,
+        [shape((2, 512, 512), bf16)] * 4, [], (place, turned, *cotangents),
     )
 
 
@@ -461,24 +463,20 @@
     return list(groups.values())
 
 
-def pieces_kernel(place, a0, a1, a2, a3, b0, b1, b2, b3, after, *outs):
-    def total(refs):
-        return sum(ref[...].astype(f32) for ref in refs).astype(bf16)
-
+def pieces_kernel(place, a, b, c, d, after, *outs):
     for slot, out_ref in enumerate(outs):
 
         @pl.when(pl.program_id(0) == slot)
         def _(out_ref=out_ref):
-            out_ref[0] = total((a0, a1, a2, a3))
-            out_ref[1] = total((b0, b1, b2, b3))
-
-
-def pieces_by_z(place, a, b, after):
-    piece = pl.BlockSpec((512, 128), lambda i, place: (0, (place[2] + i + 1) % 4))
-    return call(
-        pieces_kernel, "weight_by_z", (4,), [piece] * 8 + [ANY],
+            out_ref[...] = sum(ref[...].astype(f32) for ref in (a, b, c, d)).astype(bf16)
+
+
+def pieces_by_z(place, terms, after):
+    piece = pl.BlockSpec((2, 512, 128), lambda i, place: (0, 0, (place[2] + i + 1) % 4))
+    return call(
+        pieces_kernel, "weight_by_z", (4,), [piece] * 4 + [ANY],
         [pl.BlockSpec((2, 512, 128), lambda i, place: (0, 0, 0))] * 4,
-        [shape((2, 512, 128), bf16)] * 4, [], (place, *a, *b, after),
+        [shape((2, 512, 128), bf16)] * 4, [], (place, *terms, after),
     )
 
 
@@ -504,28 +502,12 @@
     refs[-1][...] = in_ref[...]
 
 
-def far_columns(place, weight):
+def far_columns(place, weight, after):
     return call(
         copy_kernel, "projection_quarter", (1,),
-        [pl.BlockSpec((128, 2048), lambda i, place: (place[1], 1 - place[0] // 2))],
+        [pl.BlockSpec((128, 2048), lambda i, place: (place[1], 1 - place[0] // 2)), ANY],
         pl.BlockSpec((128, 2048), lambda i, place: (0, 0)),
-        shape((128, 2048), bf16), [], (place, weight),
-    )
-
-
-def two_kernel(place, a_ref, b_ref, after, a_out, b_out):
-    a_out[...] = a_ref[...]
-    b_out[...] = b_ref[...]
-
-
-def late_copies(a, b, after):
-    def rows(value):
-        return pl.BlockSpec((512, value.shape[1]), lambda i, place: (i, 0))
-
-    return call(
-        two_kernel, "late_copies", (2,), [rows(a), rows(b), ANY], [rows(a), rows(b)],
-        [shape(a.shape, a.dtype), shape(b.shape, b.dtype)],
-        [], (jnp.zeros(1, jnp.int32), a, b, after),
+        shape((128, 2048), bf16), [], (place, weight, after),
     )
 
 
@@ -583,64 +565,58 @@
     tp = lax.axis_index("tp")
     place = jnp.stack([tp, ctx // 4 % 4, ctx % 4, ctx // 16]).astype(jnp.int32)
 
+    far_grad = to_x_hi(out_grad)
+    near_keys = along_ctx(keys, 1)
     near_pairs = [(s, s + 1) for s in range(31) if s != EDGE]
-    near_keys = lax.ppermute(keys, "ctx", near_pairs + [(EDGE, 0)])
-    crossed = lax.ppermute(values, "ctx", [(EDGE, EDGE + 16)])
+    near_values = lax.ppermute(values, "ctx", near_pairs + [(EDGE, 0)])
     core_grad = to_core(out_grad)
     far_moved = first_hop(pack(place, keys, values), 1)
-    far_weight = to_x_hi(far_columns(place, out_weight))
 
     query_block = ctx * 2 + jnp.arange(2, dtype=jnp.int32)[:, None] + jnp.zeros((1, WIN), jnp.int32)
     key_block = query_block - jnp.arange(WIN, dtype=jnp.int32)[None, :]
     flags = block_rule(spans, pairs, query_block, key_block).astype(jnp.int32).reshape(-1)
     own_state = forward_own(flags, queries, keys, values, keys)
-    held_values, held_grad = late_copies(values, out_grad, own_state[1])
-
-    near_keys, crossed, core_grad, far_moved, far_weight, held_values, held_grad = together(
-        [near_keys, crossed, core_grad, far_moved, far_weight, held_values, held_grad]
-    )
-    near_values = lax.ppermute(held_values, "ctx", near_pairs)
-    edge_keys = lax.ppermute(near_keys, "ctx", [(0, EDGE + 1)])
-    edge_values = lax.ppermute(crossed, "ctx", [(EDGE + 16, EDGE + 1)])
+    terms = grad_terms(place, 0, out_grad, core_grad, out_weight, None, own_state[1])
+
+    [far_moved] = together([far_moved], [terms])
     far = second_hop(far_moved, 1)
-    far_grad = to_x_hi(held_grad)
+    near_keys, near_values, far, far_grad = together(
+        [near_keys, near_values, far, far_grad], [far_moved]
+    )
+
+    far_core_grad = to_core(far_grad)
+    far_weight = to_x_hi(far_columns(place, out_weight, near_keys))
+    edge_values = lax.ppermute(near_values, "ctx", [(0, EDGE + 1)])
+    behind = (flags, queries, near_keys, near_values, edge_values, far)
+    attention, turned, log_sum = forward_behind(*behind, own_state, far)
+    far_weight, far_core_grad = together([far_weight, far_core_grad], [log_sum])
     far_weight = lax.all_gather(
         far_weight, "ctx", axis=0, tiled=True, axis_index_groups=groups_along(1)
     )
-    terms = grad_terms(place, 0, out_grad, core_grad, out_weight, None, near_keys)
-    behind = (flags, queries, near_keys, near_values, edge_keys, edge_values, far)
-    attention, turned, log_sum = forward_behind(*behind, own_state, terms)
 
     far_attention = to_x_hi(attention)
-    own_parts = weight_terms(place, turned, out_grad, core_grad, log_sum)
-    far_grad, far_weight, far_attention = together(
-        [far_grad, far_weight, far_attention], [own_parts[3]]
-    )
-    own_moved = over_y(own_parts)
-    far_core_grad = to_core(far_grad)
-    from_core = to_core(
-        for_core(place, out_weight, far_weight, far_attention, attention, own_parts[3])
-    )
-    far_parts = weight_terms(place, turned, far_grad, far_core_grad, far_weight)
-    attn_grad = grad_terms(place, 2, far_grad, far_core_grad, out_weight, terms, far_parts[3])
-
-    *held, from_core, attn_grad = together([*own_moved, *far_parts, from_core, attn_grad])
-    own_moved, far_parts = held[:3], held[3:]
-    far_moved = over_y(far_parts)
+    weight_parts = weight_terms(place, turned, (out_grad, core_grad, far_grad, far_core_grad))
+    attn_grad = grad_terms(place, 2, far_grad, far_core_grad, out_weight, terms, weight_parts[3])
     near_back, far_back, dq, delta = backward_behind(
-        *behind, attention, attn_grad, log_sum, attn_grad
-    )
+        *behind, attention, attn_grad, log_sum, weight_parts[3]
+    )
+    far_attention, far_weight, *weight_parts = together(
+        [far_attention, far_weight, *weight_parts], [delta]
+    )
+    weight_moved = over_y(weight_parts)
     near_back = along_ctx(near_back, -1)
     back_moved = first_hop(far_back, -1)
     query_grad, own = backward_own(
-        flags, queries, keys, values, attn_grad, log_sum, dq, delta, delta
+        flags, queries, keys, values, attn_grad, log_sum, dq, delta, far_attention
     )
     [back_moved] = together([back_moved], [own])
     far_back = second_hop(back_moved, -1)
-
-    weight_pieces = pieces_by_z(
-        place, [own_parts[3], *own_moved], [far_parts[3], *far_moved], own
-    )
+    from_core = for_core(place, out_weight, far_weight, far_attention, attention, back_moved)
+    *weight_moved, near_back, far_back, from_core = together(
+        [*weight_moved, near_back, far_back, from_core]
+    )
+    weight_pieces = pieces_by_z(place, [weight_parts[3], *weight_moved], near_back)
+    from_core = to_core(from_core)
     weight_terms_z = [weight_pieces[3]] + [to_z(weight_pieces[s], s + 1) for s in (0, 2, 1)]
     mixed = mix(
         place, attention, far_attention, out_weight, far_weight, from_core, weight_pieces[3]

time: 322 us -> 289 us (0.90)
  the two profiles are of different devices: /device:TPU:24 before, /device:TPU:30 now
where the time goes in v5:
time: 289 us; the launch traced here: 288 us
  waiting for transfers between devices  116 us (40%)
  Pallas kernels  104 us (36%)
  starting transfers between devices  47.8 us (17%)
  between operations  14.2 us (5%)
  other arithmetic  3.53 us (1%)
    pallas_call x14, Pallas kernels, call(): pl.pallas_call(kernel, grid_spec=pltpu.PrefetchScalarGridSpec(num_scalar_...  104 us
    ppermute x13, waiting for transfers between devices, move(): return lax.ppermute(value, AXES, pairs)  51.4 us
    all_gather x1, waiting for transfers between devices, per_device(): lax.all_gather(far_weight, 'ctx', axis=0, tiled=True, axis_index_groups=g...  26.2 us
    ppermute x13, starting transfers between devices, move(): return lax.ppermute(value, AXES, pairs)  25.3 us
    ppermute x2, waiting for transfers between devices, second_hop(): return lax.ppermute(value, 'ctx', [(m, t) for _, m, t in two_pairs(sign)])  12.5 us
    ppermute x1, waiting for transfers between devices, per_device(): near_values = lax.ppermute(values, 'ctx', near_pairs + [(EDGE, 0)])  10.9 us
    ppermute x2, waiting for transfers between devices, first_hop(): return lax.ppermute(value, 'ctx', [(s, m) for s, m, _ in two_pairs(sign)])  7.76 us
    ppermute x2, waiting for transfers between devices, along_ctx(): return lax.ppermute(value, 'ctx', pairs)  7.32 us
  transfers between devices with their start and end apart: 22, of which 9 were waited for; matrix products, arithmetic and copies ran while one was open for 1% of the time, Pallas kernels for 35%

profile of v5, /device:TPU:30, one launch (start us, length us, event | category | flops | bytes accessed | tf_op | source)
XLA Modules:
  0.0 288.1 jit_solution(1885820281312157181)
XLA Ops:
  7.2 0.1 collective-permute-start.3
  7.3 1.5 collective-permute-start.5
  8.8 3.8 %collective-permute-start = (bf16[1024,512]{1,0:T(8,128)(2,1)}, bf16[1024,512]{1,0:T(8,128)(2,1)}, u32[]{:S(2)}, u32[]{:S(2)}) collective-permute-start(bf16[1024,512]{1,0:T(8,128)(2,1)} %k_ref.5), channel_id=1, source_target_pairs={{0,4},{4,8},{8,12},{12,16},{16,20},{20,24},{24,28},{28,32},{32,36}... | collective-permute-start | bytes 3145736 | tf_op jit(solution)/shard_map/ppermute | solution.py:66
  12.7 0.6 pad_add_fusion.place
  13.3 3.8 %collective-permute-start.1 = (bf16[1024,512]{1,0:T(8,128)(2,1)}, bf16[1024,512]{1,0:T(8,128)(2,1)}, u32[]{:S(2)}, u32[]{:S(2)}) collective-permute-start(bf16[1024,512]{1,0:T(8,128)(2,1)} %v_ref.5), channel_id=1, source_target_pairs={{0,4},{4,8},{8,12},{12,16},{16,20},{20,24},{24,28},{28,32},{32,36}... | collective-permute-start | bytes 3145736 | tf_op jit(solution)/shard_map/ppermute | solution.py:571
  17.1 2.9 %second_blocks.1 = bf16[2,512,512]{2,1,0:T(8,128)(2,1)} custom-call(s32[4]{0:T(128)} %pad_add_fusion.place, bf16[1024,512]{1,0:T(8,128)(2,1)} %k_ref.5, bf16[1024,512]{1,0:T(8,128)(2,1)} %v_ref.5), custom_call_target="tpu_custom_call" | custom-call | flops 1 | bytes 1 | tf_op jit(solution)/shard_map/second_blocks/pallas_call | solution.py:297
  20.0 1.9 collective-permute-start.2
  21.9 0.8 bitcast_add_fusion
  22.7 0.7 slice_bitcast_fusion
  23.3 0.1 iota_subtract_fusion
  23.4 0.2 and_reduce_fusion.1
  23.6 0.8 fusion
  24.4 0.2 and_reduce_fusion
  24.6 0.7 reshape.60.flags
  25.2 7.4 %forward_own.1 = (f32[512,1024]{1,0:T(8,128)}, f32[4,2,512]{2,1,0:T(2,128)}, f32[4,2,512]{2,1,0:T(2,128)}) custom-call(s32[8]{0:T(128)} %reshape.60.flags, bf16[1024,512]{1,0:T(8,128)(2,1)} %q_ref.7, bf16[1024,512]{1,0:T(8,128)(2,1)} %k_ref.5, bf16[1024,512]{1,0:T(8,128)(2,1)} %v_ref.5, bf16[1024,512]{1,0:T(8,128)(2,1)} %k_ref.5), custom_call_target="tpu_custom_call" | custom-call | flops 1 | bytes 1 | tf_op jit(solution)/shard_map/forward_own/pallas_call | solution.py:297
  32.7 6.4 %projection_backward.2.refs_1_.rest_0_ = f32[1024,512]{1,0:T(8,128)} custom-call(s32[4]{0:T(128)} %pad_add_fusion.place, bf16[1024,1024]{1,0:T(8,128)(2,1)} %g0.1, bf16[1024,1024]{1,0:T(8,128)(2,1)} %collective-permute-done.3.b_ref.g1, bf16[512,4096]{1,0:T(8,128)(2,1)} %w_own.1, bf16[512,4096]{1,0:T(8,128)(2,1)} %w_own.1, ...), custom_call_target="tpu_custom_call" | custom-call | flops 1 | bytes 1 | tf_op jit(solution)/shard_map/projection_backward/pallas_call | solution.py:297
  39.1 7.8 %collective-permute-done.2.refs_0_ = bf16[2,512,512]{2,1,0:T(8,128)(2,1)} collective-permute-done((bf16[2,512,512]{2,1,0:T(8,128)(2,1)}, bf16[2,512,512]{2,1,0:T(8,128)(2,1)}, u32[]{:S(2)}, u32[]{:S(2)}) %collective-permute-start.2) | collective-permute-done | bytes 1048608 | tf_op jit(solution)/shard_map/ppermute | solution.py:79
  46.8 3.4 %collective-permute-start.4 = (bf16[2,512,512]{2,1,0:T(8,128)(2,1)}, bf16[2,512,512]{2,1,0:T(8,128)(2,1)}, u32[]{:S(2)}, u32[]{:S(2)}) collective-permute-start(bf16[2,512,512]{2,1,0:T(8,128)(2,1)} %order.6.refs_4_), channel_id=1, source_target_pairs={{12,8},{0,12},{4,16},{8,20},{28,24},{16,28},{20,32},{24,36},{44,40... | collective-permute-start | bytes 3145736 | tf_op jit(solution)/shard_map/ppermute | solution.py:83
  50.3 10.9 %collective-permute-done.1.refs_1_ = bf16[1024,512]{1,0:T(8,128)(2,1)} collective-permute-done((bf16[1024,512]{1,0:T(8,128)(2,1)}, bf16[1024,512]{1,0:T(8,128)(2,1)}, u32[]{:S(2)}, u32[]{:S(2)}) %collective-permute-start.1) | collective-permute-done | bytes 1048608 | tf_op jit(solution)/shard_map/ppermute | solution.py:571
  61.2 12.5 %collective-permute-done.4.refs_2_ = bf16[2,512,512]{2,1,0:T(8,128)(2,1)} collective-permute-done((bf16[2,512,512]{2,1,0:T(8,128)(2,1)}, bf16[2,512,512]{2,1,0:T(8,128)(2,1)}, u32[]{:S(2)}, u32[]{:S(2)}) %collective-permute-start.4) | collective-permute-done | bytes 1048608 | tf_op jit(solution)/shard_map/ppermute | solution.py:83
  73.7 1.7 collective-permute-start.6
  75.3 2.5 projection_quarter.1
  77.9 2.1 collective-permute-start.8
  80.0 12.2 %forward_behind.1 = (bf16[1024,512]{1,0:T(8,128)(2,1)}, bf16[512,1024]{1,0:T(8,128)(2,1)}, f32[4,2,512]{2,1,0:T(2,128)}) custom-call(s32[8]{0:T(128)} %reshape.60.flags, bf16[1024,512]{1,0:T(8,128)(2,1)} %q_ref.7, bf16[1024,512]{1,0:T(8,128)(2,1)} %get-tuple-element.48.k1_ref.refs_0_, bf16[1024,512]{1,0:T(8,128)(2,1)} %get-tuple-element.49.v1_ref, ...), custom_call_target="tpu_custom_call" | custom-call | flops 1 | bytes 1 | tf_op jit(solution)/shard_map/forward_behind/pallas_call | solution.py:297
  92.2 1.8 collective-permute-done.8.refs_0_
  94.1 2.4 collective-permute-start.7
  96.5 13.3 %weight_gradient.1 = (bf16[2,512,512]{2,1,0:T(8,128)(2,1)}, bf16[2,512,512]{2,1,0:T(8,128)(2,1)}, bf16[2,512,512]{2,1,0:T(8,128)(2,1)}, bf16[2,512,512]{2,1,0:T(8,128)(2,1)}) custom-call(s32[4]{0:T(128)} %pad_add_fusion.place, bf16[512,1024]{1,0:T(8,128)(2,1)} %get-tuple-element.57.turned_ref, bf16[1024,1024]{1,0:T(8,128)(2,1)} %g0.1, ...), custom_call_target="tpu_custom_call" | custom-call | flops 1 | bytes 1 | tf_op jit(solution)/shard_map/weight_gradient/pallas_call | solution.py:297
  109.7 6.9 %projection_backward.3.grad_ref = bf16[1024,512]{1,0:T(8,128)(2,1)} custom-call(s32[4]{0:T(128)} %pad_add_fusion.place, bf16[1024,1024]{1,0:T(8,128)(2,1)} %get-tuple-element.54.g2.a_ref, bf16[1024,1024]{1,0:T(8,128)(2,1)} %get-tuple-element.58.g3.b_ref, bf16[512,4096]{1,0:T(8,128)(2,1)} %w_own.1, bf16[512,4096]{1,0:T(8,128)(2,1)} %w_own.1, ...), custom_call_target="tpu_custom_call" | custom-call | flops 1 | bytes 1 | tf_op jit(solution)/shard_map/projection_backward/pallas_call | solution.py:297
  116.6 14.5 %backward_behind.1 = (bf16[2,1024,512]{2,1,0:T(8,128)(2,1)}, bf16[2,512,512]{2,1,0:T(8,128)(2,1)}, f32[512,1024]{1,0:T(8,128)}, f32[4,2,512]{2,1,0:T(2,128)}) custom-call(s32[8]{0:T(128)} %reshape.60.flags, bf16[1024,512]{1,0:T(8,128)(2,1)} %q_ref.7, bf16[1024,512]{1,0:T(8,128)(2,1)} %get-tuple-element.48.k1_ref.refs_0_, ...), custom_call_target="tpu_custom_call" | custom-call | flops 1 | bytes 1 | tf_op jit(solution)/shard_map/backward_behind/pallas_call | solution.py:297
  131.1 2.5 collective-permute-start.13
  133.7 3.3 %collective-permute-start.14 = (bf16[2,512,512]{2,1,0:T(8,128)(2,1)}, bf16[2,512,512]{2,1,0:T(8,128)(2,1)}, u32[]{:S(2)}, u32[]{:S(2)}) collective-permute-start(bf16[2,512,512]{2,1,0:T(8,128)(2,1)} %get-tuple-element.68), channel_id=1, source_target_pairs={{8,12},{12,0},{16,20},{20,24},{24,28},{28,16},{32,36},{36,40},{40,... | collective-permute-start | bytes 3145736 | tf_op jit(solution)/shard_map/ppermute | solution.py:79
  137.0 26.2 %all-gather.2.cloned.1.call-done.refs_1_ = bf16[512,2048]{1,0:T(8,128)(2,1)} async-done(((bf16[128,2048]{1,0:T(8,128)(2,1)}), bf16[512,2048]{1,0:T(8,128)(2,1)}) %all-gather.2.cloned.1.call-update) | async-done | bytes 2097168 | tf_op jit(solution)/shard_map/all_gather | solution.py:593
  163.2 2.7 collective-permute-start.11
  166.0 3.0 %collective-permute-start.12 = (bf16[2,512,512]{2,1,0:T(8,128)(2,1)}, bf16[2,512,512]{2,1,0:T(8,128)(2,1)}, u32[]{:S(2)}, u32[]{:S(2)}) collective-permute-start(bf16[2,512,512]{2,1,0:T(8,128)(2,1)} %get-tuple-element.66), channel_id=1, source_target_pairs={{0,32},{1,33},{2,34},{3,35},{4,36},{5,37},{6,38},{7,39},{8,40},{9,... | collective-permute-start | bytes 3145736 | tf_op jit(solution)/shard_map/ppermute | solution.py:38
  169.0 10.6 %backward_own.1 = (bf16[1024,512]{1,0:T(8,128)(2,1)}, f32[2,1024,512]{2,1,0:T(8,128)}) custom-call(s32[8]{0:T(128)} %reshape.60.flags, bf16[1024,512]{1,0:T(8,128)(2,1)} %q_ref.7, bf16[1024,512]{1,0:T(8,128)(2,1)} %k_ref.5, bf16[1024,512]{1,0:T(8,128)(2,1)} %v_ref.5, bf16[1024,512]{1,0:T(8,128)(2,1)} %projection_backward.3.grad_ref, ...), custom_call_target="tpu_custom_call" | custom-call | flops 1 | bytes 1 | tf_op jit(solution)/shard_map/backward_own/pallas_call | solution.py:297
  179.5 1.9 collective-permute-start.15
  181.5 5.2 %for_core.1.refs_5_ = bf16[4,512,1024]{2,1,0:T(8,128)(2,1)} custom-call(s32[4]{0:T(128)} %pad_add_fusion.place, bf16[512,4096]{1,0:T(8,128)(2,1)} %w_own.1, bf16[512,2048]{1,0:T(8,128)(2,1)} %get-tuple-element.72.far_ref.w_far, bf16[1024,512]{1,0:T(8,128)(2,1)} %get-tuple-element.70.after.far_rows.far, ...), custom_call_target="tpu_custom_call" | custom-call | flops 1 | bytes 1 | tf_op jit(solution)/shard_map/for_core/pallas_call | solution.py:297
  186.6 7.3 %collective-permute-done.13.refs_3_ = bf16[2,1024,512]{2,1,0:T(8,128)(2,1)} collective-permute-done((bf16[2,1024,512]{2,1,0:T(8,128)(2,1)}, bf16[2,1024,512]{2,1,0:T(8,128)(2,1)}, u32[]{:S(2)}, u32[]{:S(2)}) %collective-permute-start.13) | collective-permute-done | bytes 2097184 | tf_op jit(solution)/shard_map/ppermute | solution.py:66
  194.0 22.5 %collective-permute-done.11.refs_1_ = bf16[2,512,512]{2,1,0:T(8,128)(2,1)} collective-permute-done((bf16[2,512,512]{2,1,0:T(8,128)(2,1)}, bf16[2,512,512]{2,1,0:T(8,128)(2,1)}, u32[]{:S(2)}, u32[]{:S(2)}) %collective-permute-start.11) | collective-permute-done | bytes 1048608 | tf_op jit(solution)/shard_map/ppermute | solution.py:38
  216.4 23.9 %collective-permute-done.12.refs_2_ = bf16[2,512,512]{2,1,0:T(8,128)(2,1)} collective-permute-done((bf16[2,512,512]{2,1,0:T(8,128)(2,1)}, bf16[2,512,512]{2,1,0:T(8,128)(2,1)}, u32[]{:S(2)}, u32[]{:S(2)}) %collective-permute-start.12) | collective-permute-done | bytes 1048608 | tf_op jit(solution)/shard_map/ppermute | solution.py:38
  240.4 4.8 %weight_by_z.1 = (bf16[2,512,128]{2,1,0:T(8,128)(2,1)}, bf16[2,512,128]{2,1,0:T(8,128)(2,1)}, bf16[2,512,128]{2,1,0:T(8,128)(2,1)}, bf16[2,512,128]{2,1,0:T(8,128)(2,1)}) custom-call(s32[4]{0:T(128)} %pad_add_fusion.place, bf16[2,512,512]{2,1,0:T(8,128)(2,1)} %get-tuple-element.74.a, bf16[2,512,512]{2,1,0:T(8,128)(2,1)} %get-tuple-element.75.b, ...), custom_call_target="tpu_custom_call" | custom-call | flops 1 | bytes 1 | tf_op jit(solution)/shard_map/weight_by_z/pallas_call | solution.py:297
  245.2 3.2 %collective-permute-start.18 = (bf16[2,512,128]{2,1,0:T(8,128)(2,1)}, bf16[2,512,128]{2,1,0:T(8,128)(2,1)}, u32[]{:S(2)}, u32[]{:S(2)}) collective-permute-start(bf16[2,512,128]{2,1,0:T(8,128)(2,1)} %get-tuple-element.83), channel_id=1, source_target_pairs={{0,12},{1,13},{2,14},{3,15},{4,0},{5,1},{6,2},{7,3},{8,4},{9,5},{1... | collective-permute-start | bytes 786440 | tf_op jit(solution)/shard_map/ppermute | solution.py:38
  248.4 9.4 %projection.1.after = bf16[1024,1024]{1,0:T(8,128)(2,1)} custom-call(s32[4]{0:T(128)} %pad_add_fusion.place, bf16[1024,512]{1,0:T(8,128)(2,1)} %get-tuple-element.53.out_ref.own_rows.own, bf16[4,512,1024]{2,1,0:T(8,128)(2,1)} %collective-permute-done.16.core.far_core.w_core, bf16[1024,512]{1,0:T(8,128)(2,1)} %get-tuple-element.70.after.far_rows.far, ...), custom_call_target="tpu_custom_call" | custom-call | flops 1 | bytes 1 | tf_op jit(solution)/shard_map/projection/pallas_call | solution.py:297
  257.8 3.2 %collective-permute-done.17.b_ref = bf16[2,512,128]{2,1,0:T(8,128)(2,1)} collective-permute-done((bf16[2,512,128]{2,1,0:T(8,128)(2,1)}, bf16[2,512,128]{2,1,0:T(8,128)(2,1)}, u32[]{:S(2)}, u32[]{:S(2)}) %collective-permute-start.17) | collective-permute-done | bytes 262176 | tf_op jit(solution)/shard_map/ppermute | solution.py:38
  261.0 2.6 weight_z_sum.1
  263.7 10.3 %collective-permute-start.20 = (bf16[512,128]{1,0:T(8,128)(2,1)}, bf16[512,128]{1,0:T(8,128)(2,1)}, u32[]{:S(2)}, u32[]{:S(2)}) collective-permute-start(bf16[512,128]{1,0:T(8,128)(2,1)} %get-tuple-element.88), channel_id=1, source_target_pairs={{0,64},{1,65},{2,66},{3,67},{4,68},{5,69},{6,70},{7,71},{8,72},{9,... | collective-permute-start | bytes 393224 | tf_op jit(solution)/shard_map/ppermute | solution.py:38
  274.0 5.6 %key_value_sum.1 = (bf16[1024,512]{1,0:T(8,128)(2,1)}, bf16[1024,512]{1,0:T(8,128)(2,1)}) custom-call(s32[4]{0:T(128)} %pad_add_fusion.place, f32[2,1024,512]{2,1,0:T(8,128)} %get-tuple-element.71.refs_1_.own_ref, bf16[2,1024,512]{2,1,0:T(8,128)(2,1)} %get-tuple-element.78.after.near_ref, bf16[2,512,512]{2,1,0:T(8,128)(2,1)} %get-tuple-element.81.far_ref, ...), custom_call_target="tpu_custom_call" | custom-call | flops 1 | bytes 1 | tf_op jit(solution)/shard_map/key_value_sum/pallas_call | solution.py:297
  279.6 1.7 convert_add_fusion
  (28 shorter events, 0.1 us)
Async XLA Ops:
  7.2 156.1 %all-gather.2.cloned.1.call-start = ((), (), s32[]{:S(2)}) async-start(), calls=%async_computation | async-start | bytes 2621440 | tf_op jit(solution)/shard_map/all_gather | solution.py:593
  7.2 25.4 %collective-permute-start.3 = (bf16[1024,1024]{1,0:T(8,128)(2,1)}, bf16[1024,1024]{1,0:T(8,128)(2,1)}, u32[]{:S(2)}, u32[]{:S(2)}) collective-permute-start(bf16[1024,1024]{1,0:T(8,128)(2,1)} %g0.1), channel_id=1, source_target_pairs={{0,1},{1,0},{2,3},{3,2},{4,5},{5,4},{6,7},{7,6},{8,9},{9,8},{10,11... | collective-permute-start | bytes 6291464 | tf_op jit(solution)/shard_map/ppermute | solution.py:38
  7.3 53.9 %collective-permute-start.5 = (bf16[1024,1024]{1,0:T(8,128)(2,1)}, bf16[1024,1024]{1,0:T(8,128)(2,1)}, u32[]{:S(2)}, u32[]{:S(2)}) collective-permute-start(bf16[1024,1024]{1,0:T(8,128)(2,1)} %g0.1), channel_id=1, source_target_pairs={{0,2},{1,3},{2,0},{3,1},{4,6},{5,7},{6,4},{7,5},{8,10},{9,11},{10,... | collective-permute-start | bytes 6291464 | tf_op jit(solution)/shard_map/ppermute | solution.py:38
  8.8 41.5 %collective-permute-start = (bf16[1024,512]{1,0:T(8,128)(2,1)}, bf16[1024,512]{1,0:T(8,128)(2,1)}, u32[]{:S(2)}, u32[]{:S(2)}) collective-permute-start(bf16[1024,512]{1,0:T(8,128)(2,1)} %k_ref.5), channel_id=1, source_target_pairs={{0,4},{4,8},{8,12},{12,16},{16,20},{20,24},{24,28},{28,32},{32,36}... | collective-permute-start | bytes 3145736 | tf_op jit(solution)/shard_map/ppermute | solution.py:66
  13.3 47.9 %collective-permute-start.1 = (bf16[1024,512]{1,0:T(8,128)(2,1)}, bf16[1024,512]{1,0:T(8,128)(2,1)}, u32[]{:S(2)}, u32[]{:S(2)}) collective-permute-start(bf16[1024,512]{1,0:T(8,128)(2,1)} %v_ref.5), channel_id=1, source_target_pairs={{0,4},{4,8},{8,12},{12,16},{16,20},{20,24},{24,28},{28,32},{32,36}... | collective-permute-start | bytes 3145736 | tf_op jit(solution)/shard_map/ppermute | solution.py:571
  20.0 26.9 %collective-permute-start.2 = (bf16[2,512,512]{2,1,0:T(8,128)(2,1)}, bf16[2,512,512]{2,1,0:T(8,128)(2,1)}, u32[]{:S(2)}, u32[]{:S(2)}) collective-permute-start(bf16[2,512,512]{2,1,0:T(8,128)(2,1)} %second_blocks.1), channel_id=1, source_target_pairs={{0,12},{4,0},{8,4},{12,8},{16,28},{20,16},{24,20},{28,24},{32,44},... | collective-permute-start | bytes 3145736 | tf_op jit(solution)/shard_map/ppermute | solution.py:79
  46.8 26.8 %collective-permute-start.4 = (bf16[2,512,512]{2,1,0:T(8,128)(2,1)}, bf16[2,512,512]{2,1,0:T(8,128)(2,1)}, u32[]{:S(2)}, u32[]{:S(2)}) collective-permute-start(bf16[2,512,512]{2,1,0:T(8,128)(2,1)} %order.6.refs_4_), channel_id=1, source_target_pairs={{12,8},{0,12},{4,16},{8,20},{28,24},{16,28},{20,32},{24,36},{44,40... | collective-permute-start | bytes 3145736 | tf_op jit(solution)/shard_map/ppermute | solution.py:83
  73.7 20.4 %collective-permute-start.9 = (bf16[1024,1024]{1,0:T(8,128)(2,1)}, bf16[1024,1024]{1,0:T(8,128)(2,1)}, u32[]{:S(2)}, u32[]{:S(2)}) collective-permute-start(bf16[1024,1024]{1,0:T(8,128)(2,1)} %get-tuple-element.54.g2.a_ref), channel_id=1, source_target_pairs={{0,1},{1,0},{2,3},{3,2},{4,5},{5,4},{6,7},{7,6},{8,9},{9,8},{10,11... | collective-permute-start | bytes 6291464 | tf_op jit(solution)/shard_map/ppermute | solution.py:38
  73.7 6.3 %collective-permute-start.6 = (bf16[1024,512]{1,0:T(8,128)(2,1)}, bf16[1024,512]{1,0:T(8,128)(2,1)}, u32[]{:S(2)}, u32[]{:S(2)}) collective-permute-start(bf16[1024,512]{1,0:T(8,128)(2,1)} %get-tuple-element.49.v1_ref), channel_id=1, source_target_pairs={{0,64},{1,65},{2,66},{3,67}} | collective-permute-start | bytes 3145736 | tf_op jit(solution)/shard_map/ppermute | solution.py:589
  77.9 16.2 %collective-permute-start.8 = (bf16[128,2048]{1,0:T(8,128)(2,1)}, bf16[128,2048]{1,0:T(8,128)(2,1)}, u32[]{:S(2)}, u32[]{:S(2)}) collective-permute-start(bf16[128,2048]{1,0:T(8,128)(2,1)} %projection_quarter.1), channel_id=1, source_target_pairs={{0,2},{1,3},{2,0},{3,1},{4,6},{5,7},{6,4},{7,5},{8,10},{9,11},{10,... | collective-permute-start | bytes 1572872 | tf_op jit(solution)/shard_map/ppermute | solution.py:38
  94.1 42.9 %collective-permute-start.7 = (bf16[1024,512]{1,0:T(8,128)(2,1)}, bf16[1024,512]{1,0:T(8,128)(2,1)}, u32[]{:S(2)}, u32[]{:S(2)}) collective-permute-start(bf16[1024,512]{1,0:T(8,128)(2,1)} %get-tuple-element.53.out_ref.own_rows.own), channel_id=1, source_target_pairs={{0,2},{1,3},{2,0},{3,1},{4,6},{5,7},{6,4},{7,5},{8,10},{9,11},{10,... | collective-permute-start | bytes 3145736 | tf_op jit(solution)/shard_map/ppermute | solution.py:38
  131.1 62.8 %collective-permute-start.13 = (bf16[2,1024,512]{2,1,0:T(8,128)(2,1)}, bf16[2,1024,512]{2,1,0:T(8,128)(2,1)}, u32[]{:S(2)}, u32[]{:S(2)}) collective-permute-start(bf16[2,1024,512]{2,1,0:T(8,128)(2,1)} %get-tuple-element.67), channel_id=1, source_target_pairs={{4,0},{8,4},{12,8},{16,12},{20,16},{24,20},{28,24},{32,28},{36,32}... | collective-permute-start | bytes 6291464 | tf_op jit(solution)/shard_map/ppermute | solution.py:66
  133.7 45.9 %collective-permute-start.14 = (bf16[2,512,512]{2,1,0:T(8,128)(2,1)}, bf16[2,512,512]{2,1,0:T(8,128)(2,1)}, u32[]{:S(2)}, u32[]{:S(2)}) collective-permute-start(bf16[2,512,512]{2,1,0:T(8,128)(2,1)} %get-tuple-element.68), channel_id=1, source_target_pairs={{8,12},{12,0},{16,20},{20,24},{24,28},{28,16},{32,36},{36,40},{40,... | collective-permute-start | bytes 3145736 | tf_op jit(solution)/shard_map/ppermute | solution.py:79
  163.2 30.7 %collective-permute-start.10 = (bf16[2,512,512]{2,1,0:T(8,128)(2,1)}, bf16[2,512,512]{2,1,0:T(8,128)(2,1)}, u32[]{:S(2)}, u32[]{:S(2)}) collective-permute-start(bf16[2,512,512]{2,1,0:T(8,128)(2,1)} %get-tuple-element.64), channel_id=1, source_target_pairs={{0,16},{1,17},{2,18},{3,19},{4,20},{5,21},{6,22},{7,23},{8,24},{9,... | collective-permute-start | bytes 3145736 | tf_op jit(solution)/shard_map/ppermute | solution.py:38
  163.2 53.2 %collective-permute-start.11 = (bf16[2,512,512]{2,1,0:T(8,128)(2,1)}, bf16[2,512,512]{2,1,0:T(8,128)(2,1)}, u32[]{:S(2)}, u32[]{:S(2)}) collective-permute-start(bf16[2,512,512]{2,1,0:T(8,128)(2,1)} %get-tuple-element.65), channel_id=1, source_target_pairs={{0,48},{1,49},{2,50},{3,51},{4,52},{5,53},{6,54},{7,55},{8,56},{9,... | collective-permute-start | bytes 3145736 | tf_op jit(solution)/shard_map/ppermute | solution.py:38
  166.0 74.4 %collective-permute-start.12 = (bf16[2,512,512]{2,1,0:T(8,128)(2,1)}, bf16[2,512,512]{2,1,0:T(8,128)(2,1)}, u32[]{:S(2)}, u32[]{:S(2)}) collective-permute-start(bf16[2,512,512]{2,1,0:T(8,128)(2,1)} %get-tuple-element.66), channel_id=1, source_target_pairs={{0,32},{1,33},{2,34},{3,35},{4,36},{5,37},{6,38},{7,39},{8,40},{9,... | collective-permute-start | bytes 3145736 | tf_op jit(solution)/shard_map/ppermute | solution.py:38
  179.5 60.8 %collective-permute-start.15 = (bf16[2,512,512]{2,1,0:T(8,128)(2,1)}, bf16[2,512,512]{2,1,0:T(8,128)(2,1)}, u32[]{:S(2)}, u32[]{:S(2)}) collective-permute-start(bf16[2,512,512]{2,1,0:T(8,128)(2,1)} %order.10.after), channel_id=1, source_target_pairs={{12,0},{0,4},{20,8},{24,12},{28,16},{16,20},{36,24},{40,28},{44,32... | collective-permute-start | bytes 3145736 | tf_op jit(solution)/shard_map/ppermute | solution.py:83
  240.4 8.1 %collective-permute-start.16 = (bf16[4,512,1024]{2,1,0:T(8,128)(2,1)}, bf16[4,512,1024]{2,1,0:T(8,128)(2,1)}, u32[]{:S(2)}, u32[]{:S(2)}) collective-permute-start(bf16[4,512,1024]{2,1,0:T(8,128)(2,1)} %get-tuple-element.73), channel_id=1, source_target_pairs={{0,1},{1,0},{2,3},{3,2},{4,5},{5,4},{6,7},{7,6},{8,9},{9,8},{10,11... | collective-permute-start | bytes 12582920 | tf_op jit(solution)/shard_map/ppermute | solution.py:38
  245.2 15.9 %collective-permute-start.17 = (bf16[2,512,128]{2,1,0:T(8,128)(2,1)}, bf16[2,512,128]{2,1,0:T(8,128)(2,1)}, u32[]{:S(2)}, u32[]{:S(2)}) collective-permute-start(bf16[2,512,128]{2,1,0:T(8,128)(2,1)} %get-tuple-element.82), channel_id=1, source_target_pairs={{0,4},{1,5},{2,6},{3,7},{4,8},{5,9},{6,10},{7,11},{8,12},{9,13},{1... | collective-permute-start | bytes 786440 | tf_op jit(solution)/shard_map/ppermute | solution.py:38
  245.2 15.9 %collective-permute-start.18 = (bf16[2,512,128]{2,1,0:T(8,128)(2,1)}, bf16[2,512,128]{2,1,0:T(8,128)(2,1)}, u32[]{:S(2)}, u32[]{:S(2)}) collective-permute-start(bf16[2,512,128]{2,1,0:T(8,128)(2,1)} %get-tuple-element.83), channel_id=1, source_target_pairs={{0,12},{1,13},{2,14},{3,15},{4,0},{5,1},{6,2},{7,3},{8,4},{9,5},{1... | collective-permute-start | bytes 786440 | tf_op jit(solution)/shard_map/ppermute | solution.py:38
  248.4 12.6 %collective-permute-start.19 = (bf16[2,512,128]{2,1,0:T(8,128)(2,1)}, bf16[2,512,128]{2,1,0:T(8,128)(2,1)}, u32[]{:S(2)}, u32[]{:S(2)}) collective-permute-start(bf16[2,512,128]{2,1,0:T(8,128)(2,1)} %get-tuple-element.84), channel_id=1, source_target_pairs={{0,8},{1,9},{2,10},{3,11},{4,12},{5,13},{6,14},{7,15},{8,0},{9,1},... | collective-permute-start | bytes 786440 | tf_op jit(solution)/shard_map/ppermute | solution.py:38
  263.7 15.9 %collective-permute-start.20 = (bf16[512,128]{1,0:T(8,128)(2,1)}, bf16[512,128]{1,0:T(8,128)(2,1)}, u32[]{:S(2)}, u32[]{:S(2)}) collective-permute-start(bf16[512,128]{1,0:T(8,128)(2,1)} %get-tuple-element.88), channel_id=1, source_target_pairs={{0,64},{1,65},{2,66},{3,67},{4,68},{5,69},{6,70},{7,71},{8,72},{9,... | collective-permute-start | bytes 393224 | tf_op jit(solution)/shard_map/ppermute | solution.py:38
Sparse Core Ops, SparseCore 0:
  94.2 69.0 all-gather.1

commit v6 on v5

--- a/solution.py
+++ b/solution.py
@@ -454,15 +454,6 @@
     return [to_y(parts[s], s + 1) for s in (0, 2, 1)]
 
 
-def groups_along(axis):
-    groups = {}
-    for ctx in range(32):
-        spot = [ctx // 16, ctx // 4 % 4, ctx % 4]
-        spot[axis] = None
-        groups.setdefault(tuple(spot), []).append(ctx)
-    return list(groups.values())
-
-
 def pieces_kernel(place, a, b, c, d, after, *outs):
     for slot, out_ref in enumerate(outs):
 
@@ -504,10 +495,10 @@
 
 def far_columns(place, weight, after):
     return call(
-        copy_kernel, "projection_quarter", (1,),
-        [pl.BlockSpec((128, 2048), lambda i, place: (place[1], 1 - place[0] // 2)), ANY],
-        pl.BlockSpec((128, 2048), lambda i, place: (0, 0)),
-        shape((128, 2048), bf16), [], (place, weight, after),
+        copy_kernel, "projection_far", (2,),
+        [pl.BlockSpec((256, 2048), lambda i, place: (i, 1 - place[0] // 2)), ANY],
+        pl.BlockSpec((256, 2048), lambda i, place: (i, 0)),
+        shape((512, 2048), bf16), [], (place, weight, after),
     )
 
 
@@ -580,48 +571,43 @@
 
     [far_moved] = together([far_moved], [terms])
     far = second_hop(far_moved, 1)
-    near_keys, near_values, far, far_grad = together(
-        [near_keys, near_values, far, far_grad], [far_moved]
+    [near_values] = together([near_values], [far_moved])
+    edge_values = lax.ppermute(near_values, "ctx", [(0, EDGE + 1)])
+    near_keys, far, far_grad, edge_values = together(
+        [near_keys, far, far_grad, edge_values], [far_moved]
     )
 
     far_core_grad = to_core(far_grad)
     far_weight = to_x_hi(far_columns(place, out_weight, near_keys))
-    edge_values = lax.ppermute(near_values, "ctx", [(0, EDGE + 1)])
     behind = (flags, queries, near_keys, near_values, edge_values, far)
     attention, turned, log_sum = forward_behind(*behind, own_state, far)
-    far_weight, far_core_grad = together([far_weight, far_core_grad], [log_sum])
-    far_weight = lax.all_gather(
-        far_weight, "ctx", axis=0, tiled=True, axis_index_groups=groups_along(1)
-    )
-
+    [far_core_grad] = together([far_core_grad], [log_sum])
     far_attention = to_x_hi(attention)
     weight_parts = weight_terms(place, turned, (out_grad, core_grad, far_grad, far_core_grad))
+    weight_moved = over_y(weight_parts)
     attn_grad = grad_terms(place, 2, far_grad, far_core_grad, out_weight, terms, weight_parts[3])
     near_back, far_back, dq, delta = backward_behind(
         *behind, attention, attn_grad, log_sum, weight_parts[3]
     )
-    far_attention, far_weight, *weight_parts = together(
-        [far_attention, far_weight, *weight_parts], [delta]
-    )
-    weight_moved = over_y(weight_parts)
+    query_grad, own = backward_own(
+        flags, queries, keys, values, attn_grad, log_sum, dq, delta, delta
+    )
+
+    *weight_moved, near_back, far_back, far_attention, far_weight = together(
+        [*weight_moved, near_back, far_back, far_attention, far_weight], [own]
+    )
     near_back = along_ctx(near_back, -1)
     back_moved = first_hop(far_back, -1)
-    query_grad, own = backward_own(
-        flags, queries, keys, values, attn_grad, log_sum, dq, delta, far_attention
-    )
-    [back_moved] = together([back_moved], [own])
+    from_core = to_core(
+        for_core(place, out_weight, far_weight, far_attention, attention, weight_moved[0])
+    )
+    weight_pieces = pieces_by_z(place, [weight_parts[3], *weight_moved], weight_moved[0])
+    back_moved, from_core = together([back_moved, from_core], [weight_pieces[3]])
     far_back = second_hop(back_moved, -1)
-    from_core = for_core(place, out_weight, far_weight, far_attention, attention, back_moved)
-    *weight_moved, near_back, far_back, from_core = together(
-        [*weight_moved, near_back, far_back, from_core]
-    )
-    weight_pieces = pieces_by_z(place, [weight_parts[3], *weight_moved], near_back)
-    from_core = to_core(from_core)
-    weight_terms_z = [weight_pieces[3]] + [to_z(weight_pieces[s], s + 1) for s in (0, 2, 1)]
-    mixed = mix(
-        place, attention, far_attention, out_weight, far_weight, from_core, weight_pieces[3]
-    )
-    kept, sent = weight_z_sum(place, weight_terms_z, mixed)
+    weight_moved = [to_z(weight_pieces[s], s + 1) for s in (0, 2, 1)]
+    mixed = mix(place, attention, far_attention, out_weight, far_weight, from_core, back_moved)
+    near_back, far_back, *weight_moved = together([near_back, far_back, *weight_moved], [mixed])
+    kept, sent = weight_z_sum(place, [weight_pieces[3], *weight_moved], near_back)
     weight_grad = kept + to_x_lo(sent).astype(f32)
     key_grad, value_grad = finish(place, own, near_back, far_back, kept)
     return (mixed, query_grad, key_grad, value_grad, weight_grad)

time: 289 us -> 254 us (0.88)
  the two profiles are of different devices: /device:TPU:30 before, /device:TPU:0 now
where the time goes in v6:
time: 254 us; the launch traced here: 251 us
  waiting for transfers between devices  97.7 us (38%)
  Pallas kernels  97 us (38%)
  starting transfers between devices  50.3 us (20%)
  other arithmetic  3.6 us (1%)
    pallas_call x14, Pallas kernels, call(): pl.pallas_call(kernel, grid_spec=pltpu.PrefetchScalarGridSpec(num_scalar_...  97 us
    ppermute x13, waiting for transfers between devices, move(): return lax.ppermute(value, AXES, pairs)  40.8 us
    ppermute x13, starting transfers between devices, move(): return lax.ppermute(value, AXES, pairs)  24.8 us
    ppermute x2, waiting for transfers between devices, first_hop(): return lax.ppermute(value, 'ctx', [(s, m) for s, m, _ in two_pairs(sign)])  24.5 us
    ppermute x1, waiting for transfers between devices, per_device(): edge_values = lax.ppermute(near_values, 'ctx', [(0, EDGE + 1)])  15.6 us
    ppermute x1, waiting for transfers between devices, per_device(): near_values = lax.ppermute(values, 'ctx', near_pairs + [(EDGE, 0)])  11.2 us
    ppermute x2, starting transfers between devices, second_hop(): return lax.ppermute(value, 'ctx', [(m, t) for _, m, t in two_pairs(sign)])  7.57 us
    ppermute x2, starting transfers between devices, along_ctx(): return lax.ppermute(value, 'ctx', pairs)  6.1 us
  transfers between devices with their start and end apart: 21, of which 10 were waited for; matrix products, arithmetic and copies ran while one was open for 2% of the time, Pallas kernels for 35%

profile of v6, /device:TPU:0, one launch (start us, length us, event | category | flops | bytes accessed | tf_op | source)
XLA Modules:
  0.0 251.5 jit_solution(1895742096639052532)
XLA Ops:
  0.7 3.2 %collective-permute-start.4 = (bf16[1024,1024]{1,0:T(8,128)(2,1)}, bf16[1024,1024]{1,0:T(8,128)(2,1)}, u32[]{:S(2)}, u32[]{:S(2)}) collective-permute-start(bf16[1024,1024]{1,0:T(8,128)(2,1)} %g0.1), channel_id=1, source_target_pairs={{0,2},{1,3},{2,0},{3,1},{4,6},{5,7},{6,4},{7,5},{8,10},{9,11},{10,... | collective-permute-start | bytes 6291464 | tf_op jit(solution)/shard_map/ppermute | solution.py:38
  3.9 4.8 %collective-permute-start = (bf16[1024,512]{1,0:T(8,128)(2,1)}, bf16[1024,512]{1,0:T(8,128)(2,1)}, u32[]{:S(2)}, u32[]{:S(2)}) collective-permute-start(bf16[1024,512]{1,0:T(8,128)(2,1)} %k_ref.5), channel_id=1, source_target_pairs={{0,4},{4,8},{8,12},{12,16},{16,20},{20,24},{24,28},{28,32},{32,36}... | collective-permute-start | bytes 3145736 | tf_op jit(solution)/shard_map/ppermute | solution.py:66
  8.7 0.7 pad_add_fusion.place
  9.4 2.9 %collective-permute-start.5 = (bf16[1024,512]{1,0:T(8,128)(2,1)}, bf16[1024,512]{1,0:T(8,128)(2,1)}, u32[]{:S(2)}, u32[]{:S(2)}) collective-permute-start(bf16[1024,512]{1,0:T(8,128)(2,1)} %v_ref.5), channel_id=1, source_target_pairs={{0,4},{4,8},{8,12},{12,16},{16,20},{20,24},{24,28},{28,32},{32,36}... | collective-permute-start | bytes 3145736 | tf_op jit(solution)/shard_map/ppermute | solution.py:562
  12.3 2.9 %second_blocks.1 = bf16[2,512,512]{2,1,0:T(8,128)(2,1)} custom-call(s32[4]{0:T(128)} %pad_add_fusion.place, bf16[1024,512]{1,0:T(8,128)(2,1)} %k_ref.5, bf16[1024,512]{1,0:T(8,128)(2,1)} %v_ref.5), custom_call_target="tpu_custom_call" | custom-call | flops 1 | bytes 1 | tf_op jit(solution)/shard_map/second_blocks/pallas_call | solution.py:297
  15.2 4.2 %collective-permute-start.1 = (bf16[2,512,512]{2,1,0:T(8,128)(2,1)}, bf16[2,512,512]{2,1,0:T(8,128)(2,1)}, u32[]{:S(2)}, u32[]{:S(2)}) collective-permute-start(bf16[2,512,512]{2,1,0:T(8,128)(2,1)} %second_blocks.1), channel_id=1, source_target_pairs={{0,12},{4,0},{8,4},{12,8},{16,28},{20,16},{24,20},{28,24},{32,44},... | collective-permute-start | bytes 3145736 | tf_op jit(solution)/shard_map/ppermute | solution.py:79
  19.4 0.8 bitcast_add_fusion
  20.2 0.7 slice_bitcast_fusion
  20.9 0.2 and_reduce_fusion.1
  21.1 0.8 fusion
  22.1 0.7 reshape.60.flags
  22.7 9.9 %forward_own.1 = (f32[512,1024]{1,0:T(8,128)}, f32[4,2,512]{2,1,0:T(2,128)}, f32[4,2,512]{2,1,0:T(2,128)}) custom-call(s32[8]{0:T(128)} %reshape.60.flags, bf16[1024,512]{1,0:T(8,128)(2,1)} %q_ref.7, bf16[1024,512]{1,0:T(8,128)(2,1)} %k_ref.5, bf16[1024,512]{1,0:T(8,128)(2,1)} %v_ref.5, bf16[1024,512]{1,0:T(8,128)(2,1)} %k_ref.5), custom_call_target="tpu_custom_call" | custom-call | flops 1 | bytes 1 | tf_op jit(solution)/shard_map/forward_own/pallas_call | solution.py:297
  32.7 6.5 %projection_backward.2.refs_1_.rest_0_ = f32[1024,512]{1,0:T(8,128)} custom-call(s32[4]{0:T(128)} %pad_add_fusion.place, bf16[1024,1024]{1,0:T(8,128)(2,1)} %g0.1, bf16[1024,1024]{1,0:T(8,128)(2,1)} %collective-permute-done.2.b_ref.g1, bf16[512,4096]{1,0:T(8,128)(2,1)} %w_own.1, bf16[512,4096]{1,0:T(8,128)(2,1)} %w_own.1, ...), custom_call_target="tpu_custom_call" | custom-call | flops 1 | bytes 1 | tf_op jit(solution)/shard_map/projection_backward/pallas_call | solution.py:297
  39.2 2.9 %collective-permute-done.1.refs_0_ = bf16[2,512,512]{2,1,0:T(8,128)(2,1)} collective-permute-done((bf16[2,512,512]{2,1,0:T(8,128)(2,1)}, bf16[2,512,512]{2,1,0:T(8,128)(2,1)}, u32[]{:S(2)}, u32[]{:S(2)}) %collective-permute-start.1) | collective-permute-done | bytes 1048608 | tf_op jit(solution)/shard_map/ppermute | solution.py:79
  42.0 11.2 %collective-permute-done.5.refs_0_ = bf16[1024,512]{1,0:T(8,128)(2,1)} collective-permute-done((bf16[1024,512]{1,0:T(8,128)(2,1)}, bf16[1024,512]{1,0:T(8,128)(2,1)}, u32[]{:S(2)}, u32[]{:S(2)}) %collective-permute-start.5) | collective-permute-done | bytes 1048608 | tf_op jit(solution)/shard_map/ppermute | solution.py:562
  53.2 3.5 %collective-permute-start.6 = (bf16[1024,512]{1,0:T(8,128)(2,1)}, bf16[1024,512]{1,0:T(8,128)(2,1)}, u32[]{:S(2)}, u32[]{:S(2)}) collective-permute-start(bf16[1024,512]{1,0:T(8,128)(2,1)} %order.8.v1_ref), channel_id=1, source_target_pairs={{0,64},{1,65},{2,66},{3,67}} | collective-permute-start | bytes 3145736 | tf_op jit(solution)/shard_map/ppermute | solution.py:575
  56.7 5.7 %collective-permute-start.3 = (bf16[2,512,512]{2,1,0:T(8,128)(2,1)}, bf16[2,512,512]{2,1,0:T(8,128)(2,1)}, u32[]{:S(2)}, u32[]{:S(2)}) collective-permute-start(bf16[2,512,512]{2,1,0:T(8,128)(2,1)} %order.7.refs_1_.refs_4_), channel_id=1, source_target_pairs={{12,8},{0,12},{4,16},{8,20},{28,24},{16,28},{20,32},{24,36},{44,40... | collective-permute-start | bytes 3145736 | tf_op jit(solution)/shard_map/ppermute | solution.py:83
  62.4 15.6 %collective-permute-done.6.refs_3_ = bf16[1024,512]{1,0:T(8,128)(2,1)} collective-permute-done((bf16[1024,512]{1,0:T(8,128)(2,1)}, bf16[1024,512]{1,0:T(8,128)(2,1)}, u32[]{:S(2)}, u32[]{:S(2)}) %collective-permute-start.6) | collective-permute-done | bytes 1048608 | tf_op jit(solution)/shard_map/ppermute | solution.py:575
  77.9 5.6 %collective-permute-done.3.refs_1_ = bf16[2,512,512]{2,1,0:T(8,128)(2,1)} collective-permute-done((bf16[2,512,512]{2,1,0:T(8,128)(2,1)}, bf16[2,512,512]{2,1,0:T(8,128)(2,1)}, u32[]{:S(2)}, u32[]{:S(2)}) %collective-permute-start.3) | collective-permute-done | bytes 1048608 | tf_op jit(solution)/shard_map/ppermute | solution.py:83
  83.6 3.3 %projection_far.1 = bf16[512,2048]{1,0:T(8,128)(2,1)} custom-call(s32[4]{0:T(128)} %pad_add_fusion.place, bf16[512,4096]{1,0:T(8,128)(2,1)} %w_own.1, bf16[1024,512]{1,0:T(8,128)(2,1)} %get-tuple-element.48.k1_ref.refs_0_), custom_call_target="tpu_custom_call" | custom-call | flops 1 | bytes 1 | tf_op jit(solution)/shard_map/projection_far/pallas_call | solution.py:297
  86.9 0.5 collective-permute-start.12
  87.4 5.7 %forward_behind.1 = (bf16[1024,512]{1,0:T(8,128)(2,1)}, bf16[512,1024]{1,0:T(8,128)(2,1)}, f32[4,2,512]{2,1,0:T(2,128)}) custom-call(s32[8]{0:T(128)} %reshape.60.flags, bf16[1024,512]{1,0:T(8,128)(2,1)} %q_ref.7, bf16[1024,512]{1,0:T(8,128)(2,1)} %get-tuple-element.48.k1_ref.refs_0_, bf16[1024,512]{1,0:T(8,128)(2,1)} %order.8.v1_ref, ...), custom_call_target="tpu_custom_call" | custom-call | flops 1 | bytes 1 | tf_op jit(solution)/shard_map/forward_behind/pallas_call | solution.py:297
  93.2 3.3 %collective-permute-start.11 = (bf16[1024,512]{1,0:T(8,128)(2,1)}, bf16[1024,512]{1,0:T(8,128)(2,1)}, u32[]{:S(2)}, u32[]{:S(2)}) collective-permute-start(bf16[1024,512]{1,0:T(8,128)(2,1)} %get-tuple-element.53.out_ref.own_rows.own), channel_id=1, source_target_pairs={{0,2},{1,3},{2,0},{3,1},{4,6},{5,7},{6,4},{7,5},{8,10},{9,11},{10,... | collective-permute-start | bytes 3145736 | tf_op jit(solution)/shard_map/ppermute | solution.py:38
  96.4 13.2 %weight_gradient.1 = (bf16[2,512,512]{2,1,0:T(8,128)(2,1)}, bf16[2,512,512]{2,1,0:T(8,128)(2,1)}, bf16[2,512,512]{2,1,0:T(8,128)(2,1)}, bf16[2,512,512]{2,1,0:T(8,128)(2,1)}) custom-call(s32[4]{0:T(128)} %pad_add_fusion.place, bf16[512,1024]{1,0:T(8,128)(2,1)} %get-tuple-element.54.turned_ref, bf16[1024,1024]{1,0:T(8,128)(2,1)} %g0.1, ...), custom_call_target="tpu_custom_call" | custom-call | flops 1 | bytes 1 | tf_op jit(solution)/shard_map/weight_gradient/pallas_call | solution.py:297
  109.7 3.2 %collective-permute-start.8 = (bf16[2,512,512]{2,1,0:T(8,128)(2,1)}, bf16[2,512,512]{2,1,0:T(8,128)(2,1)}, u32[]{:S(2)}, u32[]{:S(2)}) collective-permute-start(bf16[2,512,512]{2,1,0:T(8,128)(2,1)} %get-tuple-element.57), channel_id=1, source_target_pairs={{0,16},{1,17},{2,18},{3,19},{4,20},{5,21},{6,22},{7,23},{8,24},{9,... | collective-permute-start | bytes 3145736 | tf_op jit(solution)/shard_map/ppermute | solution.py:38
  112.9 2.0 collective-permute-start.9
  114.9 5.4 %collective-permute-start.10 = (bf16[2,512,512]{2,1,0:T(8,128)(2,1)}, bf16[2,512,512]{2,1,0:T(8,128)(2,1)}, u32[]{:S(2)}, u32[]{:S(2)}) collective-permute-start(bf16[2,512,512]{2,1,0:T(8,128)(2,1)} %get-tuple-element.59), channel_id=1, source_target_pairs={{0,32},{1,33},{2,34},{3,35},{4,36},{5,37},{6,38},{7,39},{8,40},{9,... | collective-permute-start | bytes 3145736 | tf_op jit(solution)/shard_map/ppermute | solution.py:38
  120.4 6.9 %projection_backward.3.grad_ref = bf16[1024,512]{1,0:T(8,128)(2,1)} custom-call(s32[4]{0:T(128)} %pad_add_fusion.place, bf16[1024,1024]{1,0:T(8,128)(2,1)} %get-tuple-element.55.g2.a_ref, bf16[1024,1024]{1,0:T(8,128)(2,1)} %order.10.g3.b_ref, bf16[512,4096]{1,0:T(8,128)(2,1)} %w_own.1, bf16[512,4096]{1,0:T(8,128)(2,1)} %w_own.1, ...), custom_call_target="tpu_custom_call" | custom-call | flops 1 | bytes 1 | tf_op jit(solution)/shard_map/projection_backward/pallas_call | solution.py:297
  127.3 7.2 %backward_behind.1 = (bf16[2,1024,512]{2,1,0:T(8,128)(2,1)}, bf16[2,512,512]{2,1,0:T(8,128)(2,1)}, f32[512,1024]{1,0:T(8,128)}, f32[4,2,512]{2,1,0:T(2,128)}) custom-call(s32[8]{0:T(128)} %reshape.60.flags, bf16[1024,512]{1,0:T(8,128)(2,1)} %q_ref.7, bf16[1024,512]{1,0:T(8,128)(2,1)} %get-tuple-element.48.k1_ref.refs_0_, bf16[1024,512]{1,0:T(8,128)(2,1)} %order.8.v1_ref, ...), custom_call_target="tpu_custom_call" | custom-call | flops 1 | bytes 1 | tf_op jit(solution)/shard_map/backward_behind/pallas_call | solution.py:297
  134.5 13.7 %backward_own.1 = (bf16[1024,512]{1,0:T(8,128)(2,1)}, f32[2,1024,512]{2,1,0:T(8,128)}) custom-call(s32[8]{0:T(128)} %reshape.60.flags, bf16[1024,512]{1,0:T(8,128)(2,1)} %q_ref.7, bf16[1024,512]{1,0:T(8,128)(2,1)} %k_ref.5, bf16[1024,512]{1,0:T(8,128)(2,1)} %v_ref.5, bf16[1024,512]{1,0:T(8,128)(2,1)} %projection_backward.3.grad_ref, ...), custom_call_target="tpu_custom_call" | custom-call | flops 1 | bytes 1 | tf_op jit(solution)/shard_map/backward_own/pallas_call | solution.py:297
  148.2 11.0 %collective-permute-done.11.refs_5_ = bf16[1024,512]{1,0:T(8,128)(2,1)} collective-permute-done((bf16[1024,512]{1,0:T(8,128)(2,1)}, bf16[1024,512]{1,0:T(8,128)(2,1)}, u32[]{:S(2)}, u32[]{:S(2)}) %collective-permute-start.11) | collective-permute-done | bytes 1048608 | tf_op jit(solution)/shard_map/ppermute | solution.py:38
  159.2 5.1 %collective-permute-done.10.refs_2_ = bf16[2,512,512]{2,1,0:T(8,128)(2,1)} collective-permute-done((bf16[2,512,512]{2,1,0:T(8,128)(2,1)}, bf16[2,512,512]{2,1,0:T(8,128)(2,1)}, u32[]{:S(2)}, u32[]{:S(2)}) %collective-permute-start.10) | collective-permute-done | bytes 1048608 | tf_op jit(solution)/shard_map/ppermute | solution.py:38
  164.3 5.2 %for_core.1 = bf16[4,512,1024]{2,1,0:T(8,128)(2,1)} custom-call(s32[4]{0:T(128)} %pad_add_fusion.place, bf16[512,4096]{1,0:T(8,128)(2,1)} %w_own.1, bf16[512,2048]{1,0:T(8,128)(2,1)} %get-tuple-element.67.far_ref.w_far, bf16[1024,512]{1,0:T(8,128)(2,1)} %get-tuple-element.68.far_rows.far, bf16[1024,512]{1,0:T(8,128)(2,1)} %get-tuple-element.53.out_ref.own_rows.own, ...), custom_call_target="tpu_custom_call" | custom-call | flops 1 | bytes 1 | tf_op jit(solution)/shard_map/for_core/pallas_call | solution.py:297
  169.5 1.3 collective-permute-start.13
  170.8 1.3 collective-permute-start.15
  172.1 4.8 %weight_by_z.1 = (bf16[2,512,128]{2,1,0:T(8,128)(2,1)}, bf16[2,512,128]{2,1,0:T(8,128)(2,1)}, bf16[2,512,128]{2,1,0:T(8,128)(2,1)}, bf16[2,512,128]{2,1,0:T(8,128)(2,1)}) custom-call(s32[4]{0:T(128)} %pad_add_fusion.place, bf16[2,512,512]{2,1,0:T(8,128)(2,1)} %get-tuple-element.60.rest_1_.after.a, bf16[2,512,512]{2,1,0:T(8,128)(2,1)} %get-tuple-element.69.after.b, ...), custom_call_target="tpu_custom_call" | custom-call | flops 1 | bytes 1 | tf_op jit(solution)/shard_map/weight_by_z/pallas_call | solution.py:297
  176.9 21.6 %collective-permute-done.13.refs_0_ = bf16[2,512,512]{2,1,0:T(8,128)(2,1)} collective-permute-done((bf16[2,512,512]{2,1,0:T(8,128)(2,1)}, bf16[2,512,512]{2,1,0:T(8,128)(2,1)}, u32[]{:S(2)}, u32[]{:S(2)}) %collective-permute-start.13) | collective-permute-done | bytes 1048608 | tf_op jit(solution)/shard_map/ppermute | solution.py:79
  198.5 1.9 collective-permute-start.16
  200.5 3.3 %collective-permute-start.18 = (bf16[2,512,128]{2,1,0:T(8,128)(2,1)}, bf16[2,512,128]{2,1,0:T(8,128)(2,1)}, u32[]{:S(2)}, u32[]{:S(2)}) collective-permute-start(bf16[2,512,128]{2,1,0:T(8,128)(2,1)} %get-tuple-element.78), channel_id=1, source_target_pairs={{0,12},{1,13},{2,14},{3,15},{4,0},{5,1},{6,2},{7,3},{8,4},{9,5},{1... | collective-permute-start | bytes 786440 | tf_op jit(solution)/shard_map/ppermute | solution.py:38
  203.8 1.4 collective-permute-start.19
  205.2 9.4 %projection.1.refs_5_ = bf16[1024,1024]{1,0:T(8,128)(2,1)} custom-call(s32[4]{0:T(128)} %pad_add_fusion.place, bf16[1024,512]{1,0:T(8,128)(2,1)} %get-tuple-element.53.out_ref.own_rows.own, bf16[4,512,1024]{2,1,0:T(8,128)(2,1)} %get-tuple-element.73.core.far_core.w_core, bf16[1024,512]{1,0:T(8,128)(2,1)} %get-tuple-element.68.far_rows.far, ...), custom_call_target="tpu_custom_call" | custom-call | flops 1 | bytes 1 | tf_op jit(solution)/shard_map/projection/pallas_call | solution.py:297
  214.6 17.7 %collective-permute-done.17.refs_2_ = bf16[2,512,128]{2,1,0:T(8,128)(2,1)} collective-permute-done((bf16[2,512,128]{2,1,0:T(8,128)(2,1)}, bf16[2,512,128]{2,1,0:T(8,128)(2,1)}, u32[]{:S(2)}, u32[]{:S(2)}) %collective-permute-start.17) | collective-permute-done | bytes 262176 | tf_op jit(solution)/shard_map/ppermute | solution.py:38
  232.3 2.0 collective-permute-done.18.refs_3_
  234.3 4.9 %collective-permute-done.19.refs_4_ = bf16[2,512,128]{2,1,0:T(8,128)(2,1)} collective-permute-done((bf16[2,512,128]{2,1,0:T(8,128)(2,1)}, bf16[2,512,128]{2,1,0:T(8,128)(2,1)}, u32[]{:S(2)}, u32[]{:S(2)}) %collective-permute-start.19) | collective-permute-done | bytes 262176 | tf_op jit(solution)/shard_map/ppermute | solution.py:38
  239.2 2.6 %weight_z_sum.1 = (f32[512,128]{1,0:T(8,128)}, bf16[512,128]{1,0:T(8,128)(2,1)}) custom-call(s32[4]{0:T(128)} %pad_add_fusion.place, bf16[2,512,128]{2,1,0:T(8,128)(2,1)} %get-tuple-element.72.refs_2_.a_ref, bf16[2,512,128]{2,1,0:T(8,128)(2,1)} %get-tuple-element.82.b_ref, bf16[2,512,128]{2,1,0:T(8,128)(2,1)} %get-tuple-element.83.c_ref, ...), custom_call_target="tpu_custom_call" | custom-call | flops 1 | bytes 1 | tf_op jit(solution)/shard_map/weight_z_sum/pallas_call | solution.py:297
  241.9 2.3 collective-permute-start.20
  244.2 5.6 %key_value_sum.1 = (bf16[1024,512]{1,0:T(8,128)(2,1)}, bf16[1024,512]{1,0:T(8,128)(2,1)}) custom-call(s32[4]{0:T(128)} %pad_add_fusion.place, f32[2,1024,512]{2,1,0:T(8,128)} %get-tuple-element.65.refs_7_.own_ref, bf16[2,1024,512]{2,1,0:T(8,128)(2,1)} %get-tuple-element.80.after.near_ref, bf16[2,512,512]{2,1,0:T(8,128)(2,1)} %get-tuple-element.81.far_ref, ...), custom_call_target="tpu_custom_call" | custom-call | flops 1 | bytes 1 | tf_op jit(solution)/shard_map/key_value_sum/pallas_call | solution.py:297
  249.8 1.7 convert_add_fusion
  (26 shorter events, 0.5 us)
Async XLA Ops:
  0.6 32.1 %collective-permute-start.2 = (bf16[1024,1024]{1,0:T(8,128)(2,1)}, bf16[1024,1024]{1,0:T(8,128)(2,1)}, u32[]{:S(2)}, u32[]{:S(2)}) collective-permute-start(bf16[1024,1024]{1,0:T(8,128)(2,1)} %g0.1), channel_id=1, source_target_pairs={{0,1},{1,0},{2,3},{3,2},{4,5},{5,4},{6,7},{7,6},{8,9},{9,8},{10,11... | collective-permute-start | bytes 6291464 | tf_op jit(solution)/shard_map/ppermute | solution.py:38
  0.7 61.6 %collective-permute-start.4 = (bf16[1024,1024]{1,0:T(8,128)(2,1)}, bf16[1024,1024]{1,0:T(8,128)(2,1)}, u32[]{:S(2)}, u32[]{:S(2)}) collective-permute-start(bf16[1024,1024]{1,0:T(8,128)(2,1)} %g0.1), channel_id=1, source_target_pairs={{0,2},{1,3},{2,0},{3,1},{4,6},{5,7},{6,4},{7,5},{8,10},{9,11},{10,... | collective-permute-start | bytes 6291464 | tf_op jit(solution)/shard_map/ppermute | solution.py:38
  3.9 58.4 %collective-permute-start = (bf16[1024,512]{1,0:T(8,128)(2,1)}, bf16[1024,512]{1,0:T(8,128)(2,1)}, u32[]{:S(2)}, u32[]{:S(2)}) collective-permute-start(bf16[1024,512]{1,0:T(8,128)(2,1)} %k_ref.5), channel_id=1, source_target_pairs={{0,4},{4,8},{8,12},{12,16},{16,20},{20,24},{24,28},{28,32},{32,36}... | collective-permute-start | bytes 3145736 | tf_op jit(solution)/shard_map/ppermute | solution.py:66
  9.4 43.8 %collective-permute-start.5 = (bf16[1024,512]{1,0:T(8,128)(2,1)}, bf16[1024,512]{1,0:T(8,128)(2,1)}, u32[]{:S(2)}, u32[]{:S(2)}) collective-permute-start(bf16[1024,512]{1,0:T(8,128)(2,1)} %v_ref.5), channel_id=1, source_target_pairs={{0,4},{4,8},{8,12},{12,16},{16,20},{20,24},{24,28},{28,32},{32,36}... | collective-permute-start | bytes 3145736 | tf_op jit(solution)/shard_map/ppermute | solution.py:562
  15.2 26.9 %collective-permute-start.1 = (bf16[2,512,512]{2,1,0:T(8,128)(2,1)}, bf16[2,512,512]{2,1,0:T(8,128)(2,1)}, u32[]{:S(2)}, u32[]{:S(2)}) collective-permute-start(bf16[2,512,512]{2,1,0:T(8,128)(2,1)} %second_blocks.1), channel_id=1, source_target_pairs={{0,12},{4,0},{8,4},{12,8},{16,28},{20,16},{24,20},{28,24},{32,44},... | collective-permute-start | bytes 3145736 | tf_op jit(solution)/shard_map/ppermute | solution.py:79
  53.2 24.7 %collective-permute-start.6 = (bf16[1024,512]{1,0:T(8,128)(2,1)}, bf16[1024,512]{1,0:T(8,128)(2,1)}, u32[]{:S(2)}, u32[]{:S(2)}) collective-permute-start(bf16[1024,512]{1,0:T(8,128)(2,1)} %order.8.v1_ref), channel_id=1, source_target_pairs={{0,64},{1,65},{2,66},{3,67}} | collective-permute-start | bytes 3145736 | tf_op jit(solution)/shard_map/ppermute | solution.py:575
  56.7 26.9 %collective-permute-start.3 = (bf16[2,512,512]{2,1,0:T(8,128)(2,1)}, bf16[2,512,512]{2,1,0:T(8,128)(2,1)}, u32[]{:S(2)}, u32[]{:S(2)}) collective-permute-start(bf16[2,512,512]{2,1,0:T(8,128)(2,1)} %order.7.refs_1_.refs_4_), channel_id=1, source_target_pairs={{12,8},{0,12},{4,16},{8,20},{28,24},{16,28},{20,32},{24,36},{44,40... | collective-permute-start | bytes 3145736 | tf_op jit(solution)/shard_map/ppermute | solution.py:83
  83.6 12.9 %collective-permute-start.7 = (bf16[1024,1024]{1,0:T(8,128)(2,1)}, bf16[1024,1024]{1,0:T(8,128)(2,1)}, u32[]{:S(2)}, u32[]{:S(2)}) collective-permute-start(bf16[1024,1024]{1,0:T(8,128)(2,1)} %get-tuple-element.55.g2.a_ref), channel_id=1, source_target_pairs={{0,1},{1,0},{2,3},{3,2},{4,5},{5,4},{6,7},{7,6},{8,9},{9,8},{10,11... | collective-permute-start | bytes 6291464 | tf_op jit(solution)/shard_map/ppermute | solution.py:38
  86.9 72.3 %collective-permute-start.12 = (bf16[512,2048]{1,0:T(8,128)(2,1)}, bf16[512,2048]{1,0:T(8,128)(2,1)}, u32[]{:S(2)}, u32[]{:S(2)}) collective-permute-start(bf16[512,2048]{1,0:T(8,128)(2,1)} %projection_far.1), channel_id=1, source_target_pairs={{0,2},{1,3},{2,0},{3,1},{4,6},{5,7},{6,4},{7,5},{8,10},{9,11},{10,... | collective-permute-start | bytes 6291464 | tf_op jit(solution)/shard_map/ppermute | solution.py:38
  93.2 66.1 %collective-permute-start.11 = (bf16[1024,512]{1,0:T(8,128)(2,1)}, bf16[1024,512]{1,0:T(8,128)(2,1)}, u32[]{:S(2)}, u32[]{:S(2)}) collective-permute-start(bf16[1024,512]{1,0:T(8,128)(2,1)} %get-tuple-element.53.out_ref.own_rows.own), channel_id=1, source_target_pairs={{0,2},{1,3},{2,0},{3,1},{4,6},{5,7},{6,4},{7,5},{8,10},{9,11},{10,... | collective-permute-start | bytes 3145736 | tf_op jit(solution)/shard_map/ppermute | solution.py:38
  109.7 49.6 %collective-permute-start.8 = (bf16[2,512,512]{2,1,0:T(8,128)(2,1)}, bf16[2,512,512]{2,1,0:T(8,128)(2,1)}, u32[]{:S(2)}, u32[]{:S(2)}) collective-permute-start(bf16[2,512,512]{2,1,0:T(8,128)(2,1)} %get-tuple-element.57), channel_id=1, source_target_pairs={{0,16},{1,17},{2,18},{3,19},{4,20},{5,21},{6,22},{7,23},{8,24},{9,... | collective-permute-start | bytes 3145736 | tf_op jit(solution)/shard_map/ppermute | solution.py:38
  112.9 46.4 %collective-permute-start.9 = (bf16[2,512,512]{2,1,0:T(8,128)(2,1)}, bf16[2,512,512]{2,1,0:T(8,128)(2,1)}, u32[]{:S(2)}, u32[]{:S(2)}) collective-permute-start(bf16[2,512,512]{2,1,0:T(8,128)(2,1)} %get-tuple-element.58), channel_id=1, source_target_pairs={{0,48},{1,49},{2,50},{3,51},{4,52},{5,53},{6,54},{7,55},{8,56},{9,... | collective-permute-start | bytes 3145736 | tf_op jit(solution)/shard_map/ppermute | solution.py:38
  114.9 49.4 %collective-permute-start.10 = (bf16[2,512,512]{2,1,0:T(8,128)(2,1)}, bf16[2,512,512]{2,1,0:T(8,128)(2,1)}, u32[]{:S(2)}, u32[]{:S(2)}) collective-permute-start(bf16[2,512,512]{2,1,0:T(8,128)(2,1)} %get-tuple-element.59), channel_id=1, source_target_pairs={{0,32},{1,33},{2,34},{3,35},{4,36},{5,37},{6,38},{7,39},{8,40},{9,... | collective-permute-start | bytes 3145736 | tf_op jit(solution)/shard_map/ppermute | solution.py:38
  169.5 29.0 %collective-permute-start.14 = (bf16[4,512,1024]{2,1,0:T(8,128)(2,1)}, bf16[4,512,1024]{2,1,0:T(8,128)(2,1)}, u32[]{:S(2)}, u32[]{:S(2)}) collective-permute-start(bf16[4,512,1024]{2,1,0:T(8,128)(2,1)} %for_core.1), channel_id=1, source_target_pairs={{0,1},{1,0},{2,3},{3,2},{4,5},{5,4},{6,7},{7,6},{8,9},{9,8},{10,11... | collective-permute-start | bytes 12582920 | tf_op jit(solution)/shard_map/ppermute | solution.py:38
  169.5 29.0 %collective-permute-start.13 = (bf16[2,512,512]{2,1,0:T(8,128)(2,1)}, bf16[2,512,512]{2,1,0:T(8,128)(2,1)}, u32[]{:S(2)}, u32[]{:S(2)}) collective-permute-start(bf16[2,512,512]{2,1,0:T(8,128)(2,1)} %get-tuple-element.66), channel_id=1, source_target_pairs={{8,12},{12,0},{16,20},{20,24},{24,28},{28,16},{32,36},{36,40},{40,... | collective-permute-start | bytes 3145736 | tf_op jit(solution)/shard_map/ppermute | solution.py:79
  170.8 68.4 %collective-permute-start.15 = (bf16[2,1024,512]{2,1,0:T(8,128)(2,1)}, bf16[2,1024,512]{2,1,0:T(8,128)(2,1)}, u32[]{:S(2)}, u32[]{:S(2)}) collective-permute-start(bf16[2,1024,512]{2,1,0:T(8,128)(2,1)} %get-tuple-element.76), channel_id=1, source_target_pairs={{4,0},{8,4},{12,8},{16,12},{20,16},{24,20},{28,24},{32,28},{36,32}... | collective-permute-start | bytes 6291464 | tf_op jit(solution)/shard_map/ppermute | solution.py:66
  198.5 40.7 %collective-permute-start.16 = (bf16[2,512,512]{2,1,0:T(8,128)(2,1)}, bf16[2,512,512]{2,1,0:T(8,128)(2,1)}, u32[]{:S(2)}, u32[]{:S(2)}) collective-permute-start(bf16[2,512,512]{2,1,0:T(8,128)(2,1)} %get-tuple-element.74.after), channel_id=1, source_target_pairs={{12,0},{0,4},{20,8},{24,12},{28,16},{16,20},{36,24},{40,28},{44,32... | collective-permute-start | bytes 3145736 | tf_op jit(solution)/shard_map/ppermute | solution.py:83
  200.4 31.9 %collective-permute-start.17 = (bf16[2,512,128]{2,1,0:T(8,128)(2,1)}, bf16[2,512,128]{2,1,0:T(8,128)(2,1)}, u32[]{:S(2)}, u32[]{:S(2)}) collective-permute-start(bf16[2,512,128]{2,1,0:T(8,128)(2,1)} %get-tuple-element.77), channel_id=1, source_target_pairs={{0,4},{1,5},{2,6},{3,7},{4,8},{5,9},{6,10},{7,11},{8,12},{9,13},{1... | collective-permute-start | bytes 786440 | tf_op jit(solution)/shard_map/ppermute | solution.py:38
  200.5 33.8 %collective-permute-start.18 = (bf16[2,512,128]{2,1,0:T(8,128)(2,1)}, bf16[2,512,128]{2,1,0:T(8,128)(2,1)}, u32[]{:S(2)}, u32[]{:S(2)}) collective-permute-start(bf16[2,512,128]{2,1,0:T(8,128)(2,1)} %get-tuple-element.78), channel_id=1, source_target_pairs={{0,12},{1,13},{2,14},{3,15},{4,0},{5,1},{6,2},{7,3},{8,4},{9,5},{1... | collective-permute-start | bytes 786440 | tf_op jit(solution)/shard_map/ppermute | solution.py:38
  203.8 35.4 %collective-permute-start.19 = (bf16[2,512,128]{2,1,0:T(8,128)(2,1)}, bf16[2,512,128]{2,1,0:T(8,128)(2,1)}, u32[]{:S(2)}, u32[]{:S(2)}) collective-permute-start(bf16[2,512,128]{2,1,0:T(8,128)(2,1)} %get-tuple-element.79), channel_id=1, source_target_pairs={{0,8},{1,9},{2,10},{3,11},{4,12},{5,13},{6,14},{7,15},{8,0},{9,1},... | collective-permute-start | bytes 786440 | tf_op jit(solution)/shard_map/ppermute | solution.py:38
  241.9 7.9 %collective-permute-start.20 = (bf16[512,128]{1,0:T(8,128)(2,1)}, bf16[512,128]{1,0:T(8,128)(2,1)}, u32[]{:S(2)}, u32[]{:S(2)}) collective-permute-start(bf16[512,128]{1,0:T(8,128)(2,1)} %get-tuple-element.88), channel_id=1, source_target_pairs={{0,64},{1,65},{2,66},{3,67},{4,68},{5,69},{6,70},{7,71},{8,72},{9,... | collective-permute-start | bytes 393224 | tf_op jit(solution)/shard_map/ppermute | solution.py:38

commit v7 on v6

--- a/solution.py
+++ b/solution.py
@@ -255,8 +255,8 @@
             dv[held, :] += value_part
             dq[:, rows] += query_part
 
-    own_ref[0] = dk[...] * SCALE
-    own_ref[1] = dv[...]
+    own_ref[0] = (dk[...] * SCALE).astype(bf16)
+    own_ref[1] = dv[...].astype(bf16)
     dq_ref[...] = (dq[...] * SCALE).T.astype(bf16)
 
 
@@ -264,7 +264,7 @@
     for part, result in enumerate((key_ref, value_ref)):
         for block in range(2):
             rows = block_rows(block)
-            total = own_ref[part, rows, :] + near_ref[part, rows, :].astype(f32)
+            total = own_ref[part, rows, :].astype(f32) + near_ref[part, rows, :].astype(f32)
             if block == 1:
                 total += far_ref[part].astype(f32)
             result[rows, :] = total.astype(bf16)
@@ -353,7 +353,7 @@
         backward_own_kernel, "backward_own", (HEADS,),
         [head(1024)] * 4 + [HEAD_LINES, HEAD_TURNED, HEAD_LINES, ANY],
         [head(1024), head_pair(1024)],
-        [shape((1024, WIDTH), bf16), shape((2, 1024, WIDTH), f32)],
+        [shape((1024, WIDTH), bf16), shape((2, 1024, WIDTH), bf16)],
         [held, held, pltpu.VMEM((HDIM, 1024), f32)],
         (flags, q, k, v, grad, log_sum, dq, delta, after),
     )
@@ -567,18 +567,19 @@
     key_block = query_block - jnp.arange(WIN, dtype=jnp.int32)[None, :]
     flags = block_rule(spans, pairs, query_block, key_block).astype(jnp.int32).reshape(-1)
     own_state = forward_own(flags, queries, keys, values, keys)
-    terms = grad_terms(place, 0, out_grad, core_grad, out_weight, None, own_state[1])
+    far_weight = far_columns(place, out_weight, own_state[1])
+    terms = grad_terms(place, 0, out_grad, core_grad, out_weight, None, far_weight)
 
     [far_moved] = together([far_moved], [terms])
     far = second_hop(far_moved, 1)
     [near_values] = together([near_values], [far_moved])
     edge_values = lax.ppermute(near_values, "ctx", [(0, EDGE + 1)])
-    near_keys, far, far_grad, edge_values = together(
-        [near_keys, far, far_grad, edge_values], [far_moved]
+    near_keys, far, far_grad, edge_values, far_weight = together(
+        [near_keys, far, far_grad, edge_values, far_weight], [far_moved]
     )
 
     far_core_grad = to_core(far_grad)
-    far_weight = to_x_hi(far_columns(place, out_weight, near_keys))
+    far_weight = to_x_hi(far_weight)
     behind = (flags, queries, near_keys, near_values, edge_values, far)
     attention, turned, log_sum = forward_behind(*behind, own_state, far)
     [far_core_grad] = together([far_core_grad], [log_sum])
@@ -593,21 +594,23 @@
         flags, queries, keys, values, attn_grad, log_sum, dq, delta, delta
     )
 
-    *weight_moved, near_back, far_back, far_attention, far_weight = together(
-        [*weight_moved, near_back, far_back, far_attention, far_weight], [own]
+    far_attention, far_weight = together([far_attention, far_weight], [own])
+    from_core = for_core(place, out_weight, far_weight, far_attention, attention, own)
+
+    *weight_moved, near_back, far_back, from_core = together(
+        [*weight_moved, near_back, far_back, from_core]
     )
     near_back = along_ctx(near_back, -1)
     back_moved = first_hop(far_back, -1)
-    from_core = to_core(
-        for_core(place, out_weight, far_weight, far_attention, attention, weight_moved[0])
-    )
+    from_core = to_core(from_core)
     weight_pieces = pieces_by_z(place, [weight_parts[3], *weight_moved], weight_moved[0])
-    back_moved, from_core = together([back_moved, from_core], [weight_pieces[3]])
+    weight_moved = [to_z(weight_pieces[s], s + 1) for s in (0, 2, 1)]
+    mixed = mix(
+        place, attention, far_attention, out_weight, far_weight, from_core, weight_pieces[3]
+    )
+    [back_moved] = together([back_moved], [mixed])
     far_back = second_hop(back_moved, -1)
-    weight_moved = [to_z(weight_pieces[s], s + 1) for s in (0, 2, 1)]
-    mixed = mix(place, attention, far_attention, out_weight, far_weight, from_core, back_moved)
-    near_back, far_back, *weight_moved = together([near_back, far_back, *weight_moved], [mixed])
-    kept, sent = weight_z_sum(place, [weight_pieces[3], *weight_moved], near_back)
+    kept, sent = weight_z_sum(place, [weight_pieces[3], *weight_moved], back_moved)
     weight_grad = kept + to_x_lo(sent).astype(f32)
     key_grad, value_grad = finish(place, own, near_back, far_back, kept)
     return (mixed, query_grad, key_grad, value_grad, weight_grad)

time: 254 us -> 251 us (0.988)
  the two profiles are of different devices: /device:TPU:0 before, /device:TPU:30 now
where the time goes in v7:
time: 251 us; the launch traced here: 247 us
  waiting for transfers between devices  101 us (40%)
  Pallas kernels  96.5 us (38%)
  starting transfers between devices  43.4 us (17%)
  other arithmetic  3.56 us (1%)
    pallas_call x14, Pallas kernels, call(): pl.pallas_call(kernel, grid_spec=pltpu.PrefetchScalarGridSpec(num_scalar_...  96.5 us
    ppermute x13, waiting for transfers between devices, move(): return lax.ppermute(value, AXES, pairs)  50.1 us
    ppermute x2, waiting for transfers between devices, second_hop(): return lax.ppermute(value, 'ctx', [(m, t) for _, m, t in two_pairs(sign)])  24.3 us
    ppermute x13, starting transfers between devices, move(): return lax.ppermute(value, AXES, pairs)  20.1 us
    ppermute x1, waiting for transfers between devices, per_device(): near_values = lax.ppermute(values, 'ctx', near_pairs + [(EDGE, 0)])  14.3 us
    ppermute x2, waiting for transfers between devices, first_hop(): return lax.ppermute(value, 'ctx', [(s, m) for s, m, _ in two_pairs(sign)])  12 us
    ppermute x2, starting transfers between devices, along_ctx(): return lax.ppermute(value, 'ctx', pairs)  8.61 us
    ppermute x2, starting transfers between devices, second_hop(): return lax.ppermute(value, 'ctx', [(m, t) for _, m, t in two_pairs(sign)])  5.36 us
  transfers between devices with their start and end apart: 21, of which 7 were waited for; matrix products, arithmetic and copies ran while one was open for 2% of the time, Pallas kernels for 37%

profile of v7, /device:TPU:30, one launch (start us, length us, event | category | flops | bytes accessed | tf_op | source)
XLA Modules:
  0.0 247.1 jit_solution(17677700171606992697)
XLA Ops:
  0.6 0.1 collective-permute-start.2
  0.7 1.5 collective-permute-start.4
  2.2 3.8 %collective-permute-start = (bf16[1024,512]{1,0:T(8,128)(2,1)}, bf16[1024,512]{1,0:T(8,128)(2,1)}, u32[]{:S(2)}, u32[]{:S(2)}) collective-permute-start(bf16[1024,512]{1,0:T(8,128)(2,1)} %k_ref.5), channel_id=1, source_target_pairs={{0,4},{4,8},{8,12},{12,16},{16,20},{20,24},{24,28},{28,32},{32,36}... | collective-permute-start | bytes 3145736 | tf_op jit(solution)/shard_map/ppermute | solution.py:66
  6.1 0.7 pad_add_fusion.place
  6.7 3.8 %collective-permute-start.5 = (bf16[1024,512]{1,0:T(8,128)(2,1)}, bf16[1024,512]{1,0:T(8,128)(2,1)}, u32[]{:S(2)}, u32[]{:S(2)}) collective-permute-start(bf16[1024,512]{1,0:T(8,128)(2,1)} %v_ref.5), channel_id=1, source_target_pairs={{0,4},{4,8},{8,12},{12,16},{16,20},{20,24},{24,28},{28,32},{32,36}... | collective-permute-start | bytes 3145736 | tf_op jit(solution)/shard_map/ppermute | solution.py:562
  10.6 2.9 %second_blocks.1 = bf16[2,512,512]{2,1,0:T(8,128)(2,1)} custom-call(s32[4]{0:T(128)} %pad_add_fusion.place, bf16[1024,512]{1,0:T(8,128)(2,1)} %k_ref.5, bf16[1024,512]{1,0:T(8,128)(2,1)} %v_ref.5), custom_call_target="tpu_custom_call" | custom-call | flops 1 | bytes 1 | tf_op jit(solution)/shard_map/second_blocks/pallas_call | solution.py:297
  13.5 1.9 collective-permute-start.1
  15.4 0.8 bitcast_add_fusion
  16.1 0.7 slice_bitcast_fusion
  16.8 0.1 iota_subtract_fusion
  16.9 0.2 and_reduce_fusion.1
  17.1 0.8 fusion
  17.9 0.2 and_reduce_fusion
  18.1 0.7 reshape.60.flags
  18.7 9.9 %forward_own.1 = (f32[512,1024]{1,0:T(8,128)}, f32[4,2,512]{2,1,0:T(2,128)}, f32[4,2,512]{2,1,0:T(2,128)}) custom-call(s32[8]{0:T(128)} %reshape.60.flags, bf16[1024,512]{1,0:T(8,128)(2,1)} %q_ref.7, bf16[1024,512]{1,0:T(8,128)(2,1)} %k_ref.5, bf16[1024,512]{1,0:T(8,128)(2,1)} %v_ref.5, bf16[1024,512]{1,0:T(8,128)(2,1)} %k_ref.5), custom_call_target="tpu_custom_call" | custom-call | flops 1 | bytes 1 | tf_op jit(solution)/shard_map/forward_own/pallas_call | solution.py:297
  28.7 3.4 %projection_far.1.rest_0_.refs_4_ = bf16[512,2048]{1,0:T(8,128)(2,1)} custom-call(s32[4]{0:T(128)} %pad_add_fusion.place, bf16[512,4096]{1,0:T(8,128)(2,1)} %w_own.1, f32[4,2,512]{2,1,0:T(2,128)} %get-tuple-element.42.refs_0_.top_in), custom_call_target="tpu_custom_call" | custom-call | flops 1 | bytes 1 | tf_op jit(solution)/shard_map/projection_far/pallas_call | solution.py:297
  32.0 6.4 %projection_backward.2.refs_1_.rest_0_ = f32[1024,512]{1,0:T(8,128)} custom-call(s32[4]{0:T(128)} %pad_add_fusion.place, bf16[1024,1024]{1,0:T(8,128)(2,1)} %g0.1, bf16[1024,1024]{1,0:T(8,128)(2,1)} %collective-permute-done.2.b_ref.g1, bf16[512,4096]{1,0:T(8,128)(2,1)} %w_own.1, bf16[512,4096]{1,0:T(8,128)(2,1)} %w_own.1, ...), custom_call_target="tpu_custom_call" | custom-call | flops 1 | bytes 1 | tf_op jit(solution)/shard_map/projection_backward/pallas_call | solution.py:297
  38.5 1.8 collective-permute-done.1.refs_0_
  40.3 14.3 %collective-permute-done.5.refs_0_ = bf16[1024,512]{1,0:T(8,128)(2,1)} collective-permute-done((bf16[1024,512]{1,0:T(8,128)(2,1)}, bf16[1024,512]{1,0:T(8,128)(2,1)}, u32[]{:S(2)}, u32[]{:S(2)}) %collective-permute-start.5) | collective-permute-done | bytes 1048608 | tf_op jit(solution)/shard_map/ppermute | solution.py:562
  54.6 1.7 collective-permute-start.6
  56.2 3.5 %collective-permute-start.3 = (bf16[2,512,512]{2,1,0:T(8,128)(2,1)}, bf16[2,512,512]{2,1,0:T(8,128)(2,1)}, u32[]{:S(2)}, u32[]{:S(2)}) collective-permute-start(bf16[2,512,512]{2,1,0:T(8,128)(2,1)} %order.7.refs_1_.refs_5_), channel_id=1, source_target_pairs={{12,8},{0,12},{4,16},{8,20},{28,24},{16,28},{20,32},{24,36},{44,40... | collective-permute-start | bytes 3145736 | tf_op jit(solution)/shard_map/ppermute | solution.py:83
  59.7 24.3 %collective-permute-done.3.refs_1_ = bf16[2,512,512]{2,1,0:T(8,128)(2,1)} collective-permute-done((bf16[2,512,512]{2,1,0:T(8,128)(2,1)}, bf16[2,512,512]{2,1,0:T(8,128)(2,1)}, u32[]{:S(2)}, u32[]{:S(2)}) %collective-permute-start.3) | collective-permute-done | bytes 1048608 | tf_op jit(solution)/shard_map/ppermute | solution.py:83
  84.0 2.1 collective-permute-start.12
  86.2 5.7 %forward_behind.1 = (bf16[1024,512]{1,0:T(8,128)(2,1)}, bf16[512,1024]{1,0:T(8,128)(2,1)}, f32[4,2,512]{2,1,0:T(2,128)}) custom-call(s32[8]{0:T(128)} %reshape.60.flags, bf16[1024,512]{1,0:T(8,128)(2,1)} %q_ref.7, bf16[1024,512]{1,0:T(8,128)(2,1)} %get-tuple-element.43.k1_ref, bf16[1024,512]{1,0:T(8,128)(2,1)} %order.8.v1_ref, ...), custom_call_target="tpu_custom_call" | custom-call | flops 1 | bytes 1 | tf_op jit(solution)/shard_map/forward_behind/pallas_call | solution.py:297
  91.9 1.7 collective-permute-start.11
  93.6 13.3 %weight_gradient.1 = (bf16[2,512,512]{2,1,0:T(8,128)(2,1)}, bf16[2,512,512]{2,1,0:T(8,128)(2,1)}, bf16[2,512,512]{2,1,0:T(8,128)(2,1)}, bf16[2,512,512]{2,1,0:T(8,128)(2,1)}) custom-call(s32[4]{0:T(128)} %pad_add_fusion.place, bf16[512,1024]{1,0:T(8,128)(2,1)} %get-tuple-element.49.turned_ref, bf16[1024,1024]{1,0:T(8,128)(2,1)} %g0.1, ...), custom_call_target="tpu_custom_call" | custom-call | flops 1 | bytes 1 | tf_op jit(solution)/shard_map/weight_gradient/pallas_call | solution.py:297
  106.9 6.9 %collective-permute-start.9 = (bf16[2,512,512]{2,1,0:T(8,128)(2,1)}, bf16[2,512,512]{2,1,0:T(8,128)(2,1)}, u32[]{:S(2)}, u32[]{:S(2)}) collective-permute-start(bf16[2,512,512]{2,1,0:T(8,128)(2,1)} %get-tuple-element.53), channel_id=1, source_target_pairs={{0,48},{1,49},{2,50},{3,51},{4,52},{5,53},{6,54},{7,55},{8,56},{9,... | collective-permute-start | bytes 3145736 | tf_op jit(solution)/shard_map/ppermute | solution.py:38
  113.8 2.0 collective-permute-start.10
  115.8 6.9 %projection_backward.3.grad_ref = bf16[1024,512]{1,0:T(8,128)(2,1)} custom-call(s32[4]{0:T(128)} %pad_add_fusion.place, bf16[1024,1024]{1,0:T(8,128)(2,1)} %get-tuple-element.50.g2.a_ref, bf16[1024,1024]{1,0:T(8,128)(2,1)} %order.10.g3.b_ref, bf16[512,4096]{1,0:T(8,128)(2,1)} %w_own.1, bf16[512,4096]{1,0:T(8,128)(2,1)} %w_own.1, ...), custom_call_target="tpu_custom_call" | custom-call | flops 1 | bytes 1 | tf_op jit(solution)/shard_map/projection_backward/pallas_call | solution.py:297
  122.7 7.2 %backward_behind.1 = (bf16[2,1024,512]{2,1,0:T(8,128)(2,1)}, bf16[2,512,512]{2,1,0:T(8,128)(2,1)}, f32[512,1024]{1,0:T(8,128)}, f32[4,2,512]{2,1,0:T(2,128)}) custom-call(s32[8]{0:T(128)} %reshape.60.flags, bf16[1024,512]{1,0:T(8,128)(2,1)} %q_ref.7, bf16[1024,512]{1,0:T(8,128)(2,1)} %get-tuple-element.43.k1_ref, bf16[1024,512]{1,0:T(8,128)(2,1)} %order.8.v1_ref, ...), custom_call_target="tpu_custom_call" | custom-call | flops 1 | bytes 1 | tf_op jit(solution)/shard_map/backward_behind/pallas_call | solution.py:297
  129.9 13.6 %backward_own.1 = (bf16[1024,512]{1,0:T(8,128)(2,1)}, bf16[2,1024,512]{2,1,0:T(8,128)(2,1)}) custom-call(s32[8]{0:T(128)} %reshape.60.flags, bf16[1024,512]{1,0:T(8,128)(2,1)} %q_ref.7, bf16[1024,512]{1,0:T(8,128)(2,1)} %k_ref.5, bf16[1024,512]{1,0:T(8,128)(2,1)} %v_ref.5, bf16[1024,512]{1,0:T(8,128)(2,1)} %projection_backward.3.grad_ref, ...), custom_call_target="tpu_custom_call" | custom-call | flops 1 | bytes 1 | tf_op jit(solution)/shard_map/backward_own/pallas_call | solution.py:297
  143.5 12.9 %collective-permute-done.11.refs_0_ = bf16[1024,512]{1,0:T(8,128)(2,1)} collective-permute-done((bf16[1024,512]{1,0:T(8,128)(2,1)}, bf16[1024,512]{1,0:T(8,128)(2,1)}, u32[]{:S(2)}, u32[]{:S(2)}) %collective-permute-start.11) | collective-permute-done | bytes 1048608 | tf_op jit(solution)/shard_map/ppermute | solution.py:38
  156.4 5.2 %for_core.1.refs_5_ = bf16[4,512,1024]{2,1,0:T(8,128)(2,1)} custom-call(s32[4]{0:T(128)} %pad_add_fusion.place, bf16[512,4096]{1,0:T(8,128)(2,1)} %w_own.1, bf16[512,2048]{1,0:T(8,128)(2,1)} %get-tuple-element.62.far_ref.w_far, bf16[1024,512]{1,0:T(8,128)(2,1)} %get-tuple-element.63.far_rows.far, bf16[1024,512]{1,0:T(8,128)(2,1)} %get-tuple-element.48.out_ref.own_rows.own, ...), custom_call_target="tpu_custom_call" | custom-call | flops 1 | bytes 1 | tf_op jit(solution)/shard_map/for_core/pallas_call | solution.py:297
  161.6 0.1 collective-permute-start.13
  161.7 1.9 collective-permute-start.15
  163.6 4.8 %collective-permute-start.14 = (bf16[2,1024,512]{2,1,0:T(8,128)(2,1)}, bf16[2,1024,512]{2,1,0:T(8,128)(2,1)}, u32[]{:S(2)}, u32[]{:S(2)}) collective-permute-start(bf16[2,1024,512]{2,1,0:T(8,128)(2,1)} %get-tuple-element.70), channel_id=1, source_target_pairs={{4,0},{8,4},{12,8},{16,12},{20,16},{24,20},{28,24},{32,28},{36,32}... | collective-permute-start | bytes 6291464 | tf_op jit(solution)/shard_map/ppermute | solution.py:66
  168.4 4.8 %weight_by_z.1 = (bf16[2,512,128]{2,1,0:T(8,128)(2,1)}, bf16[2,512,128]{2,1,0:T(8,128)(2,1)}, bf16[2,512,128]{2,1,0:T(8,128)(2,1)}, bf16[2,512,128]{2,1,0:T(8,128)(2,1)}) custom-call(s32[4]{0:T(128)} %pad_add_fusion.place, bf16[2,512,512]{2,1,0:T(8,128)(2,1)} %get-tuple-element.55.rest_1_.after.a, bf16[2,512,512]{2,1,0:T(8,128)(2,1)} %get-tuple-element.65.b.after, ...), custom_call_target="tpu_custom_call" | custom-call | flops 1 | bytes 1 | tf_op jit(solution)/shard_map/weight_by_z/pallas_call | solution.py:297
  173.2 9.4 %projection.1.refs_1_ = bf16[1024,1024]{1,0:T(8,128)(2,1)} custom-call(s32[4]{0:T(128)} %pad_add_fusion.place, bf16[1024,512]{1,0:T(8,128)(2,1)} %get-tuple-element.48.out_ref.own_rows.own, bf16[4,512,1024]{2,1,0:T(8,128)(2,1)} %collective-permute-done.13.core.far_core.w_core, bf16[1024,512]{1,0:T(8,128)(2,1)} %get-tuple-element.63.far_rows.far, ...), custom_call_target="tpu_custom_call" | custom-call | flops 1 | bytes 1 | tf_op jit(solution)/shard_map/projection/pallas_call | solution.py:297
  182.6 10.2 %collective-permute-done.15.refs_0_ = bf16[2,512,512]{2,1,0:T(8,128)(2,1)} collective-permute-done((bf16[2,512,512]{2,1,0:T(8,128)(2,1)}, bf16[2,512,512]{2,1,0:T(8,128)(2,1)}, u32[]{:S(2)}, u32[]{:S(2)}) %collective-permute-start.15) | collective-permute-done | bytes 1048608 | tf_op jit(solution)/shard_map/ppermute | solution.py:79
  192.8 1.9 collective-permute-start.16
  194.7 0.1 collective-permute-start.17
  194.8 4.2 %collective-permute-start.18 = (bf16[2,512,128]{2,1,0:T(8,128)(2,1)}, bf16[2,512,128]{2,1,0:T(8,128)(2,1)}, u32[]{:S(2)}, u32[]{:S(2)}) collective-permute-start(bf16[2,512,128]{2,1,0:T(8,128)(2,1)} %get-tuple-element.73), channel_id=1, source_target_pairs={{0,12},{1,13},{2,14},{3,15},{4,0},{5,1},{6,2},{7,3},{8,4},{9,5},{1... | collective-permute-start | bytes 786440 | tf_op jit(solution)/shard_map/ppermute | solution.py:38
  199.0 1.5 collective-permute-start.19
  200.4 32.0 %collective-permute-done.17.b_ref = bf16[2,512,128]{2,1,0:T(8,128)(2,1)} collective-permute-done((bf16[2,512,128]{2,1,0:T(8,128)(2,1)}, bf16[2,512,128]{2,1,0:T(8,128)(2,1)}, u32[]{:S(2)}, u32[]{:S(2)}) %collective-permute-start.17) | collective-permute-done | bytes 262176 | tf_op jit(solution)/shard_map/ppermute | solution.py:38
  232.5 2.7 %weight_z_sum.1 = (f32[512,128]{1,0:T(8,128)}, bf16[512,128]{1,0:T(8,128)(2,1)}) custom-call(s32[4]{0:T(128)} %pad_add_fusion.place, bf16[2,512,128]{2,1,0:T(8,128)(2,1)} %get-tuple-element.68.after.a_ref, bf16[2,512,128]{2,1,0:T(8,128)(2,1)} %collective-permute-done.17.b_ref, bf16[2,512,128]{2,1,0:T(8,128)(2,1)} %collective-permute-done.18.c_ref, ...), custom_call_target="tpu_custom_call" | custom-call | flops 1 | bytes 1 | tf_op jit(solution)/shard_map/weight_z_sum/pallas_call | solution.py:297
  235.1 5.2 %collective-permute-done.20 = bf16[512,128]{1,0:T(8,128)(2,1)S(1)} collective-permute-done((bf16[512,128]{1,0:T(8,128)(2,1)}, bf16[512,128]{1,0:T(8,128)(2,1)S(1)}, u32[]{:S(2)}, u32[]{:S(2)}) %collective-permute-start.20) | collective-permute-done | bytes 131104 | tf_op jit(solution)/shard_map/ppermute | solution.py:38
  240.3 1.7 convert_add_fusion
  242.0 5.2 %key_value_sum.1 = (bf16[1024,512]{1,0:T(8,128)(2,1)}, bf16[1024,512]{1,0:T(8,128)(2,1)}) custom-call(s32[4]{0:T(128)} %pad_add_fusion.place, bf16[2,1024,512]{2,1,0:T(8,128)(2,1)} %get-tuple-element.61.refs_2_.after.own_ref, bf16[2,1024,512]{2,1,0:T(8,128)(2,1)} %collective-permute-done.14.near_ref, bf16[2,512,512]{2,1,0:T(8,128)(2,1)} %collective-permute-done.16.far_ref, ...), custom_call_target="tpu_custom_call" | custom-call | flops 1 | bytes 1 | tf_op jit(solution)/shard_map/key_value_sum/pallas_call | solution.py:297
  (26 shorter events, 0.1 us)
Async XLA Ops:
  0.6 31.4 %collective-permute-start.2 = (bf16[1024,1024]{1,0:T(8,128)(2,1)}, bf16[1024,1024]{1,0:T(8,128)(2,1)}, u32[]{:S(2)}, u32[]{:S(2)}) collective-permute-start(bf16[1024,1024]{1,0:T(8,128)(2,1)} %g0.1), channel_id=1, source_target_pairs={{0,1},{1,0},{2,3},{3,2},{4,5},{5,4},{6,7},{7,6},{8,9},{9,8},{10,11... | collective-permute-start | bytes 6291464 | tf_op jit(solution)/shard_map/ppermute | solution.py:38
  0.7 59.0 %collective-permute-start.4 = (bf16[1024,1024]{1,0:T(8,128)(2,1)}, bf16[1024,1024]{1,0:T(8,128)(2,1)}, u32[]{:S(2)}, u32[]{:S(2)}) collective-permute-start(bf16[1024,1024]{1,0:T(8,128)(2,1)} %g0.1), channel_id=1, source_target_pairs={{0,2},{1,3},{2,0},{3,1},{4,6},{5,7},{6,4},{7,5},{8,10},{9,11},{10,... | collective-permute-start | bytes 6291464 | tf_op jit(solution)/shard_map/ppermute | solution.py:38
  2.2 57.5 %collective-permute-start = (bf16[1024,512]{1,0:T(8,128)(2,1)}, bf16[1024,512]{1,0:T(8,128)(2,1)}, u32[]{:S(2)}, u32[]{:S(2)}) collective-permute-start(bf16[1024,512]{1,0:T(8,128)(2,1)} %k_ref.5), channel_id=1, source_target_pairs={{0,4},{4,8},{8,12},{12,16},{16,20},{20,24},{24,28},{28,32},{32,36}... | collective-permute-start | bytes 3145736 | tf_op jit(solution)/shard_map/ppermute | solution.py:66
  6.7 47.8 %collective-permute-start.5 = (bf16[1024,512]{1,0:T(8,128)(2,1)}, bf16[1024,512]{1,0:T(8,128)(2,1)}, u32[]{:S(2)}, u32[]{:S(2)}) collective-permute-start(bf16[1024,512]{1,0:T(8,128)(2,1)} %v_ref.5), channel_id=1, source_target_pairs={{0,4},{4,8},{8,12},{12,16},{16,20},{20,24},{24,28},{28,32},{32,36}... | collective-permute-start | bytes 3145736 | tf_op jit(solution)/shard_map/ppermute | solution.py:562
  13.5 26.9 %collective-permute-start.1 = (bf16[2,512,512]{2,1,0:T(8,128)(2,1)}, bf16[2,512,512]{2,1,0:T(8,128)(2,1)}, u32[]{:S(2)}, u32[]{:S(2)}) collective-permute-start(bf16[2,512,512]{2,1,0:T(8,128)(2,1)} %second_blocks.1), channel_id=1, source_target_pairs={{0,12},{4,0},{8,4},{12,8},{16,28},{20,16},{24,20},{28,24},{32,44},... | collective-permute-start | bytes 3145736 | tf_op jit(solution)/shard_map/ppermute | solution.py:79
  54.6 5.1 %collective-permute-start.6 = (bf16[1024,512]{1,0:T(8,128)(2,1)}, bf16[1024,512]{1,0:T(8,128)(2,1)}, u32[]{:S(2)}, u32[]{:S(2)}) collective-permute-start(bf16[1024,512]{1,0:T(8,128)(2,1)} %order.8.v1_ref), channel_id=1, source_target_pairs={{0,64},{1,65},{2,66},{3,67}} | collective-permute-start | bytes 3145736 | tf_op jit(solution)/shard_map/ppermute | solution.py:576
  56.2 27.8 %collective-permute-start.3 = (bf16[2,512,512]{2,1,0:T(8,128)(2,1)}, bf16[2,512,512]{2,1,0:T(8,128)(2,1)}, u32[]{:S(2)}, u32[]{:S(2)}) collective-permute-start(bf16[2,512,512]{2,1,0:T(8,128)(2,1)} %order.7.refs_1_.refs_5_), channel_id=1, source_target_pairs={{12,8},{0,12},{4,16},{8,20},{28,24},{16,28},{20,32},{24,36},{44,40... | collective-permute-start | bytes 3145736 | tf_op jit(solution)/shard_map/ppermute | solution.py:83
  84.0 9.5 %collective-permute-start.7 = (bf16[1024,1024]{1,0:T(8,128)(2,1)}, bf16[1024,1024]{1,0:T(8,128)(2,1)}, u32[]{:S(2)}, u32[]{:S(2)}) collective-permute-start(bf16[1024,1024]{1,0:T(8,128)(2,1)} %get-tuple-element.50.g2.a_ref), channel_id=1, source_target_pairs={{0,1},{1,0},{2,3},{3,2},{4,5},{5,4},{6,7},{7,6},{8,9},{9,8},{10,11... | collective-permute-start | bytes 6291464 | tf_op jit(solution)/shard_map/ppermute | solution.py:38
  84.0 72.3 %collective-permute-start.12 = (bf16[512,2048]{1,0:T(8,128)(2,1)}, bf16[512,2048]{1,0:T(8,128)(2,1)}, u32[]{:S(2)}, u32[]{:S(2)}) collective-permute-start(bf16[512,2048]{1,0:T(8,128)(2,1)} %get-tuple-element.58), channel_id=1, source_target_pairs={{0,2},{1,3},{2,0},{3,1},{4,6},{5,7},{6,4},{7,5},{8,10},{9,11},{10,... | collective-permute-start | bytes 6291464 | tf_op jit(solution)/shard_map/ppermute | solution.py:38
  91.9 64.5 %collective-permute-start.11 = (bf16[1024,512]{1,0:T(8,128)(2,1)}, bf16[1024,512]{1,0:T(8,128)(2,1)}, u32[]{:S(2)}, u32[]{:S(2)}) collective-permute-start(bf16[1024,512]{1,0:T(8,128)(2,1)} %get-tuple-element.48.out_ref.own_rows.own), channel_id=1, source_target_pairs={{0,2},{1,3},{2,0},{3,1},{4,6},{5,7},{6,4},{7,5},{8,10},{9,11},{10,... | collective-permute-start | bytes 3145736 | tf_op jit(solution)/shard_map/ppermute | solution.py:38
  106.9 54.7 %collective-permute-start.8 = (bf16[2,512,512]{2,1,0:T(8,128)(2,1)}, bf16[2,512,512]{2,1,0:T(8,128)(2,1)}, u32[]{:S(2)}, u32[]{:S(2)}) collective-permute-start(bf16[2,512,512]{2,1,0:T(8,128)(2,1)} %get-tuple-element.52), channel_id=1, source_target_pairs={{0,16},{1,17},{2,18},{3,19},{4,20},{5,21},{6,22},{7,23},{8,24},{9,... | collective-permute-start | bytes 3145736 | tf_op jit(solution)/shard_map/ppermute | solution.py:38
  106.9 54.7 %collective-permute-start.9 = (bf16[2,512,512]{2,1,0:T(8,128)(2,1)}, bf16[2,512,512]{2,1,0:T(8,128)(2,1)}, u32[]{:S(2)}, u32[]{:S(2)}) collective-permute-start(bf16[2,512,512]{2,1,0:T(8,128)(2,1)} %get-tuple-element.53), channel_id=1, source_target_pairs={{0,48},{1,49},{2,50},{3,51},{4,52},{5,53},{6,54},{7,55},{8,56},{9,... | collective-permute-start | bytes 3145736 | tf_op jit(solution)/shard_map/ppermute | solution.py:38
  113.8 47.8 %collective-permute-start.10 = (bf16[2,512,512]{2,1,0:T(8,128)(2,1)}, bf16[2,512,512]{2,1,0:T(8,128)(2,1)}, u32[]{:S(2)}, u32[]{:S(2)}) collective-permute-start(bf16[2,512,512]{2,1,0:T(8,128)(2,1)} %get-tuple-element.54), channel_id=1, source_target_pairs={{0,32},{1,33},{2,34},{3,35},{4,36},{5,37},{6,38},{7,39},{8,40},{9,... | collective-permute-start | bytes 3145736 | tf_op jit(solution)/shard_map/ppermute | solution.py:38
  161.6 11.6 %collective-permute-start.13 = (bf16[4,512,1024]{2,1,0:T(8,128)(2,1)}, bf16[4,512,1024]{2,1,0:T(8,128)(2,1)}, u32[]{:S(2)}, u32[]{:S(2)}) collective-permute-start(bf16[4,512,1024]{2,1,0:T(8,128)(2,1)} %get-tuple-element.64), channel_id=1, source_target_pairs={{0,1},{1,0},{2,3},{3,2},{4,5},{5,4},{6,7},{7,6},{8,9},{9,8},{10,11... | collective-permute-start | bytes 12582920 | tf_op jit(solution)/shard_map/ppermute | solution.py:38
  161.7 31.1 %collective-permute-start.15 = (bf16[2,512,512]{2,1,0:T(8,128)(2,1)}, bf16[2,512,512]{2,1,0:T(8,128)(2,1)}, u32[]{:S(2)}, u32[]{:S(2)}) collective-permute-start(bf16[2,512,512]{2,1,0:T(8,128)(2,1)} %get-tuple-element.71), channel_id=1, source_target_pairs={{8,12},{12,0},{16,20},{20,24},{24,28},{28,16},{32,36},{36,40},{40,... | collective-permute-start | bytes 3145736 | tf_op jit(solution)/shard_map/ppermute | solution.py:79
  163.6 78.4 %collective-permute-start.14 = (bf16[2,1024,512]{2,1,0:T(8,128)(2,1)}, bf16[2,1024,512]{2,1,0:T(8,128)(2,1)}, u32[]{:S(2)}, u32[]{:S(2)}) collective-permute-start(bf16[2,1024,512]{2,1,0:T(8,128)(2,1)} %get-tuple-element.70), channel_id=1, source_target_pairs={{4,0},{8,4},{12,8},{16,12},{20,16},{24,20},{28,24},{32,28},{36,32}... | collective-permute-start | bytes 6291464 | tf_op jit(solution)/shard_map/ppermute | solution.py:66
  192.8 49.2 %collective-permute-start.16 = (bf16[2,512,512]{2,1,0:T(8,128)(2,1)}, bf16[2,512,512]{2,1,0:T(8,128)(2,1)}, u32[]{:S(2)}, u32[]{:S(2)}) collective-permute-start(bf16[2,512,512]{2,1,0:T(8,128)(2,1)} %order.13.after), channel_id=1, source_target_pairs={{12,0},{0,4},{20,8},{24,12},{28,16},{16,20},{36,24},{40,28},{44,32... | collective-permute-start | bytes 3145736 | tf_op jit(solution)/shard_map/ppermute | solution.py:83
  194.7 37.7 %collective-permute-start.17 = (bf16[2,512,128]{2,1,0:T(8,128)(2,1)}, bf16[2,512,128]{2,1,0:T(8,128)(2,1)}, u32[]{:S(2)}, u32[]{:S(2)}) collective-permute-start(bf16[2,512,128]{2,1,0:T(8,128)(2,1)} %get-tuple-element.72), channel_id=1, source_target_pairs={{0,4},{1,5},{2,6},{3,7},{4,8},{5,9},{6,10},{7,11},{8,12},{9,13},{1... | collective-permute-start | bytes 786440 | tf_op jit(solution)/shard_map/ppermute | solution.py:38
  194.8 37.6 %collective-permute-start.18 = (bf16[2,512,128]{2,1,0:T(8,128)(2,1)}, bf16[2,512,128]{2,1,0:T(8,128)(2,1)}, u32[]{:S(2)}, u32[]{:S(2)}) collective-permute-start(bf16[2,512,128]{2,1,0:T(8,128)(2,1)} %get-tuple-element.73), channel_id=1, source_target_pairs={{0,12},{1,13},{2,14},{3,15},{4,0},{5,1},{6,2},{7,3},{8,4},{9,5},{1... | collective-permute-start | bytes 786440 | tf_op jit(solution)/shard_map/ppermute | solution.py:38
  199.0 33.5 %collective-permute-start.19 = (bf16[2,512,128]{2,1,0:T(8,128)(2,1)}, bf16[2,512,128]{2,1,0:T(8,128)(2,1)}, u32[]{:S(2)}, u32[]{:S(2)}) collective-permute-start(bf16[2,512,128]{2,1,0:T(8,128)(2,1)} %get-tuple-element.74), channel_id=1, source_target_pairs={{0,8},{1,9},{2,10},{3,11},{4,12},{5,13},{6,14},{7,15},{8,0},{9,1},... | collective-permute-start | bytes 786440 | tf_op jit(solution)/shard_map/ppermute | solution.py:38
  235.1 5.2 %collective-permute-start.20 = (bf16[512,128]{1,0:T(8,128)(2,1)}, bf16[512,128]{1,0:T(8,128)(2,1)S(1)}, u32[]{:S(2)}, u32[]{:S(2)}) collective-permute-start(bf16[512,128]{1,0:T(8,128)(2,1)} %get-tuple-element.78), channel_id=1, source_target_pairs={{0,64},{1,65},{2,66},{3,67},{4,68},{5,69},{6,70},{7,71},{8,72},{9,... | collective-permute-start | bytes 393224 | tf_op jit(solution)/shard_map/ppermute | solution.py:38

commit v8 on v7

--- a/solution.py
+++ b/solution.py
@@ -369,17 +369,22 @@
     )
 
 
-def pack_kernel(place, k_ref, v_ref, second_ref):
-    second_ref[0] = k_ref[...]
-    second_ref[1] = v_ref[...]
+def pack_kernel(place, k_ref, v_ref, second_ref, held_ref):
+    held_ref[...] = k_ref[...]
+
+    @pl.when(pl.program_id(0) == 1)
+    def _():
+        second_ref[0] = k_ref[...]
+        second_ref[1] = v_ref[...]
 
 
 def pack(place, k, v):
-    second = pl.BlockSpec((BLK, WIDTH), lambda i, place: (1, 0))
-    return call(
-        pack_kernel, "second_blocks", (1,), [second, second],
-        pl.BlockSpec((2, BLK, WIDTH), lambda i, place: (0, 0, 0)),
-        shape((2, BLK, WIDTH), bf16), [], (place, k, v),
+    block = pl.BlockSpec((BLK, WIDTH), lambda i, place: (i, 0))
+    return call(
+        pack_kernel, "second_blocks", (2,),
+        [block, pl.BlockSpec((BLK, WIDTH), lambda i, place: (1, 0))],
+        [pl.BlockSpec((2, BLK, WIDTH), lambda i, place: (0, 0, 0)), block],
+        [shape((2, BLK, WIDTH), bf16), shape(k.shape, bf16)], [], (place, k, v),
     )
 
 
@@ -422,7 +427,7 @@
     )
 
 
-def weight_kernel(place, turned_ref, g0, g1, g2, g3, *outs):
+def weight_kernel(place, turned_ref, g0, g1, g2, g3, after, *outs):
     owner = place[0] ^ pl.program_id(0)
     y = owner % 2 * 2 + pl.program_id(1)
     for part, ref in enumerate((g0, g1, g2, g3)):
@@ -433,7 +438,7 @@
                 out_ref[part // 2] = dot(turned_ref[...], ref[...], NN).astype(bf16)
 
 
-def weight_terms(place, turned, cotangents):
+def weight_terms(place, turned, cotangents, after):
     def piece(part):
         return pl.BlockSpec(
             (1024, 512),
@@ -444,9 +449,10 @@
 
     return call(
         weight_kernel, "weight_gradient", (4, 2),
-        [pl.BlockSpec((512, 1024), lambda i, half, place: (0, 0))] + [piece(p) for p in range(4)],
+        [pl.BlockSpec((512, 1024), lambda i, half, place: (0, 0))] + [piece(p) for p in range(4)]
+        + [ANY],
         [pl.BlockSpec((2, 512, 512), lambda i, half, place: (0, 0, 0))] * 4,
-        [shape((2, 512, 512), bf16)] * 4, [], (place, turned, *cotangents),
+        [shape((2, 512, 512), bf16)] * 4, [], (place, turned, *cotangents, after),
     )
 
 
@@ -495,11 +501,15 @@
 
 def far_columns(place, weight, after):
     return call(
-        copy_kernel, "projection_far", (2,),
-        [pl.BlockSpec((256, 2048), lambda i, place: (i, 1 - place[0] // 2)), ANY],
-        pl.BlockSpec((256, 2048), lambda i, place: (i, 0)),
-        shape((512, 2048), bf16), [], (place, weight, after),
-    )
+        copy_kernel, "projection_far", (1,),
+        [pl.BlockSpec((128, 2048), lambda i, place: (place[2], 1 - place[0] // 2)), ANY],
+        pl.BlockSpec((128, 2048), lambda i, place: (0, 0)),
+        shape((128, 2048), bf16), [], (place, weight, after),
+    )
+
+
+def along_z():
+    return [[line * 4 + z for z in range(4)] for line in range(8)]
 
 
 def core_kernel(place, own_ref, far_ref, far_rows, own_rows, after, out_ref):
@@ -557,11 +567,11 @@
     place = jnp.stack([tp, ctx // 4 % 4, ctx % 4, ctx // 16]).astype(jnp.int32)
 
     far_grad = to_x_hi(out_grad)
-    near_keys = along_ctx(keys, 1)
     near_pairs = [(s, s + 1) for s in range(31) if s != EDGE]
     near_values = lax.ppermute(values, "ctx", near_pairs + [(EDGE, 0)])
     core_grad = to_core(out_grad)
-    far_moved = first_hop(pack(place, keys, values), 1)
+    second, held_keys = pack(place, keys, values)
+    far_moved = first_hop(second, 1)
 
     query_block = ctx * 2 + jnp.arange(2, dtype=jnp.int32)[:, None] + jnp.zeros((1, WIN), jnp.int32)
     key_block = query_block - jnp.arange(WIN, dtype=jnp.int32)[None, :]
@@ -572,7 +582,8 @@
 
     [far_moved] = together([far_moved], [terms])
     far = second_hop(far_moved, 1)
-    [near_values] = together([near_values], [far_moved])
+    near_values, held_keys = together([near_values, held_keys], [far_moved])
+    near_keys = along_ctx(held_keys, 1)
     edge_values = lax.ppermute(near_values, "ctx", [(0, EDGE + 1)])
     near_keys, far, far_grad, edge_values, far_weight = together(
         [near_keys, far, far_grad, edge_values, far_weight], [far_moved]
@@ -582,11 +593,15 @@
     far_weight = to_x_hi(far_weight)
     behind = (flags, queries, near_keys, near_values, edge_values, far)
     attention, turned, log_sum = forward_behind(*behind, own_state, far)
-    [far_core_grad] = together([far_core_grad], [log_sum])
+    far_core_grad, far_weight = together([far_core_grad, far_weight], [log_sum])
+    far_weight = lax.all_gather(
+        far_weight, "ctx", axis=0, tiled=True, axis_index_groups=along_z()
+    )
     far_attention = to_x_hi(attention)
-    weight_parts = weight_terms(place, turned, (out_grad, core_grad, far_grad, far_core_grad))
+    attn_grad = grad_terms(place, 2, far_grad, far_core_grad, out_weight, terms, far_core_grad)
+    cotangents = (out_grad, core_grad, far_grad, far_core_grad)
+    weight_parts = weight_terms(place, turned, cotangents, attn_grad)
     weight_moved = over_y(weight_parts)
-    attn_grad = grad_terms(place, 2, far_grad, far_core_grad, out_weight, terms, weight_parts[3])
     near_back, far_back, dq, delta = backward_behind(
         *behind, attention, attn_grad, log_sum, weight_parts[3]
     )
@@ -594,25 +609,25 @@
         flags, queries, keys, values, attn_grad, log_sum, dq, delta, delta
     )
 
+    back_moved = first_hop(far_back, -1)
     far_attention, far_weight = together([far_attention, far_weight], [own])
     from_core = for_core(place, out_weight, far_weight, far_attention, attention, own)
 
-    *weight_moved, near_back, far_back, from_core = together(
-        [*weight_moved, near_back, far_back, from_core]
+    *weight_moved, near_back, back_moved, from_core = together(
+        [*weight_moved, near_back, back_moved, from_core]
     )
     near_back = along_ctx(near_back, -1)
-    back_moved = first_hop(far_back, -1)
+    far_back = second_hop(back_moved, -1)
     from_core = to_core(from_core)
     weight_pieces = pieces_by_z(place, [weight_parts[3], *weight_moved], weight_moved[0])
     weight_moved = [to_z(weight_pieces[s], s + 1) for s in (0, 2, 1)]
     mixed = mix(
         place, attention, far_attention, out_weight, far_weight, from_core, weight_pieces[3]
     )
-    [back_moved] = together([back_moved], [mixed])
-    far_back = second_hop(back_moved, -1)
-    kept, sent = weight_z_sum(place, [weight_pieces[3], *weight_moved], back_moved)
-    weight_grad = kept + to_x_lo(sent).astype(f32)
+    kept, sent = weight_z_sum(place, [weight_pieces[3], *weight_moved], mixed)
     key_grad, value_grad = finish(place, own, near_back, far_back, kept)
+    [sent] = together([to_x_lo(sent)], [key_grad])
+    weight_grad = kept + sent.astype(f32)
     return (mixed, query_grad, key_grad, value_grad, weight_grad)
 
 

time: 251 us -> 252 us (level)
  between operations: 0.83 us -> 14.2 us
  Pallas kernels: 96.5 us -> 86.4 us
  waiting for transfers between devices: 101 us -> 94.2 us
  starting transfers between devices: 43.4 us -> 48.7 us
    ppermute x2, waiting for transfers between devices: 24.3 us -> 2.89 us  [second_hop(): return lax.ppermute(value, 'ctx', [(m, t) for _, m, t in two_pairs(sign)])]
    ppermute x13, waiting for transfers between devices: 50.1 us -> 70.4 us  [move(): return lax.ppermute(value, AXES, pairs)]
    ppermute x2, waiting for transfers between devices: 0.01 us -> 15.2 us  [along_ctx(): return lax.ppermute(value, 'ctx', pairs)]
    ppermute x1, waiting for transfers between devices: 14.3 us -> 0.01 us  [per_device(): near_values = lax.ppermute(values, 'ctx', near_pairs + [(EDGE, 0)])]
    pallas_call x14, Pallas kernels: 96.5 us -> 86.4 us  [call(): pl.pallas_call(kernel, grid_spec=pltpu.PrefetchScalarGridSpec(num_scalar_...]
    ppermute x2, waiting for transfers between devices: 12 us -> 5.64 us  [first_hop(): return lax.ppermute(value, 'ctx', [(s, m) for s, m, _ in two_pairs(sign)])]
    ppermute x13, starting transfers between devices: 20.1 us -> 25.6 us  [move(): return lax.ppermute(value, AXES, pairs)]
    ppermute x2, starting transfers between devices: 8.61 us -> 3.86 us  [along_ctx(): return lax.ppermute(value, 'ctx', pairs)]
  transfers between devices with their start and end apart: 21 -> 22, of which waited for: 7 -> 9; matrix products, arithmetic and copies ran while one was open for 2% -> 2% of each run, Pallas kernels for 37% -> 35%
where the time goes in v8:
time: 252 us; the launch traced here: 249 us
  waiting for transfers between devices  94.2 us (37%)
  Pallas kernels  86.4 us (34%)
  starting transfers between devices  48.7 us (19%)
  between operations  14.2 us (6%)
  other arithmetic  3.59 us (1%)
    pallas_call x14, Pallas kernels, call(): pl.pallas_call(kernel, grid_spec=pltpu.PrefetchScalarGridSpec(num_scalar_...  86.4 us
    ppermute x13, waiting for transfers between devices, move(): return lax.ppermute(value, AXES, pairs)  70.4 us
    ppermute x13, starting transfers between devices, move(): return lax.ppermute(value, AXES, pairs)  25.6 us
    ppermute x2, waiting for transfers between devices, along_ctx(): return lax.ppermute(value, 'ctx', pairs)  15.2 us
    ppermute x2, starting transfers between devices, second_hop(): return lax.ppermute(value, 'ctx', [(m, t) for _, m, t in two_pairs(sign)])  8.15 us
    ppermute x2, waiting for transfers between devices, first_hop(): return lax.ppermute(value, 'ctx', [(s, m) for s, m, _ in two_pairs(sign)])  5.64 us
    ppermute x2, starting transfers between devices, first_hop(): return lax.ppermute(value, 'ctx', [(s, m) for s, m, _ in two_pairs(sign)])  5.54 us
  transfers between devices with their start and end apart: 22, of which 9 were waited for; matrix products, arithmetic and copies ran while one was open for 2% of the time, Pallas kernels for 35%

profile of v8, /device:TPU:30, one launch (start us, length us, event | category | flops | bytes accessed | tf_op | source)
XLA Modules:
  0.0 249.2 jit_solution(13704736284425292415)
XLA Ops:
  7.2 0.1 collective-permute-start.2
  7.3 1.5 collective-permute-start.5
  8.8 3.8 %collective-permute-start = (bf16[1024,512]{1,0:T(8,128)(2,1)}, bf16[1024,512]{1,0:T(8,128)(2,1)}, u32[]{:S(2)}, u32[]{:S(2)}) collective-permute-start(bf16[1024,512]{1,0:T(8,128)(2,1)} %v_ref.5), channel_id=1, source_target_pairs={{0,4},{4,8},{8,12},{12,16},{16,20},{20,24},{24,28},{28,32},{32,36}... | collective-permute-start | bytes 3145736 | tf_op jit(solution)/shard_map/ppermute | solution.py:571
  12.7 0.7 pad_add_fusion.place
  13.3 3.3 %second_blocks.1 = (bf16[2,512,512]{2,1,0:T(8,128)(2,1)}, bf16[1024,512]{1,0:T(8,128)(2,1)}) custom-call(s32[4]{0:T(128)} %pad_add_fusion.place, bf16[1024,512]{1,0:T(8,128)(2,1)} %k_ref.5, bf16[1024,512]{1,0:T(8,128)(2,1)} %v_ref.5), custom_call_target="tpu_custom_call" | custom-call | flops 1 | bytes 1 | tf_op jit(solution)/shard_map/second_blocks/pallas_call | solution.py:297
  16.6 3.4 %collective-permute-start.1 = (bf16[2,512,512]{2,1,0:T(8,128)(2,1)}, bf16[2,512,512]{2,1,0:T(8,128)(2,1)}, u32[]{:S(2)}, u32[]{:S(2)}) collective-permute-start(bf16[2,512,512]{2,1,0:T(8,128)(2,1)} %get-tuple-element.49), channel_id=1, source_target_pairs={{0,12},{4,0},{8,4},{12,8},{16,28},{20,16},{24,20},{28,24},{32,44},... | collective-permute-start | bytes 3145736 | tf_op jit(solution)/shard_map/ppermute | solution.py:79
  20.0 0.8 bitcast_add_fusion
  20.8 0.7 slice_bitcast_fusion
  21.5 0.2 and_reduce_fusion.1
  21.7 0.8 fusion
  22.5 0.2 and_reduce_fusion
  22.7 0.6 reshape.60.flags
  23.3 5.8 %forward_own.1 = (f32[512,1024]{1,0:T(8,128)}, f32[4,2,512]{2,1,0:T(2,128)}, f32[4,2,512]{2,1,0:T(2,128)}) custom-call(s32[8]{0:T(128)} %reshape.60.flags, bf16[1024,512]{1,0:T(8,128)(2,1)} %q_ref.7, bf16[1024,512]{1,0:T(8,128)(2,1)} %k_ref.5, bf16[1024,512]{1,0:T(8,128)(2,1)} %v_ref.5, bf16[1024,512]{1,0:T(8,128)(2,1)} %k_ref.5), custom_call_target="tpu_custom_call" | custom-call | flops 1 | bytes 1 | tf_op jit(solution)/shard_map/forward_own/pallas_call | solution.py:297
  29.1 2.5 %projection_far.1.rest_0_.refs_4_ = bf16[128,2048]{1,0:T(8,128)(2,1)} custom-call(s32[4]{0:T(128)} %pad_add_fusion.place, bf16[512,4096]{1,0:T(8,128)(2,1)} %w_own.1, f32[4,2,512]{2,1,0:T(2,128)} %get-tuple-element.50.refs_0_.top_in), custom_call_target="tpu_custom_call" | custom-call | flops 1 | bytes 1 | tf_op jit(solution)/shard_map/projection_far/pallas_call | solution.py:297
  31.6 6.5 %projection_backward.2.refs_1_.rest_0_ = f32[1024,512]{1,0:T(8,128)} custom-call(s32[4]{0:T(128)} %pad_add_fusion.place, bf16[1024,1024]{1,0:T(8,128)(2,1)} %g0.1, bf16[1024,1024]{1,0:T(8,128)(2,1)} %collective-permute-done.2.b_ref.g1, bf16[512,4096]{1,0:T(8,128)(2,1)} %w_own.1, bf16[512,4096]{1,0:T(8,128)(2,1)} %w_own.1, ...), custom_call_target="tpu_custom_call" | custom-call | flops 1 | bytes 1 | tf_op jit(solution)/shard_map/projection_backward/pallas_call | solution.py:297
  38.1 5.6 %collective-permute-done.1.refs_0_ = bf16[2,512,512]{2,1,0:T(8,128)(2,1)} collective-permute-done((bf16[2,512,512]{2,1,0:T(8,128)(2,1)}, bf16[2,512,512]{2,1,0:T(8,128)(2,1)}, u32[]{:S(2)}, u32[]{:S(2)}) %collective-permute-start.1) | collective-permute-done | bytes 1048608 | tf_op jit(solution)/shard_map/ppermute | solution.py:79
  43.7 1.9 collective-permute-start.3
  45.7 1.7 collective-permute-start.6
  47.3 4.2 %collective-permute-start.4 = (bf16[2,512,512]{2,1,0:T(8,128)(2,1)}, bf16[2,512,512]{2,1,0:T(8,128)(2,1)}, u32[]{:S(2)}, u32[]{:S(2)}) collective-permute-start(bf16[2,512,512]{2,1,0:T(8,128)(2,1)} %order.7.refs_2_.refs_5_), channel_id=1, source_target_pairs={{12,8},{0,12},{4,16},{8,20},{28,24},{16,28},{20,32},{24,36},{44,40... | collective-permute-start | bytes 3145736 | tf_op jit(solution)/shard_map/ppermute | solution.py:83
  51.6 5.6 %collective-permute-done.5.refs_2_ = bf16[1024,1024]{1,0:T(8,128)(2,1)} collective-permute-done((bf16[1024,1024]{1,0:T(8,128)(2,1)}, bf16[1024,1024]{1,0:T(8,128)(2,1)}, u32[]{:S(2)}, u32[]{:S(2)}) %collective-permute-start.5) | collective-permute-done | bytes 2097184 | tf_op jit(solution)/shard_map/ppermute | solution.py:38
  57.2 15.2 %collective-permute-done.3.refs_0_ = bf16[1024,512]{1,0:T(8,128)(2,1)} collective-permute-done((bf16[1024,512]{1,0:T(8,128)(2,1)}, bf16[1024,512]{1,0:T(8,128)(2,1)}, u32[]{:S(2)}, u32[]{:S(2)}) %collective-permute-start.3) | collective-permute-done | bytes 1048608 | tf_op jit(solution)/shard_map/ppermute | solution.py:66
  72.4 2.9 %collective-permute-done.4.refs_1_ = bf16[2,512,512]{2,1,0:T(8,128)(2,1)} collective-permute-done((bf16[2,512,512]{2,1,0:T(8,128)(2,1)}, bf16[2,512,512]{2,1,0:T(8,128)(2,1)}, u32[]{:S(2)}, u32[]{:S(2)}) %collective-permute-start.4) | collective-permute-done | bytes 1048608 | tf_op jit(solution)/shard_map/ppermute | solution.py:83
  75.3 2.1 collective-permute-start.8
  77.4 5.7 %forward_behind.1 = (bf16[1024,512]{1,0:T(8,128)(2,1)}, bf16[512,1024]{1,0:T(8,128)(2,1)}, f32[4,2,512]{2,1,0:T(2,128)}) custom-call(s32[8]{0:T(128)} %reshape.60.flags, bf16[1024,512]{1,0:T(8,128)(2,1)} %q_ref.7, bf16[1024,512]{1,0:T(8,128)(2,1)} %get-tuple-element.53.k1_ref, bf16[1024,512]{1,0:T(8,128)(2,1)} %get-tuple-element.52.v1_ref, ...), custom_call_target="tpu_custom_call" | custom-call | flops 1 | bytes 1 | tf_op jit(solution)/shard_map/forward_behind/pallas_call | solution.py:297
  83.1 8.3 %collective-permute-done.8.refs_1_ = bf16[128,2048]{1,0:T(8,128)(2,1)} collective-permute-done((bf16[128,2048]{1,0:T(8,128)(2,1)}, bf16[128,2048]{1,0:T(8,128)(2,1)}, u32[]{:S(2)}, u32[]{:S(2)}) %collective-permute-start.8) | collective-permute-done | bytes 524320 | tf_op jit(solution)/shard_map/ppermute | solution.py:38
  91.5 2.4 collective-permute-start.13
  93.9 6.9 %projection_backward.3.after.grad_ref = bf16[1024,512]{1,0:T(8,128)(2,1)} custom-call(s32[4]{0:T(128)} %pad_add_fusion.place, bf16[1024,1024]{1,0:T(8,128)(2,1)} %get-tuple-element.60.a_ref.g2, bf16[1024,1024]{1,0:T(8,128)(2,1)} %get-tuple-element.63.b_ref.rest_1_.g3, bf16[512,4096]{1,0:T(8,128)(2,1)} %w_own.1, bf16[512,4096]{1,0:T(8,128)(2,1)} %w_own.1, ...), custom_call_target="tpu_custom_call" | custom-call | flops 1 | bytes 1 | tf_op jit(solution)/shard_map/projection_backward/pallas_call | solution.py:297
  100.8 13.5 %weight_gradient.1 = (bf16[2,512,512]{2,1,0:T(8,128)(2,1)}, bf16[2,512,512]{2,1,0:T(8,128)(2,1)}, bf16[2,512,512]{2,1,0:T(8,128)(2,1)}, bf16[2,512,512]{2,1,0:T(8,128)(2,1)}) custom-call(s32[4]{0:T(128)} %pad_add_fusion.place, bf16[512,1024]{1,0:T(8,128)(2,1)} %get-tuple-element.59.turned_ref, bf16[1024,1024]{1,0:T(8,128)(2,1)} %g0.1, ...), custom_call_target="tpu_custom_call" | custom-call | flops 1 | bytes 1 | tf_op jit(solution)/shard_map/weight_gradient/pallas_call | solution.py:297
  114.2 10.0 %collective-permute-start.9 = (bf16[2,512,512]{2,1,0:T(8,128)(2,1)}, bf16[2,512,512]{2,1,0:T(8,128)(2,1)}, u32[]{:S(2)}, u32[]{:S(2)}) collective-permute-start(bf16[2,512,512]{2,1,0:T(8,128)(2,1)} %get-tuple-element.64), channel_id=1, source_target_pairs={{0,16},{1,17},{2,18},{3,19},{4,20},{5,21},{6,22},{7,23},{8,24},{9,... | collective-permute-start | bytes 3145736 | tf_op jit(solution)/shard_map/ppermute | solution.py:38
  124.2 1.5 collective-permute-start.11
  125.8 7.3 %backward_behind.1 = (bf16[2,1024,512]{2,1,0:T(8,128)(2,1)}, bf16[2,512,512]{2,1,0:T(8,128)(2,1)}, f32[512,1024]{1,0:T(8,128)}, f32[4,2,512]{2,1,0:T(2,128)}) custom-call(s32[8]{0:T(128)} %reshape.60.flags, bf16[1024,512]{1,0:T(8,128)(2,1)} %q_ref.7, bf16[1024,512]{1,0:T(8,128)(2,1)} %get-tuple-element.53.k1_ref, ...), custom_call_target="tpu_custom_call" | custom-call | flops 1 | bytes 1 | tf_op jit(solution)/shard_map/backward_behind/pallas_call | solution.py:297
  133.0 2.1 collective-permute-start.12
  135.2 7.9 %backward_own.1 = (bf16[1024,512]{1,0:T(8,128)(2,1)}, bf16[2,1024,512]{2,1,0:T(8,128)(2,1)}) custom-call(s32[8]{0:T(128)} %reshape.60.flags, bf16[1024,512]{1,0:T(8,128)(2,1)} %q_ref.7, bf16[1024,512]{1,0:T(8,128)(2,1)} %k_ref.5, bf16[1024,512]{1,0:T(8,128)(2,1)} %v_ref.5, bf16[1024,512]{1,0:T(8,128)(2,1)} %projection_backward.3.after.grad_ref, ...), custom_call_target="tpu_custom_call" | custom-call | flops 1 | bytes 1 | tf_op jit(solution)/shard_map/backward_own/pallas_call | solution.py:297
  143.2 5.1 %for_core.1.refs_5_ = bf16[4,512,1024]{2,1,0:T(8,128)(2,1)} custom-call(s32[4]{0:T(128)} %pad_add_fusion.place, bf16[512,4096]{1,0:T(8,128)(2,1)} %w_own.1, bf16[512,2048]{1,0:T(8,128)(2,1)} %get-tuple-element.74.far_ref.w_far, bf16[1024,512]{1,0:T(8,128)(2,1)} %get-tuple-element.75.far_rows.far, bf16[1024,512]{1,0:T(8,128)(2,1)} %get-tuple-element.58.out_ref.own_rows.own, ...), custom_call_target="tpu_custom_call" | custom-call | flops 1 | bytes 1 | tf_op jit(solution)/shard_map/for_core/pallas_call | solution.py:297
  148.2 20.6 %collective-permute-done.9.refs_0_ = bf16[2,512,512]{2,1,0:T(8,128)(2,1)} collective-permute-done((bf16[2,512,512]{2,1,0:T(8,128)(2,1)}, bf16[2,512,512]{2,1,0:T(8,128)(2,1)}, u32[]{:S(2)}, u32[]{:S(2)}) %collective-permute-start.9) | collective-permute-done | bytes 1048608 | tf_op jit(solution)/shard_map/ppermute | solution.py:38
  168.9 3.4 %collective-permute-done.10.refs_1_ = bf16[2,512,512]{2,1,0:T(8,128)(2,1)} collective-permute-done((bf16[2,512,512]{2,1,0:T(8,128)(2,1)}, bf16[2,512,512]{2,1,0:T(8,128)(2,1)}, u32[]{:S(2)}, u32[]{:S(2)}) %collective-permute-start.10) | collective-permute-done | bytes 1048608 | tf_op jit(solution)/shard_map/ppermute | solution.py:38
  172.4 1.9 collective-permute-start.15
  174.3 3.9 %collective-permute-start.16 = (bf16[2,512,512]{2,1,0:T(8,128)(2,1)}, bf16[2,512,512]{2,1,0:T(8,128)(2,1)}, u32[]{:S(2)}, u32[]{:S(2)}) collective-permute-start(bf16[2,512,512]{2,1,0:T(8,128)(2,1)} %get-tuple-element.83), channel_id=1, source_target_pairs={{12,0},{0,4},{20,8},{24,12},{28,16},{16,20},{36,24},{40,28},{44,32... | collective-permute-start | bytes 3145736 | tf_op jit(solution)/shard_map/ppermute | solution.py:83
  178.2 4.8 %weight_by_z.1 = (bf16[2,512,128]{2,1,0:T(8,128)(2,1)}, bf16[2,512,128]{2,1,0:T(8,128)(2,1)}, bf16[2,512,128]{2,1,0:T(8,128)(2,1)}, bf16[2,512,128]{2,1,0:T(8,128)(2,1)}) custom-call(s32[4]{0:T(128)} %pad_add_fusion.place, bf16[2,512,512]{2,1,0:T(8,128)(2,1)} %get-tuple-element.67.after.a, bf16[2,512,512]{2,1,0:T(8,128)(2,1)} %get-tuple-element.77.b.after, ...), custom_call_target="tpu_custom_call" | custom-call | flops 1 | bytes 1 | tf_op jit(solution)/shard_map/weight_by_z/pallas_call | solution.py:297
  183.0 3.2 %collective-permute-start.18 = (bf16[2,512,128]{2,1,0:T(8,128)(2,1)}, bf16[2,512,128]{2,1,0:T(8,128)(2,1)}, u32[]{:S(2)}, u32[]{:S(2)}) collective-permute-start(bf16[2,512,128]{2,1,0:T(8,128)(2,1)} %get-tuple-element.85), channel_id=1, source_target_pairs={{0,12},{1,13},{2,14},{3,15},{4,0},{5,1},{6,2},{7,3},{8,4},{9,5},{1... | collective-permute-start | bytes 786440 | tf_op jit(solution)/shard_map/ppermute | solution.py:38
  186.3 0.4 collective-permute-start.19
  186.7 9.4 %projection.1.after = bf16[1024,1024]{1,0:T(8,128)(2,1)} custom-call(s32[4]{0:T(128)} %pad_add_fusion.place, bf16[1024,512]{1,0:T(8,128)(2,1)} %get-tuple-element.58.out_ref.own_rows.own, bf16[4,512,1024]{2,1,0:T(8,128)(2,1)} %collective-permute-done.14.core.far_core.w_core, bf16[1024,512]{1,0:T(8,128)(2,1)} %get-tuple-element.75.far_rows.far, ...), custom_call_target="tpu_custom_call" | custom-call | flops 1 | bytes 1 | tf_op jit(solution)/shard_map/projection/pallas_call | solution.py:297
  196.1 18.4 %collective-permute-done.17.b_ref = bf16[2,512,128]{2,1,0:T(8,128)(2,1)} collective-permute-done((bf16[2,512,128]{2,1,0:T(8,128)(2,1)}, bf16[2,512,128]{2,1,0:T(8,128)(2,1)}, u32[]{:S(2)}, u32[]{:S(2)}) %collective-permute-start.17) | collective-permute-done | bytes 262176 | tf_op jit(solution)/shard_map/ppermute | solution.py:38
  214.5 14.1 %collective-permute-done.18.c_ref = bf16[2,512,128]{2,1,0:T(8,128)(2,1)} collective-permute-done((bf16[2,512,128]{2,1,0:T(8,128)(2,1)}, bf16[2,512,128]{2,1,0:T(8,128)(2,1)}, u32[]{:S(2)}, u32[]{:S(2)}) %collective-permute-start.18) | collective-permute-done | bytes 262176 | tf_op jit(solution)/shard_map/ppermute | solution.py:38
  228.6 2.6 %weight_z_sum.1 = (f32[512,128]{1,0:T(8,128)}, bf16[512,128]{1,0:T(8,128)(2,1)}) custom-call(s32[4]{0:T(128)} %pad_add_fusion.place, bf16[2,512,128]{2,1,0:T(8,128)(2,1)} %get-tuple-element.80.after.a_ref, bf16[2,512,128]{2,1,0:T(8,128)(2,1)} %collective-permute-done.17.b_ref, bf16[2,512,128]{2,1,0:T(8,128)(2,1)} %collective-permute-done.18.c_ref, ...), custom_call_target="tpu_custom_call" | custom-call | flops 1 | bytes 1 | tf_op jit(solution)/shard_map/weight_z_sum/pallas_call | solution.py:297
  231.3 4.2 %collective-permute-start.20 = (bf16[512,128]{1,0:T(8,128)(2,1)}, bf16[512,128]{1,0:T(8,128)(2,1)}, u32[]{:S(2)}, u32[]{:S(2)}) collective-permute-start(bf16[512,128]{1,0:T(8,128)(2,1)} %get-tuple-element.90), channel_id=1, source_target_pairs={{0,64},{1,65},{2,66},{3,67},{4,68},{5,69},{6,70},{7,71},{8,72},{9,... | collective-permute-start | bytes 393224 | tf_op jit(solution)/shard_map/ppermute | solution.py:38
  235.5 5.1 %key_value_sum.1 = (bf16[1024,512]{1,0:T(8,128)(2,1)}, bf16[1024,512]{1,0:T(8,128)(2,1)}) custom-call(s32[4]{0:T(128)} %pad_add_fusion.place, bf16[2,1024,512]{2,1,0:T(8,128)(2,1)} %get-tuple-element.73.refs_2_.after.own_ref, bf16[2,1024,512]{2,1,0:T(8,128)(2,1)} %collective-permute-done.15.near_ref, bf16[2,512,512]{2,1,0:T(8,128)(2,1)} %collective-permute-done.16.far_ref, ...), custom_call_target="tpu_custom_call" | custom-call | flops 1 | bytes 1 | tf_op jit(solution)/shard_map/key_value_sum/pallas_call | solution.py:297
  240.6 1.7 convert_add_fusion
  (29 shorter events, 0.3 us)
Async XLA Ops:
  7.2 136.0 %all-gather.2.cloned.1.call-start = ((), (), s32[]{:S(2)}) async-start(), calls=%async_computation | async-start | bytes 2621440 | tf_op jit(solution)/shard_map/all_gather | solution.py:597
  7.2 24.4 %collective-permute-start.2 = (bf16[1024,1024]{1,0:T(8,128)(2,1)}, bf16[1024,1024]{1,0:T(8,128)(2,1)}, u32[]{:S(2)}, u32[]{:S(2)}) collective-permute-start(bf16[1024,1024]{1,0:T(8,128)(2,1)} %g0.1), channel_id=1, source_target_pairs={{0,1},{1,0},{2,3},{3,2},{4,5},{5,4},{6,7},{7,6},{8,9},{9,8},{10,11... | collective-permute-start | bytes 6291464 | tf_op jit(solution)/shard_map/ppermute | solution.py:38
  7.3 49.9 %collective-permute-start.5 = (bf16[1024,1024]{1,0:T(8,128)(2,1)}, bf16[1024,1024]{1,0:T(8,128)(2,1)}, u32[]{:S(2)}, u32[]{:S(2)}) collective-permute-start(bf16[1024,1024]{1,0:T(8,128)(2,1)} %g0.1), channel_id=1, source_target_pairs={{0,2},{1,3},{2,0},{3,1},{4,6},{5,7},{6,4},{7,5},{8,10},{9,11},{10,... | collective-permute-start | bytes 6291464 | tf_op jit(solution)/shard_map/ppermute | solution.py:38
  8.8 34.9 %collective-permute-start = (bf16[1024,512]{1,0:T(8,128)(2,1)}, bf16[1024,512]{1,0:T(8,128)(2,1)}, u32[]{:S(2)}, u32[]{:S(2)}) collective-permute-start(bf16[1024,512]{1,0:T(8,128)(2,1)} %v_ref.5), channel_id=1, source_target_pairs={{0,4},{4,8},{8,12},{12,16},{16,20},{20,24},{24,28},{28,32},{32,36}... | collective-permute-start | bytes 3145736 | tf_op jit(solution)/shard_map/ppermute | solution.py:571
  16.6 27.1 %collective-permute-start.1 = (bf16[2,512,512]{2,1,0:T(8,128)(2,1)}, bf16[2,512,512]{2,1,0:T(8,128)(2,1)}, u32[]{:S(2)}, u32[]{:S(2)}) collective-permute-start(bf16[2,512,512]{2,1,0:T(8,128)(2,1)} %get-tuple-element.49), channel_id=1, source_target_pairs={{0,12},{4,0},{8,4},{12,8},{16,28},{20,16},{24,20},{28,24},{32,44},... | collective-permute-start | bytes 3145736 | tf_op jit(solution)/shard_map/ppermute | solution.py:79
  43.7 28.7 %collective-permute-start.3 = (bf16[1024,512]{1,0:T(8,128)(2,1)}, bf16[1024,512]{1,0:T(8,128)(2,1)}, u32[]{:S(2)}, u32[]{:S(2)}) collective-permute-start(bf16[1024,512]{1,0:T(8,128)(2,1)} %get-tuple-element.51), channel_id=1, source_target_pairs={{0,4},{4,8},{8,12},{12,16},{16,20},{20,24},{24,28},{28,32},{32,36}... | collective-permute-start | bytes 3145736 | tf_op jit(solution)/shard_map/ppermute | solution.py:66
  45.7 26.7 %collective-permute-start.6 = (bf16[1024,512]{1,0:T(8,128)(2,1)}, bf16[1024,512]{1,0:T(8,128)(2,1)}, u32[]{:S(2)}, u32[]{:S(2)}) collective-permute-start(bf16[1024,512]{1,0:T(8,128)(2,1)} %get-tuple-element.52.v1_ref), channel_id=1, source_target_pairs={{0,64},{1,65},{2,66},{3,67}} | collective-permute-start | bytes 3145736 | tf_op jit(solution)/shard_map/ppermute | solution.py:587
  47.3 27.9 %collective-permute-start.4 = (bf16[2,512,512]{2,1,0:T(8,128)(2,1)}, bf16[2,512,512]{2,1,0:T(8,128)(2,1)}, u32[]{:S(2)}, u32[]{:S(2)}) collective-permute-start(bf16[2,512,512]{2,1,0:T(8,128)(2,1)} %order.7.refs_2_.refs_5_), channel_id=1, source_target_pairs={{12,8},{0,12},{4,16},{8,20},{28,24},{16,28},{20,32},{24,36},{44,40... | collective-permute-start | bytes 3145736 | tf_op jit(solution)/shard_map/ppermute | solution.py:83
  75.3 16.2 %collective-permute-start.7 = (bf16[1024,1024]{1,0:T(8,128)(2,1)}, bf16[1024,1024]{1,0:T(8,128)(2,1)}, u32[]{:S(2)}, u32[]{:S(2)}) collective-permute-start(bf16[1024,1024]{1,0:T(8,128)(2,1)} %get-tuple-element.60.a_ref.g2), channel_id=1, source_target_pairs={{0,1},{1,0},{2,3},{3,2},{4,5},{5,4},{6,7},{7,6},{8,9},{9,8},{10,11... | collective-permute-start | bytes 6291464 | tf_op jit(solution)/shard_map/ppermute | solution.py:38
  75.3 16.2 %collective-permute-start.8 = (bf16[128,2048]{1,0:T(8,128)(2,1)}, bf16[128,2048]{1,0:T(8,128)(2,1)}, u32[]{:S(2)}, u32[]{:S(2)}) collective-permute-start(bf16[128,2048]{1,0:T(8,128)(2,1)} %get-tuple-element.61), channel_id=1, source_target_pairs={{0,2},{1,3},{2,0},{3,1},{4,6},{5,7},{6,4},{7,5},{8,10},{9,11},{10,... | collective-permute-start | bytes 1572872 | tf_op jit(solution)/shard_map/ppermute | solution.py:38
  91.5 51.6 %collective-permute-start.13 = (bf16[1024,512]{1,0:T(8,128)(2,1)}, bf16[1024,512]{1,0:T(8,128)(2,1)}, u32[]{:S(2)}, u32[]{:S(2)}) collective-permute-start(bf16[1024,512]{1,0:T(8,128)(2,1)} %get-tuple-element.58.out_ref.own_rows.own), channel_id=1, source_target_pairs={{0,2},{1,3},{2,0},{3,1},{4,6},{5,7},{6,4},{7,5},{8,10},{9,11},{10,... | collective-permute-start | bytes 3145736 | tf_op jit(solution)/shard_map/ppermute | solution.py:38
  114.2 54.6 %collective-permute-start.9 = (bf16[2,512,512]{2,1,0:T(8,128)(2,1)}, bf16[2,512,512]{2,1,0:T(8,128)(2,1)}, u32[]{:S(2)}, u32[]{:S(2)}) collective-permute-start(bf16[2,512,512]{2,1,0:T(8,128)(2,1)} %get-tuple-element.64), channel_id=1, source_target_pairs={{0,16},{1,17},{2,18},{3,19},{4,20},{5,21},{6,22},{7,23},{8,24},{9,... | collective-permute-start | bytes 3145736 | tf_op jit(solution)/shard_map/ppermute | solution.py:38
  124.2 48.0 %collective-permute-start.10 = (bf16[2,512,512]{2,1,0:T(8,128)(2,1)}, bf16[2,512,512]{2,1,0:T(8,128)(2,1)}, u32[]{:S(2)}, u32[]{:S(2)}) collective-permute-start(bf16[2,512,512]{2,1,0:T(8,128)(2,1)} %get-tuple-element.65), channel_id=1, source_target_pairs={{0,48},{1,49},{2,50},{3,51},{4,52},{5,53},{6,54},{7,55},{8,56},{9,... | collective-permute-start | bytes 3145736 | tf_op jit(solution)/shard_map/ppermute | solution.py:38
  124.2 48.0 %collective-permute-start.11 = (bf16[2,512,512]{2,1,0:T(8,128)(2,1)}, bf16[2,512,512]{2,1,0:T(8,128)(2,1)}, u32[]{:S(2)}, u32[]{:S(2)}) collective-permute-start(bf16[2,512,512]{2,1,0:T(8,128)(2,1)} %get-tuple-element.66), channel_id=1, source_target_pairs={{0,32},{1,33},{2,34},{3,35},{4,36},{5,37},{6,38},{7,39},{8,40},{9,... | collective-permute-start | bytes 3145736 | tf_op jit(solution)/shard_map/ppermute | solution.py:38
  133.0 39.2 %collective-permute-start.12 = (bf16[2,512,512]{2,1,0:T(8,128)(2,1)}, bf16[2,512,512]{2,1,0:T(8,128)(2,1)}, u32[]{:S(2)}, u32[]{:S(2)}) collective-permute-start(bf16[2,512,512]{2,1,0:T(8,128)(2,1)} %get-tuple-element.69), channel_id=1, source_target_pairs={{8,12},{12,0},{16,20},{20,24},{24,28},{28,16},{32,36},{36,40},{40,... | collective-permute-start | bytes 3145736 | tf_op jit(solution)/shard_map/ppermute | solution.py:79
  172.3 14.0 %collective-permute-start.14 = (bf16[4,512,1024]{2,1,0:T(8,128)(2,1)}, bf16[4,512,1024]{2,1,0:T(8,128)(2,1)}, u32[]{:S(2)}, u32[]{:S(2)}) collective-permute-start(bf16[4,512,1024]{2,1,0:T(8,128)(2,1)} %get-tuple-element.76), channel_id=1, source_target_pairs={{0,1},{1,0},{2,3},{3,2},{4,5},{5,4},{6,7},{7,6},{8,9},{9,8},{10,11... | collective-permute-start | bytes 12582920 | tf_op jit(solution)/shard_map/ppermute | solution.py:38
  172.4 63.1 %collective-permute-start.15 = (bf16[2,1024,512]{2,1,0:T(8,128)(2,1)}, bf16[2,1024,512]{2,1,0:T(8,128)(2,1)}, u32[]{:S(2)}, u32[]{:S(2)}) collective-permute-start(bf16[2,1024,512]{2,1,0:T(8,128)(2,1)} %get-tuple-element.82), channel_id=1, source_target_pairs={{4,0},{8,4},{12,8},{16,12},{20,16},{24,20},{28,24},{32,28},{36,32}... | collective-permute-start | bytes 6291464 | tf_op jit(solution)/shard_map/ppermute | solution.py:66
  174.3 61.2 %collective-permute-start.16 = (bf16[2,512,512]{2,1,0:T(8,128)(2,1)}, bf16[2,512,512]{2,1,0:T(8,128)(2,1)}, u32[]{:S(2)}, u32[]{:S(2)}) collective-permute-start(bf16[2,512,512]{2,1,0:T(8,128)(2,1)} %get-tuple-element.83), channel_id=1, source_target_pairs={{12,0},{0,4},{20,8},{24,12},{28,16},{16,20},{36,24},{40,28},{44,32... | collective-permute-start | bytes 3145736 | tf_op jit(solution)/shard_map/ppermute | solution.py:83
  183.0 31.5 %collective-permute-start.17 = (bf16[2,512,128]{2,1,0:T(8,128)(2,1)}, bf16[2,512,128]{2,1,0:T(8,128)(2,1)}, u32[]{:S(2)}, u32[]{:S(2)}) collective-permute-start(bf16[2,512,128]{2,1,0:T(8,128)(2,1)} %get-tuple-element.84), channel_id=1, source_target_pairs={{0,4},{1,5},{2,6},{3,7},{4,8},{5,9},{6,10},{7,11},{8,12},{9,13},{1... | collective-permute-start | bytes 786440 | tf_op jit(solution)/shard_map/ppermute | solution.py:38
  183.0 45.6 %collective-permute-start.18 = (bf16[2,512,128]{2,1,0:T(8,128)(2,1)}, bf16[2,512,128]{2,1,0:T(8,128)(2,1)}, u32[]{:S(2)}, u32[]{:S(2)}) collective-permute-start(bf16[2,512,128]{2,1,0:T(8,128)(2,1)} %get-tuple-element.85), channel_id=1, source_target_pairs={{0,12},{1,13},{2,14},{3,15},{4,0},{5,1},{6,2},{7,3},{8,4},{9,5},{1... | collective-permute-start | bytes 786440 | tf_op jit(solution)/shard_map/ppermute | solution.py:38
  186.3 42.3 %collective-permute-start.19 = (bf16[2,512,128]{2,1,0:T(8,128)(2,1)}, bf16[2,512,128]{2,1,0:T(8,128)(2,1)}, u32[]{:S(2)}, u32[]{:S(2)}) collective-permute-start(bf16[2,512,128]{2,1,0:T(8,128)(2,1)} %get-tuple-element.86), channel_id=1, source_target_pairs={{0,8},{1,9},{2,10},{3,11},{4,12},{5,13},{6,14},{7,15},{8,0},{9,1},... | collective-permute-start | bytes 786440 | tf_op jit(solution)/shard_map/ppermute | solution.py:38
  231.3 9.4 %collective-permute-start.20 = (bf16[512,128]{1,0:T(8,128)(2,1)}, bf16[512,128]{1,0:T(8,128)(2,1)}, u32[]{:S(2)}, u32[]{:S(2)}) collective-permute-start(bf16[512,128]{1,0:T(8,128)(2,1)} %get-tuple-element.90), channel_id=1, source_target_pairs={{0,64},{1,65},{2,66},{3,67},{4,68},{5,69},{6,70},{7,71},{8,72},{9,... | collective-permute-start | bytes 393224 | tf_op jit(solution)/shard_map/ppermute | solution.py:38
Sparse Core Ops, SparseCore 0:
  91.6 36.6 all-gather.1

commit v9 on v8

--- a/solution.py
+++ b/solution.py
@@ -501,15 +501,11 @@
 
 def far_columns(place, weight, after):
     return call(
-        copy_kernel, "projection_far", (1,),
-        [pl.BlockSpec((128, 2048), lambda i, place: (place[2], 1 - place[0] // 2)), ANY],
-        pl.BlockSpec((128, 2048), lambda i, place: (0, 0)),
-        shape((128, 2048), bf16), [], (place, weight, after),
-    )
-
-
-def along_z():
-    return [[line * 4 + z for z in range(4)] for line in range(8)]
+        copy_kernel, "projection_far", (2,),
+        [pl.BlockSpec((256, 2048), lambda i, place: (i, 1 - place[0] // 2)), ANY],
+        pl.BlockSpec((256, 2048), lambda i, place: (i, 0)),
+        shape((512, 2048), bf16), [], (place, weight, after),
+    )
 
 
 def core_kernel(place, own_ref, far_ref, far_rows, own_rows, after, out_ref):
@@ -593,10 +589,7 @@
     far_weight = to_x_hi(far_weight)
     behind = (flags, queries, near_keys, near_values, edge_values, far)
     attention, turned, log_sum = forward_behind(*behind, own_state, far)
-    far_core_grad, far_weight = together([far_core_grad, far_weight], [log_sum])
-    far_weight = lax.all_gather(
-        far_weight, "ctx", axis=0, tiled=True, axis_index_groups=along_z()
-    )
+    [far_core_grad] = together([far_core_grad], [log_sum])
     far_attention = to_x_hi(attention)
     attn_grad = grad_terms(place, 2, far_grad, far_core_grad, out_weight, terms, far_core_grad)
     cotangents = (out_grad, core_grad, far_grad, far_core_grad)
@@ -605,12 +598,13 @@
     near_back, far_back, dq, delta = backward_behind(
         *behind, attention, attn_grad, log_sum, weight_parts[3]
     )
+    far_back, far_weight = together([far_back, far_weight])
     query_grad, own = backward_own(
         flags, queries, keys, values, attn_grad, log_sum, dq, delta, delta
     )
 
     back_moved = first_hop(far_back, -1)
-    far_attention, far_weight = together([far_attention, far_weight], [own])
+    [far_attention] = together([far_attention], [own])
     from_core = for_core(place, out_weight, far_weight, far_attention, attention, own)
 
     *weight_moved, near_back, back_moved, from_core = together(

time: 252 us -> 234 us (0.929)
  waiting for transfers between devices: 94.2 us -> 77.7 us
  between operations: 14.2 us -> 0.8 us
  Pallas kernels: 86.4 us -> 94.5 us
  starting transfers between devices: 48.7 us -> 53.5 us
    ppermute x13, waiting for transfers between devices: 70.4 us -> 56 us  [move(): return lax.ppermute(value, AXES, pairs)]
    pallas_call x14, Pallas kernels: 86.4 us -> 94.5 us  [call(): pl.pallas_call(kernel, grid_spec=pltpu.PrefetchScalarGridSpec(num_scalar_...]
    ppermute x2, starting transfers between devices: 5.54 us -> 8.31 us  [first_hop(): return lax.ppermute(value, 'ctx', [(s, m) for s, m, _ in two_pairs(sign)])]
  transfers between devices with their start and end apart: 22 -> 21, of which waited for: 9 -> 10; matrix products, arithmetic and copies ran while one was open for 2% -> 2% of each run, Pallas kernels for 35% -> 41%
where the time goes in v9:
time: 234 us; the launch traced here: 232 us
  Pallas kernels  94.5 us (40%)
  waiting for transfers between devices  77.7 us (33%)
  starting transfers between devices  53.5 us (23%)
  other arithmetic  3.55 us (2%)
    pallas_call x14, Pallas kernels, call(): pl.pallas_call(kernel, grid_spec=pltpu.PrefetchScalarGridSpec(num_scalar_...  94.5 us
    ppermute x13, waiting for transfers between devices, move(): return lax.ppermute(value, AXES, pairs)  56 us
    ppermute x13, starting transfers between devices, move(): return lax.ppermute(value, AXES, pairs)  27.7 us
    ppermute x2, waiting for transfers between devices, along_ctx(): return lax.ppermute(value, 'ctx', pairs)  15.2 us
    ppermute x2, starting transfers between devices, first_hop(): return lax.ppermute(value, 'ctx', [(s, m) for s, m, _ in two_pairs(sign)])  8.31 us
    ppermute x2, starting transfers between devices, second_hop(): return lax.ppermute(value, 'ctx', [(m, t) for _, m, t in two_pairs(sign)])  7.37 us
  transfers between devices with their start and end apart: 21, of which 10 were waited for; matrix products, arithmetic and copies ran while one was open for 2% of the time, Pallas kernels for 41%

profile of v9, /device:TPU:30, one launch (start us, length us, event | category | flops | bytes accessed | tf_op | source)
XLA Modules:
  0.0 232.1 jit_solution(7260633058898562331)
XLA Ops:
  0.7 1.5 collective-permute-start.5
  2.2 3.8 %collective-permute-start = (bf16[1024,512]{1,0:T(8,128)(2,1)}, bf16[1024,512]{1,0:T(8,128)(2,1)}, u32[]{:S(2)}, u32[]{:S(2)}) collective-permute-start(bf16[1024,512]{1,0:T(8,128)(2,1)} %v_ref.5), channel_id=1, source_target_pairs={{0,4},{4,8},{8,12},{12,16},{16,20},{20,24},{24,28},{28,32},{32,36}... | collective-permute-start | bytes 3145736 | tf_op jit(solution)/shard_map/ppermute | solution.py:567
  6.1 0.6 pad_add_fusion.place
  6.7 3.3 %second_blocks.1 = (bf16[2,512,512]{2,1,0:T(8,128)(2,1)}, bf16[1024,512]{1,0:T(8,128)(2,1)}) custom-call(s32[4]{0:T(128)} %pad_add_fusion.place, bf16[1024,512]{1,0:T(8,128)(2,1)} %k_ref.5, bf16[1024,512]{1,0:T(8,128)(2,1)} %v_ref.5), custom_call_target="tpu_custom_call" | custom-call | flops 1 | bytes 1 | tf_op jit(solution)/shard_map/second_blocks/pallas_call | solution.py:297
  10.0 3.4 %collective-permute-start.1 = (bf16[2,512,512]{2,1,0:T(8,128)(2,1)}, bf16[2,512,512]{2,1,0:T(8,128)(2,1)}, u32[]{:S(2)}, u32[]{:S(2)}) collective-permute-start(bf16[2,512,512]{2,1,0:T(8,128)(2,1)} %get-tuple-element.47), channel_id=1, source_target_pairs={{0,12},{4,0},{8,4},{12,8},{16,28},{20,16},{24,20},{28,24},{32,44},... | collective-permute-start | bytes 3145736 | tf_op jit(solution)/shard_map/ppermute | solution.py:79
  13.4 0.8 bitcast_add_fusion
  14.1 0.7 slice_bitcast_fusion
  14.9 0.2 and_reduce_fusion.1
  15.1 0.8 fusion
  15.8 0.2 and_reduce_fusion
  16.0 0.6 reshape.60.flags
  16.7 7.4 %forward_own.1 = (f32[512,1024]{1,0:T(8,128)}, f32[4,2,512]{2,1,0:T(2,128)}, f32[4,2,512]{2,1,0:T(2,128)}) custom-call(s32[8]{0:T(128)} %reshape.60.flags, bf16[1024,512]{1,0:T(8,128)(2,1)} %q_ref.7, bf16[1024,512]{1,0:T(8,128)(2,1)} %k_ref.5, bf16[1024,512]{1,0:T(8,128)(2,1)} %v_ref.5, bf16[1024,512]{1,0:T(8,128)(2,1)} %k_ref.5), custom_call_target="tpu_custom_call" | custom-call | flops 1 | bytes 1 | tf_op jit(solution)/shard_map/forward_own/pallas_call | solution.py:297
  24.1 3.3 %projection_far.1.rest_0_.refs_4_ = bf16[512,2048]{1,0:T(8,128)(2,1)} custom-call(s32[4]{0:T(128)} %pad_add_fusion.place, bf16[512,4096]{1,0:T(8,128)(2,1)} %w_own.1, f32[4,2,512]{2,1,0:T(2,128)} %get-tuple-element.48.refs_0_.top_in), custom_call_target="tpu_custom_call" | custom-call | flops 1 | bytes 1 | tf_op jit(solution)/shard_map/projection_far/pallas_call | solution.py:297
  27.4 6.4 %projection_backward.2.refs_1_.rest_0_ = f32[1024,512]{1,0:T(8,128)} custom-call(s32[4]{0:T(128)} %pad_add_fusion.place, bf16[1024,1024]{1,0:T(8,128)(2,1)} %g0.1, bf16[1024,1024]{1,0:T(8,128)(2,1)} %collective-permute-done.2.b_ref.g1, bf16[512,4096]{1,0:T(8,128)(2,1)} %w_own.1, bf16[512,4096]{1,0:T(8,128)(2,1)} %w_own.1, ...), custom_call_target="tpu_custom_call" | custom-call | flops 1 | bytes 1 | tf_op jit(solution)/shard_map/projection_backward/pallas_call | solution.py:297
  33.8 3.3 %collective-permute-done.1.refs_0_ = bf16[2,512,512]{2,1,0:T(8,128)(2,1)} collective-permute-done((bf16[2,512,512]{2,1,0:T(8,128)(2,1)}, bf16[2,512,512]{2,1,0:T(8,128)(2,1)}, u32[]{:S(2)}, u32[]{:S(2)}) %collective-permute-start.1) | collective-permute-done | bytes 1048608 | tf_op jit(solution)/shard_map/ppermute | solution.py:79
  37.1 2.7 %collective-permute-start.3 = (bf16[1024,512]{1,0:T(8,128)(2,1)}, bf16[1024,512]{1,0:T(8,128)(2,1)}, u32[]{:S(2)}, u32[]{:S(2)}) collective-permute-start(bf16[1024,512]{1,0:T(8,128)(2,1)} %get-tuple-element.49), channel_id=1, source_target_pairs={{0,4},{4,8},{8,12},{12,16},{16,20},{20,24},{24,28},{28,32},{32,36}... | collective-permute-start | bytes 3145736 | tf_op jit(solution)/shard_map/ppermute | solution.py:66
  39.8 1.7 collective-permute-start.6
  41.5 3.4 %collective-permute-start.4 = (bf16[2,512,512]{2,1,0:T(8,128)(2,1)}, bf16[2,512,512]{2,1,0:T(8,128)(2,1)}, u32[]{:S(2)}, u32[]{:S(2)}) collective-permute-start(bf16[2,512,512]{2,1,0:T(8,128)(2,1)} %order.8.refs_2_.refs_5_), channel_id=1, source_target_pairs={{12,8},{0,12},{4,16},{8,20},{28,24},{16,28},{20,32},{24,36},{44,40... | collective-permute-start | bytes 3145736 | tf_op jit(solution)/shard_map/ppermute | solution.py:83
  45.0 5.6 %collective-permute-done.5.refs_2_ = bf16[1024,1024]{1,0:T(8,128)(2,1)} collective-permute-done((bf16[1024,1024]{1,0:T(8,128)(2,1)}, bf16[1024,1024]{1,0:T(8,128)(2,1)}, u32[]{:S(2)}, u32[]{:S(2)}) %collective-permute-start.5) | collective-permute-done | bytes 2097184 | tf_op jit(solution)/shard_map/ppermute | solution.py:38
  50.6 15.2 %collective-permute-done.3.refs_0_ = bf16[1024,512]{1,0:T(8,128)(2,1)} collective-permute-done((bf16[1024,512]{1,0:T(8,128)(2,1)}, bf16[1024,512]{1,0:T(8,128)(2,1)}, u32[]{:S(2)}, u32[]{:S(2)}) %collective-permute-start.3) | collective-permute-done | bytes 1048608 | tf_op jit(solution)/shard_map/ppermute | solution.py:66
  65.8 3.2 %collective-permute-done.4.refs_1_ = bf16[2,512,512]{2,1,0:T(8,128)(2,1)} collective-permute-done((bf16[2,512,512]{2,1,0:T(8,128)(2,1)}, bf16[2,512,512]{2,1,0:T(8,128)(2,1)}, u32[]{:S(2)}, u32[]{:S(2)}) %collective-permute-start.4) | collective-permute-done | bytes 1048608 | tf_op jit(solution)/shard_map/ppermute | solution.py:83
  69.0 2.1 collective-permute-start.11
  71.1 7.4 %forward_behind.1 = (bf16[1024,512]{1,0:T(8,128)(2,1)}, bf16[512,1024]{1,0:T(8,128)(2,1)}, f32[4,2,512]{2,1,0:T(2,128)}) custom-call(s32[8]{0:T(128)} %reshape.60.flags, bf16[1024,512]{1,0:T(8,128)(2,1)} %q_ref.7, bf16[1024,512]{1,0:T(8,128)(2,1)} %get-tuple-element.51.k1_ref, bf16[1024,512]{1,0:T(8,128)(2,1)} %get-tuple-element.50.v1_ref, ...), custom_call_target="tpu_custom_call" | custom-call | flops 1 | bytes 1 | tf_op jit(solution)/shard_map/forward_behind/pallas_call | solution.py:297
  78.5 1.7 collective-permute-start.13
  80.2 6.9 %projection_backward.3.after.grad_ref = bf16[1024,512]{1,0:T(8,128)(2,1)} custom-call(s32[4]{0:T(128)} %pad_add_fusion.place, bf16[1024,1024]{1,0:T(8,128)(2,1)} %get-tuple-element.58.a_ref.g2, bf16[1024,1024]{1,0:T(8,128)(2,1)} %order.11.b_ref.rest_1_.g3, bf16[512,4096]{1,0:T(8,128)(2,1)} %w_own.1, bf16[512,4096]{1,0:T(8,128)(2,1)} %w_own.1, ...), custom_call_target="tpu_custom_call" | custom-call | flops 1 | bytes 1 | tf_op jit(solution)/shard_map/projection_backward/pallas_call | solution.py:297
  87.1 13.3 %weight_gradient.1 = (bf16[2,512,512]{2,1,0:T(8,128)(2,1)}, bf16[2,512,512]{2,1,0:T(8,128)(2,1)}, bf16[2,512,512]{2,1,0:T(8,128)(2,1)}, bf16[2,512,512]{2,1,0:T(8,128)(2,1)}) custom-call(s32[4]{0:T(128)} %pad_add_fusion.place, bf16[512,1024]{1,0:T(8,128)(2,1)} %get-tuple-element.57.turned_ref, bf16[1024,1024]{1,0:T(8,128)(2,1)} %g0.1, ...), custom_call_target="tpu_custom_call" | custom-call | flops 1 | bytes 1 | tf_op jit(solution)/shard_map/weight_gradient/pallas_call | solution.py:297
  100.3 6.7 %collective-permute-start.8 = (bf16[2,512,512]{2,1,0:T(8,128)(2,1)}, bf16[2,512,512]{2,1,0:T(8,128)(2,1)}, u32[]{:S(2)}, u32[]{:S(2)}) collective-permute-start(bf16[2,512,512]{2,1,0:T(8,128)(2,1)} %get-tuple-element.60), channel_id=1, source_target_pairs={{0,16},{1,17},{2,18},{3,19},{4,20},{5,21},{6,22},{7,23},{8,24},{9,... | collective-permute-start | bytes 3145736 | tf_op jit(solution)/shard_map/ppermute | solution.py:38
  107.1 1.5 collective-permute-start.10
  108.6 9.1 %backward_behind.1 = (bf16[2,1024,512]{2,1,0:T(8,128)(2,1)}, bf16[2,512,512]{2,1,0:T(8,128)(2,1)}, f32[512,1024]{1,0:T(8,128)}, f32[4,2,512]{2,1,0:T(2,128)}) custom-call(s32[8]{0:T(128)} %reshape.60.flags, bf16[1024,512]{1,0:T(8,128)(2,1)} %q_ref.7, bf16[1024,512]{1,0:T(8,128)(2,1)} %get-tuple-element.51.k1_ref, ...), custom_call_target="tpu_custom_call" | custom-call | flops 1 | bytes 1 | tf_op jit(solution)/shard_map/backward_behind/pallas_call | solution.py:297
  117.6 1.6 collective-permute-done.11.refs_1_
  119.2 4.9 %collective-permute-start.12 = (bf16[2,512,512]{2,1,0:T(8,128)(2,1)}, bf16[2,512,512]{2,1,0:T(8,128)(2,1)}, u32[]{:S(2)}, u32[]{:S(2)}) collective-permute-start(bf16[2,512,512]{2,1,0:T(8,128)(2,1)} %get-tuple-element.67), channel_id=1, source_target_pairs={{8,12},{12,0},{16,20},{20,24},{24,28},{28,16},{32,36},{36,40},{40,... | collective-permute-start | bytes 3145736 | tf_op jit(solution)/shard_map/ppermute | solution.py:79
  124.1 10.5 %backward_own.1 = (bf16[1024,512]{1,0:T(8,128)(2,1)}, bf16[2,1024,512]{2,1,0:T(8,128)(2,1)}) custom-call(s32[8]{0:T(128)} %reshape.60.flags, bf16[1024,512]{1,0:T(8,128)(2,1)} %q_ref.7, bf16[1024,512]{1,0:T(8,128)(2,1)} %k_ref.5, bf16[1024,512]{1,0:T(8,128)(2,1)} %v_ref.5, bf16[1024,512]{1,0:T(8,128)(2,1)} %projection_backward.3.after.grad_ref, ...), custom_call_target="tpu_custom_call" | custom-call | flops 1 | bytes 1 | tf_op jit(solution)/shard_map/backward_own/pallas_call | solution.py:297
  134.6 6.7 %collective-permute-done.13.refs_0_ = bf16[1024,512]{1,0:T(8,128)(2,1)} collective-permute-done((bf16[1024,512]{1,0:T(8,128)(2,1)}, bf16[1024,512]{1,0:T(8,128)(2,1)}, u32[]{:S(2)}, u32[]{:S(2)}) %collective-permute-start.13) | collective-permute-done | bytes 1048608 | tf_op jit(solution)/shard_map/ppermute | solution.py:38
  141.3 5.1 %for_core.1.refs_5_ = bf16[4,512,1024]{2,1,0:T(8,128)(2,1)} custom-call(s32[4]{0:T(128)} %pad_add_fusion.place, bf16[512,4096]{1,0:T(8,128)(2,1)} %w_own.1, bf16[512,2048]{1,0:T(8,128)(2,1)} %get-tuple-element.68.far_ref.w_far, bf16[1024,512]{1,0:T(8,128)(2,1)} %order.13.far_rows.far, bf16[1024,512]{1,0:T(8,128)(2,1)} %get-tuple-element.56.out_ref.own_rows.own, ...), custom_call_target="tpu_custom_call" | custom-call | flops 1 | bytes 1 | tf_op jit(solution)/shard_map/for_core/pallas_call | solution.py:297
  146.4 6.2 %collective-permute-done.8.refs_0_ = bf16[2,512,512]{2,1,0:T(8,128)(2,1)} collective-permute-done((bf16[2,512,512]{2,1,0:T(8,128)(2,1)}, bf16[2,512,512]{2,1,0:T(8,128)(2,1)}, u32[]{:S(2)}, u32[]{:S(2)}) %collective-permute-start.8) | collective-permute-done | bytes 1048608 | tf_op jit(solution)/shard_map/ppermute | solution.py:38
  152.6 3.4 %collective-permute-done.9.refs_1_ = bf16[2,512,512]{2,1,0:T(8,128)(2,1)} collective-permute-done((bf16[2,512,512]{2,1,0:T(8,128)(2,1)}, bf16[2,512,512]{2,1,0:T(8,128)(2,1)}, u32[]{:S(2)}, u32[]{:S(2)}) %collective-permute-start.9) | collective-permute-done | bytes 1048608 | tf_op jit(solution)/shard_map/ppermute | solution.py:38
  156.1 1.9 collective-permute-start.15
  158.0 3.9 %collective-permute-start.16 = (bf16[2,512,512]{2,1,0:T(8,128)(2,1)}, bf16[2,512,512]{2,1,0:T(8,128)(2,1)}, u32[]{:S(2)}, u32[]{:S(2)}) collective-permute-start(bf16[2,512,512]{2,1,0:T(8,128)(2,1)} %get-tuple-element.79), channel_id=1, source_target_pairs={{12,0},{0,4},{20,8},{24,12},{28,16},{16,20},{36,24},{40,28},{44,32... | collective-permute-start | bytes 3145736 | tf_op jit(solution)/shard_map/ppermute | solution.py:83
  162.0 4.8 %weight_by_z.1 = (bf16[2,512,128]{2,1,0:T(8,128)(2,1)}, bf16[2,512,128]{2,1,0:T(8,128)(2,1)}, bf16[2,512,128]{2,1,0:T(8,128)(2,1)}, bf16[2,512,128]{2,1,0:T(8,128)(2,1)}) custom-call(s32[4]{0:T(128)} %pad_add_fusion.place, bf16[2,512,512]{2,1,0:T(8,128)(2,1)} %get-tuple-element.63.after.a, bf16[2,512,512]{2,1,0:T(8,128)(2,1)} %get-tuple-element.73.b.after, ...), custom_call_target="tpu_custom_call" | custom-call | flops 1 | bytes 1 | tf_op jit(solution)/shard_map/weight_by_z/pallas_call | solution.py:297
  166.8 3.2 %collective-permute-start.18 = (bf16[2,512,128]{2,1,0:T(8,128)(2,1)}, bf16[2,512,128]{2,1,0:T(8,128)(2,1)}, u32[]{:S(2)}, u32[]{:S(2)}) collective-permute-start(bf16[2,512,128]{2,1,0:T(8,128)(2,1)} %get-tuple-element.81), channel_id=1, source_target_pairs={{0,12},{1,13},{2,14},{3,15},{4,0},{5,1},{6,2},{7,3},{8,4},{9,5},{1... | collective-permute-start | bytes 786440 | tf_op jit(solution)/shard_map/ppermute | solution.py:38
  170.0 0.5 collective-permute-start.19
  170.5 9.4 %projection.1.after = bf16[1024,1024]{1,0:T(8,128)(2,1)} custom-call(s32[4]{0:T(128)} %pad_add_fusion.place, bf16[1024,512]{1,0:T(8,128)(2,1)} %get-tuple-element.56.out_ref.own_rows.own, bf16[4,512,1024]{2,1,0:T(8,128)(2,1)} %collective-permute-done.14.core.far_core.w_core, bf16[1024,512]{1,0:T(8,128)(2,1)} %order.13.far_rows.far, ...), custom_call_target="tpu_custom_call" | custom-call | flops 1 | bytes 1 | tf_op jit(solution)/shard_map/projection/pallas_call | solution.py:297
  179.9 18.3 %collective-permute-done.17.b_ref = bf16[2,512,128]{2,1,0:T(8,128)(2,1)} collective-permute-done((bf16[2,512,128]{2,1,0:T(8,128)(2,1)}, bf16[2,512,128]{2,1,0:T(8,128)(2,1)}, u32[]{:S(2)}, u32[]{:S(2)}) %collective-permute-start.17) | collective-permute-done | bytes 262176 | tf_op jit(solution)/shard_map/ppermute | solution.py:38
  198.2 14.1 %collective-permute-done.18.c_ref = bf16[2,512,128]{2,1,0:T(8,128)(2,1)} collective-permute-done((bf16[2,512,128]{2,1,0:T(8,128)(2,1)}, bf16[2,512,128]{2,1,0:T(8,128)(2,1)}, u32[]{:S(2)}, u32[]{:S(2)}) %collective-permute-start.18) | collective-permute-done | bytes 262176 | tf_op jit(solution)/shard_map/ppermute | solution.py:38
  212.4 2.6 %weight_z_sum.1 = (f32[512,128]{1,0:T(8,128)}, bf16[512,128]{1,0:T(8,128)(2,1)}) custom-call(s32[4]{0:T(128)} %pad_add_fusion.place, bf16[2,512,128]{2,1,0:T(8,128)(2,1)} %get-tuple-element.76.after.a_ref, bf16[2,512,128]{2,1,0:T(8,128)(2,1)} %collective-permute-done.17.b_ref, bf16[2,512,128]{2,1,0:T(8,128)(2,1)} %collective-permute-done.18.c_ref, ...), custom_call_target="tpu_custom_call" | custom-call | flops 1 | bytes 1 | tf_op jit(solution)/shard_map/weight_z_sum/pallas_call | solution.py:297
  215.0 10.2 %collective-permute-start.20 = (bf16[512,128]{1,0:T(8,128)(2,1)}, bf16[512,128]{1,0:T(8,128)(2,1)}, u32[]{:S(2)}, u32[]{:S(2)}) collective-permute-start(bf16[512,128]{1,0:T(8,128)(2,1)} %get-tuple-element.86), channel_id=1, source_target_pairs={{0,64},{1,65},{2,66},{3,67},{4,68},{5,69},{6,70},{7,71},{8,72},{9,... | collective-permute-start | bytes 393224 | tf_op jit(solution)/shard_map/ppermute | solution.py:38
  225.2 5.1 %key_value_sum.1 = (bf16[1024,512]{1,0:T(8,128)(2,1)}, bf16[1024,512]{1,0:T(8,128)(2,1)}) custom-call(s32[4]{0:T(128)} %pad_add_fusion.place, bf16[2,1024,512]{2,1,0:T(8,128)(2,1)} %get-tuple-element.71.refs_1_.after.own_ref, bf16[2,1024,512]{2,1,0:T(8,128)(2,1)} %collective-permute-done.15.near_ref, bf16[2,512,512]{2,1,0:T(8,128)(2,1)} %collective-permute-done.16.far_ref, ...), custom_call_target="tpu_custom_call" | custom-call | flops 1 | bytes 1 | tf_op jit(solution)/shard_map/key_value_sum/pallas_call | solution.py:297
  230.3 1.7 convert_add_fusion
  (27 shorter events, 0.3 us)
Async XLA Ops:
  0.6 26.7 %collective-permute-start.2 = (bf16[1024,1024]{1,0:T(8,128)(2,1)}, bf16[1024,1024]{1,0:T(8,128)(2,1)}, u32[]{:S(2)}, u32[]{:S(2)}) collective-permute-start(bf16[1024,1024]{1,0:T(8,128)(2,1)} %g0.1), channel_id=1, source_target_pairs={{0,1},{1,0},{2,3},{3,2},{4,5},{5,4},{6,7},{7,6},{8,9},{9,8},{10,11... | collective-permute-start | bytes 6291464 | tf_op jit(solution)/shard_map/ppermute | solution.py:38
  0.7 49.9 %collective-permute-start.5 = (bf16[1024,1024]{1,0:T(8,128)(2,1)}, bf16[1024,1024]{1,0:T(8,128)(2,1)}, u32[]{:S(2)}, u32[]{:S(2)}) collective-permute-start(bf16[1024,1024]{1,0:T(8,128)(2,1)} %g0.1), channel_id=1, source_target_pairs={{0,2},{1,3},{2,0},{3,1},{4,6},{5,7},{6,4},{7,5},{8,10},{9,11},{10,... | collective-permute-start | bytes 6291464 | tf_op jit(solution)/shard_map/ppermute | solution.py:38
  2.2 34.9 %collective-permute-start = (bf16[1024,512]{1,0:T(8,128)(2,1)}, bf16[1024,512]{1,0:T(8,128)(2,1)}, u32[]{:S(2)}, u32[]{:S(2)}) collective-permute-start(bf16[1024,512]{1,0:T(8,128)(2,1)} %v_ref.5), channel_id=1, source_target_pairs={{0,4},{4,8},{8,12},{12,16},{16,20},{20,24},{24,28},{28,32},{32,36}... | collective-permute-start | bytes 3145736 | tf_op jit(solution)/shard_map/ppermute | solution.py:567
  10.0 27.1 %collective-permute-start.1 = (bf16[2,512,512]{2,1,0:T(8,128)(2,1)}, bf16[2,512,512]{2,1,0:T(8,128)(2,1)}, u32[]{:S(2)}, u32[]{:S(2)}) collective-permute-start(bf16[2,512,512]{2,1,0:T(8,128)(2,1)} %get-tuple-element.47), channel_id=1, source_target_pairs={{0,12},{4,0},{8,4},{12,8},{16,28},{20,16},{24,20},{28,24},{32,44},... | collective-permute-start | bytes 3145736 | tf_op jit(solution)/shard_map/ppermute | solution.py:79
  37.1 28.7 %collective-permute-start.3 = (bf16[1024,512]{1,0:T(8,128)(2,1)}, bf16[1024,512]{1,0:T(8,128)(2,1)}, u32[]{:S(2)}, u32[]{:S(2)}) collective-permute-start(bf16[1024,512]{1,0:T(8,128)(2,1)} %get-tuple-element.49), channel_id=1, source_target_pairs={{0,4},{4,8},{8,12},{12,16},{16,20},{20,24},{24,28},{28,32},{32,36}... | collective-permute-start | bytes 3145736 | tf_op jit(solution)/shard_map/ppermute | solution.py:66
  39.8 25.9 %collective-permute-start.6 = (bf16[1024,512]{1,0:T(8,128)(2,1)}, bf16[1024,512]{1,0:T(8,128)(2,1)}, u32[]{:S(2)}, u32[]{:S(2)}) collective-permute-start(bf16[1024,512]{1,0:T(8,128)(2,1)} %get-tuple-element.50.v1_ref), channel_id=1, source_target_pairs={{0,64},{1,65},{2,66},{3,67}} | collective-permute-start | bytes 3145736 | tf_op jit(solution)/shard_map/ppermute | solution.py:583
  41.5 27.5 %collective-permute-start.4 = (bf16[2,512,512]{2,1,0:T(8,128)(2,1)}, bf16[2,512,512]{2,1,0:T(8,128)(2,1)}, u32[]{:S(2)}, u32[]{:S(2)}) collective-permute-start(bf16[2,512,512]{2,1,0:T(8,128)(2,1)} %order.8.refs_2_.refs_5_), channel_id=1, source_target_pairs={{12,8},{0,12},{4,16},{8,20},{28,24},{16,28},{20,32},{24,36},{44,40... | collective-permute-start | bytes 3145736 | tf_op jit(solution)/shard_map/ppermute | solution.py:83
  69.0 9.5 %collective-permute-start.7 = (bf16[1024,1024]{1,0:T(8,128)(2,1)}, bf16[1024,1024]{1,0:T(8,128)(2,1)}, u32[]{:S(2)}, u32[]{:S(2)}) collective-permute-start(bf16[1024,1024]{1,0:T(8,128)(2,1)} %get-tuple-element.58.a_ref.g2), channel_id=1, source_target_pairs={{0,1},{1,0},{2,3},{3,2},{4,5},{5,4},{6,7},{7,6},{8,9},{9,8},{10,11... | collective-permute-start | bytes 6291464 | tf_op jit(solution)/shard_map/ppermute | solution.py:38
  69.0 50.2 %collective-permute-start.11 = (bf16[512,2048]{1,0:T(8,128)(2,1)}, bf16[512,2048]{1,0:T(8,128)(2,1)}, u32[]{:S(2)}, u32[]{:S(2)}) collective-permute-start(bf16[512,2048]{1,0:T(8,128)(2,1)} %get-tuple-element.66), channel_id=1, source_target_pairs={{0,2},{1,3},{2,0},{3,1},{4,6},{5,7},{6,4},{7,5},{8,10},{9,11},{10,... | collective-permute-start | bytes 6291464 | tf_op jit(solution)/shard_map/ppermute | solution.py:38
  78.5 62.8 %collective-permute-start.13 = (bf16[1024,512]{1,0:T(8,128)(2,1)}, bf16[1024,512]{1,0:T(8,128)(2,1)}, u32[]{:S(2)}, u32[]{:S(2)}) collective-permute-start(bf16[1024,512]{1,0:T(8,128)(2,1)} %get-tuple-element.56.out_ref.own_rows.own), channel_id=1, source_target_pairs={{0,2},{1,3},{2,0},{3,1},{4,6},{5,7},{6,4},{7,5},{8,10},{9,11},{10,... | collective-permute-start | bytes 3145736 | tf_op jit(solution)/shard_map/ppermute | solution.py:38
  100.3 52.3 %collective-permute-start.8 = (bf16[2,512,512]{2,1,0:T(8,128)(2,1)}, bf16[2,512,512]{2,1,0:T(8,128)(2,1)}, u32[]{:S(2)}, u32[]{:S(2)}) collective-permute-start(bf16[2,512,512]{2,1,0:T(8,128)(2,1)} %get-tuple-element.60), channel_id=1, source_target_pairs={{0,16},{1,17},{2,18},{3,19},{4,20},{5,21},{6,22},{7,23},{8,24},{9,... | collective-permute-start | bytes 3145736 | tf_op jit(solution)/shard_map/ppermute | solution.py:38
  107.1 48.9 %collective-permute-start.9 = (bf16[2,512,512]{2,1,0:T(8,128)(2,1)}, bf16[2,512,512]{2,1,0:T(8,128)(2,1)}, u32[]{:S(2)}, u32[]{:S(2)}) collective-permute-start(bf16[2,512,512]{2,1,0:T(8,128)(2,1)} %get-tuple-element.61), channel_id=1, source_target_pairs={{0,48},{1,49},{2,50},{3,51},{4,52},{5,53},{6,54},{7,55},{8,56},{9,... | collective-permute-start | bytes 3145736 | tf_op jit(solution)/shard_map/ppermute | solution.py:38
  107.1 48.9 %collective-permute-start.10 = (bf16[2,512,512]{2,1,0:T(8,128)(2,1)}, bf16[2,512,512]{2,1,0:T(8,128)(2,1)}, u32[]{:S(2)}, u32[]{:S(2)}) collective-permute-start(bf16[2,512,512]{2,1,0:T(8,128)(2,1)} %get-tuple-element.62), channel_id=1, source_target_pairs={{0,32},{1,33},{2,34},{3,35},{4,36},{5,37},{6,38},{7,39},{8,40},{9,... | collective-permute-start | bytes 3145736 | tf_op jit(solution)/shard_map/ppermute | solution.py:38
  119.2 36.8 %collective-permute-start.12 = (bf16[2,512,512]{2,1,0:T(8,128)(2,1)}, bf16[2,512,512]{2,1,0:T(8,128)(2,1)}, u32[]{:S(2)}, u32[]{:S(2)}) collective-permute-start(bf16[2,512,512]{2,1,0:T(8,128)(2,1)} %get-tuple-element.67), channel_id=1, source_target_pairs={{8,12},{12,0},{16,20},{20,24},{24,28},{28,16},{32,36},{36,40},{40,... | collective-permute-start | bytes 3145736 | tf_op jit(solution)/shard_map/ppermute | solution.py:79
  156.0 14.0 %collective-permute-start.14 = (bf16[4,512,1024]{2,1,0:T(8,128)(2,1)}, bf16[4,512,1024]{2,1,0:T(8,128)(2,1)}, u32[]{:S(2)}, u32[]{:S(2)}) collective-permute-start(bf16[4,512,1024]{2,1,0:T(8,128)(2,1)} %get-tuple-element.72), channel_id=1, source_target_pairs={{0,1},{1,0},{2,3},{3,2},{4,5},{5,4},{6,7},{7,6},{8,9},{9,8},{10,11... | collective-permute-start | bytes 12582920 | tf_op jit(solution)/shard_map/ppermute | solution.py:38
  156.1 69.1 %collective-permute-start.15 = (bf16[2,1024,512]{2,1,0:T(8,128)(2,1)}, bf16[2,1024,512]{2,1,0:T(8,128)(2,1)}, u32[]{:S(2)}, u32[]{:S(2)}) collective-permute-start(bf16[2,1024,512]{2,1,0:T(8,128)(2,1)} %get-tuple-element.78), channel_id=1, source_target_pairs={{4,0},{8,4},{12,8},{16,12},{20,16},{24,20},{28,24},{32,28},{36,32}... | collective-permute-start | bytes 6291464 | tf_op jit(solution)/shard_map/ppermute | solution.py:66
  158.0 67.2 %collective-permute-start.16 = (bf16[2,512,512]{2,1,0:T(8,128)(2,1)}, bf16[2,512,512]{2,1,0:T(8,128)(2,1)}, u32[]{:S(2)}, u32[]{:S(2)}) collective-permute-start(bf16[2,512,512]{2,1,0:T(8,128)(2,1)} %get-tuple-element.79), channel_id=1, source_target_pairs={{12,0},{0,4},{20,8},{24,12},{28,16},{16,20},{36,24},{40,28},{44,32... | collective-permute-start | bytes 3145736 | tf_op jit(solution)/shard_map/ppermute | solution.py:83
  166.7 31.5 %collective-permute-start.17 = (bf16[2,512,128]{2,1,0:T(8,128)(2,1)}, bf16[2,512,128]{2,1,0:T(8,128)(2,1)}, u32[]{:S(2)}, u32[]{:S(2)}) collective-permute-start(bf16[2,512,128]{2,1,0:T(8,128)(2,1)} %get-tuple-element.80), channel_id=1, source_target_pairs={{0,4},{1,5},{2,6},{3,7},{4,8},{5,9},{6,10},{7,11},{8,12},{9,13},{1... | collective-permute-start | bytes 786440 | tf_op jit(solution)/shard_map/ppermute | solution.py:38
  166.8 45.6 %collective-permute-start.18 = (bf16[2,512,128]{2,1,0:T(8,128)(2,1)}, bf16[2,512,128]{2,1,0:T(8,128)(2,1)}, u32[]{:S(2)}, u32[]{:S(2)}) collective-permute-start(bf16[2,512,128]{2,1,0:T(8,128)(2,1)} %get-tuple-element.81), channel_id=1, source_target_pairs={{0,12},{1,13},{2,14},{3,15},{4,0},{5,1},{6,2},{7,3},{8,4},{9,5},{1... | collective-permute-start | bytes 786440 | tf_op jit(solution)/shard_map/ppermute | solution.py:38
  170.0 42.4 %collective-permute-start.19 = (bf16[2,512,128]{2,1,0:T(8,128)(2,1)}, bf16[2,512,128]{2,1,0:T(8,128)(2,1)}, u32[]{:S(2)}, u32[]{:S(2)}) collective-permute-start(bf16[2,512,128]{2,1,0:T(8,128)(2,1)} %get-tuple-element.82), channel_id=1, source_target_pairs={{0,8},{1,9},{2,10},{3,11},{4,12},{5,13},{6,14},{7,15},{8,0},{9,1},... | collective-permute-start | bytes 786440 | tf_op jit(solution)/shard_map/ppermute | solution.py:38
  215.0 15.3 %collective-permute-start.20 = (bf16[512,128]{1,0:T(8,128)(2,1)}, bf16[512,128]{1,0:T(8,128)(2,1)}, u32[]{:S(2)}, u32[]{:S(2)}) collective-permute-start(bf16[512,128]{1,0:T(8,128)(2,1)} %get-tuple-element.86), channel_id=1, source_target_pairs={{0,64},{1,65},{2,66},{3,67},{4,68},{5,69},{6,70},{7,71},{8,72},{9,... | collective-permute-start | bytes 393224 | tf_op jit(solution)/shard_map/ppermute | solution.py:38

commit v10 on v9

--- a/solution.py
+++ b/solution.py
@@ -460,38 +460,38 @@
     return [to_y(parts[s], s + 1) for s in (0, 2, 1)]
 
 
-def pieces_kernel(place, a, b, c, d, after, *outs):
+def y_sum_kernel(place, a, b, c, d, after, kept_ref, sent_ref):
+    def total(index):
+        return sum(ref[index].astype(f32) for ref in (a, b, c, d)).astype(bf16)
+
+    kept = place[3] ^ (place[0] // 2)
+    kept_ref[...] = total(kept)
+    sent_ref[...] = total(1 - kept)
+
+
+def weight_y_sum(place, terms, after):
+    result = pl.BlockSpec((256, 512), lambda i, place: (i, 0))
+    return call(
+        y_sum_kernel, "weight_y_sum", (2,),
+        [pl.BlockSpec((2, 256, 512), lambda i, place: (0, i, 0))] * 4 + [ANY],
+        [result] * 2, [shape((512, 512), bf16)] * 2, [], (place, *terms, after),
+    )
+
+
+def pieces_kernel(place, a, b, after, *outs):
     for slot, out_ref in enumerate(outs):
 
         @pl.when(pl.program_id(0) == slot)
         def _(out_ref=out_ref):
-            out_ref[...] = sum(ref[...].astype(f32) for ref in (a, b, c, d)).astype(bf16)
-
-
-def pieces_by_z(place, terms, after):
-    piece = pl.BlockSpec((2, 512, 128), lambda i, place: (0, 0, (place[2] + i + 1) % 4))
-    return call(
-        pieces_kernel, "weight_by_z", (4,), [piece] * 4 + [ANY],
-        [pl.BlockSpec((2, 512, 128), lambda i, place: (0, 0, 0))] * 4,
-        [shape((2, 512, 128), bf16)] * 4, [], (place, *terms, after),
-    )
-
-
-def weight_z_kernel(place, a_ref, b_ref, c_ref, d_ref, after, kept_ref, sent_ref):
-    def total(index):
-        return sum(ref[index].astype(f32) for ref in (a_ref, b_ref, c_ref, d_ref))
-
-    kept = place[3] ^ (place[0] // 2)
-    kept_ref[...] = total(kept)
-    sent_ref[...] = total(1 - kept).astype(bf16)
-
-
-def weight_z_sum(place, terms, after):
-    whole = pl.BlockSpec((2, 512, 128), lambda i, place: (0, 0, 0))
-    result = pl.BlockSpec((512, 128), lambda i, place: (0, 0))
-    return call(
-        weight_z_kernel, "weight_z_sum", (1,), [whole] * 4 + [ANY], [result] * 2,
-        [shape((512, 128), f32), shape((512, 128), bf16)], [], (place, *terms, after),
+            out_ref[...] = (a[...].astype(f32) + b[...].astype(f32)).astype(bf16)
+
+
+def pieces_by_z(place, a, b, after):
+    piece = pl.BlockSpec((512, 128), lambda i, place: (0, (place[2] + i + 1) % 4))
+    return call(
+        pieces_kernel, "weight_by_z", (4,), [piece] * 2 + [ANY],
+        [pl.BlockSpec((512, 128), lambda i, place: (0, 0))] * 4,
+        [shape((512, 128), bf16)] * 4, [], (place, a, b, after),
     )
 
 
@@ -613,15 +613,14 @@
     near_back = along_ctx(near_back, -1)
     far_back = second_hop(back_moved, -1)
     from_core = to_core(from_core)
-    weight_pieces = pieces_by_z(place, [weight_parts[3], *weight_moved], weight_moved[0])
+    kept, sent = weight_y_sum(place, [weight_parts[3], *weight_moved], weight_moved[0])
+    sent = to_x_lo(sent)
+    mixed = mix(place, attention, far_attention, out_weight, far_weight, from_core, kept)
+    weight_pieces = pieces_by_z(place, kept, sent, mixed)
     weight_moved = [to_z(weight_pieces[s], s + 1) for s in (0, 2, 1)]
-    mixed = mix(
-        place, attention, far_attention, out_weight, far_weight, from_core, weight_pieces[3]
-    )
-    kept, sent = weight_z_sum(place, [weight_pieces[3], *weight_moved], mixed)
-    key_grad, value_grad = finish(place, own, near_back, far_back, kept)
-    [sent] = together([to_x_lo(sent)], [key_grad])
-    weight_grad = kept + sent.astype(f32)
+    key_grad, value_grad = finish(place, own, near_back, far_back, weight_pieces[3])
+    weight_moved = together(weight_moved, [key_grad])
+    weight_grad = sum(piece.astype(f32) for piece in [weight_pieces[3], *weight_moved])
     return (mixed, query_grad, key_grad, value_grad, weight_grad)
 
 

time: 234 us -> 240 us (1.026)
  the two profiles are of different devices: /device:TPU:30 before, /device:TPU:0 now
where the time goes in v10:
time: 240 us; the launch traced here: 236 us
  waiting for transfers between devices  91.9 us (38%)
  Pallas kernels  87.1 us (36%)
  starting transfers between devices  50.1 us (21%)
  other arithmetic  3.71 us (2%)
    pallas_call x14, Pallas kernels, call(): pl.pallas_call(kernel, grid_spec=pltpu.PrefetchScalarGridSpec(num_scalar_...  87.1 us
    ppermute x13, waiting for transfers between devices, move(): return lax.ppermute(value, AXES, pairs)  66.6 us
    ppermute x13, starting transfers between devices, move(): return lax.ppermute(value, AXES, pairs)  21.7 us
    ppermute x2, waiting for transfers between devices, along_ctx(): return lax.ppermute(value, 'ctx', pairs)  13.5 us
    ppermute x2, starting transfers between devices, second_hop(): return lax.ppermute(value, 'ctx', [(m, t) for _, m, t in two_pairs(sign)])  10.4 us
    ppermute x1, waiting for transfers between devices, per_device(): edge_values = lax.ppermute(near_values, 'ctx', [(0, EDGE + 1)])  7.66 us
    ppermute x2, starting transfers between devices, along_ctx(): return lax.ppermute(value, 'ctx', pairs)  5.92 us
    ppermute x2, starting transfers between devices, first_hop(): return lax.ppermute(value, 'ctx', [(s, m) for s, m, _ in two_pairs(sign)])  5.73 us
  transfers between devices with their start and end apart: 21, of which 10 were waited for; matrix products, arithmetic and copies ran while one was open for 2% of the time, Pallas kernels for 37%

profile of v10, /device:TPU:0, one launch (start us, length us, event | category | flops | bytes accessed | tf_op | source)
XLA Modules:
  0.0 235.7 jit_solution(9949975696504405427)
XLA Ops:
  0.6 0.1 collective-permute-start.2
  0.7 3.2 %collective-permute-start.5 = (bf16[1024,1024]{1,0:T(8,128)(2,1)}, bf16[1024,1024]{1,0:T(8,128)(2,1)}, u32[]{:S(2)}, u32[]{:S(2)}) collective-permute-start(bf16[1024,1024]{1,0:T(8,128)(2,1)} %g0.1), channel_id=1, source_target_pairs={{0,2},{1,3},{2,0},{3,1},{4,6},{5,7},{6,4},{7,5},{8,10},{9,11},{10,... | collective-permute-start | bytes 6291464 | tf_op jit(solution)/shard_map/ppermute | solution.py:38
  3.9 3.8 %collective-permute-start = (bf16[1024,512]{1,0:T(8,128)(2,1)}, bf16[1024,512]{1,0:T(8,128)(2,1)}, u32[]{:S(2)}, u32[]{:S(2)}) collective-permute-start(bf16[1024,512]{1,0:T(8,128)(2,1)} %v_ref.5), channel_id=1, source_target_pairs={{0,4},{4,8},{8,12},{12,16},{16,20},{20,24},{24,28},{28,32},{32,36}... | collective-permute-start | bytes 3145736 | tf_op jit(solution)/shard_map/ppermute | solution.py:567
  7.8 0.6 pad_add_fusion.place
  8.4 3.3 %second_blocks.1 = (bf16[2,512,512]{2,1,0:T(8,128)(2,1)}, bf16[1024,512]{1,0:T(8,128)(2,1)}) custom-call(s32[4]{0:T(128)} %pad_add_fusion.place, bf16[1024,512]{1,0:T(8,128)(2,1)} %k_ref.5, bf16[1024,512]{1,0:T(8,128)(2,1)} %v_ref.5), custom_call_target="tpu_custom_call" | custom-call | flops 1 | bytes 1 | tf_op jit(solution)/shard_map/second_blocks/pallas_call | solution.py:297
  11.7 4.2 %collective-permute-start.1 = (bf16[2,512,512]{2,1,0:T(8,128)(2,1)}, bf16[2,512,512]{2,1,0:T(8,128)(2,1)}, u32[]{:S(2)}, u32[]{:S(2)}) collective-permute-start(bf16[2,512,512]{2,1,0:T(8,128)(2,1)} %get-tuple-element.50), channel_id=1, source_target_pairs={{0,12},{4,0},{8,4},{12,8},{16,28},{20,16},{24,20},{28,24},{32,44},... | collective-permute-start | bytes 3145736 | tf_op jit(solution)/shard_map/ppermute | solution.py:79
  15.9 0.8 bitcast_add_fusion
  16.7 0.7 slice_bitcast_fusion
  17.4 0.2 and_reduce_fusion.1
  17.6 0.8 fusion
  18.4 0.2 and_reduce_fusion
  18.6 0.7 reshape.60.flags
  19.3 5.8 %forward_own.1 = (f32[512,1024]{1,0:T(8,128)}, f32[4,2,512]{2,1,0:T(2,128)}, f32[4,2,512]{2,1,0:T(2,128)}) custom-call(s32[8]{0:T(128)} %reshape.60.flags, bf16[1024,512]{1,0:T(8,128)(2,1)} %q_ref.7, bf16[1024,512]{1,0:T(8,128)(2,1)} %k_ref.5, bf16[1024,512]{1,0:T(8,128)(2,1)} %v_ref.5, bf16[1024,512]{1,0:T(8,128)(2,1)} %k_ref.5), custom_call_target="tpu_custom_call" | custom-call | flops 1 | bytes 1 | tf_op jit(solution)/shard_map/forward_own/pallas_call | solution.py:297
  25.1 3.3 %projection_far.1.rest_0_.refs_4_ = bf16[512,2048]{1,0:T(8,128)(2,1)} custom-call(s32[4]{0:T(128)} %pad_add_fusion.place, bf16[512,4096]{1,0:T(8,128)(2,1)} %w_own.1, f32[4,2,512]{2,1,0:T(2,128)} %get-tuple-element.51.refs_0_.top_in), custom_call_target="tpu_custom_call" | custom-call | flops 1 | bytes 1 | tf_op jit(solution)/shard_map/projection_far/pallas_call | solution.py:297
  28.3 6.4 %projection_backward.2.refs_1_.rest_0_ = f32[1024,512]{1,0:T(8,128)} custom-call(s32[4]{0:T(128)} %pad_add_fusion.place, bf16[1024,1024]{1,0:T(8,128)(2,1)} %g0.1, bf16[1024,1024]{1,0:T(8,128)(2,1)} %collective-permute-done.2.b_ref.g1, bf16[512,4096]{1,0:T(8,128)(2,1)} %w_own.1, bf16[512,4096]{1,0:T(8,128)(2,1)} %w_own.1, ...), custom_call_target="tpu_custom_call" | custom-call | flops 1 | bytes 1 | tf_op jit(solution)/shard_map/projection_backward/pallas_call | solution.py:297
  34.8 4.2 %collective-permute-done.1.refs_0_ = bf16[2,512,512]{2,1,0:T(8,128)(2,1)} collective-permute-done((bf16[2,512,512]{2,1,0:T(8,128)(2,1)}, bf16[2,512,512]{2,1,0:T(8,128)(2,1)}, u32[]{:S(2)}, u32[]{:S(2)}) %collective-permute-start.1) | collective-permute-done | bytes 1048608 | tf_op jit(solution)/shard_map/ppermute | solution.py:79
  39.0 4.6 %collective-permute-start.3 = (bf16[1024,512]{1,0:T(8,128)(2,1)}, bf16[1024,512]{1,0:T(8,128)(2,1)}, u32[]{:S(2)}, u32[]{:S(2)}) collective-permute-start(bf16[1024,512]{1,0:T(8,128)(2,1)} %get-tuple-element.52), channel_id=1, source_target_pairs={{0,4},{4,8},{8,12},{12,16},{16,20},{20,24},{24,28},{28,32},{32,36}... | collective-permute-start | bytes 3145736 | tf_op jit(solution)/shard_map/ppermute | solution.py:66
  43.6 2.5 %collective-permute-start.6 = (bf16[1024,512]{1,0:T(8,128)(2,1)}, bf16[1024,512]{1,0:T(8,128)(2,1)}, u32[]{:S(2)}, u32[]{:S(2)}) collective-permute-start(bf16[1024,512]{1,0:T(8,128)(2,1)} %get-tuple-element.53.v1_ref), channel_id=1, source_target_pairs={{0,64},{1,65},{2,66},{3,67}} | collective-permute-start | bytes 3145736 | tf_op jit(solution)/shard_map/ppermute | solution.py:583
  46.1 3.6 %collective-permute-start.4 = (bf16[2,512,512]{2,1,0:T(8,128)(2,1)}, bf16[2,512,512]{2,1,0:T(8,128)(2,1)}, u32[]{:S(2)}, u32[]{:S(2)}) collective-permute-start(bf16[2,512,512]{2,1,0:T(8,128)(2,1)} %order.8.refs_2_.refs_5_), channel_id=1, source_target_pairs={{12,8},{0,12},{4,16},{8,20},{28,24},{16,28},{20,32},{24,36},{44,40... | collective-permute-start | bytes 3145736 | tf_op jit(solution)/shard_map/ppermute | solution.py:83
  49.7 1.3 collective-permute-done.5.refs_2_
  51.1 13.5 %collective-permute-done.3.refs_0_ = bf16[1024,512]{1,0:T(8,128)(2,1)} collective-permute-done((bf16[1024,512]{1,0:T(8,128)(2,1)}, bf16[1024,512]{1,0:T(8,128)(2,1)}, u32[]{:S(2)}, u32[]{:S(2)}) %collective-permute-start.3) | collective-permute-done | bytes 1048608 | tf_op jit(solution)/shard_map/ppermute | solution.py:66
  64.5 7.7 %collective-permute-done.6.refs_3_ = bf16[1024,512]{1,0:T(8,128)(2,1)} collective-permute-done((bf16[1024,512]{1,0:T(8,128)(2,1)}, bf16[1024,512]{1,0:T(8,128)(2,1)}, u32[]{:S(2)}, u32[]{:S(2)}) %collective-permute-start.6) | collective-permute-done | bytes 1048608 | tf_op jit(solution)/shard_map/ppermute | solution.py:583
  72.2 0.4 collective-permute-start.11
  72.6 5.7 %forward_behind.1 = (bf16[1024,512]{1,0:T(8,128)(2,1)}, bf16[512,1024]{1,0:T(8,128)(2,1)}, f32[4,2,512]{2,1,0:T(2,128)}) custom-call(s32[8]{0:T(128)} %reshape.60.flags, bf16[1024,512]{1,0:T(8,128)(2,1)} %q_ref.7, bf16[1024,512]{1,0:T(8,128)(2,1)} %get-tuple-element.54.k1_ref, bf16[1024,512]{1,0:T(8,128)(2,1)} %get-tuple-element.53.v1_ref, ...), custom_call_target="tpu_custom_call" | custom-call | flops 1 | bytes 1 | tf_op jit(solution)/shard_map/forward_behind/pallas_call | solution.py:297
  78.4 3.4 %collective-permute-start.13 = (bf16[1024,512]{1,0:T(8,128)(2,1)}, bf16[1024,512]{1,0:T(8,128)(2,1)}, u32[]{:S(2)}, u32[]{:S(2)}) collective-permute-start(bf16[1024,512]{1,0:T(8,128)(2,1)} %get-tuple-element.59.out_ref.own_rows.own), channel_id=1, source_target_pairs={{0,2},{1,3},{2,0},{3,1},{4,6},{5,7},{6,4},{7,5},{8,10},{9,11},{10,... | collective-permute-start | bytes 3145736 | tf_op jit(solution)/shard_map/ppermute | solution.py:38
  81.8 6.9 %projection_backward.3.after.grad_ref = bf16[1024,512]{1,0:T(8,128)(2,1)} custom-call(s32[4]{0:T(128)} %pad_add_fusion.place, bf16[1024,1024]{1,0:T(8,128)(2,1)} %get-tuple-element.61.a_ref.g2, bf16[1024,1024]{1,0:T(8,128)(2,1)} %order.11.b_ref.rest_1_.g3, bf16[512,4096]{1,0:T(8,128)(2,1)} %w_own.1, bf16[512,4096]{1,0:T(8,128)(2,1)} %w_own.1, ...), custom_call_target="tpu_custom_call" | custom-call | flops 1 | bytes 1 | tf_op jit(solution)/shard_map/projection_backward/pallas_call | solution.py:297
  88.6 13.3 %weight_gradient.1 = (bf16[2,512,512]{2,1,0:T(8,128)(2,1)}, bf16[2,512,512]{2,1,0:T(8,128)(2,1)}, bf16[2,512,512]{2,1,0:T(8,128)(2,1)}, bf16[2,512,512]{2,1,0:T(8,128)(2,1)}) custom-call(s32[4]{0:T(128)} %pad_add_fusion.place, bf16[512,1024]{1,0:T(8,128)(2,1)} %get-tuple-element.60.turned_ref, bf16[1024,1024]{1,0:T(8,128)(2,1)} %g0.1, ...), custom_call_target="tpu_custom_call" | custom-call | flops 1 | bytes 1 | tf_op jit(solution)/shard_map/weight_gradient/pallas_call | solution.py:297
  101.9 4.2 %collective-permute-start.8 = (bf16[2,512,512]{2,1,0:T(8,128)(2,1)}, bf16[2,512,512]{2,1,0:T(8,128)(2,1)}, u32[]{:S(2)}, u32[]{:S(2)}) collective-permute-start(bf16[2,512,512]{2,1,0:T(8,128)(2,1)} %get-tuple-element.63), channel_id=1, source_target_pairs={{0,16},{1,17},{2,18},{3,19},{4,20},{5,21},{6,22},{7,23},{8,24},{9,... | collective-permute-start | bytes 3145736 | tf_op jit(solution)/shard_map/ppermute | solution.py:38
  106.2 3.8 %collective-permute-start.10 = (bf16[2,512,512]{2,1,0:T(8,128)(2,1)}, bf16[2,512,512]{2,1,0:T(8,128)(2,1)}, u32[]{:S(2)}, u32[]{:S(2)}) collective-permute-start(bf16[2,512,512]{2,1,0:T(8,128)(2,1)} %get-tuple-element.65), channel_id=1, source_target_pairs={{0,32},{1,33},{2,34},{3,35},{4,36},{5,37},{6,38},{7,39},{8,40},{9,... | collective-permute-start | bytes 3145736 | tf_op jit(solution)/shard_map/ppermute | solution.py:38
  110.0 7.2 %backward_behind.1 = (bf16[2,1024,512]{2,1,0:T(8,128)(2,1)}, bf16[2,512,512]{2,1,0:T(8,128)(2,1)}, f32[512,1024]{1,0:T(8,128)}, f32[4,2,512]{2,1,0:T(2,128)}) custom-call(s32[8]{0:T(128)} %reshape.60.flags, bf16[1024,512]{1,0:T(8,128)(2,1)} %q_ref.7, bf16[1024,512]{1,0:T(8,128)(2,1)} %get-tuple-element.54.k1_ref, ...), custom_call_target="tpu_custom_call" | custom-call | flops 1 | bytes 1 | tf_op jit(solution)/shard_map/backward_behind/pallas_call | solution.py:297
  117.3 5.2 %collective-permute-done.11.refs_1_ = bf16[512,2048]{1,0:T(8,128)(2,1)} collective-permute-done((bf16[512,2048]{1,0:T(8,128)(2,1)}, bf16[512,2048]{1,0:T(8,128)(2,1)}, u32[]{:S(2)}, u32[]{:S(2)}) %collective-permute-start.11) | collective-permute-done | bytes 2097184 | tf_op jit(solution)/shard_map/ppermute | solution.py:38
  122.4 1.5 collective-permute-start.12
  123.9 7.9 %backward_own.1 = (bf16[1024,512]{1,0:T(8,128)(2,1)}, bf16[2,1024,512]{2,1,0:T(8,128)(2,1)}) custom-call(s32[8]{0:T(128)} %reshape.60.flags, bf16[1024,512]{1,0:T(8,128)(2,1)} %q_ref.7, bf16[1024,512]{1,0:T(8,128)(2,1)} %k_ref.5, bf16[1024,512]{1,0:T(8,128)(2,1)} %v_ref.5, bf16[1024,512]{1,0:T(8,128)(2,1)} %projection_backward.3.after.grad_ref, ...), custom_call_target="tpu_custom_call" | custom-call | flops 1 | bytes 1 | tf_op jit(solution)/shard_map/backward_own/pallas_call | solution.py:297
  131.9 12.6 %collective-permute-done.13.refs_0_ = bf16[1024,512]{1,0:T(8,128)(2,1)} collective-permute-done((bf16[1024,512]{1,0:T(8,128)(2,1)}, bf16[1024,512]{1,0:T(8,128)(2,1)}, u32[]{:S(2)}, u32[]{:S(2)}) %collective-permute-start.13) | collective-permute-done | bytes 1048608 | tf_op jit(solution)/shard_map/ppermute | solution.py:38
  144.5 5.1 %for_core.1.refs_5_ = bf16[4,512,1024]{2,1,0:T(8,128)(2,1)} custom-call(s32[4]{0:T(128)} %pad_add_fusion.place, bf16[512,4096]{1,0:T(8,128)(2,1)} %w_own.1, bf16[512,2048]{1,0:T(8,128)(2,1)} %get-tuple-element.71.far_ref.w_far, bf16[1024,512]{1,0:T(8,128)(2,1)} %order.13.far_rows.far, bf16[1024,512]{1,0:T(8,128)(2,1)} %get-tuple-element.59.out_ref.own_rows.own, ...), custom_call_target="tpu_custom_call" | custom-call | flops 1 | bytes 1 | tf_op jit(solution)/shard_map/for_core/pallas_call | solution.py:297
  149.7 4.3 %collective-permute-done.10.refs_2_ = bf16[2,512,512]{2,1,0:T(8,128)(2,1)} collective-permute-done((bf16[2,512,512]{2,1,0:T(8,128)(2,1)}, bf16[2,512,512]{2,1,0:T(8,128)(2,1)}, u32[]{:S(2)}, u32[]{:S(2)}) %collective-permute-start.10) | collective-permute-done | bytes 1048608 | tf_op jit(solution)/shard_map/ppermute | solution.py:38
  154.0 1.3 collective-permute-start.15
  155.3 6.8 %collective-permute-start.16 = (bf16[2,512,512]{2,1,0:T(8,128)(2,1)}, bf16[2,512,512]{2,1,0:T(8,128)(2,1)}, u32[]{:S(2)}, u32[]{:S(2)}) collective-permute-start(bf16[2,512,512]{2,1,0:T(8,128)(2,1)} %get-tuple-element.82), channel_id=1, source_target_pairs={{12,0},{0,4},{20,8},{24,12},{28,16},{16,20},{36,24},{40,28},{44,32... | collective-permute-start | bytes 3145736 | tf_op jit(solution)/shard_map/ppermute | solution.py:83
  162.1 3.8 %weight_y_sum.1 = (bf16[512,512]{1,0:T(8,128)(2,1)}, bf16[512,512]{1,0:T(8,128)(2,1)}) custom-call(s32[4]{0:T(128)} %pad_add_fusion.place, bf16[2,512,512]{2,1,0:T(8,128)(2,1)} %get-tuple-element.66.after.a, bf16[2,512,512]{2,1,0:T(8,128)(2,1)} %get-tuple-element.76.b.after, bf16[2,512,512]{2,1,0:T(8,128)(2,1)} %get-tuple-element.77.c, ...), custom_call_target="tpu_custom_call" | custom-call | flops 1 | bytes 1 | tf_op jit(solution)/shard_map/weight_y_sum/pallas_call | solution.py:297
  166.0 3.4 %collective-permute-start.17 = (bf16[512,512]{1,0:T(8,128)(2,1)}, bf16[512,512]{1,0:T(8,128)(2,1)}, u32[]{:S(2)}, u32[]{:S(2)}) collective-permute-start(bf16[512,512]{1,0:T(8,128)(2,1)} %get-tuple-element.83), channel_id=1, source_target_pairs={{0,64},{1,65},{2,66},{3,67},{4,68},{5,69},{6,70},{7,71},{8,72},{9,... | collective-permute-start | bytes 1572872 | tf_op jit(solution)/shard_map/ppermute | solution.py:38
  169.3 9.4 %projection.1.after = bf16[1024,1024]{1,0:T(8,128)(2,1)} custom-call(s32[4]{0:T(128)} %pad_add_fusion.place, bf16[1024,512]{1,0:T(8,128)(2,1)} %get-tuple-element.59.out_ref.own_rows.own, bf16[4,512,1024]{2,1,0:T(8,128)(2,1)} %collective-permute-done.14.core.far_core.w_core, bf16[1024,512]{1,0:T(8,128)(2,1)} %order.13.far_rows.far, ...), custom_call_target="tpu_custom_call" | custom-call | flops 1 | bytes 1 | tf_op jit(solution)/shard_map/projection/pallas_call | solution.py:297
  178.7 41.5 %collective-permute-done.17.b = bf16[512,512]{1,0:T(8,128)(2,1)} collective-permute-done((bf16[512,512]{1,0:T(8,128)(2,1)}, bf16[512,512]{1,0:T(8,128)(2,1)}, u32[]{:S(2)}, u32[]{:S(2)}) %collective-permute-start.17) | collective-permute-done | bytes 524320 | tf_op jit(solution)/shard_map/ppermute | solution.py:38
  220.2 3.7 %weight_by_z.1 = (bf16[512,128]{1,0:T(8,128)(2,1)}, bf16[512,128]{1,0:T(8,128)(2,1)}, bf16[512,128]{1,0:T(8,128)(2,1)}, bf16[512,128]{1,0:T(8,128)(2,1)}) custom-call(s32[4]{0:T(128)} %pad_add_fusion.place, bf16[512,512]{1,0:T(8,128)(2,1)} %get-tuple-element.79.after.a, bf16[512,512]{1,0:T(8,128)(2,1)} %collective-permute-done.17.b, ...), custom_call_target="tpu_custom_call" | custom-call | flops 1 | bytes 1 | tf_op jit(solution)/shard_map/weight_by_z/pallas_call | solution.py:297
  223.9 3.2 %collective-permute-start.19 = (bf16[512,128]{1,0:T(8,128)(2,1)}, bf16[512,128]{1,0:T(8,128)(2,1)}, u32[]{:S(2)}, u32[]{:S(2)}) collective-permute-start(bf16[512,128]{1,0:T(8,128)(2,1)} %get-tuple-element.88), channel_id=1, source_target_pairs={{0,12},{1,13},{2,14},{3,15},{4,0},{5,1},{6,2},{7,3},{8,4},{9,5},{1... | collective-permute-start | bytes 393224 | tf_op jit(solution)/shard_map/ppermute | solution.py:38
  227.1 5.1 %key_value_sum.1 = (bf16[1024,512]{1,0:T(8,128)(2,1)}, bf16[1024,512]{1,0:T(8,128)(2,1)}) custom-call(s32[4]{0:T(128)} %pad_add_fusion.place, bf16[2,1024,512]{2,1,0:T(8,128)(2,1)} %get-tuple-element.74.refs_1_.after.own_ref, bf16[2,1024,512]{2,1,0:T(8,128)(2,1)} %collective-permute-done.15.near_ref, bf16[2,512,512]{2,1,0:T(8,128)(2,1)} %collective-permute-done.16.far_ref, ...), custom_call_target="tpu_custom_call" | custom-call | flops 1 | bytes 1 | tf_op jit(solution)/shard_map/key_value_sum/pallas_call | solution.py:297
  232.2 0.3 collective-permute-done.19.refs_1_
  232.6 1.3 collective-permute-done.20.refs_2_
  233.9 1.9 convert_add_fusion
  (27 shorter events, 0.1 us)
Async XLA Ops:
  0.6 27.7 %collective-permute-start.2 = (bf16[1024,1024]{1,0:T(8,128)(2,1)}, bf16[1024,1024]{1,0:T(8,128)(2,1)}, u32[]{:S(2)}, u32[]{:S(2)}) collective-permute-start(bf16[1024,1024]{1,0:T(8,128)(2,1)} %g0.1), channel_id=1, source_target_pairs={{0,1},{1,0},{2,3},{3,2},{4,5},{5,4},{6,7},{7,6},{8,9},{9,8},{10,11... | collective-permute-start | bytes 6291464 | tf_op jit(solution)/shard_map/ppermute | solution.py:38
  0.7 50.3 %collective-permute-start.5 = (bf16[1024,1024]{1,0:T(8,128)(2,1)}, bf16[1024,1024]{1,0:T(8,128)(2,1)}, u32[]{:S(2)}, u32[]{:S(2)}) collective-permute-start(bf16[1024,1024]{1,0:T(8,128)(2,1)} %g0.1), channel_id=1, source_target_pairs={{0,2},{1,3},{2,0},{3,1},{4,6},{5,7},{6,4},{7,5},{8,10},{9,11},{10,... | collective-permute-start | bytes 6291464 | tf_op jit(solution)/shard_map/ppermute | solution.py:38
  3.9 35.1 %collective-permute-start = (bf16[1024,512]{1,0:T(8,128)(2,1)}, bf16[1024,512]{1,0:T(8,128)(2,1)}, u32[]{:S(2)}, u32[]{:S(2)}) collective-permute-start(bf16[1024,512]{1,0:T(8,128)(2,1)} %v_ref.5), channel_id=1, source_target_pairs={{0,4},{4,8},{8,12},{12,16},{16,20},{20,24},{24,28},{28,32},{32,36}... | collective-permute-start | bytes 3145736 | tf_op jit(solution)/shard_map/ppermute | solution.py:567
  11.7 27.3 %collective-permute-start.1 = (bf16[2,512,512]{2,1,0:T(8,128)(2,1)}, bf16[2,512,512]{2,1,0:T(8,128)(2,1)}, u32[]{:S(2)}, u32[]{:S(2)}) collective-permute-start(bf16[2,512,512]{2,1,0:T(8,128)(2,1)} %get-tuple-element.50), channel_id=1, source_target_pairs={{0,12},{4,0},{8,4},{12,8},{16,28},{20,16},{24,20},{28,24},{32,44},... | collective-permute-start | bytes 3145736 | tf_op jit(solution)/shard_map/ppermute | solution.py:79
  39.0 25.5 %collective-permute-start.3 = (bf16[1024,512]{1,0:T(8,128)(2,1)}, bf16[1024,512]{1,0:T(8,128)(2,1)}, u32[]{:S(2)}, u32[]{:S(2)}) collective-permute-start(bf16[1024,512]{1,0:T(8,128)(2,1)} %get-tuple-element.52), channel_id=1, source_target_pairs={{0,4},{4,8},{8,12},{12,16},{16,20},{20,24},{24,28},{28,32},{32,36}... | collective-permute-start | bytes 3145736 | tf_op jit(solution)/shard_map/ppermute | solution.py:66
  43.6 28.6 %collective-permute-start.6 = (bf16[1024,512]{1,0:T(8,128)(2,1)}, bf16[1024,512]{1,0:T(8,128)(2,1)}, u32[]{:S(2)}, u32[]{:S(2)}) collective-permute-start(bf16[1024,512]{1,0:T(8,128)(2,1)} %get-tuple-element.53.v1_ref), channel_id=1, source_target_pairs={{0,64},{1,65},{2,66},{3,67}} | collective-permute-start | bytes 3145736 | tf_op jit(solution)/shard_map/ppermute | solution.py:583
  46.1 26.0 %collective-permute-start.4 = (bf16[2,512,512]{2,1,0:T(8,128)(2,1)}, bf16[2,512,512]{2,1,0:T(8,128)(2,1)}, u32[]{:S(2)}, u32[]{:S(2)}) collective-permute-start(bf16[2,512,512]{2,1,0:T(8,128)(2,1)} %order.8.refs_2_.refs_5_), channel_id=1, source_target_pairs={{12,8},{0,12},{4,16},{8,20},{28,24},{16,28},{20,32},{24,36},{44,40... | collective-permute-start | bytes 3145736 | tf_op jit(solution)/shard_map/ppermute | solution.py:83
  72.2 6.2 %collective-permute-start.7 = (bf16[1024,1024]{1,0:T(8,128)(2,1)}, bf16[1024,1024]{1,0:T(8,128)(2,1)}, u32[]{:S(2)}, u32[]{:S(2)}) collective-permute-start(bf16[1024,1024]{1,0:T(8,128)(2,1)} %get-tuple-element.61.a_ref.g2), channel_id=1, source_target_pairs={{0,1},{1,0},{2,3},{3,2},{4,5},{5,4},{6,7},{7,6},{8,9},{9,8},{10,11... | collective-permute-start | bytes 6291464 | tf_op jit(solution)/shard_map/ppermute | solution.py:38
  72.2 50.2 %collective-permute-start.11 = (bf16[512,2048]{1,0:T(8,128)(2,1)}, bf16[512,2048]{1,0:T(8,128)(2,1)}, u32[]{:S(2)}, u32[]{:S(2)}) collective-permute-start(bf16[512,2048]{1,0:T(8,128)(2,1)} %get-tuple-element.69), channel_id=1, source_target_pairs={{0,2},{1,3},{2,0},{3,1},{4,6},{5,7},{6,4},{7,5},{8,10},{9,11},{10,... | collective-permute-start | bytes 6291464 | tf_op jit(solution)/shard_map/ppermute | solution.py:38
  78.4 66.1 %collective-permute-start.13 = (bf16[1024,512]{1,0:T(8,128)(2,1)}, bf16[1024,512]{1,0:T(8,128)(2,1)}, u32[]{:S(2)}, u32[]{:S(2)}) collective-permute-start(bf16[1024,512]{1,0:T(8,128)(2,1)} %get-tuple-element.59.out_ref.own_rows.own), channel_id=1, source_target_pairs={{0,2},{1,3},{2,0},{3,1},{4,6},{5,7},{6,4},{7,5},{8,10},{9,11},{10,... | collective-permute-start | bytes 3145736 | tf_op jit(solution)/shard_map/ppermute | solution.py:38
  101.9 47.7 %collective-permute-start.8 = (bf16[2,512,512]{2,1,0:T(8,128)(2,1)}, bf16[2,512,512]{2,1,0:T(8,128)(2,1)}, u32[]{:S(2)}, u32[]{:S(2)}) collective-permute-start(bf16[2,512,512]{2,1,0:T(8,128)(2,1)} %get-tuple-element.63), channel_id=1, source_target_pairs={{0,16},{1,17},{2,18},{3,19},{4,20},{5,21},{6,22},{7,23},{8,24},{9,... | collective-permute-start | bytes 3145736 | tf_op jit(solution)/shard_map/ppermute | solution.py:38
  106.2 43.5 %collective-permute-start.9 = (bf16[2,512,512]{2,1,0:T(8,128)(2,1)}, bf16[2,512,512]{2,1,0:T(8,128)(2,1)}, u32[]{:S(2)}, u32[]{:S(2)}) collective-permute-start(bf16[2,512,512]{2,1,0:T(8,128)(2,1)} %get-tuple-element.64), channel_id=1, source_target_pairs={{0,48},{1,49},{2,50},{3,51},{4,52},{5,53},{6,54},{7,55},{8,56},{9,... | collective-permute-start | bytes 3145736 | tf_op jit(solution)/shard_map/ppermute | solution.py:38
  106.2 47.8 %collective-permute-start.10 = (bf16[2,512,512]{2,1,0:T(8,128)(2,1)}, bf16[2,512,512]{2,1,0:T(8,128)(2,1)}, u32[]{:S(2)}, u32[]{:S(2)}) collective-permute-start(bf16[2,512,512]{2,1,0:T(8,128)(2,1)} %get-tuple-element.65), channel_id=1, source_target_pairs={{0,32},{1,33},{2,34},{3,35},{4,36},{5,37},{6,38},{7,39},{8,40},{9,... | collective-permute-start | bytes 3145736 | tf_op jit(solution)/shard_map/ppermute | solution.py:38
  122.4 31.5 %collective-permute-start.12 = (bf16[2,512,512]{2,1,0:T(8,128)(2,1)}, bf16[2,512,512]{2,1,0:T(8,128)(2,1)}, u32[]{:S(2)}, u32[]{:S(2)}) collective-permute-start(bf16[2,512,512]{2,1,0:T(8,128)(2,1)} %get-tuple-element.70), channel_id=1, source_target_pairs={{8,12},{12,0},{16,20},{20,24},{24,28},{28,16},{32,36},{36,40},{40,... | collective-permute-start | bytes 3145736 | tf_op jit(solution)/shard_map/ppermute | solution.py:79
  154.0 15.3 %collective-permute-start.14 = (bf16[4,512,1024]{2,1,0:T(8,128)(2,1)}, bf16[4,512,1024]{2,1,0:T(8,128)(2,1)}, u32[]{:S(2)}, u32[]{:S(2)}) collective-permute-start(bf16[4,512,1024]{2,1,0:T(8,128)(2,1)} %get-tuple-element.75), channel_id=1, source_target_pairs={{0,1},{1,0},{2,3},{3,2},{4,5},{5,4},{6,7},{7,6},{8,9},{9,8},{10,11... | collective-permute-start | bytes 12582920 | tf_op jit(solution)/shard_map/ppermute | solution.py:38
  154.0 73.1 %collective-permute-start.15 = (bf16[2,1024,512]{2,1,0:T(8,128)(2,1)}, bf16[2,1024,512]{2,1,0:T(8,128)(2,1)}, u32[]{:S(2)}, u32[]{:S(2)}) collective-permute-start(bf16[2,1024,512]{2,1,0:T(8,128)(2,1)} %get-tuple-element.81), channel_id=1, source_target_pairs={{4,0},{8,4},{12,8},{16,12},{20,16},{24,20},{28,24},{32,28},{36,32}... | collective-permute-start | bytes 6291464 | tf_op jit(solution)/shard_map/ppermute | solution.py:66
  155.3 71.8 %collective-permute-start.16 = (bf16[2,512,512]{2,1,0:T(8,128)(2,1)}, bf16[2,512,512]{2,1,0:T(8,128)(2,1)}, u32[]{:S(2)}, u32[]{:S(2)}) collective-permute-start(bf16[2,512,512]{2,1,0:T(8,128)(2,1)} %get-tuple-element.82), channel_id=1, source_target_pairs={{12,0},{0,4},{20,8},{24,12},{28,16},{16,20},{36,24},{40,28},{44,32... | collective-permute-start | bytes 3145736 | tf_op jit(solution)/shard_map/ppermute | solution.py:83
  166.0 54.2 %collective-permute-start.17 = (bf16[512,512]{1,0:T(8,128)(2,1)}, bf16[512,512]{1,0:T(8,128)(2,1)}, u32[]{:S(2)}, u32[]{:S(2)}) collective-permute-start(bf16[512,512]{1,0:T(8,128)(2,1)} %get-tuple-element.83), channel_id=1, source_target_pairs={{0,64},{1,65},{2,66},{3,67},{4,68},{5,69},{6,70},{7,71},{8,72},{9,... | collective-permute-start | bytes 1572872 | tf_op jit(solution)/shard_map/ppermute | solution.py:38
  223.9 8.4 %collective-permute-start.18 = (bf16[512,128]{1,0:T(8,128)(2,1)}, bf16[512,128]{1,0:T(8,128)(2,1)}, u32[]{:S(2)}, u32[]{:S(2)}) collective-permute-start(bf16[512,128]{1,0:T(8,128)(2,1)} %get-tuple-element.87), channel_id=1, source_target_pairs={{0,4},{1,5},{2,6},{3,7},{4,8},{5,9},{6,10},{7,11},{8,12},{9,13},{1... | collective-permute-start | bytes 393224 | tf_op jit(solution)/shard_map/ppermute | solution.py:38
  223.9 8.7 %collective-permute-start.19 = (bf16[512,128]{1,0:T(8,128)(2,1)}, bf16[512,128]{1,0:T(8,128)(2,1)}, u32[]{:S(2)}, u32[]{:S(2)}) collective-permute-start(bf16[512,128]{1,0:T(8,128)(2,1)} %get-tuple-element.88), channel_id=1, source_target_pairs={{0,12},{1,13},{2,14},{3,15},{4,0},{5,1},{6,2},{7,3},{8,4},{9,5},{1... | collective-permute-start | bytes 393224 | tf_op jit(solution)/shard_map/ppermute | solution.py:38
  227.1 6.8 %collective-permute-start.20 = (bf16[512,128]{1,0:T(8,128)(2,1)}, bf16[512,128]{1,0:T(8,128)(2,1)}, u32[]{:S(2)}, u32[]{:S(2)}) collective-permute-start(bf16[512,128]{1,0:T(8,128)(2,1)} %get-tuple-element.89), channel_id=1, source_target_pairs={{0,8},{1,9},{2,10},{3,11},{4,12},{5,13},{6,14},{7,15},{8,0},{9,1},... | collective-permute-start | bytes 393224 | tf_op jit(solution)/shard_map/ppermute | solution.py:38

commit v11 on v9

--- a/solution.py
+++ b/solution.py
@@ -457,7 +457,7 @@
 
 
 def over_y(parts):
-    return [to_y(parts[s], s + 1) for s in (0, 2, 1)]
+    return [to_y(parts[s], s + 1) for s in (1, 0, 2)]
 
 
 def pieces_kernel(place, a, b, c, d, after, *outs):
@@ -610,11 +610,11 @@
     *weight_moved, near_back, back_moved, from_core = together(
         [*weight_moved, near_back, back_moved, from_core]
     )
+    far_back = second_hop(back_moved, -1)
     near_back = along_ctx(near_back, -1)
-    far_back = second_hop(back_moved, -1)
     from_core = to_core(from_core)
     weight_pieces = pieces_by_z(place, [weight_parts[3], *weight_moved], weight_moved[0])
-    weight_moved = [to_z(weight_pieces[s], s + 1) for s in (0, 2, 1)]
+    weight_moved = [to_z(weight_pieces[s], s + 1) for s in (1, 0, 2)]
     mixed = mix(
         place, attention, far_attention, out_weight, far_weight, from_core, weight_pieces[3]
     )

time: 234 us -> 234 us (level)
  no operation moved by 1% of the time
where the time goes in v11:
time: 234 us; the launch traced here: 230 us
  Pallas kernels  94.5 us (40%)
  waiting for transfers between devices  76.9 us (33%)
  starting transfers between devices  52.4 us (22%)
  other arithmetic  3.55 us (2%)
    pallas_call x14, Pallas kernels, call(): pl.pallas_call(kernel, grid_spec=pltpu.PrefetchScalarGridSpec(num_scalar_...  94.5 us
    ppermute x13, waiting for transfers between devices, move(): return lax.ppermute(value, AXES, pairs)  55.2 us
    ppermute x13, starting transfers between devices, move(): return lax.ppermute(value, AXES, pairs)  27.9 us
    ppermute x2, waiting for transfers between devices, along_ctx(): return lax.ppermute(value, 'ctx', pairs)  15.2 us
    ppermute x2, starting transfers between devices, first_hop(): return lax.ppermute(value, 'ctx', [(s, m) for s, m, _ in two_pairs(sign)])  7.01 us
    ppermute x2, starting transfers between devices, second_hop(): return lax.ppermute(value, 'ctx', [(m, t) for _, m, t in two_pairs(sign)])  6.99 us
    ppermute x2, starting transfers between devices, along_ctx(): return lax.ppermute(value, 'ctx', pairs)  5.03 us
  transfers between devices with their start and end apart: 21, of which 10 were waited for; matrix products, arithmetic and copies ran while one was open for 2% of the time, Pallas kernels for 41%

profile of v11, /device:TPU:30, one launch (start us, length us, event | category | flops | bytes accessed | tf_op | source)
XLA Modules:
  0.0 230.2 jit_solution(5955333528229889414)
XLA Ops:
  0.7 1.5 collective-permute-start.5
  2.2 3.8 %collective-permute-start = (bf16[1024,512]{1,0:T(8,128)(2,1)}, bf16[1024,512]{1,0:T(8,128)(2,1)}, u32[]{:S(2)}, u32[]{:S(2)}) collective-permute-start(bf16[1024,512]{1,0:T(8,128)(2,1)} %v_ref.5), channel_id=1, source_target_pairs={{0,4},{4,8},{8,12},{12,16},{16,20},{20,24},{24,28},{28,32},{32,36}... | collective-permute-start | bytes 3145736 | tf_op jit(solution)/shard_map/ppermute | solution.py:567
  6.1 0.6 pad_add_fusion.place
  6.7 3.3 %second_blocks.1 = (bf16[2,512,512]{2,1,0:T(8,128)(2,1)}, bf16[1024,512]{1,0:T(8,128)(2,1)}) custom-call(s32[4]{0:T(128)} %pad_add_fusion.place, bf16[1024,512]{1,0:T(8,128)(2,1)} %k_ref.5, bf16[1024,512]{1,0:T(8,128)(2,1)} %v_ref.5), custom_call_target="tpu_custom_call" | custom-call | flops 1 | bytes 1 | tf_op jit(solution)/shard_map/second_blocks/pallas_call | solution.py:297
  10.0 3.4 %collective-permute-start.1 = (bf16[2,512,512]{2,1,0:T(8,128)(2,1)}, bf16[2,512,512]{2,1,0:T(8,128)(2,1)}, u32[]{:S(2)}, u32[]{:S(2)}) collective-permute-start(bf16[2,512,512]{2,1,0:T(8,128)(2,1)} %get-tuple-element.47), channel_id=1, source_target_pairs={{0,12},{4,0},{8,4},{12,8},{16,28},{20,16},{24,20},{28,24},{32,44},... | collective-permute-start | bytes 3145736 | tf_op jit(solution)/shard_map/ppermute | solution.py:79
  13.4 0.8 bitcast_add_fusion
  14.1 0.7 slice_bitcast_fusion
  14.9 0.2 and_reduce_fusion.1
  15.1 0.8 fusion
  16.0 0.6 reshape.60.flags
  16.7 7.4 %forward_own.1 = (f32[512,1024]{1,0:T(8,128)}, f32[4,2,512]{2,1,0:T(2,128)}, f32[4,2,512]{2,1,0:T(2,128)}) custom-call(s32[8]{0:T(128)} %reshape.60.flags, bf16[1024,512]{1,0:T(8,128)(2,1)} %q_ref.7, bf16[1024,512]{1,0:T(8,128)(2,1)} %k_ref.5, bf16[1024,512]{1,0:T(8,128)(2,1)} %v_ref.5, bf16[1024,512]{1,0:T(8,128)(2,1)} %k_ref.5), custom_call_target="tpu_custom_call" | custom-call | flops 1 | bytes 1 | tf_op jit(solution)/shard_map/forward_own/pallas_call | solution.py:297
  24.1 3.3 %projection_far.1.rest_0_.refs_4_ = bf16[512,2048]{1,0:T(8,128)(2,1)} custom-call(s32[4]{0:T(128)} %pad_add_fusion.place, bf16[512,4096]{1,0:T(8,128)(2,1)} %w_own.1, f32[4,2,512]{2,1,0:T(2,128)} %get-tuple-element.48.refs_0_.top_in), custom_call_target="tpu_custom_call" | custom-call | flops 1 | bytes 1 | tf_op jit(solution)/shard_map/projection_far/pallas_call | solution.py:297
  27.4 6.4 %projection_backward.2.refs_1_.rest_0_ = f32[1024,512]{1,0:T(8,128)} custom-call(s32[4]{0:T(128)} %pad_add_fusion.place, bf16[1024,1024]{1,0:T(8,128)(2,1)} %g0.1, bf16[1024,1024]{1,0:T(8,128)(2,1)} %collective-permute-done.2.b_ref.g1, bf16[512,4096]{1,0:T(8,128)(2,1)} %w_own.1, bf16[512,4096]{1,0:T(8,128)(2,1)} %w_own.1, ...), custom_call_target="tpu_custom_call" | custom-call | flops 1 | bytes 1 | tf_op jit(solution)/shard_map/projection_backward/pallas_call | solution.py:297
  33.8 3.3 %collective-permute-done.1.refs_0_ = bf16[2,512,512]{2,1,0:T(8,128)(2,1)} collective-permute-done((bf16[2,512,512]{2,1,0:T(8,128)(2,1)}, bf16[2,512,512]{2,1,0:T(8,128)(2,1)}, u32[]{:S(2)}, u32[]{:S(2)}) %collective-permute-start.1) | collective-permute-done | bytes 1048608 | tf_op jit(solution)/shard_map/ppermute | solution.py:79
  37.1 2.7 %collective-permute-start.3 = (bf16[1024,512]{1,0:T(8,128)(2,1)}, bf16[1024,512]{1,0:T(8,128)(2,1)}, u32[]{:S(2)}, u32[]{:S(2)}) collective-permute-start(bf16[1024,512]{1,0:T(8,128)(2,1)} %get-tuple-element.49), channel_id=1, source_target_pairs={{0,4},{4,8},{8,12},{12,16},{16,20},{20,24},{24,28},{28,32},{32,36}... | collective-permute-start | bytes 3145736 | tf_op jit(solution)/shard_map/ppermute | solution.py:66
  39.8 1.7 collective-permute-start.6
  41.5 3.4 %collective-permute-start.4 = (bf16[2,512,512]{2,1,0:T(8,128)(2,1)}, bf16[2,512,512]{2,1,0:T(8,128)(2,1)}, u32[]{:S(2)}, u32[]{:S(2)}) collective-permute-start(bf16[2,512,512]{2,1,0:T(8,128)(2,1)} %order.8.refs_2_.refs_5_), channel_id=1, source_target_pairs={{12,8},{0,12},{4,16},{8,20},{28,24},{16,28},{20,32},{24,36},{44,40... | collective-permute-start | bytes 3145736 | tf_op jit(solution)/shard_map/ppermute | solution.py:83
  45.0 5.6 %collective-permute-done.5.refs_2_ = bf16[1024,1024]{1,0:T(8,128)(2,1)} collective-permute-done((bf16[1024,1024]{1,0:T(8,128)(2,1)}, bf16[1024,1024]{1,0:T(8,128)(2,1)}, u32[]{:S(2)}, u32[]{:S(2)}) %collective-permute-start.5) | collective-permute-done | bytes 2097184 | tf_op jit(solution)/shard_map/ppermute | solution.py:38
  50.6 15.2 %collective-permute-done.3.refs_0_ = bf16[1024,512]{1,0:T(8,128)(2,1)} collective-permute-done((bf16[1024,512]{1,0:T(8,128)(2,1)}, bf16[1024,512]{1,0:T(8,128)(2,1)}, u32[]{:S(2)}, u32[]{:S(2)}) %collective-permute-start.3) | collective-permute-done | bytes 1048608 | tf_op jit(solution)/shard_map/ppermute | solution.py:66
  65.8 3.2 %collective-permute-done.4.refs_1_ = bf16[2,512,512]{2,1,0:T(8,128)(2,1)} collective-permute-done((bf16[2,512,512]{2,1,0:T(8,128)(2,1)}, bf16[2,512,512]{2,1,0:T(8,128)(2,1)}, u32[]{:S(2)}, u32[]{:S(2)}) %collective-permute-start.4) | collective-permute-done | bytes 1048608 | tf_op jit(solution)/shard_map/ppermute | solution.py:83
  69.0 2.1 collective-permute-start.11
  71.1 7.3 %forward_behind.1 = (bf16[1024,512]{1,0:T(8,128)(2,1)}, bf16[512,1024]{1,0:T(8,128)(2,1)}, f32[4,2,512]{2,1,0:T(2,128)}) custom-call(s32[8]{0:T(128)} %reshape.60.flags, bf16[1024,512]{1,0:T(8,128)(2,1)} %q_ref.7, bf16[1024,512]{1,0:T(8,128)(2,1)} %get-tuple-element.51.k1_ref, bf16[1024,512]{1,0:T(8,128)(2,1)} %get-tuple-element.50.v1_ref, ...), custom_call_target="tpu_custom_call" | custom-call | flops 1 | bytes 1 | tf_op jit(solution)/shard_map/forward_behind/pallas_call | solution.py:297
  78.5 1.7 collective-permute-start.13
  80.1 6.9 %projection_backward.3.after.grad_ref = bf16[1024,512]{1,0:T(8,128)(2,1)} custom-call(s32[4]{0:T(128)} %pad_add_fusion.place, bf16[1024,1024]{1,0:T(8,128)(2,1)} %get-tuple-element.58.a_ref.g2, bf16[1024,1024]{1,0:T(8,128)(2,1)} %order.11.b_ref.rest_1_.g3, bf16[512,4096]{1,0:T(8,128)(2,1)} %w_own.1, bf16[512,4096]{1,0:T(8,128)(2,1)} %w_own.1, ...), custom_call_target="tpu_custom_call" | custom-call | flops 1 | bytes 1 | tf_op jit(solution)/shard_map/projection_backward/pallas_call | solution.py:297
  87.0 13.3 %weight_gradient.1 = (bf16[2,512,512]{2,1,0:T(8,128)(2,1)}, bf16[2,512,512]{2,1,0:T(8,128)(2,1)}, bf16[2,512,512]{2,1,0:T(8,128)(2,1)}, bf16[2,512,512]{2,1,0:T(8,128)(2,1)}) custom-call(s32[4]{0:T(128)} %pad_add_fusion.place, bf16[512,1024]{1,0:T(8,128)(2,1)} %get-tuple-element.57.turned_ref, bf16[1024,1024]{1,0:T(8,128)(2,1)} %g0.1, ...), custom_call_target="tpu_custom_call" | custom-call | flops 1 | bytes 1 | tf_op jit(solution)/shard_map/weight_gradient/pallas_call | solution.py:297
  100.3 3.9 %collective-permute-start.8 = (bf16[2,512,512]{2,1,0:T(8,128)(2,1)}, bf16[2,512,512]{2,1,0:T(8,128)(2,1)}, u32[]{:S(2)}, u32[]{:S(2)}) collective-permute-start(bf16[2,512,512]{2,1,0:T(8,128)(2,1)} %get-tuple-element.60), channel_id=1, source_target_pairs={{0,32},{1,33},{2,34},{3,35},{4,36},{5,37},{6,38},{7,39},{8,40},{9,... | collective-permute-start | bytes 3145736 | tf_op jit(solution)/shard_map/ppermute | solution.py:38
  104.2 2.9 %collective-permute-start.9 = (bf16[2,512,512]{2,1,0:T(8,128)(2,1)}, bf16[2,512,512]{2,1,0:T(8,128)(2,1)}, u32[]{:S(2)}, u32[]{:S(2)}) collective-permute-start(bf16[2,512,512]{2,1,0:T(8,128)(2,1)} %get-tuple-element.61), channel_id=1, source_target_pairs={{0,16},{1,17},{2,18},{3,19},{4,20},{5,21},{6,22},{7,23},{8,24},{9,... | collective-permute-start | bytes 3145736 | tf_op jit(solution)/shard_map/ppermute | solution.py:38
  107.1 0.8 collective-permute-start.10
  107.9 9.1 %backward_behind.1 = (bf16[2,1024,512]{2,1,0:T(8,128)(2,1)}, bf16[2,512,512]{2,1,0:T(8,128)(2,1)}, f32[512,1024]{1,0:T(8,128)}, f32[4,2,512]{2,1,0:T(2,128)}) custom-call(s32[8]{0:T(128)} %reshape.60.flags, bf16[1024,512]{1,0:T(8,128)(2,1)} %q_ref.7, bf16[1024,512]{1,0:T(8,128)(2,1)} %get-tuple-element.51.k1_ref, ...), custom_call_target="tpu_custom_call" | custom-call | flops 1 | bytes 1 | tf_op jit(solution)/shard_map/backward_behind/pallas_call | solution.py:297
  117.0 2.2 collective-permute-done.11.refs_1_
  119.2 3.6 %collective-permute-start.12 = (bf16[2,512,512]{2,1,0:T(8,128)(2,1)}, bf16[2,512,512]{2,1,0:T(8,128)(2,1)}, u32[]{:S(2)}, u32[]{:S(2)}) collective-permute-start(bf16[2,512,512]{2,1,0:T(8,128)(2,1)} %get-tuple-element.67), channel_id=1, source_target_pairs={{8,12},{12,0},{16,20},{20,24},{24,28},{28,16},{32,36},{36,40},{40,... | collective-permute-start | bytes 3145736 | tf_op jit(solution)/shard_map/ppermute | solution.py:79
  122.8 10.5 %backward_own.1 = (bf16[1024,512]{1,0:T(8,128)(2,1)}, bf16[2,1024,512]{2,1,0:T(8,128)(2,1)}) custom-call(s32[8]{0:T(128)} %reshape.60.flags, bf16[1024,512]{1,0:T(8,128)(2,1)} %q_ref.7, bf16[1024,512]{1,0:T(8,128)(2,1)} %k_ref.5, bf16[1024,512]{1,0:T(8,128)(2,1)} %v_ref.5, bf16[1024,512]{1,0:T(8,128)(2,1)} %projection_backward.3.after.grad_ref, ...), custom_call_target="tpu_custom_call" | custom-call | flops 1 | bytes 1 | tf_op jit(solution)/shard_map/backward_own/pallas_call | solution.py:297
  133.3 8.0 %collective-permute-done.13.refs_0_ = bf16[1024,512]{1,0:T(8,128)(2,1)} collective-permute-done((bf16[1024,512]{1,0:T(8,128)(2,1)}, bf16[1024,512]{1,0:T(8,128)(2,1)}, u32[]{:S(2)}, u32[]{:S(2)}) %collective-permute-start.13) | collective-permute-done | bytes 1048608 | tf_op jit(solution)/shard_map/ppermute | solution.py:38
  141.3 5.1 %for_core.1.refs_5_ = bf16[4,512,1024]{2,1,0:T(8,128)(2,1)} custom-call(s32[4]{0:T(128)} %pad_add_fusion.place, bf16[512,4096]{1,0:T(8,128)(2,1)} %w_own.1, bf16[512,2048]{1,0:T(8,128)(2,1)} %get-tuple-element.68.far_ref.w_far, bf16[1024,512]{1,0:T(8,128)(2,1)} %order.13.far_rows.far, bf16[1024,512]{1,0:T(8,128)(2,1)} %get-tuple-element.56.out_ref.own_rows.own, ...), custom_call_target="tpu_custom_call" | custom-call | flops 1 | bytes 1 | tf_op jit(solution)/shard_map/for_core/pallas_call | solution.py:297
  146.4 7.5 %collective-permute-done.9.refs_1_ = bf16[2,512,512]{2,1,0:T(8,128)(2,1)} collective-permute-done((bf16[2,512,512]{2,1,0:T(8,128)(2,1)}, bf16[2,512,512]{2,1,0:T(8,128)(2,1)}, u32[]{:S(2)}, u32[]{:S(2)}) %collective-permute-start.9) | collective-permute-done | bytes 1048608 | tf_op jit(solution)/shard_map/ppermute | solution.py:38
  154.0 2.3 %collective-permute-start.15 = (bf16[2,1024,512]{2,1,0:T(8,128)(2,1)}, bf16[2,1024,512]{2,1,0:T(8,128)(2,1)}, u32[]{:S(2)}, u32[]{:S(2)}) collective-permute-start(bf16[2,1024,512]{2,1,0:T(8,128)(2,1)} %get-tuple-element.78), channel_id=1, source_target_pairs={{4,0},{8,4},{12,8},{16,12},{20,16},{24,20},{28,24},{32,28},{36,32}... | collective-permute-start | bytes 6291464 | tf_op jit(solution)/shard_map/ppermute | solution.py:66
  156.4 3.5 %collective-permute-start.16 = (bf16[2,512,512]{2,1,0:T(8,128)(2,1)}, bf16[2,512,512]{2,1,0:T(8,128)(2,1)}, u32[]{:S(2)}, u32[]{:S(2)}) collective-permute-start(bf16[2,512,512]{2,1,0:T(8,128)(2,1)} %get-tuple-element.79), channel_id=1, source_target_pairs={{12,0},{0,4},{20,8},{24,12},{28,16},{16,20},{36,24},{40,28},{44,32... | collective-permute-start | bytes 3145736 | tf_op jit(solution)/shard_map/ppermute | solution.py:83
  159.9 4.8 %weight_by_z.1 = (bf16[2,512,128]{2,1,0:T(8,128)(2,1)}, bf16[2,512,128]{2,1,0:T(8,128)(2,1)}, bf16[2,512,128]{2,1,0:T(8,128)(2,1)}, bf16[2,512,128]{2,1,0:T(8,128)(2,1)}) custom-call(s32[4]{0:T(128)} %pad_add_fusion.place, bf16[2,512,512]{2,1,0:T(8,128)(2,1)} %get-tuple-element.63.after.a, bf16[2,512,512]{2,1,0:T(8,128)(2,1)} %get-tuple-element.73.b.after, ...), custom_call_target="tpu_custom_call" | custom-call | flops 1 | bytes 1 | tf_op jit(solution)/shard_map/weight_by_z/pallas_call | solution.py:297
  164.7 6.3 %collective-permute-start.17 = (bf16[2,512,128]{2,1,0:T(8,128)(2,1)}, bf16[2,512,128]{2,1,0:T(8,128)(2,1)}, u32[]{:S(2)}, u32[]{:S(2)}) collective-permute-start(bf16[2,512,128]{2,1,0:T(8,128)(2,1)} %get-tuple-element.80), channel_id=1, source_target_pairs={{0,8},{1,9},{2,10},{3,11},{4,12},{5,13},{6,14},{7,15},{8,0},{9,1},... | collective-permute-start | bytes 786440 | tf_op jit(solution)/shard_map/ppermute | solution.py:38
  171.1 3.2 %collective-permute-start.19 = (bf16[2,512,128]{2,1,0:T(8,128)(2,1)}, bf16[2,512,128]{2,1,0:T(8,128)(2,1)}, u32[]{:S(2)}, u32[]{:S(2)}) collective-permute-start(bf16[2,512,128]{2,1,0:T(8,128)(2,1)} %get-tuple-element.82), channel_id=1, source_target_pairs={{0,12},{1,13},{2,14},{3,15},{4,0},{5,1},{6,2},{7,3},{8,4},{9,5},{1... | collective-permute-start | bytes 786440 | tf_op jit(solution)/shard_map/ppermute | solution.py:38
  174.3 9.4 %projection.1.after = bf16[1024,1024]{1,0:T(8,128)(2,1)} custom-call(s32[4]{0:T(128)} %pad_add_fusion.place, bf16[1024,512]{1,0:T(8,128)(2,1)} %get-tuple-element.56.out_ref.own_rows.own, bf16[4,512,1024]{2,1,0:T(8,128)(2,1)} %collective-permute-done.14.core.far_core.w_core, bf16[1024,512]{1,0:T(8,128)(2,1)} %order.13.far_rows.far, ...), custom_call_target="tpu_custom_call" | custom-call | flops 1 | bytes 1 | tf_op jit(solution)/shard_map/projection/pallas_call | solution.py:297
  183.7 5.6 %collective-permute-done.17.b_ref = bf16[2,512,128]{2,1,0:T(8,128)(2,1)} collective-permute-done((bf16[2,512,128]{2,1,0:T(8,128)(2,1)}, bf16[2,512,128]{2,1,0:T(8,128)(2,1)}, u32[]{:S(2)}, u32[]{:S(2)}) %collective-permute-start.17) | collective-permute-done | bytes 262176 | tf_op jit(solution)/shard_map/ppermute | solution.py:38
  189.3 9.0 %collective-permute-done.18.c_ref = bf16[2,512,128]{2,1,0:T(8,128)(2,1)} collective-permute-done((bf16[2,512,128]{2,1,0:T(8,128)(2,1)}, bf16[2,512,128]{2,1,0:T(8,128)(2,1)}, u32[]{:S(2)}, u32[]{:S(2)}) %collective-permute-start.18) | collective-permute-done | bytes 262176 | tf_op jit(solution)/shard_map/ppermute | solution.py:38
  198.4 17.1 %collective-permute-done.19.d_ref = bf16[2,512,128]{2,1,0:T(8,128)(2,1)} collective-permute-done((bf16[2,512,128]{2,1,0:T(8,128)(2,1)}, bf16[2,512,128]{2,1,0:T(8,128)(2,1)}, u32[]{:S(2)}, u32[]{:S(2)}) %collective-permute-start.19) | collective-permute-done | bytes 262176 | tf_op jit(solution)/shard_map/ppermute | solution.py:38
  215.5 2.6 %weight_z_sum.1 = (f32[512,128]{1,0:T(8,128)}, bf16[512,128]{1,0:T(8,128)(2,1)}) custom-call(s32[4]{0:T(128)} %pad_add_fusion.place, bf16[2,512,128]{2,1,0:T(8,128)(2,1)} %get-tuple-element.76.after.a_ref, bf16[2,512,128]{2,1,0:T(8,128)(2,1)} %collective-permute-done.17.b_ref, bf16[2,512,128]{2,1,0:T(8,128)(2,1)} %collective-permute-done.18.c_ref, ...), custom_call_target="tpu_custom_call" | custom-call | flops 1 | bytes 1 | tf_op jit(solution)/shard_map/weight_z_sum/pallas_call | solution.py:297
  218.2 5.2 %collective-permute-start.20 = (bf16[512,128]{1,0:T(8,128)(2,1)}, bf16[512,128]{1,0:T(8,128)(2,1)}, u32[]{:S(2)}, u32[]{:S(2)}) collective-permute-start(bf16[512,128]{1,0:T(8,128)(2,1)} %get-tuple-element.86), channel_id=1, source_target_pairs={{0,64},{1,65},{2,66},{3,67},{4,68},{5,69},{6,70},{7,71},{8,72},{9,... | collective-permute-start | bytes 393224 | tf_op jit(solution)/shard_map/ppermute | solution.py:38
  223.4 5.1 %key_value_sum.1 = (bf16[1024,512]{1,0:T(8,128)(2,1)}, bf16[1024,512]{1,0:T(8,128)(2,1)}) custom-call(s32[4]{0:T(128)} %pad_add_fusion.place, bf16[2,1024,512]{2,1,0:T(8,128)(2,1)} %get-tuple-element.71.refs_1_.after.own_ref, bf16[2,1024,512]{2,1,0:T(8,128)(2,1)} %collective-permute-done.15.near_ref, bf16[2,512,512]{2,1,0:T(8,128)(2,1)} %collective-permute-done.16.far_ref, ...), custom_call_target="tpu_custom_call" | custom-call | flops 1 | bytes 1 | tf_op jit(solution)/shard_map/key_value_sum/pallas_call | solution.py:297
  228.5 1.7 convert_add_fusion
  (27 shorter events, 0.5 us)
Async XLA Ops:
  0.6 26.7 %collective-permute-start.2 = (bf16[1024,1024]{1,0:T(8,128)(2,1)}, bf16[1024,1024]{1,0:T(8,128)(2,1)}, u32[]{:S(2)}, u32[]{:S(2)}) collective-permute-start(bf16[1024,1024]{1,0:T(8,128)(2,1)} %g0.1), channel_id=1, source_target_pairs={{0,1},{1,0},{2,3},{3,2},{4,5},{5,4},{6,7},{7,6},{8,9},{9,8},{10,11... | collective-permute-start | bytes 6291464 | tf_op jit(solution)/shard_map/ppermute | solution.py:38
  0.7 49.9 %collective-permute-start.5 = (bf16[1024,1024]{1,0:T(8,128)(2,1)}, bf16[1024,1024]{1,0:T(8,128)(2,1)}, u32[]{:S(2)}, u32[]{:S(2)}) collective-permute-start(bf16[1024,1024]{1,0:T(8,128)(2,1)} %g0.1), channel_id=1, source_target_pairs={{0,2},{1,3},{2,0},{3,1},{4,6},{5,7},{6,4},{7,5},{8,10},{9,11},{10,... | collective-permute-start | bytes 6291464 | tf_op jit(solution)/shard_map/ppermute | solution.py:38
  2.2 34.9 %collective-permute-start = (bf16[1024,512]{1,0:T(8,128)(2,1)}, bf16[1024,512]{1,0:T(8,128)(2,1)}, u32[]{:S(2)}, u32[]{:S(2)}) collective-permute-start(bf16[1024,512]{1,0:T(8,128)(2,1)} %v_ref.5), channel_id=1, source_target_pairs={{0,4},{4,8},{8,12},{12,16},{16,20},{20,24},{24,28},{28,32},{32,36}... | collective-permute-start | bytes 3145736 | tf_op jit(solution)/shard_map/ppermute | solution.py:567
  10.0 27.1 %collective-permute-start.1 = (bf16[2,512,512]{2,1,0:T(8,128)(2,1)}, bf16[2,512,512]{2,1,0:T(8,128)(2,1)}, u32[]{:S(2)}, u32[]{:S(2)}) collective-permute-start(bf16[2,512,512]{2,1,0:T(8,128)(2,1)} %get-tuple-element.47), channel_id=1, source_target_pairs={{0,12},{4,0},{8,4},{12,8},{16,28},{20,16},{24,20},{28,24},{32,44},... | collective-permute-start | bytes 3145736 | tf_op jit(solution)/shard_map/ppermute | solution.py:79
  37.1 28.7 %collective-permute-start.3 = (bf16[1024,512]{1,0:T(8,128)(2,1)}, bf16[1024,512]{1,0:T(8,128)(2,1)}, u32[]{:S(2)}, u32[]{:S(2)}) collective-permute-start(bf16[1024,512]{1,0:T(8,128)(2,1)} %get-tuple-element.49), channel_id=1, source_target_pairs={{0,4},{4,8},{8,12},{12,16},{16,20},{20,24},{24,28},{28,32},{32,36}... | collective-permute-start | bytes 3145736 | tf_op jit(solution)/shard_map/ppermute | solution.py:66
  39.8 25.9 %collective-permute-start.6 = (bf16[1024,512]{1,0:T(8,128)(2,1)}, bf16[1024,512]{1,0:T(8,128)(2,1)}, u32[]{:S(2)}, u32[]{:S(2)}) collective-permute-start(bf16[1024,512]{1,0:T(8,128)(2,1)} %get-tuple-element.50.v1_ref), channel_id=1, source_target_pairs={{0,64},{1,65},{2,66},{3,67}} | collective-permute-start | bytes 3145736 | tf_op jit(solution)/shard_map/ppermute | solution.py:583
  41.5 27.5 %collective-permute-start.4 = (bf16[2,512,512]{2,1,0:T(8,128)(2,1)}, bf16[2,512,512]{2,1,0:T(8,128)(2,1)}, u32[]{:S(2)}, u32[]{:S(2)}) collective-permute-start(bf16[2,512,512]{2,1,0:T(8,128)(2,1)} %order.8.refs_2_.refs_5_), channel_id=1, source_target_pairs={{12,8},{0,12},{4,16},{8,20},{28,24},{16,28},{20,32},{24,36},{44,40... | collective-permute-start | bytes 3145736 | tf_op jit(solution)/shard_map/ppermute | solution.py:83
  69.0 9.5 %collective-permute-start.7 = (bf16[1024,1024]{1,0:T(8,128)(2,1)}, bf16[1024,1024]{1,0:T(8,128)(2,1)}, u32[]{:S(2)}, u32[]{:S(2)}) collective-permute-start(bf16[1024,1024]{1,0:T(8,128)(2,1)} %get-tuple-element.58.a_ref.g2), channel_id=1, source_target_pairs={{0,1},{1,0},{2,3},{3,2},{4,5},{5,4},{6,7},{7,6},{8,9},{9,8},{10,11... | collective-permute-start | bytes 6291464 | tf_op jit(solution)/shard_map/ppermute | solution.py:38
  69.0 50.2 %collective-permute-start.11 = (bf16[512,2048]{1,0:T(8,128)(2,1)}, bf16[512,2048]{1,0:T(8,128)(2,1)}, u32[]{:S(2)}, u32[]{:S(2)}) collective-permute-start(bf16[512,2048]{1,0:T(8,128)(2,1)} %get-tuple-element.66), channel_id=1, source_target_pairs={{0,2},{1,3},{2,0},{3,1},{4,6},{5,7},{6,4},{7,5},{8,10},{9,11},{10,... | collective-permute-start | bytes 6291464 | tf_op jit(solution)/shard_map/ppermute | solution.py:38
  78.5 62.8 %collective-permute-start.13 = (bf16[1024,512]{1,0:T(8,128)(2,1)}, bf16[1024,512]{1,0:T(8,128)(2,1)}, u32[]{:S(2)}, u32[]{:S(2)}) collective-permute-start(bf16[1024,512]{1,0:T(8,128)(2,1)} %get-tuple-element.56.out_ref.own_rows.own), channel_id=1, source_target_pairs={{0,2},{1,3},{2,0},{3,1},{4,6},{5,7},{6,4},{7,5},{8,10},{9,11},{10,... | collective-permute-start | bytes 3145736 | tf_op jit(solution)/shard_map/ppermute | solution.py:38
  100.3 46.1 %collective-permute-start.8 = (bf16[2,512,512]{2,1,0:T(8,128)(2,1)}, bf16[2,512,512]{2,1,0:T(8,128)(2,1)}, u32[]{:S(2)}, u32[]{:S(2)}) collective-permute-start(bf16[2,512,512]{2,1,0:T(8,128)(2,1)} %get-tuple-element.60), channel_id=1, source_target_pairs={{0,32},{1,33},{2,34},{3,35},{4,36},{5,37},{6,38},{7,39},{8,40},{9,... | collective-permute-start | bytes 3145736 | tf_op jit(solution)/shard_map/ppermute | solution.py:38
  104.2 49.7 %collective-permute-start.9 = (bf16[2,512,512]{2,1,0:T(8,128)(2,1)}, bf16[2,512,512]{2,1,0:T(8,128)(2,1)}, u32[]{:S(2)}, u32[]{:S(2)}) collective-permute-start(bf16[2,512,512]{2,1,0:T(8,128)(2,1)} %get-tuple-element.61), channel_id=1, source_target_pairs={{0,16},{1,17},{2,18},{3,19},{4,20},{5,21},{6,22},{7,23},{8,24},{9,... | collective-permute-start | bytes 3145736 | tf_op jit(solution)/shard_map/ppermute | solution.py:38
  107.1 46.8 %collective-permute-start.10 = (bf16[2,512,512]{2,1,0:T(8,128)(2,1)}, bf16[2,512,512]{2,1,0:T(8,128)(2,1)}, u32[]{:S(2)}, u32[]{:S(2)}) collective-permute-start(bf16[2,512,512]{2,1,0:T(8,128)(2,1)} %get-tuple-element.62), channel_id=1, source_target_pairs={{0,48},{1,49},{2,50},{3,51},{4,52},{5,53},{6,54},{7,55},{8,56},{9,... | collective-permute-start | bytes 3145736 | tf_op jit(solution)/shard_map/ppermute | solution.py:38
  119.2 34.7 %collective-permute-start.12 = (bf16[2,512,512]{2,1,0:T(8,128)(2,1)}, bf16[2,512,512]{2,1,0:T(8,128)(2,1)}, u32[]{:S(2)}, u32[]{:S(2)}) collective-permute-start(bf16[2,512,512]{2,1,0:T(8,128)(2,1)} %get-tuple-element.67), channel_id=1, source_target_pairs={{8,12},{12,0},{16,20},{20,24},{24,28},{28,16},{32,36},{36,40},{40,... | collective-permute-start | bytes 3145736 | tf_op jit(solution)/shard_map/ppermute | solution.py:79
  154.0 17.1 %collective-permute-start.14 = (bf16[4,512,1024]{2,1,0:T(8,128)(2,1)}, bf16[4,512,1024]{2,1,0:T(8,128)(2,1)}, u32[]{:S(2)}, u32[]{:S(2)}) collective-permute-start(bf16[4,512,1024]{2,1,0:T(8,128)(2,1)} %get-tuple-element.72), channel_id=1, source_target_pairs={{0,1},{1,0},{2,3},{3,2},{4,5},{5,4},{6,7},{7,6},{8,9},{9,8},{10,11... | collective-permute-start | bytes 12582920 | tf_op jit(solution)/shard_map/ppermute | solution.py:38
  154.0 69.3 %collective-permute-start.15 = (bf16[2,1024,512]{2,1,0:T(8,128)(2,1)}, bf16[2,1024,512]{2,1,0:T(8,128)(2,1)}, u32[]{:S(2)}, u32[]{:S(2)}) collective-permute-start(bf16[2,1024,512]{2,1,0:T(8,128)(2,1)} %get-tuple-element.78), channel_id=1, source_target_pairs={{4,0},{8,4},{12,8},{16,12},{20,16},{24,20},{28,24},{32,28},{36,32}... | collective-permute-start | bytes 6291464 | tf_op jit(solution)/shard_map/ppermute | solution.py:66
  156.4 67.0 %collective-permute-start.16 = (bf16[2,512,512]{2,1,0:T(8,128)(2,1)}, bf16[2,512,512]{2,1,0:T(8,128)(2,1)}, u32[]{:S(2)}, u32[]{:S(2)}) collective-permute-start(bf16[2,512,512]{2,1,0:T(8,128)(2,1)} %get-tuple-element.79), channel_id=1, source_target_pairs={{12,0},{0,4},{20,8},{24,12},{28,16},{16,20},{36,24},{40,28},{44,32... | collective-permute-start | bytes 3145736 | tf_op jit(solution)/shard_map/ppermute | solution.py:83
  164.7 24.6 %collective-permute-start.17 = (bf16[2,512,128]{2,1,0:T(8,128)(2,1)}, bf16[2,512,128]{2,1,0:T(8,128)(2,1)}, u32[]{:S(2)}, u32[]{:S(2)}) collective-permute-start(bf16[2,512,128]{2,1,0:T(8,128)(2,1)} %get-tuple-element.80), channel_id=1, source_target_pairs={{0,8},{1,9},{2,10},{3,11},{4,12},{5,13},{6,14},{7,15},{8,0},{9,1},... | collective-permute-start | bytes 786440 | tf_op jit(solution)/shard_map/ppermute | solution.py:38
  171.0 27.3 %collective-permute-start.18 = (bf16[2,512,128]{2,1,0:T(8,128)(2,1)}, bf16[2,512,128]{2,1,0:T(8,128)(2,1)}, u32[]{:S(2)}, u32[]{:S(2)}) collective-permute-start(bf16[2,512,128]{2,1,0:T(8,128)(2,1)} %get-tuple-element.81), channel_id=1, source_target_pairs={{0,4},{1,5},{2,6},{3,7},{4,8},{5,9},{6,10},{7,11},{8,12},{9,13},{1... | collective-permute-start | bytes 786440 | tf_op jit(solution)/shard_map/ppermute | solution.py:38
  171.1 44.5 %collective-permute-start.19 = (bf16[2,512,128]{2,1,0:T(8,128)(2,1)}, bf16[2,512,128]{2,1,0:T(8,128)(2,1)}, u32[]{:S(2)}, u32[]{:S(2)}) collective-permute-start(bf16[2,512,128]{2,1,0:T(8,128)(2,1)} %get-tuple-element.82), channel_id=1, source_target_pairs={{0,12},{1,13},{2,14},{3,15},{4,0},{5,1},{6,2},{7,3},{8,4},{9,5},{1... | collective-permute-start | bytes 786440 | tf_op jit(solution)/shard_map/ppermute | solution.py:38
  218.2 10.4 %collective-permute-start.20 = (bf16[512,128]{1,0:T(8,128)(2,1)}, bf16[512,128]{1,0:T(8,128)(2,1)}, u32[]{:S(2)}, u32[]{:S(2)}) collective-permute-start(bf16[512,128]{1,0:T(8,128)(2,1)} %get-tuple-element.86), channel_id=1, source_target_pairs={{0,64},{1,65},{2,66},{3,67},{4,68},{5,69},{6,70},{7,71},{8,72},{9,... | collective-permute-start | bytes 393224 | tf_op jit(solution)/shard_map/ppermute | solution.py:38
